TPU v7x, 256 devices: a whole 4x4x8 slice. The times are simulated.
256 devices in a mesh: blk: 64 (over z, y_hi, x), mp: 4 (over y_lo, core).
Axes of the slice: x: 4, y: 4 (y_hi: 2, y_lo: 2; y = y_hi * 2 + y_lo), z: 8, core: 2. Of those that a mesh axis runs over, the one named last changes fastest.
Arguments:
- struct_feats: bfloat16 [32768, 1024], P('blk', 'mp'), may hold values from -10 to 10
- seq_feats: bfloat16 [32768, 1280], P('blk', 'mp'), may hold values from -10 to 10
- struct_proj: bfloat16 [1024, 512], P('mp'), may hold values from -6 to 6
- seq_proj: bfloat16 [1280, 512], P('mp'), may hold values from -6 to 6
- cluster_ids: int32 [32768], P('blk'), may hold values from 0 to 8191
- hard_owner: int32 [32768, 16, 1], P('blk'), may hold values from 0 to 63; in each aligned block of 2048 rows (0 to 2047, 2048 to 4095, ..., all dimensions but the last counted through in order) at most 64 rows name the same one
- hard_local: int32 [32768, 16], P('blk'), may hold values from 0 to 511
- hard_valid: int32 [32768, 16], P(('blk', 'mp')), may hold values 0 or 1
Outputs:
- seq_loss: float32 [32768], P('blk')
- struct_loss: float32 [32768], P(('blk', 'mp'))
- hard_loss: float32 [32768], P(('blk', 'mp'))
Inputs may be any that keep to these rules, and one draw needn't show every extreme that they name: `hard_owner`: among the 2048 entries of each aligned block of 128 rows, no group index is named more than 64 times, and in some block one is named exactly 64 times.
All inputs are finite; a program needn't handle non-finite values. No bound on the sum of `hard_valid` on one device may be relied on, other than what follows from the above.
Results may differ from a plain program's by a relative error of at most 0.0054.
Values may be sent and summed in bfloat16 or wider, within the bound.
No kernel may reach another device: no remote copies, remote signals or barrier semaphores. Data moves between devices by JAX's collectives and lax.ppermute only.
A program may use at most 64 MiB of HBM per device.

v0:
```python
import jax
import jax.numpy as jnp
from jax import lax
from jax.sharding import PartitionSpec as P

LOGIT_SCALE = 14.285714285714286
EPSILON = 1e-06


def from_behind(value, axis, steps):
    count = lax.axis_size(axis)
    pairs = [(source, (source + steps) % count) for source in range(count)]
    return lax.ppermute(value, axis, pairs)


def normalize(raw_values):
    total = jnp.sum(raw_values * raw_values, axis=1, keepdims=True)
    return (raw_values * lax.rsqrt(total + EPSILON)).astype(jnp.bfloat16)


def visit_block(queries, query_labels, visitor, visitor_labels):
    logits = LOGIT_SCALE * jnp.einsum(
        "re,ce->rc", queries, visitor, preferred_element_type=jnp.float32
    )
    weights = jnp.exp(logits)
    matched = (query_labels[:, None] == visitor_labels[None, :]).astype(jnp.float32)
    kept = weights * matched
    return (
        logits,
        (jnp.sum(weights, axis=1), jnp.sum(kept, axis=1)),
        (jnp.sum(weights, axis=0), jnp.sum(kept, axis=0)),
    )


def per_device(
    struct_feats, seq_feats, struct_proj, seq_proj, cluster_ids, hard_owner, hard_local, hard_valid
):
    row_count = struct_feats.shape[0]
    groups = lax.axis_size("mp")
    blocks = lax.axis_size("blk")
    share_rows = row_count // groups
    mp_index = lax.axis_index("mp")
    slots = hard_local.shape[1]
    seq_raw = lax.psum(jnp.dot(seq_feats, seq_proj, preferred_element_type=jnp.float32), "mp")
    queries = normalize(seq_raw)
    own_struct = normalize(
        lax.psum_scatter(
            jnp.dot(struct_feats, struct_proj, preferred_element_type=jnp.float32),
            "mp",
            scatter_dimension=0,
            tiled=True,
        )
    )
    own_labels = lax.dynamic_slice_in_dim(cluster_ids, mp_index * share_rows, share_rows, 0)
    zero_rows = jnp.zeros((row_count,), jnp.float32)
    zero_picked = jnp.zeros((row_count, slots), jnp.float32)
    group_owner = hard_owner[:, :, 0]

    def cycle_step(step_index, carried):
        visitor, visitor_labels, row_total, row_matched, col_total, col_matched, picked = carried
        logits, (add_total, add_matched), (col_add, col_add_matched) = visit_block(
            queries, cluster_ids, visitor, visitor_labels
        )
        col_total, col_matched = from_behind(
            (col_total + col_add, col_matched + col_add_matched), "blk", 1
        )
        visitor, visitor_labels = from_behind((visitor, visitor_labels), "blk", 1)
        return (
            visitor,
            visitor_labels,
            row_total + add_total,
            row_matched + add_matched,
            col_total,
            col_matched,
            picked,
        )

    zero_cols = jnp.zeros((share_rows,), jnp.float32)
    final = lax.fori_loop(
        0,
        blocks,
        cycle_step,
        (own_struct, own_labels, zero_rows, zero_rows, zero_cols, zero_cols, zero_picked),
    )
    row_total, row_matched, col_total, col_matched, picked = (
        final[2],
        final[3],
        final[4],
        final[5],
        final[6],
    )
    row_total, row_matched = lax.psum((row_total, row_matched), "mp")
    seq_loss = jnp.log(row_total) - jnp.log(row_matched)
    struct_loss = jnp.log(col_total) - jnp.log(col_matched)
    hard_queries = lax.dynamic_slice_in_dim(queries, mp_index * share_rows, share_rows, 0)
    group_struct = lax.all_gather(own_struct, "mp", axis=0, tiled=True)
    capacity = max(2, 2 * share_rows * slots // blocks)
    owners = lax.dynamic_slice_in_dim(group_owner, mp_index * share_rows, share_rows, 0).reshape(-1)
    local_rows = lax.dynamic_slice_in_dim(hard_local, mp_index * share_rows, share_rows, 0).reshape(
        -1
    )
    onehot = (owners[:, None] == jnp.arange(blocks, dtype=jnp.int32)[None, :]).astype(jnp.int32)
    slot_index = jnp.sum((jnp.cumsum(onehot, axis=0) - onehot) * onehot, axis=1)
    requests = jnp.zeros((blocks, capacity), jnp.int32).at[owners, slot_index].set(local_rows)
    found_rows = group_struct[
        lax.all_to_all(requests, "blk", split_axis=0, concat_axis=0, tiled=True)
    ]
    replies = lax.all_to_all(found_rows, "blk", split_axis=0, concat_axis=0, tiled=True)
    fetched_rows = replies[owners, slot_index].reshape(share_rows, slots, -1)
    hard_logits = LOGIT_SCALE * jnp.einsum(
        "ske,se->sk", fetched_rows, hard_queries, preferred_element_type=jnp.float32
    )
    self_logits = LOGIT_SCALE * jnp.einsum(
        "se,se->s", hard_queries, own_struct, preferred_element_type=jnp.float32
    )
    extra = jnp.sum(hard_valid.astype(jnp.float32) * jnp.exp(hard_logits), axis=1)
    hard_loss = jnp.log(jnp.exp(self_logits) + extra) - self_logits
    return (seq_loss, struct_loss, hard_loss)


def solution(mesh):
    placed = (
        P("blk", "mp"),
        P("blk", "mp"),
        P("mp", None),
        P("mp", None),
        P("blk"),
        P("blk", None, None),
        P("blk", None),
        P(("blk", "mp"), None),
    )
    return jax.shard_map(
        per_device,
        mesh=mesh,
        in_specs=placed,
        out_specs=(P("blk"), P(("blk", "mp")), P(("blk", "mp"))),
        check_vma=False,
    )
```

profile of v0, /device:TPU:1, one launch (start us, length us, event | category | flops | bytes accessed | tf_op | source)
XLA Modules:
  0.0 970.4 jit_solution(14556708762841688830)
XLA Ops:
  13.1 18.1 %reduce-window.6 = s32[64,16,128]{2,1,0:T(8,128)S(1)} reduce-window(s32[64,16,128]{2,1,0:T(8,128)S(1)} %fusion.6, s32[]{:T(128)} %constant.16.clone.1), window={size=1x1x128 pad=0_0x0_0x127_0}, to_apply=%region_12.0 | reduce-window | flops 16646144 | bytes 1048580 | tf_op jit(solution)/shard_map/reduce-window
  33.7 8.1 scatter_custom_fusion
  42.5 15.1 %all-to-all-start = ((s32[64,1,64]{2,1,0:T(1,128)}), s32[64,1,64]{2,1,0:T(1,128)S(1)}, u32[]{:S(2)}, u32[]{:S(2)}) async-start(s32[64,1,64]{2,1,0:T(1,128)} %all_to_all.11), calls=%async_computation.1 | async-start | bytes 65536 | tf_op jit(solution)/shard_map/all_to_all | solution.py:106
  57.7 10.6 %all-to-all-done = s32[64,1,64]{2,1,0:T(1,128)S(1)} async-done(((s32[64,1,64]{2,1,0:T(1,128)}), s32[64,1,64]{2,1,0:T(1,128)S(1)}, u32[]{:S(2)}, u32[]{:S(2)}) %all-to-all-start) | async-done | bytes 16416 | tf_op jit(solution)/shard_map/all_to_all | solution.py:106
  71.2 17.1 %reduce-scatter.2.cloned.1.call-done = f32[128,512]{1,0:T(8,128)} async-done(((f32[512,512]{1,0:T(8,128)}), f32[128,512]{1,0:T(8,128)}) %reduce-scatter.2.cloned.1.call-update) | async-done | bytes 262160 | tf_op jit(solution)/shard_map/reduce_scatter | solution.py:47
  97.8 17.3 %gather_fusion = bf16[4096,512]{1,0:T(8,128)(2,1)} fusion(bf16[512,512]{1,0:T(8,128)(2,1)S(1)} %all_gather.3, s32[4096]{0:T(1024)S(1)} %broadcast_clamp_fusion), kind=kCustom, calls=%fused_computation | custom fusion | bytes 8404992 | tf_op jit(solution)/shard_map/gather | solution.py:105
  115.1 12.7 %all-to-all-start.1 = ((bf16[64,64,512]{2,1,0:T(8,128)(2,1)}), bf16[64,64,512]{2,1,0:T(8,128)(2,1)}, u32[]{:S(2)}, u32[]{:S(2)}) async-start(bf16[64,64,512]{2,1,0:T(8,128)(2,1)} %bitcast.56), calls=%async_computation.2 | async-start | bytes 8388608 | tf_op jit(solution)/shard_map/all_to_all | solution.py:108
  127.8 730.3 %while.21 = (s32[]{:T(128)}, bf16[128,512]{1,0:T(8,128)(2,1)S(1)}, s32[128]{0:T(128)S(1)}, f32[512]{0:T(512)S(1)}, f32[512]{0:T(512)S(1)}, /*index=5*/f32[128]{0...) while((s32[]{:T(128)}, bf16[128,512]{1,0:T(8,128)(2,1)S(1)}, ...), condition=%wide.region_9.0_spmd.clone, body=%wide.region_4.0_spmd.clone.sunk | while | flops 67568640 | bytes 1472279 | solution.py:79
  134.3 85.5 %collective-permute-done.1 = s32[128]{0:T(128)S(1)} collective-permute-done((s32[128]{0:T(128)S(1)}, s32[128]{0:T(128)S(1)}, u32[]{:S(2)}, u32[]{:S(2)}) %collective-permute-start.1) | collective-permute-done | bytes 544 | tf_op jit(solution)/shard_map/while/body/eval_jaxpr/ppermute | solution.py:13
  219.8 7.4 collective-permute-done.3
  267.3 7.3 collective-permute-done.1
  286.9 7.3 collective-permute-done.1
  296.7 7.6 collective-permute-done.1
  318.2 7.3 collective-permute-done.1
  328.4 7.3 collective-permute-done.1
  348.0 7.3 collective-permute-done.1
  357.8 7.3 collective-permute-done.1
  397.0 7.6 collective-permute-done.1
  407.5 7.3 collective-permute-done.1
  448.3 7.3 collective-permute-done.1
  487.5 7.3 collective-permute-done.1
  497.3 7.6 collective-permute-done.1
  558.2 7.3 collective-permute-done.1
  587.6 7.6 collective-permute-done.1
  597.4 7.6 collective-permute-done.1
  658.1 7.3 collective-permute-done.1
  667.9 7.3 collective-permute-done.1
  687.5 7.6 collective-permute-done.1
  729.1 7.3 collective-permute-done.1
  787.9 7.6 collective-permute-done.1
  858.2 76.8 %all-reduce = (f32[512]{0:T(512)S(1)}, f32[512]{0:T(512)S(1)}) all-reduce(f32[512]{0:T(512)S(1)} %get-tuple-element.54, f32[512]{0:T(512)S(1)} %get-tuple-element.53), channel_id=1, replica_groups=mesh['blk'=64,'mp'=4] {'mp'}, use_global_device_ids=true, to_apply=%region_11.0 | all-reduce | flops 1024 | bytes 8192 | tf_op jit(solution)/shard_map/psum | solution.py:92
  935.5 26.6 %gather_fusion.1 = bf16[2048,512]{1,0:T(8,128)(2,1)S(1)} fusion(bf16[64,64,512]{2,1,0:T(8,128)(2,1)} %all-to-all-done.1, s32[2048]{0:T(1024)S(1)} %bitcast.55), kind=kCustom, calls=%fused_computation.1 | custom fusion | bytes 4210688 | tf_op jit(solution)/shard_map/gather | solution.py:109
  (934 shorter events, 507.8 us)
Async XLA Ops:
  7.2 61.2 %all-reduce.3.cloned.1.call-start = ((), (), s32[]{:S(2)}) async-start(), calls=%async_computation.4 | async-start | bytes 2097152 | tf_op jit(solution)/shard_map/psum | solution.py:44
  10.6 77.7 %reduce-scatter.2.cloned.1.call-start = ((), (), s32[]{:S(2)}) async-start(), calls=%async_computation.3 | async-start | bytes 1310720 | tf_op jit(solution)/shard_map/reduce_scatter | solution.py:47
  42.5 25.9 %all-to-all-start = ((s32[64,1,64]{2,1,0:T(1,128)}), s32[64,1,64]{2,1,0:T(1,128)S(1)}, u32[]{:S(2)}, u32[]{:S(2)}) async-start(s32[64,1,64]{2,1,0:T(1,128)} %all_to_all.11), calls=%async_computation.1 | async-start | bytes 65536 | tf_op jit(solution)/shard_map/all_to_all | solution.py:106
  115.1 820.4 %all-to-all-start.1 = ((bf16[64,64,512]{2,1,0:T(8,128)(2,1)}), bf16[64,64,512]{2,1,0:T(8,128)(2,1)}, u32[]{:S(2)}, u32[]{:S(2)}) async-start(bf16[64,64,512]{2,1,0:T(8,128)(2,1)} %bitcast.56), calls=%async_computation.2 | async-start | bytes 8388608 | tf_op jit(solution)/shard_map/all_to_all | solution.py:108
  127.9 91.9 %collective-permute-start.1 = (s32[128]{0:T(128)S(1)}, s32[128]{0:T(128)S(1)}, u32[]{:S(2)}, u32[]{:S(2)}) collective-permute-start(s32[128]{0:T(128)S(1)} %copy.39), channel_id=1, source_target_pairs={{0,4},{4,8},{8,12},{12,16},{16,20},{20,24},{24,28},{28,32},{32,36}... | collective-permute-start | bytes 1544 | tf_op jit(solution)/shard_map/while/body/eval_jaxpr/ppermute | solution.py:13
  128.9 98.3 %collective-permute-start = (bf16[128,512]{1,0:T(8,128)(2,1)S(1)}, bf16[128,512]{1,0:T(8,128)(2,1)S(1)}, u32[]{:S(2)}, u32[]{:S(2)}) collective-permute-start(bf16[128,512]{1,0:T(8,128)(2,1)S(1)} %copy.38), channel_id=1, source_target_pairs={{0,4},{4,8},{8,12},{12,16},{16,20},{20,24},{24,28},{28,32},{32,36}... | collective-permute-start | bytes 393224 | tf_op jit(solution)/shard_map/while/body/eval_jaxpr/ppermute | solution.py:13
  130.6 96.6 %collective-permute-start.3 = (f32[128]{0:T(128)S(1)}, f32[128]{0:T(128)S(1)}, u32[]{:S(2)}, u32[]{:S(2)}) collective-permute-start(f32[128]{0:T(128)S(1)} %add.134), channel_id=1, source_target_pairs={{0,4},{4,8},{8,12},{12,16},{16,20},{20,24},{24,28},{28,32},{32,36}... | collective-permute-start | bytes 1544 | tf_op jit(solution)/shard_map/while/body/eval_jaxpr/ppermute | solution.py:13
  131.6 95.7 %collective-permute-start.2 = (f32[128]{0:T(128)S(1)}, f32[128]{0:T(128)S(1)}, u32[]{:S(2)}, u32[]{:S(2)}) collective-permute-start(f32[128]{0:T(128)S(1)} %add.133), channel_id=1, source_target_pairs={{0,4},{4,8},{8,12},{12,16},{16,20},{20,24},{24,28},{28,32},{32,36}... | collective-permute-start | bytes 1544 | tf_op jit(solution)/shard_map/while/body/eval_jaxpr/ppermute | solution.py:13
  295.9 10.2 %collective-permute-start = (bf16[128,512]{1,0:T(8,128)(2,1)S(1)}, bf16[128,512]{1,0:T(8,128)(2,1)S(1)}, u32[]{:S(2)}, u32[]{:S(2)}) collective-permute-start(bf16[128,512]{1,0:T(8,128)(2,1)S(1)} %copy.38), channel_id=1, source_target_pairs={{0,4},{4,8},{8,12},{12,16},{16,20},{20,24},{24,28},{28,32},{32,36}... | collective-permute-start | bytes 393224 | tf_op jit(solution)/shard_map/while/body/eval_jaxpr/ppermute | solution.py:13
  306.3 11.1 %collective-permute-start = (bf16[128,512]{1,0:T(8,128)(2,1)S(1)}, bf16[128,512]{1,0:T(8,128)(2,1)S(1)}, u32[]{:S(2)}, u32[]{:S(2)}) collective-permute-start(bf16[128,512]{1,0:T(8,128)(2,1)S(1)} %copy.38), channel_id=1, source_target_pairs={{0,4},{4,8},{8,12},{12,16},{16,20},{20,24},{24,28},{28,32},{32,36}... | collective-permute-start | bytes 393224 | tf_op jit(solution)/shard_map/while/body/eval_jaxpr/ppermute | solution.py:13
  306.8 10.5 %collective-permute-start.3 = (f32[128]{0:T(128)S(1)}, f32[128]{0:T(128)S(1)}, u32[]{:S(2)}, u32[]{:S(2)}) collective-permute-start(f32[128]{0:T(128)S(1)} %add.134), channel_id=1, source_target_pairs={{0,4},{4,8},{8,12},{12,16},{16,20},{20,24},{24,28},{28,32},{32,36}... | collective-permute-start | bytes 1544 | tf_op jit(solution)/shard_map/while/body/eval_jaxpr/ppermute | solution.py:13
  306.9 10.4 %collective-permute-start.2 = (f32[128]{0:T(128)S(1)}, f32[128]{0:T(128)S(1)}, u32[]{:S(2)}, u32[]{:S(2)}) collective-permute-start(f32[128]{0:T(128)S(1)} %add.133), channel_id=1, source_target_pairs={{0,4},{4,8},{8,12},{12,16},{16,20},{20,24},{24,28},{28,32},{32,36}... | collective-permute-start | bytes 1544 | tf_op jit(solution)/shard_map/while/body/eval_jaxpr/ppermute | solution.py:13
  317.4 10.1 %collective-permute-start = (bf16[128,512]{1,0:T(8,128)(2,1)S(1)}, bf16[128,512]{1,0:T(8,128)(2,1)S(1)}, u32[]{:S(2)}, u32[]{:S(2)}) collective-permute-start(bf16[128,512]{1,0:T(8,128)(2,1)S(1)} %copy.38), channel_id=1, source_target_pairs={{0,4},{4,8},{8,12},{12,16},{16,20},{20,24},{24,28},{28,32},{32,36}... | collective-permute-start | bytes 393224 | tf_op jit(solution)/shard_map/while/body/eval_jaxpr/ppermute | solution.py:13
  396.3 10.3 %collective-permute-start = (bf16[128,512]{1,0:T(8,128)(2,1)S(1)}, bf16[128,512]{1,0:T(8,128)(2,1)S(1)}, u32[]{:S(2)}, u32[]{:S(2)}) collective-permute-start(bf16[128,512]{1,0:T(8,128)(2,1)S(1)} %copy.38), channel_id=1, source_target_pairs={{0,4},{4,8},{8,12},{12,16},{16,20},{20,24},{24,28},{28,32},{32,36}... | collective-permute-start | bytes 393224 | tf_op jit(solution)/shard_map/while/body/eval_jaxpr/ppermute | solution.py:13
  406.7 11.0 %collective-permute-start = (bf16[128,512]{1,0:T(8,128)(2,1)S(1)}, bf16[128,512]{1,0:T(8,128)(2,1)S(1)}, u32[]{:S(2)}, u32[]{:S(2)}) collective-permute-start(bf16[128,512]{1,0:T(8,128)(2,1)S(1)} %copy.38), channel_id=1, source_target_pairs={{0,4},{4,8},{8,12},{12,16},{16,20},{20,24},{24,28},{28,32},{32,36}... | collective-permute-start | bytes 393224 | tf_op jit(solution)/shard_map/while/body/eval_jaxpr/ppermute | solution.py:13
  407.3 10.5 %collective-permute-start.3 = (f32[128]{0:T(128)S(1)}, f32[128]{0:T(128)S(1)}, u32[]{:S(2)}, u32[]{:S(2)}) collective-permute-start(f32[128]{0:T(128)S(1)} %add.134), channel_id=1, source_target_pairs={{0,4},{4,8},{8,12},{12,16},{16,20},{20,24},{24,28},{28,32},{32,36}... | collective-permute-start | bytes 1544 | tf_op jit(solution)/shard_map/while/body/eval_jaxpr/ppermute | solution.py:13
  407.4 10.4 %collective-permute-start.2 = (f32[128]{0:T(128)S(1)}, f32[128]{0:T(128)S(1)}, u32[]{:S(2)}, u32[]{:S(2)}) collective-permute-start(f32[128]{0:T(128)S(1)} %add.133), channel_id=1, source_target_pairs={{0,4},{4,8},{8,12},{12,16},{16,20},{20,24},{24,28},{28,32},{32,36}... | collective-permute-start | bytes 1544 | tf_op jit(solution)/shard_map/while/body/eval_jaxpr/ppermute | solution.py:13
  496.6 10.4 %collective-permute-start = (bf16[128,512]{1,0:T(8,128)(2,1)S(1)}, bf16[128,512]{1,0:T(8,128)(2,1)S(1)}, u32[]{:S(2)}, u32[]{:S(2)}) collective-permute-start(bf16[128,512]{1,0:T(8,128)(2,1)S(1)} %copy.38), channel_id=1, source_target_pairs={{0,4},{4,8},{8,12},{12,16},{16,20},{20,24},{24,28},{28,32},{32,36}... | collective-permute-start | bytes 393224 | tf_op jit(solution)/shard_map/while/body/eval_jaxpr/ppermute | solution.py:13
  507.1 10.9 %collective-permute-start = (bf16[128,512]{1,0:T(8,128)(2,1)S(1)}, bf16[128,512]{1,0:T(8,128)(2,1)S(1)}, u32[]{:S(2)}, u32[]{:S(2)}) collective-permute-start(bf16[128,512]{1,0:T(8,128)(2,1)S(1)} %copy.38), channel_id=1, source_target_pairs={{0,4},{4,8},{8,12},{12,16},{16,20},{20,24},{24,28},{28,32},{32,36}... | collective-permute-start | bytes 393224 | tf_op jit(solution)/shard_map/while/body/eval_jaxpr/ppermute | solution.py:13
  507.7 10.3 %collective-permute-start.3 = (f32[128]{0:T(128)S(1)}, f32[128]{0:T(128)S(1)}, u32[]{:S(2)}, u32[]{:S(2)}) collective-permute-start(f32[128]{0:T(128)S(1)} %add.134), channel_id=1, source_target_pairs={{0,4},{4,8},{8,12},{12,16},{16,20},{20,24},{24,28},{28,32},{32,36}... | collective-permute-start | bytes 1544 | tf_op jit(solution)/shard_map/while/body/eval_jaxpr/ppermute | solution.py:13
  507.8 10.2 %collective-permute-start.2 = (f32[128]{0:T(128)S(1)}, f32[128]{0:T(128)S(1)}, u32[]{:S(2)}, u32[]{:S(2)}) collective-permute-start(f32[128]{0:T(128)S(1)} %add.133), channel_id=1, source_target_pairs={{0,4},{4,8},{8,12},{12,16},{16,20},{20,24},{24,28},{28,32},{32,36}... | collective-permute-start | bytes 1544 | tf_op jit(solution)/shard_map/while/body/eval_jaxpr/ppermute | solution.py:13
  596.7 10.7 %collective-permute-start = (bf16[128,512]{1,0:T(8,128)(2,1)S(1)}, bf16[128,512]{1,0:T(8,128)(2,1)S(1)}, u32[]{:S(2)}, u32[]{:S(2)}) collective-permute-start(bf16[128,512]{1,0:T(8,128)(2,1)S(1)} %copy.38), channel_id=1, source_target_pairs={{0,4},{4,8},{8,12},{12,16},{16,20},{20,24},{24,28},{28,32},{32,36}... | collective-permute-start | bytes 393224 | tf_op jit(solution)/shard_map/while/body/eval_jaxpr/ppermute | solution.py:13
  597.2 10.1 %collective-permute-start.3 = (f32[128]{0:T(128)S(1)}, f32[128]{0:T(128)S(1)}, u32[]{:S(2)}, u32[]{:S(2)}) collective-permute-start(f32[128]{0:T(128)S(1)} %add.134), channel_id=1, source_target_pairs={{0,4},{4,8},{8,12},{12,16},{16,20},{20,24},{24,28},{28,32},{32,36}... | collective-permute-start | bytes 1544 | tf_op jit(solution)/shard_map/while/body/eval_jaxpr/ppermute | solution.py:13
  607.4 10.6 %collective-permute-start = (bf16[128,512]{1,0:T(8,128)(2,1)S(1)}, bf16[128,512]{1,0:T(8,128)(2,1)S(1)}, u32[]{:S(2)}, u32[]{:S(2)}) collective-permute-start(bf16[128,512]{1,0:T(8,128)(2,1)S(1)} %copy.38), channel_id=1, source_target_pairs={{0,4},{4,8},{8,12},{12,16},{16,20},{20,24},{24,28},{28,32},{32,36}... | collective-permute-start | bytes 393224 | tf_op jit(solution)/shard_map/while/body/eval_jaxpr/ppermute | solution.py:13
  696.7 11.1 %collective-permute-start = (bf16[128,512]{1,0:T(8,128)(2,1)S(1)}, bf16[128,512]{1,0:T(8,128)(2,1)S(1)}, u32[]{:S(2)}, u32[]{:S(2)}) collective-permute-start(bf16[128,512]{1,0:T(8,128)(2,1)S(1)} %copy.38), channel_id=1, source_target_pairs={{0,4},{4,8},{8,12},{12,16},{16,20},{20,24},{24,28},{28,32},{32,36}... | collective-permute-start | bytes 393224 | tf_op jit(solution)/shard_map/while/body/eval_jaxpr/ppermute | solution.py:13
  697.3 10.6 %collective-permute-start.3 = (f32[128]{0:T(128)S(1)}, f32[128]{0:T(128)S(1)}, u32[]{:S(2)}, u32[]{:S(2)}) collective-permute-start(f32[128]{0:T(128)S(1)} %add.134), channel_id=1, source_target_pairs={{0,4},{4,8},{8,12},{12,16},{16,20},{20,24},{24,28},{28,32},{32,36}... | collective-permute-start | bytes 1544 | tf_op jit(solution)/shard_map/while/body/eval_jaxpr/ppermute | solution.py:13
  697.4 10.5 %collective-permute-start.2 = (f32[128]{0:T(128)S(1)}, f32[128]{0:T(128)S(1)}, u32[]{:S(2)}, u32[]{:S(2)}) collective-permute-start(f32[128]{0:T(128)S(1)} %add.133), channel_id=1, source_target_pairs={{0,4},{4,8},{8,12},{12,16},{16,20},{20,24},{24,28},{28,32},{32,36}... | collective-permute-start | bytes 1544 | tf_op jit(solution)/shard_map/while/body/eval_jaxpr/ppermute | solution.py:13
  708.0 10.4 %collective-permute-start = (bf16[128,512]{1,0:T(8,128)(2,1)S(1)}, bf16[128,512]{1,0:T(8,128)(2,1)S(1)}, u32[]{:S(2)}, u32[]{:S(2)}) collective-permute-start(bf16[128,512]{1,0:T(8,128)(2,1)S(1)} %copy.38), channel_id=1, source_target_pairs={{0,4},{4,8},{8,12},{12,16},{16,20},{20,24},{24,28},{28,32},{32,36}... | collective-permute-start | bytes 393224 | tf_op jit(solution)/shard_map/while/body/eval_jaxpr/ppermute | solution.py:13
  797.3 11.3 %collective-permute-start = (bf16[128,512]{1,0:T(8,128)(2,1)S(1)}, bf16[128,512]{1,0:T(8,128)(2,1)S(1)}, u32[]{:S(2)}, u32[]{:S(2)}) collective-permute-start(bf16[128,512]{1,0:T(8,128)(2,1)S(1)} %copy.38), channel_id=1, source_target_pairs={{0,4},{4,8},{8,12},{12,16},{16,20},{20,24},{24,28},{28,32},{32,36}... | collective-permute-start | bytes 393224 | tf_op jit(solution)/shard_map/while/body/eval_jaxpr/ppermute | solution.py:13
  797.8 10.7 %collective-permute-start.3 = (f32[128]{0:T(128)S(1)}, f32[128]{0:T(128)S(1)}, u32[]{:S(2)}, u32[]{:S(2)}) collective-permute-start(f32[128]{0:T(128)S(1)} %add.134), channel_id=1, source_target_pairs={{0,4},{4,8},{8,12},{12,16},{16,20},{20,24},{24,28},{28,32},{32,36}... | collective-permute-start | bytes 1544 | tf_op jit(solution)/shard_map/while/body/eval_jaxpr/ppermute | solution.py:13
  797.9 10.6 %collective-permute-start.2 = (f32[128]{0:T(128)S(1)}, f32[128]{0:T(128)S(1)}, u32[]{:S(2)}, u32[]{:S(2)}) collective-permute-start(f32[128]{0:T(128)S(1)} %add.133), channel_id=1, source_target_pairs={{0,4},{4,8},{8,12},{12,16},{16,20},{20,24},{24,28},{28,32},{32,36}... | collective-permute-start | bytes 1544 | tf_op jit(solution)/shard_map/while/body/eval_jaxpr/ppermute | solution.py:13
  808.6 10.3 %collective-permute-start = (bf16[128,512]{1,0:T(8,128)(2,1)S(1)}, bf16[128,512]{1,0:T(8,128)(2,1)S(1)}, u32[]{:S(2)}, u32[]{:S(2)}) collective-permute-start(bf16[128,512]{1,0:T(8,128)(2,1)S(1)} %copy.38), channel_id=1, source_target_pairs={{0,4},{4,8},{8,12},{12,16},{16,20},{20,24},{24,28},{28,32},{32,36}... | collective-permute-start | bytes 393224 | tf_op jit(solution)/shard_map/while/body/eval_jaxpr/ppermute | solution.py:13
  (234 other events, 2118.1 us)
Sparse Core Ops, SparseCore 0:
  10.8 50.7 all-reduce.2
  64.3 23.9 reduce-scatter.1
where the time goes:
time: 971 us; the launch traced here: 970 us
  waiting for transfers between devices  697 us (72%)
  blocking collectives  84.1 us (9%)
  local copies, waits for them, and re-layouts  57.1 us (6%)
  starting transfers between devices  54.8 us (6%)
  matrix products  32 us (3%)
  other arithmetic  26.5 us (3%)
  between operations  14.3 us (1%)
    ppermute x256, waiting for transfers between devices, from_behind(): return lax.ppermute(value, axis, pairs)  670 us
    psum x1, blocking collectives, per_device(): row_total, row_matched = lax.psum((row_total, row_matched), 'mp')  76.8 us
    dot_general x64, matrix products, visit_block(): jnp.einsum('re,ce->rc', queries, visitor, preferred_element_type=jnp.floa...  27.6 us
    ppermute x256, starting transfers between devices, from_behind(): return lax.ppermute(value, axis, pairs)  26.9 us
    gather x1, local copies, waits for them, and re-layouts, per_device(): fetched_rows = replies[owners, slot_index].reshape(share_rows, slots, -1)  26.6 us
  transfers between devices with their start and end apart: 260, of which 130 were waited for; matrix products, arithmetic and copies ran while one was open for 7% of the time, Pallas kernels for 0%

commit v1 on v0

v1 whole, which is shorter than its diff:
```python
import math

import jax
import jax.numpy as jnp
from jax import lax
from jax.experimental import pallas as pl
from jax.experimental.pallas import tpu as pltpu
from jax.sharding import Mesh, PartitionSpec as P

LOGIT_SCALE = 14.285714285714286
EPSILON = 1e-06
LOG2E = math.log2(math.e)

SHARE = 128
SIDE = 16
EDGE = SHARE * SIDE
WIDTH = 512
SLOTS = 16
EXT = 16
TILE = 512
STRIP = 256
SUB = 32

COL_AXES = ("yh", "x", "yl")
MP_AXES = ("yl", "core")
SIZES = {"z": 8, "yh": 2, "x": 4, "yl": 2, "core": 2}

VMEM = pl.BlockSpec(memory_space=pltpu.VMEM)
SMEM = pl.BlockSpec(memory_space=pltpu.SMEM)
ANY = pl.BlockSpec(memory_space=pl.ANY)


def shifted(value, axes, steps):
    names = (axes,) if isinstance(axes, str) else axes
    count = math.prod(SIZES[name] for name in names)
    return lax.ppermute(value, axes, [((place + steps) % count, place) for place in range(count)])


def project_kernel(core_ref, seq_hbm, struct_hbm, wq_hbm, ws_hbm, keep_ref, send_ref, seq_ref, struct_ref, wq_ref, ws_ref, sems):
    core = core_ref[0]
    copies = [
        pltpu.make_async_copy(source, target, sems.at[place])
        for place, (source, target) in enumerate(
            ((seq_hbm, seq_ref), (wq_hbm, wq_ref), (struct_hbm, struct_ref), (ws_hbm, ws_ref))
        )
    ]
    for copy in copies:
        copy.start()
    copies[0].wait()
    copies[1].wait()
    for half in range(2):
        for out, which in ((keep_ref, core), (send_ref, 1 - core)):
            rows = pl.ds(pl.multiple_of((half * 2 + which) * SHARE, SHARE), SHARE)
            out[half, :, 0:WIDTH] = lax.dot_general(
                seq_ref[:, rows], wq_ref[...], (((0,), (0,)), ((), ())), preferred_element_type=jnp.float32
            )
    copies[2].wait()
    copies[3].wait()
    for half in range(2):
        for out, which in ((keep_ref, core), (send_ref, 1 - core)):
            rows = pl.ds(pl.multiple_of((half * 2 + which) * SHARE, SHARE), SHARE)
            out[half, :, WIDTH:] = jnp.dot(struct_ref[rows, :], ws_ref[...], preferred_element_type=jnp.float32)


def project(core, seq_feats, struct_feats, seq_proj, struct_proj):
    shape = jax.ShapeDtypeStruct((2, SHARE, 2 * WIDTH), jnp.float32)
    held = (seq_feats, struct_feats, seq_proj, struct_proj)
    return pl.pallas_call(
        project_kernel,
        out_shape=(shape, shape),
        in_specs=[SMEM, ANY, ANY, ANY, ANY],
        out_specs=(VMEM, VMEM),
        scratch_shapes=[pltpu.VMEM(each.shape, each.dtype) for each in held] + [pltpu.SemaphoreType.DMA((4,))],
        compiler_params=pltpu.CompilerParams(vmem_limit_bytes=56 * 1024 * 1024),
        name="project",
    )(core, *held)


def merge_kernel(yl_ref, keep_ref, got_ref, keep2_ref, send2_ref):
    yl = yl_ref[0]
    keep2_ref[...] = keep_ref[yl] + got_ref[yl]
    send2_ref[...] = (keep_ref[1 - yl] + got_ref[1 - yl]).astype(jnp.bfloat16)


def merge(yl, keep, got):
    return pl.pallas_call(
        merge_kernel,
        out_shape=(
            jax.ShapeDtypeStruct((SHARE, 2 * WIDTH), jnp.float32),
            jax.ShapeDtypeStruct((SHARE, 2 * WIDTH), jnp.bfloat16),
        ),
        in_specs=[SMEM, VMEM, VMEM],
        out_specs=(VMEM, VMEM),
        compiler_params=pltpu.CompilerParams(vmem_limit_bytes=24 * 1024 * 1024),
        name="merge",
    )(yl, keep, got)


def lanes_summed(values):
    return lax.dot_general(
        jnp.ones((8, values.shape[1]), jnp.float32),
        values,
        (((1,), (1,)), ((), ())),
        precision=lax.Precision.HIGHEST,
        preferred_element_type=jnp.float32,
    )


def finish_kernel(keep2_ref, got2_ref, ext_ref, seq_ref, struct_ref, self_ref):
    def normalized(at):
        raw = keep2_ref[:, at] + got2_ref[:, at].astype(jnp.float32)
        total = jnp.sum(raw * raw, axis=1, keepdims=True)
        return (raw * lax.rsqrt(total + EPSILON)).astype(jnp.bfloat16)

    seq = normalized(slice(0, WIDTH))
    struct = normalized(slice(WIDTH, 2 * WIDTH))
    ext = ext_ref[...]
    seq_ref[0:SHARE, :] = seq
    seq_ref[SHARE:, :] = ext
    for peer in range(SIDE):
        struct_ref[peer, 0:SHARE, :] = struct
        struct_ref[peer, SHARE:, :] = ext
    self_ref[...] = lanes_summed(seq.astype(jnp.float32) * struct.astype(jnp.float32))


def finish(keep2, got2, ext):
    return pl.pallas_call(
        finish_kernel,
        out_shape=(
            jax.ShapeDtypeStruct((SHARE + EXT, WIDTH), jnp.bfloat16),
            jax.ShapeDtypeStruct((SIDE, SHARE + EXT, WIDTH), jnp.bfloat16),
            jax.ShapeDtypeStruct((8, SHARE), jnp.float32),
        ),
        in_specs=[VMEM] * 3,
        out_specs=(VMEM,) * 3,
        compiler_params=pltpu.CompilerParams(vmem_limit_bytes=24 * 1024 * 1024),
        name="finish",
    )(keep2, got2, ext)


def pair_kernel(place_ref, *refs):
    seq_refs, s, rows_ref, cols_ref = refs[0:SIDE], refs[SIDE], refs[SIDE + 1], refs[SIDE + 2]
    q, buf0, buf1, info, lab8, ct, cm, row_acc = refs[SIDE + 3 :]
    tiles = EDGE // TILE
    strips = EDGE // STRIP
    part = TILE // strips
    buffers = (buf0, buf1)
    my_z, my_core = place_ref[0], place_ref[1]
    my_block = my_z * 2 + my_core

    ct[...] = jnp.zeros_like(ct)
    cm[...] = jnp.zeros_like(cm)
    row_acc[...] = jnp.zeros_like(row_acc)
    lane_less_row = lax.broadcasted_iota(jnp.int32, (8, 128), 1) - lax.broadcasted_iota(jnp.int32, (8, 128), 0)

    def integers(values):
        return values.astype(jnp.float32).astype(jnp.int32)

    for chunk in range(SIDE):
        labels = integers(s[chunk, SHARE:, 2 * SHARE :])
        labels = labels[:, 0:SHARE] * 128 + labels[:, SHARE:]
        lab8[:, chunk * 128 : (chunk + 1) * 128] = labels[0:8]
    for block in range(SIDE):
        at = slice(block * SHARE, (block + 1) * SHARE)
        q[at, :] = seq_refs[block][0:SHARE, :]
        ext = integers(seq_refs[block][SHARE:, :])
        high, low = ext[:, 0:SHARE], ext[:, SHARE : 2 * SHARE]
        label = ext[:, 2 * SHARE : 3 * SHARE] * 128 + ext[:, 3 * SHARE :]
        code = jnp.where((high >> 4) == my_block, (high & 15) * 128 + low, -1)
        whole = jnp.concatenate(
            [code, -1 - label, jnp.full((128 - 2 * EXT, SHARE), -1, jnp.int32)], axis=0
        ).astype(jnp.float32)
        info[at, :] = whole.T.astype(jnp.int32)

    for tile in range(tiles + 1):

        def body(step, carry, tile=tile):
            if tile < tiles:
                cols = s[pl.ds(step * (STRIP // SHARE), STRIP // SHARE), 0:SHARE, :].reshape(STRIP, WIDTH)
                start = pl.multiple_of(step * STRIP, STRIP)
                buffers[tile % 2][:, pl.ds(start, STRIP)] = lax.dot_general(
                    q[tile * TILE : (tile + 1) * TILE, :],
                    cols,
                    (((1,), (1,)), ((), ())),
                    preferred_element_type=jnp.float32,
                )
            if tile > 0:
                logits = buffers[(tile - 1) % 2]
                block = (tile - 1) * (TILE // SHARE) + step // 2
                groups = range(SUB // 8)
                for sub in range(part // SUB):
                    local = [pl.multiple_of(step * part + sub * SUB + group * 8, 8) for group in groups]
                    code = [info[pl.ds(pl.multiple_of((tile - 1) * TILE + each, 8), 8), :] for each in local]
                    label = [jnp.broadcast_to(-1 - each[:, SLOTS : SLOTS + 1], (8, 128)) for each in code]
                    lane = [each & 127 for each in code]
                    chunk_of = [each >> 7 for each in code]
                    row_total = [jnp.zeros((8, 128), jnp.float32) for _ in groups]
                    row_matched = list(row_total)
                    picked = list(row_total)
                    for chunk in range(SIDE):
                        at = slice(chunk * 128, (chunk + 1) * 128)
                        col_label = lab8[:, at]
                        col_total, col_matched = ct[:, at], cm[:, at]
                        for group in groups:
                            expo = jnp.exp2(logits[pl.ds(local[group], 8), at] * (LOGIT_SCALE * LOG2E))
                            kept = jnp.where(label[group] == col_label, expo, 0.0)
                            row_total[group] += expo
                            row_matched[group] += kept
                            col_total += expo
                            col_matched += kept
                            found = jnp.take_along_axis(expo, lane[group], axis=1, mode="promise_in_bounds")
                            picked[group] = jnp.where(chunk_of[group] == chunk, found, picked[group])
                        ct[:, at] = col_total
                        cm[:, at] = col_matched
                    for which, each in enumerate((row_total, row_matched, picked)):
                        sums = row_acc[which, block]
                        for group in groups:
                            here = lane_less_row == (step % 2) * part + sub * SUB + group * 8
                            sums = jnp.where(here, jnp.sum(each[group], axis=1, keepdims=True), sums)
                        row_acc[which, block] = sums
            return carry

        lax.fori_loop(0, strips, body, 0)

    row_of = lax.broadcasted_iota(jnp.int32, (8, SHARE), 0)
    for far in range(8):
        out = jnp.zeros((8, SHARE), jnp.float32)
        for mate in range(2):
            for which in range(3):
                row = jnp.sum(row_acc[which, far * 2 + mate], axis=0, keepdims=True)
                out = jnp.where(row_of == (my_core ^ mate) * 3 + which, row, out)
        z = (my_z + far) & 7
        for peer in range(4):
            rows_ref[z * 4 + peer] = out
    for chunk in range(SIDE):
        at = slice(chunk * 128, (chunk + 1) * 128)
        total = jnp.sum(ct[:, at], axis=0, keepdims=True)
        matched = jnp.sum(cm[:, at], axis=0, keepdims=True)
        cols_ref[chunk] = jnp.where(row_of == 0, total, matched)


def pair_sums(place, seq_blocks, struct_blocks):
    return pl.pallas_call(
        pair_kernel,
        out_shape=(
            jax.ShapeDtypeStruct((32, 8, SHARE), jnp.float32),
            jax.ShapeDtypeStruct((SIDE, 8, SHARE), jnp.float32),
        ),
        in_specs=[SMEM] + [VMEM] * 17,
        out_specs=(VMEM, VMEM),
        scratch_shapes=[
            pltpu.VMEM((EDGE, WIDTH), jnp.bfloat16),
            pltpu.VMEM((TILE, EDGE), jnp.float32),
            pltpu.VMEM((TILE, EDGE), jnp.float32),
            pltpu.VMEM((EDGE, 128), jnp.int32),
            pltpu.VMEM((8, EDGE), jnp.int32),
            pltpu.VMEM((8, EDGE), jnp.float32),
            pltpu.VMEM((8, EDGE), jnp.float32),
            pltpu.VMEM((3, SIDE, 8, 128), jnp.float32),
        ],
        compiler_params=pltpu.CompilerParams(vmem_limit_bytes=28 * 1024 * 1024),
        cost_estimate=pl.CostEstimate(
            flops=2 * EDGE * EDGE * WIDTH, bytes_accessed=4 * EDGE * WIDTH, transcendentals=EDGE * EDGE
        ),
        name="pair_sums",
    )(place, *seq_blocks, struct_blocks)


def over_z(block):
    found = {0: block, 1: shifted(block, "z", 1), 7: shifted(block, "z", -1)}
    found[2], found[6] = shifted(found[1], "z", 1), shifted(found[7], "z", -1)
    found[3], found[5] = shifted(found[2], "z", 1), shifted(found[6], "z", -1)
    found[4] = shifted(found[3], "z", 1)
    return [found[place] for place in range(8)]


def per_device(struct_feats, seq_feats, struct_proj, seq_proj, cluster_ids, hard_owner, hard_local, hard_valid):
    place = lambda axes: lax.axis_index(axes).astype(jnp.int32)
    core, yl = place("core"), place("yl")
    keep, send = project(core.reshape(1), seq_feats.T, struct_feats, seq_proj, struct_proj)
    got = shifted(send, "core", 1)

    own = lambda value: lax.dynamic_slice_in_dim(value, place(MP_AXES) * SHARE, SHARE, 0)
    labels = own(cluster_ids)
    owner = own(hard_owner[:, :, 0])
    local = own(hard_local)
    block = (owner >> 3) * 2 + ((local >> 7) & 1)
    chunk = (owner & 7) * 2 + (local >> 8)
    high = jnp.where(hard_valid > 0, block * 16 + chunk, -1).T
    low = (local & 127).T
    wide = lambda value: jnp.broadcast_to(value[None], (EXT, SHARE))
    ext = jnp.concatenate([high, low, wide(labels >> 7), wide(labels & 127)], axis=1).astype(jnp.bfloat16)

    keep2, send2 = merge(yl.reshape(1), keep, got)
    got2 = shifted(send2, "yl", 1)
    seq_block, struct_block, self_dot = finish(keep2, got2, ext)

    struct_blocks = lax.all_to_all(struct_block, COL_AXES, split_axis=0, concat_axis=0, tiled=True)
    seq_blocks = [each for held in over_z(seq_block) for each in (held, shifted(held, "core", 1))]

    rows, cols = pair_sums(jnp.stack([place("z"), core]), seq_blocks, struct_blocks)
    rows = lax.all_to_all(rows, ("z",) + MP_AXES, split_axis=0, concat_axis=0, tiled=True)
    cols = jnp.sum(lax.all_to_all(cols, COL_AXES, split_axis=0, concat_axis=0, tiled=True), axis=0)
    rows = jnp.sum(rows.reshape(8, 2, 2, 8, SHARE), axis=(0, 2))[:, 0:6].reshape(2, 2, 3, SHARE)

    seq_loss = (jnp.log(rows[:, :, 0]) - jnp.log(rows[:, :, 1])).reshape(4 * SHARE)
    struct_loss = jnp.log(cols[0]) - jnp.log(cols[1])
    self_logits = LOGIT_SCALE * self_dot[0]
    extra = rows[:, :, 2].reshape(4, SHARE)[place(MP_AXES)]
    hard_loss = jnp.log(jnp.exp(self_logits) + extra) - self_logits
    return (seq_loss, struct_loss, hard_loss)


def solution(mesh):
    fine = Mesh(mesh.devices.reshape(8, 2, 4, 2, 2), ("z", "yh", "x", "yl", "core"))
    blk = ("z", "yh", "x")
    both = blk + MP_AXES
    placed = (
        P(blk, MP_AXES),
        P(blk, MP_AXES),
        P(MP_AXES, None),
        P(MP_AXES, None),
        P(blk),
        P(blk, None, None),
        P(blk, None),
        P(both, None),
    )
    return jax.shard_map(
        per_device,
        mesh=fine,
        in_specs=placed,
        out_specs=(P(blk), P(both), P(both)),
        check_vma=False,
    )
```

time: 971 us -> 117 us (0.12)
  waiting for transfers between devices: 697 us -> 26.3 us
  blocking collectives: 84.1 us -> 9.51 us
  local copies, waits for them, and re-layouts: 57.1 us -> 6.44 us
  matrix products: 32 us -> 0 us
  Pallas kernels: 0 us -> 28.6 us
  other arithmetic: 26.5 us -> 2.68 us
  between operations: 14.3 us -> 0.74 us
  starting transfers between devices: 54.8 us -> 42.5 us
    ppermute x256 -> x17, waiting for transfers between devices: 670 us -> 13.9 us  [shifted(): lax.ppermute(value, axes, [((place + steps) % count, place) for place in...]
    psum x1 -> x0, blocking collectives: 76.8 us -> none  [per_device(): row_total, row_matched = lax.psum((row_total, row_matched), 'mp')]
    gather x2 -> x0, local copies, waits for them, and re-layouts: 43.9 us -> none  [the longest x1 26.6 us: per_device(): fetched_rows = replies[owners, slot_index].reshape(share_rows, slots, -1)]
    dot_general x67 -> x0, matrix products: 32 us -> none  [the longest x64 27.6 us: visit_block(): jnp.einsum('re,ce->rc', queries, visitor, preferred_element_type=jnp.floa...]
    pallas_call x0 -> x4, Pallas kernels: none -> 28.6 us  [the longest x1 24.7 us: pair_sums(): pl.pallas_call(pair_kernel, out_shape=(jax.ShapeDtypeStruct((32, 8, SHARE...]
    another operation x3 -> x2, other arithmetic: 18.5 us -> 0.84 us
    reduce_scatter x1 -> x0, waiting for transfers between devices: 17.1 us -> none  [per_device(): lax.psum_scatter(jnp.dot(struct_feats, struct_proj, preferred_element_typ...]
    all_to_all x2, starting transfers between devices: 27.8 us -> 15.5 us  [the longest x1 10.4 us: per_device(): lax.all_to_all(rows, ('z',) + MP_AXES, split_axis=0, concat_axis=0, tiled...]
  transfers between devices with their start and end apart: 260 -> 19, of which waited for: 130 -> 9; matrix products, arithmetic and copies ran while one was open for 7% -> 2% of each run, Pallas kernels for 0% -> 0%
where the time goes in v1:
time: 117 us
  starting transfers between devices  42.5 us (36%)
  Pallas kernels  28.6 us (24%)
  waiting for transfers between devices  26.3 us (22%)
  blocking collectives  9.51 us (8%)
  local copies, waits for them, and re-layouts  6.44 us (6%)
  other arithmetic  2.68 us (2%)
    ppermute x17, starting transfers between devices, shifted(): lax.ppermute(value, axes, [((place + steps) % count, place) for place in...  27 us
    pallas_call x1, Pallas kernels, pair_sums(): pl.pallas_call(pair_kernel, out_shape=(jax.ShapeDtypeStruct((32, 8, SHARE...  24.7 us
    ppermute x17, waiting for transfers between devices, shifted(): lax.ppermute(value, axes, [((place + steps) % count, place) for place in...  13.9 us
    all_to_all x1, starting transfers between devices, per_device(): lax.all_to_all(rows, ('z',) + MP_AXES, split_axis=0, concat_axis=0, tiled...  10.4 us
    all_to_all x1, blocking collectives, per_device(): lax.all_to_all(cols, COL_AXES, split_axis=0, concat_axis=0, tiled=True)  9.51 us
    all_to_all x1, waiting for transfers between devices, per_device(): lax.all_to_all(rows, ('z',) + MP_AXES, split_axis=0, concat_axis=0, tiled...  8.72 us
    unnamed x14, local copies, waits for them, and re-layouts  5.82 us
    all_to_all x1, starting transfers between devices, per_device(): lax.all_to_all(struct_block, COL_AXES, split_axis=0, concat_axis=0, tiled...  5.02 us
  transfers between devices with their start and end apart: 19, of which 9 were waited for; matrix products, arithmetic and copies ran while one was open for 2% of the time, Pallas kernels for 0%

profile of v1, /device:TPU:1, one launch (start us, length us, event | category | flops | bytes accessed | tf_op | source)
XLA Modules:
  0.0 116.8 jit_solution(14677834572088388839)
XLA Ops:
  0.7 3.2 %project.1 = (f32[2,128,1024]{2,1,0:T(8,128)}, f32[2,128,1024]{2,1,0:T(8,128)}) custom-call(s32[1]{0:T(128)} %bitcast.1.core_ref, bf16[320,512]{1,0:T(8,128)(2,1)} %bitcast.48, bf16[512,256]{1,0:T(8,128)(2,1)} %struct_hbm.1, bf16[320,512]{1,0:T(8,128)(2,1)} %wq_hbm.1, bf16[256,512]{1,0:T(8,128)(2,1)} %ws_hbm.1), custom_call_target="tpu_custom_call" | custom-call | tf_op jit(solution)/shard_map/project/pallas_call | solution.py:68
  3.8 3.3 %collective-permute-start = (f32[2,128,1024]{2,1,0:T(8,128)}, f32[2,128,1024]{2,1,0:T(8,128)S(1)}, u32[]{:S(2)}, u32[]{:S(2)}) collective-permute-start(f32[2,128,1024]{2,1,0:T(8,128)} %get-tuple-element.13), channel_id=1, source_target_pairs={{1,0},{0,1},{3,2},{2,3},{5,4},{4,5},{7,6},{6,7},{9,8},{8,9},{11,10... | collective-permute-start | bytes 3145736 | tf_op jit(solution)/shard_map/ppermute | solution.py:36
  7.2 0.7 fusion.5
  7.9 1.8 %collective-permute-done.got_ref = f32[2,128,1024]{2,1,0:T(8,128)S(1)} collective-permute-done((f32[2,128,1024]{2,1,0:T(8,128)}, f32[2,128,1024]{2,1,0:T(8,128)S(1)}, u32[]{:S(2)}, u32[]{:S(2)}) %collective-permute-start) | collective-permute-done | bytes 1048608 | tf_op jit(solution)/shard_map/ppermute | solution.py:36
  9.7 1.2 %copy-done.2 = f32[2,128,1024]{2,1,0:T(8,128)S(1)} copy-done((f32[2,128,1024]{2,1,0:T(8,128)S(1)}, f32[2,128,1024]{2,1,0:T(8,128)}, u32[]{:S(2)}) %copy-start.2) | copy-done | bytes 1048600
  11.1 0.8 shift-right-arithmetic_convert_fusion
  11.9 6.7 %collective-permute-done.1.got2_ref = bf16[128,1024]{1,0:T(8,128)(2,1)S(1)} collective-permute-done((bf16[128,1024]{1,0:T(8,128)(2,1)S(1)}, bf16[128,1024]{1,0:T(8,128)(2,1)S(1)}, u32[]{:S(2)}, u32[]{:S(2)}) %collective-permute-start.1) | collective-permute-done | bytes 262176 | tf_op jit(solution)/shard_map/ppermute | solution.py:36
  18.6 0.6 finish.1
  19.2 1.4 %copy-done.1 = bf16[16,144,512]{2,1,0:T(8,128)(2,1)} copy-done((bf16[16,144,512]{2,1,0:T(8,128)(2,1)}, bf16[16,144,512]{2,1,0:T(8,128)(2,1)S(1)}, u32[]{:S(2)}) %copy-start.1) | copy-done | bytes 2359320
  20.7 5.0 %all-to-all-start = ((bf16[16,144,512]{2,1,0:T(8,128)(2,1)}), bf16[16,144,512]{2,1,0:T(8,128)(2,1)S(1)}, u32[]{:S(2)}, u32[]{:S(2)}) async-start(bf16[16,144,512]{2,1,0:T(8,128)(2,1)} %copy-done.1), calls=%async_computation | async-start | bytes 4718592 | tf_op jit(solution)/shard_map/all_to_all | solution.py:298
  25.7 5.7 %collective-permute-start.3 = (bf16[144,512]{1,0:T(8,128)(2,1)S(1)}, bf16[144,512]{1,0:T(8,128)(2,1)S(1)}, u32[]{:S(2)}, u32[]{:S(2)}) collective-permute-start(bf16[144,512]{1,0:T(8,128)(2,1)S(1)} %get-tuple-element.16.refs_0_), channel_id=1, source_target_pairs={{32,0},{64,32},{96,64},{128,96},{160,128},{192,160},{224,192},{0,2... | collective-permute-start | bytes 442376 | tf_op jit(solution)/shard_map/ppermute | solution.py:36
  31.4 2.1 %collective-permute-done.3.refs_2_ = bf16[144,512]{1,0:T(8,128)(2,1)S(1)} collective-permute-done((bf16[144,512]{1,0:T(8,128)(2,1)S(1)}, bf16[144,512]{1,0:T(8,128)(2,1)S(1)}, u32[]{:S(2)}, u32[]{:S(2)}) %collective-permute-start.3) | collective-permute-done | bytes 147488 | tf_op jit(solution)/shard_map/ppermute | solution.py:36
  33.5 3.1 %collective-permute-start.5 = (bf16[144,512]{1,0:T(8,128)(2,1)S(1)}, bf16[144,512]{1,0:T(8,128)(2,1)S(1)}, u32[]{:S(2)}, u32[]{:S(2)}) collective-permute-start(bf16[144,512]{1,0:T(8,128)(2,1)S(1)} %collective-permute-done.3.refs_2_), channel_id=1, source_target_pairs={{32,0},{64,32},{96,64},{128,96},{160,128},{192,160},{224,192},{0,2... | collective-permute-start | bytes 442376 | tf_op jit(solution)/shard_map/ppermute | solution.py:36
  36.9 1.8 %collective-permute-done.5.refs_4_ = bf16[144,512]{1,0:T(8,128)(2,1)S(1)} collective-permute-done((bf16[144,512]{1,0:T(8,128)(2,1)S(1)}, bf16[144,512]{1,0:T(8,128)(2,1)S(1)}, u32[]{:S(2)}, u32[]{:S(2)}) %collective-permute-start.5) | collective-permute-done | bytes 147488 | tf_op jit(solution)/shard_map/ppermute | solution.py:36
  38.7 3.4 %collective-permute-start.7 = (bf16[144,512]{1,0:T(8,128)(2,1)S(1)}, bf16[144,512]{1,0:T(8,128)(2,1)S(1)}, u32[]{:S(2)}, u32[]{:S(2)}) collective-permute-start(bf16[144,512]{1,0:T(8,128)(2,1)S(1)} %collective-permute-done.5.refs_4_), channel_id=1, source_target_pairs={{32,0},{64,32},{96,64},{128,96},{160,128},{192,160},{224,192},{0,2... | collective-permute-start | bytes 442376 | tf_op jit(solution)/shard_map/ppermute | solution.py:36
  42.1 3.8 %collective-permute-start.2 = (bf16[144,512]{1,0:T(8,128)(2,1)S(1)}, bf16[144,512]{1,0:T(8,128)(2,1)S(1)}, u32[]{:S(2)}, u32[]{:S(2)}) collective-permute-start(bf16[144,512]{1,0:T(8,128)(2,1)S(1)} %get-tuple-element.16.refs_0_), channel_id=1, source_target_pairs={{1,0},{0,1},{3,2},{2,3},{5,4},{4,5},{7,6},{6,7},{9,8},{8,9},{11,10... | collective-permute-start | bytes 442376 | tf_op jit(solution)/shard_map/ppermute | solution.py:36
  46.4 2.7 %collective-permute-start.9 = (bf16[144,512]{1,0:T(8,128)(2,1)S(1)}, bf16[144,512]{1,0:T(8,128)(2,1)}, u32[]{:S(2)}, u32[]{:S(2)}) collective-permute-start(bf16[144,512]{1,0:T(8,128)(2,1)S(1)} %collective-permute-done.7.refs_6_), channel_id=1, source_target_pairs={{32,0},{64,32},{96,64},{128,96},{160,128},{192,160},{224,192},{0,2... | collective-permute-start | bytes 442376 | tf_op jit(solution)/shard_map/ppermute | solution.py:36
  49.0 3.2 %collective-permute-start.15 = (bf16[144,512]{1,0:T(8,128)(2,1)S(1)}, bf16[144,512]{1,0:T(8,128)(2,1)}, u32[]{:S(2)}, u32[]{:S(2)}) collective-permute-start(bf16[144,512]{1,0:T(8,128)(2,1)S(1)} %collective-permute-done.12.refs_12_), channel_id=1, source_target_pairs={{1,0},{0,1},{3,2},{2,3},{5,4},{4,5},{7,6},{6,7},{9,8},{8,9},{11,10... | collective-permute-start | bytes 442376 | tf_op jit(solution)/shard_map/ppermute | solution.py:36
  52.2 0.6 copy-done.3
  52.9 0.7 copy-done.5
  54.0 0.8 collective-permute-start.10
  54.9 0.8 collective-permute-done.14.refs_11_
  56.2 3.6 %all-to-all-done.refs_16_ = bf16[16,144,512]{2,1,0:T(8,128)(2,1)S(1)} async-done(((bf16[16,144,512]{2,1,0:T(8,128)(2,1)}), bf16[16,144,512]{2,1,0:T(8,128)(2,1)S(1)}, u32[]{:S(2)}, u32[]{:S(2)}) %all-to-all-start) | async-done | bytes 2359328 | tf_op jit(solution)/shard_map/all_to_all | solution.py:298
  59.8 0.9 copy-done.4
  60.7 0.9 copy-done.6
  61.6 24.7 %pair_sums.1 = (f32[32,8,128]{2,1,0:T(8,128)}, f32[16,8,128]{2,1,0:T(8,128)S(1)}) custom-call(s32[2]{0:T(128)S(1)} %pad_add_fusion.place_ref, bf16[144,512]{1,0:T(8,128)(2,1)S(1)} %get-tuple-element.16.refs_0_, bf16[144,512]{1,0:T(8,128)(2,1)S(1)} %collective-permute-done.2.refs_1_, bf16[144,512]{1,0:T(8,128)(2,1)S(1)} %collective-permute-done.3.refs_2_, ...), custom_call_target="tpu_custom_call" | custom-call | flops 4294967296 | bytes 4194304 | tf_op jit(solution)/shard_map/pair_sums/pallas_call | solution.py:243
  86.4 9.5 %all_to_all.15 = f32[16,8,128]{2,1,0:T(8,128)S(1)} all-to-all(f32[16,8,128]{2,1,0:T(8,128)S(1)} %get-tuple-element.19), channel_id=1, replica_groups=mesh['z'=8,'yh'=2,'x'=4,'yl'=2,'core'=2] {'yh','x','yl'}, dimensions={0} | all-to-all | bytes 131072 | tf_op jit(solution)/shard_map/all_to_all | solution.py:303
  95.9 10.4 %all-to-all-start.1 = ((f32[32,8,128]{2,1,0:T(8,128)}), f32[32,8,128]{2,1,0:T(8,128)S(1)}, u32[]{:S(2)}, u32[]{:S(2)}) async-start(f32[32,8,128]{2,1,0:T(8,128)} %get-tuple-element.18), calls=%async_computation.1 | async-start | bytes 262144 | tf_op jit(solution)/shard_map/all_to_all | solution.py:302
  106.4 0.5 subtract_bitcast_fusion
  106.9 8.7 %all-to-all-done.1 = f32[32,8,128]{2,1,0:T(8,128)S(1)} async-done(((f32[32,8,128]{2,1,0:T(8,128)}), f32[32,8,128]{2,1,0:T(8,128)S(1)}, u32[]{:S(2)}, u32[]{:S(2)}) %all-to-all-start.1) | async-done | bytes 131104 | tf_op jit(solution)/shard_map/all_to_all | solution.py:302
  115.7 0.6 copy.18
  116.2 0.5 fusion.10
  (40 shorter events, 2.2 us)
Async XLA Ops:
  0.6 6.5 %copy-start = (s32[512,16,1]{0,2,1:T(1,128)S(1)}, s32[512,16,1]{0,2,1:T(1,128)}, u32[]{:S(2)}) copy-start(s32[512,16,1]{0,2,1:T(1,128)} %param.13) | copy-start | bytes 98308
  3.8 5.8 %collective-permute-start = (f32[2,128,1024]{2,1,0:T(8,128)}, f32[2,128,1024]{2,1,0:T(8,128)S(1)}, u32[]{:S(2)}, u32[]{:S(2)}) collective-permute-start(f32[2,128,1024]{2,1,0:T(8,128)} %get-tuple-element.13), channel_id=1, source_target_pairs={{1,0},{0,1},{3,2},{2,3},{5,4},{4,5},{7,6},{6,7},{9,8},{8,9},{11,10... | collective-permute-start | bytes 3145736 | tf_op jit(solution)/shard_map/ppermute | solution.py:36
  9.7 1.2 %copy-start.2 = (f32[2,128,1024]{2,1,0:T(8,128)S(1)}, f32[2,128,1024]{2,1,0:T(8,128)}, u32[]{:S(2)}) copy-start(f32[2,128,1024]{2,1,0:T(8,128)} %get-tuple-element.12.keep_ref) | copy-start | bytes 3145732
  11.0 7.6 %collective-permute-start.1 = (bf16[128,1024]{1,0:T(8,128)(2,1)S(1)}, bf16[128,1024]{1,0:T(8,128)(2,1)S(1)}, u32[]{:S(2)}, u32[]{:S(2)}) collective-permute-start(bf16[128,1024]{1,0:T(8,128)(2,1)S(1)} %get-tuple-element.15), channel_id=1, source_target_pairs={{2,0},{0,2},{3,1},{1,3},{6,4},{4,6},{7,5},{5,7},{10,8},{8,10},{11,... | collective-permute-start | bytes 786440 | tf_op jit(solution)/shard_map/ppermute | solution.py:36
  19.2 1.4 %copy-start.1 = (bf16[16,144,512]{2,1,0:T(8,128)(2,1)}, bf16[16,144,512]{2,1,0:T(8,128)(2,1)S(1)}, u32[]{:S(2)}) copy-start(bf16[16,144,512]{2,1,0:T(8,128)(2,1)S(1)} %get-tuple-element.17) | copy-start | bytes 7077892
  20.7 39.1 %all-to-all-start = ((bf16[16,144,512]{2,1,0:T(8,128)(2,1)}), bf16[16,144,512]{2,1,0:T(8,128)(2,1)S(1)}, u32[]{:S(2)}, u32[]{:S(2)}) async-start(bf16[16,144,512]{2,1,0:T(8,128)(2,1)} %copy-done.1), calls=%async_computation | async-start | bytes 4718592 | tf_op jit(solution)/shard_map/all_to_all | solution.py:298
  25.7 7.8 %collective-permute-start.3 = (bf16[144,512]{1,0:T(8,128)(2,1)S(1)}, bf16[144,512]{1,0:T(8,128)(2,1)S(1)}, u32[]{:S(2)}, u32[]{:S(2)}) collective-permute-start(bf16[144,512]{1,0:T(8,128)(2,1)S(1)} %get-tuple-element.16.refs_0_), channel_id=1, source_target_pairs={{32,0},{64,32},{96,64},{128,96},{160,128},{192,160},{224,192},{0,2... | collective-permute-start | bytes 442376 | tf_op jit(solution)/shard_map/ppermute | solution.py:36
  31.4 5.5 %collective-permute-start.11 = (bf16[144,512]{1,0:T(8,128)(2,1)S(1)}, bf16[144,512]{1,0:T(8,128)(2,1)S(1)}, u32[]{:S(2)}, u32[]{:S(2)}) collective-permute-start(bf16[144,512]{1,0:T(8,128)(2,1)S(1)} %get-tuple-element.16.refs_0_), channel_id=1, source_target_pairs={{224,0},{0,32},{32,64},{64,96},{96,128},{128,160},{160,192},{192,2... | collective-permute-start | bytes 442376 | tf_op jit(solution)/shard_map/ppermute | solution.py:36
  33.5 5.2 %collective-permute-start.5 = (bf16[144,512]{1,0:T(8,128)(2,1)S(1)}, bf16[144,512]{1,0:T(8,128)(2,1)S(1)}, u32[]{:S(2)}, u32[]{:S(2)}) collective-permute-start(bf16[144,512]{1,0:T(8,128)(2,1)S(1)} %collective-permute-done.3.refs_2_), channel_id=1, source_target_pairs={{32,0},{64,32},{96,64},{128,96},{160,128},{192,160},{224,192},{0,2... | collective-permute-start | bytes 442376 | tf_op jit(solution)/shard_map/ppermute | solution.py:36
  36.9 9.5 %collective-permute-start.12 = (bf16[144,512]{1,0:T(8,128)(2,1)S(1)}, bf16[144,512]{1,0:T(8,128)(2,1)S(1)}, u32[]{:S(2)}, u32[]{:S(2)}) collective-permute-start(bf16[144,512]{1,0:T(8,128)(2,1)S(1)} %collective-permute-done.11.refs_14_), channel_id=1, source_target_pairs={{224,0},{0,32},{32,64},{64,96},{96,128},{128,160},{160,192},{192,2... | collective-permute-start | bytes 442376 | tf_op jit(solution)/shard_map/ppermute | solution.py:36
  38.7 7.7 %collective-permute-start.7 = (bf16[144,512]{1,0:T(8,128)(2,1)S(1)}, bf16[144,512]{1,0:T(8,128)(2,1)S(1)}, u32[]{:S(2)}, u32[]{:S(2)}) collective-permute-start(bf16[144,512]{1,0:T(8,128)(2,1)S(1)} %collective-permute-done.5.refs_4_), channel_id=1, source_target_pairs={{32,0},{64,32},{96,64},{128,96},{160,128},{192,160},{224,192},{0,2... | collective-permute-start | bytes 442376 | tf_op jit(solution)/shard_map/ppermute | solution.py:36
  42.1 7.0 %collective-permute-start.2 = (bf16[144,512]{1,0:T(8,128)(2,1)S(1)}, bf16[144,512]{1,0:T(8,128)(2,1)S(1)}, u32[]{:S(2)}, u32[]{:S(2)}) collective-permute-start(bf16[144,512]{1,0:T(8,128)(2,1)S(1)} %get-tuple-element.16.refs_0_), channel_id=1, source_target_pairs={{1,0},{0,1},{3,2},{2,3},{5,4},{4,5},{7,6},{6,7},{9,8},{8,9},{11,10... | collective-permute-start | bytes 442376 | tf_op jit(solution)/shard_map/ppermute | solution.py:36
  45.8 6.4 %collective-permute-start.16 = (bf16[144,512]{1,0:T(8,128)(2,1)S(1)}, bf16[144,512]{1,0:T(8,128)(2,1)S(1)}, u32[]{:S(2)}, u32[]{:S(2)}) collective-permute-start(bf16[144,512]{1,0:T(8,128)(2,1)S(1)} %collective-permute-done.11.refs_14_), channel_id=1, source_target_pairs={{1,0},{0,1},{3,2},{2,3},{5,4},{4,5},{7,6},{6,7},{9,8},{8,9},{11,10... | collective-permute-start | bytes 442376 | tf_op jit(solution)/shard_map/ppermute | solution.py:36
  45.8 7.0 %collective-permute-start.4 = (bf16[144,512]{1,0:T(8,128)(2,1)S(1)}, bf16[144,512]{1,0:T(8,128)(2,1)S(1)}, u32[]{:S(2)}, u32[]{:S(2)}) collective-permute-start(bf16[144,512]{1,0:T(8,128)(2,1)S(1)} %collective-permute-done.3.refs_2_), channel_id=1, source_target_pairs={{1,0},{0,1},{3,2},{2,3},{5,4},{4,5},{7,6},{6,7},{9,8},{8,9},{11,10... | collective-permute-start | bytes 442376 | tf_op jit(solution)/shard_map/ppermute | solution.py:36
  46.3 7.7 %collective-permute-start.13 = (bf16[144,512]{1,0:T(8,128)(2,1)S(1)}, bf16[144,512]{1,0:T(8,128)(2,1)}, u32[]{:S(2)}, u32[]{:S(2)}) collective-permute-start(bf16[144,512]{1,0:T(8,128)(2,1)S(1)} %collective-permute-done.12.refs_12_), channel_id=1, source_target_pairs={{224,0},{0,32},{32,64},{64,96},{96,128},{128,160},{160,192},{192,2... | collective-permute-start | bytes 442376 | tf_op jit(solution)/shard_map/ppermute | solution.py:36
  46.4 7.7 %collective-permute-start.9 = (bf16[144,512]{1,0:T(8,128)(2,1)S(1)}, bf16[144,512]{1,0:T(8,128)(2,1)}, u32[]{:S(2)}, u32[]{:S(2)}) collective-permute-start(bf16[144,512]{1,0:T(8,128)(2,1)S(1)} %collective-permute-done.7.refs_6_), channel_id=1, source_target_pairs={{32,0},{64,32},{96,64},{128,96},{160,128},{192,160},{224,192},{0,2... | collective-permute-start | bytes 442376 | tf_op jit(solution)/shard_map/ppermute | solution.py:36
  49.0 5.9 %collective-permute-start.15 = (bf16[144,512]{1,0:T(8,128)(2,1)S(1)}, bf16[144,512]{1,0:T(8,128)(2,1)}, u32[]{:S(2)}, u32[]{:S(2)}) collective-permute-start(bf16[144,512]{1,0:T(8,128)(2,1)S(1)} %collective-permute-done.12.refs_12_), channel_id=1, source_target_pairs={{1,0},{0,1},{3,2},{2,3},{5,4},{4,5},{7,6},{6,7},{9,8},{8,9},{11,10... | collective-permute-start | bytes 442376 | tf_op jit(solution)/shard_map/ppermute | solution.py:36
  52.2 0.7 copy-start.3
  52.8 2.1 %collective-permute-start.6 = (bf16[144,512]{1,0:T(8,128)(2,1)S(1)}, bf16[144,512]{1,0:T(8,128)(2,1)}, u32[]{:S(2)}, u32[]{:S(2)}) collective-permute-start(bf16[144,512]{1,0:T(8,128)(2,1)S(1)} %collective-permute-done.5.refs_4_), channel_id=1, source_target_pairs={{1,0},{0,1},{3,2},{2,3},{5,4},{4,5},{7,6},{6,7},{9,8},{8,9},{11,10... | collective-permute-start | bytes 442376 | tf_op jit(solution)/shard_map/ppermute | solution.py:36
  52.9 0.7 copy-start.5
  53.5 2.2 %collective-permute-start.8 = (bf16[144,512]{1,0:T(8,128)(2,1)S(1)}, bf16[144,512]{1,0:T(8,128)(2,1)}, u32[]{:S(2)}, u32[]{:S(2)}) collective-permute-start(bf16[144,512]{1,0:T(8,128)(2,1)S(1)} %collective-permute-done.7.refs_6_), channel_id=1, source_target_pairs={{1,0},{0,1},{3,2},{2,3},{5,4},{4,5},{7,6},{6,7},{9,8},{8,9},{11,10... | collective-permute-start | bytes 442376 | tf_op jit(solution)/shard_map/ppermute | solution.py:36
  54.0 1.7 %collective-permute-start.14 = (bf16[144,512]{1,0:T(8,128)(2,1)}, bf16[144,512]{1,0:T(8,128)(2,1)}, u32[]{:S(2)}, u32[]{:S(2)}) collective-permute-start(bf16[144,512]{1,0:T(8,128)(2,1)} %collective-permute-done.13.refs_10_), channel_id=1, source_target_pairs={{1,0},{0,1},{3,2},{2,3},{5,4},{4,5},{7,6},{6,7},{9,8},{8,9},{11,10... | collective-permute-start | bytes 442376 | tf_op jit(solution)/shard_map/ppermute | solution.py:36
  54.0 2.2 %collective-permute-start.10 = (bf16[144,512]{1,0:T(8,128)(2,1)}, bf16[144,512]{1,0:T(8,128)(2,1)}, u32[]{:S(2)}, u32[]{:S(2)}) collective-permute-start(bf16[144,512]{1,0:T(8,128)(2,1)} %collective-permute-done.9.refs_8_), channel_id=1, source_target_pairs={{1,0},{0,1},{3,2},{2,3},{5,4},{4,5},{7,6},{6,7},{9,8},{8,9},{11,10... | collective-permute-start | bytes 442376 | tf_op jit(solution)/shard_map/ppermute | solution.py:36
  59.8 0.9 copy-start.4
  60.7 0.9 copy-start.6
  95.9 19.7 %all-to-all-start.1 = ((f32[32,8,128]{2,1,0:T(8,128)}), f32[32,8,128]{2,1,0:T(8,128)S(1)}, u32[]{:S(2)}, u32[]{:S(2)}) async-start(f32[32,8,128]{2,1,0:T(8,128)} %get-tuple-element.18), calls=%async_computation.1 | async-start | bytes 262144 | tf_op jit(solution)/shard_map/all_to_all | solution.py:302

commit v2 on v1

v2 whole, which is shorter than its diff:
```python
import functools
import math

import jax
import jax.numpy as jnp
from jax import lax
from jax.experimental import pallas as pl
from jax.experimental.pallas import tpu as pltpu
from jax.sharding import Mesh, PartitionSpec as P

LOGIT_SCALE = 14.285714285714286
EPSILON = 1e-06
LOG2E = math.log2(math.e)

SHARE = 128
SIDE = 16
EDGE = SHARE * SIDE
WIDTH = 512
SLOTS = 16
EXT = 16
TILE = 512
STRIP = 256
SUB = 32
PICKS = 3

COL_AXES = ("yh", "x", "yl")
MP_AXES = ("yl", "core")
SIZES = {"z": 8, "yh": 2, "x": 4, "yl": 2, "core": 2}

VMEM = pl.BlockSpec(memory_space=pltpu.VMEM)
SMEM = pl.BlockSpec(memory_space=pltpu.SMEM)
HBM = pl.BlockSpec(memory_space=pltpu.HBM)


def shifted(value, axes, steps):
    names = (axes,) if isinstance(axes, str) else axes
    count = math.prod(SIZES[name] for name in names)
    return lax.ppermute(value, axes, [((place + steps) % count, place) for place in range(count)])


def project_kernel(core_ref, feats_hbm, proj_hbm, keep_ref, send_ref, feats_ref, proj_ref, sems, *, turned):
    core = core_ref[0]
    copies = [
        pltpu.make_async_copy(feats_hbm, feats_ref, sems.at[0]),
        pltpu.make_async_copy(proj_hbm, proj_ref, sems.at[1]),
    ]
    for copy in copies:
        copy.start()
    for copy in copies:
        copy.wait()
    for out, which in ((send_ref, 1 - core), (keep_ref, core)):
        for half in range(2):
            rows = pl.ds(pl.multiple_of((half * 2 + which) * SHARE, SHARE), SHARE)
            feats, over = (feats_ref[:, rows], 0) if turned else (feats_ref[rows, :], 1)
            out[half] = lax.dot_general(
                feats, proj_ref[...], (((over,), (0,)), ((), ())), preferred_element_type=jnp.float32
            )


def project(core, feats, proj, turned, name):
    shape = jax.ShapeDtypeStruct((2, SHARE, WIDTH), jnp.float32)
    return pl.pallas_call(
        functools.partial(project_kernel, turned=turned),
        out_shape=(shape, shape),
        in_specs=[SMEM, HBM, HBM],
        out_specs=(VMEM, VMEM),
        scratch_shapes=[
            pltpu.VMEM(feats.shape, feats.dtype),
            pltpu.VMEM(proj.shape, proj.dtype),
            pltpu.SemaphoreType.DMA((2,)),
        ],
        compiler_params=pltpu.CompilerParams(vmem_limit_bytes=12 * 1024 * 1024),
        name=name,
    )(core, feats, proj)


def merge_kernel(yl_ref, keep_ref, got_ref, keep2_ref, send2_ref):
    yl = yl_ref[0]
    send2_ref[...] = (keep_ref[1 - yl] + got_ref[1 - yl]).astype(jnp.bfloat16)
    keep2_ref[...] = keep_ref[yl] + got_ref[yl]


def merge(yl, keep, got, name):
    return pl.pallas_call(
        merge_kernel,
        out_shape=(
            jax.ShapeDtypeStruct((SHARE, WIDTH), jnp.float32),
            jax.ShapeDtypeStruct((SHARE, WIDTH), jnp.bfloat16),
        ),
        in_specs=[SMEM, VMEM, VMEM],
        out_specs=(VMEM, VMEM),
        compiler_params=pltpu.CompilerParams(vmem_limit_bytes=12 * 1024 * 1024),
        name=name,
    )(yl, keep, got)


def lanes_summed(values):
    return lax.dot_general(
        jnp.ones((8, values.shape[1]), jnp.float32),
        values,
        (((1,), (1,)), ((), ())),
        precision=lax.Precision.HIGHEST,
        preferred_element_type=jnp.float32,
    )


def normalized(keep2_ref, got2_ref):
    raw = keep2_ref[...] + got2_ref[...].astype(jnp.float32)
    total = jnp.sum(raw * raw, axis=1, keepdims=True)
    return (raw * lax.rsqrt(total + EPSILON)).astype(jnp.bfloat16)


def finish_kernel(keep2_s, got2_s, keep2_q, got2_q, struct_ext_ref, seq_ext_ref, peers_ref, seq_ref, self_ref):
    struct = normalized(keep2_s, got2_s)
    turned = struct.astype(jnp.float32).T.astype(jnp.bfloat16)
    struct_ext = struct_ext_ref[...]
    for peer in range(SIDE):
        peers_ref[peer, 0:WIDTH, :] = turned
        peers_ref[peer, WIDTH:, :] = struct_ext
    seq = normalized(keep2_q, got2_q)
    seq_ref[0:SHARE, :] = seq
    seq_ref[SHARE:, :] = seq_ext_ref[...]
    self_ref[...] = lanes_summed(seq.astype(jnp.float32) * struct.astype(jnp.float32))


def finish(*held):
    return pl.pallas_call(
        finish_kernel,
        out_shape=(
            jax.ShapeDtypeStruct((SIDE, WIDTH + EXT, SHARE), jnp.bfloat16),
            jax.ShapeDtypeStruct((SHARE + EXT, WIDTH), jnp.bfloat16),
            jax.ShapeDtypeStruct((8, SHARE), jnp.float32),
        ),
        in_specs=[VMEM] * 6,
        out_specs=(VMEM,) * 3,
        compiler_params=pltpu.CompilerParams(vmem_limit_bytes=12 * 1024 * 1024),
        name="finish",
    )(*held)


def integers(values):
    return values.astype(jnp.float32).astype(jnp.int32)


def pair_kernel(place_ref, *refs):
    seq_refs, s, rows_ref, cols_ref = refs[0:SIDE], refs[SIDE], refs[SIDE + 1], refs[SIDE + 2]
    q, ext_all, slots, info, counts, counts_smem, buf0, buf1, lab8, ct, cm, rt, rm, ex, sem = refs[SIDE + 3 :]
    tiles = EDGE // TILE
    strips = EDGE // STRIP
    part = TILE // strips
    buffers = (buf0, buf1)
    my_z, my_core = place_ref[0], place_ref[1]
    my_block = my_z * 2 + my_core
    lane = lax.broadcasted_iota(jnp.int32, (8, 128), 1)

    for block in range(SIDE):
        ext_all[block] = seq_refs[block][SHARE:, :]

    def decode(block, carry):
        ext = integers(ext_all[block])
        high, low = ext[:, 0:SHARE], ext[:, SHARE : 2 * SHARE]
        label = ext[:, 2 * SHARE : 3 * SHARE] * 128 + ext[:, 3 * SHARE :]
        hit = (high >> 4) == my_block
        slots[0] = jnp.where(hit, 1, 0)
        slots[1] = jnp.where(hit, (high & 15) * 128 + low + 1, 0)
        order = lax.broadcasted_iota(jnp.int32, (SLOTS, SHARE), 0)
        packed = jnp.zeros((SLOTS, SHARE), jnp.int32)
        found = jnp.zeros((SLOTS, SHARE), jnp.int32)
        for slot in range(SLOTS):
            code = jnp.broadcast_to(slots[1, slot : slot + 1, :], (SLOTS, SHARE))
            packed = packed + jnp.where(order == found, code, 0)
            found = found + jnp.broadcast_to(slots[0, slot : slot + 1, :], (SLOTS, SHARE))
        counts[block] = found[0:8]
        whole = jnp.concatenate(
            [packed - 1, label, jnp.zeros((128 - 2 * EXT, SHARE), jnp.int32)], axis=0
        ).astype(jnp.float32)
        info[pl.ds(pl.multiple_of(block * SHARE, SHARE), SHARE), :] = whole.T.astype(jnp.int32)
        return carry

    lax.fori_loop(0, SIDE, decode, 0)
    most = counts[...].reshape(SIDE * 8, 128)
    for step in (1, 2, 4, 8, 16, 32):
        most = jnp.maximum(most, pltpu.roll(most, step, axis=1))
    counts[...] = most.reshape(SIDE, 8, 128)
    to_smem = pltpu.make_async_copy(counts, counts_smem, sem)
    to_smem.start()

    for block in range(SIDE):
        q[block * SHARE : (block + 1) * SHARE, :] = seq_refs[block][0:SHARE, :]
    for chunk in range(SIDE):
        labels = integers(s[chunk, WIDTH:, :])
        lab8[:, chunk * 128 : (chunk + 1) * 128] = labels[0:8] * 128 + labels[8:16]
    ct[...] = jnp.zeros_like(ct)
    cm[...] = jnp.zeros_like(cm)
    to_smem.wait()
    row_of = lax.broadcasted_iota(jnp.int32, (8, SHARE), 0)

    for tile in range(tiles + 1):

        def body(step, carry, tile=tile):
            if tile < tiles:
                cols = jnp.concatenate([s[step * 2, 0:WIDTH, :], s[step * 2 + 1, 0:WIDTH, :]], axis=1)
                start = pl.multiple_of(step * STRIP, STRIP)
                buffers[tile % 2][:, pl.ds(start, STRIP)] = lax.dot_general(
                    q[tile * TILE : (tile + 1) * TILE, :],
                    cols,
                    (((1,), (0,)), ((), ())),
                    preferred_element_type=jnp.float32,
                )
            if tile > 0:
                logits = buffers[(tile - 1) % 2]

                def rows_at(group):
                    local = pl.multiple_of(step * part + group * 8, 8)
                    return local, info[pl.ds(pl.multiple_of((tile - 1) * TILE + local, 8), 8), :]

                def weights(local, chunk):
                    at = slice(chunk * 128, (chunk + 1) * 128)
                    return jnp.exp2(logits[pl.ds(local, 8), at] * (LOGIT_SCALE * LOG2E))

                zero = jnp.zeros((8, 128), jnp.float32)
                for sub in range(part // SUB):
                    groups = range(SUB // 8)
                    held = [rows_at(sub * (SUB // 8) + group) for group in groups]
                    label = [jnp.broadcast_to(code[:, SLOTS : SLOTS + 1], (8, 128)) for _, code in held]
                    wanted = [
                        [jnp.broadcast_to(code[:, pick : pick + 1], (8, 128)) for pick in range(PICKS)] for _, code in held
                    ]
                    row_total = [zero for _ in groups]
                    row_matched = [zero for _ in groups]
                    picked = [[zero] * PICKS for _ in groups]
                    for chunk in range(SIDE):
                        at = slice(chunk * 128, (chunk + 1) * 128)
                        col_label, col = lab8[:, at], lane + chunk * 128
                        col_total, col_matched = ct[:, at], cm[:, at]
                        for group in groups:
                            expo = weights(held[group][0], chunk)
                            kept = jnp.where(label[group] == col_label, expo, 0.0)
                            row_total[group] += expo
                            row_matched[group] += kept
                            col_total += expo
                            col_matched += kept
                            for pick in range(PICKS):
                                picked[group][pick] = jnp.where(
                                    wanted[group][pick] == col, expo, picked[group][pick]
                                )
                        ct[:, at] = col_total
                        cm[:, at] = col_matched
                    for group in groups:
                        local = held[group][0]
                        rt[pl.ds(local, 8), :] = row_total[group]
                        rm[pl.ds(local, 8), :] = row_matched[group]
                        ex[pl.ds(local, 8), :] = sum(picked[group][1:], picked[group][0])

                def pick_more(pick, carry):
                    for group in range(part // 8):
                        local, code = rows_at(group)
                        want = jnp.sum(jnp.where(lane == pick, code.astype(jnp.float32), 0.0), axis=1, keepdims=True)
                        want = jnp.broadcast_to(want.astype(jnp.int32), (8, 128))
                        found = zero
                        for chunk in range(SIDE):
                            found = jnp.where(want == lane + chunk * 128, weights(local, chunk), found)
                        ex[pl.ds(local, 8), :] += found
                    return carry

                block = (tile - 1) * (TILE // SHARE) + step // 2
                lax.fori_loop(PICKS, counts_smem[block, 0, (step % 2) * part + part - 1], pick_more, 0)
            return carry

        lax.fori_loop(0, strips, body, 0)
        if tile > 0:
            sums = [lanes_summed(each[...]) for each in (rt, rm, ex)]
            for inner in range(TILE // SHARE):
                block = (tile - 1) * (TILE // SHARE) + inner
                at = slice(inner * SHARE, (inner + 1) * SHARE)
                z, first = (my_z + block // 2) & 7, (my_core ^ (block % 2)) * 3
                out = jnp.zeros((8, SHARE), jnp.float32) if block % 2 == 0 else rows_ref[z]
                for which in range(3):
                    out = jnp.where(row_of == first + which, sums[which][:, at], out)
                rows_ref[z] = out

    for chunk in range(SIDE):
        at = slice(chunk * 128, (chunk + 1) * 128)
        total = jnp.sum(ct[:, at], axis=0, keepdims=True)
        matched = jnp.sum(cm[:, at], axis=0, keepdims=True)
        cols_ref[chunk] = jnp.where(row_of == 0, total, matched)


def pair_sums(place, seq_blocks, struct_blocks):
    return pl.pallas_call(
        pair_kernel,
        out_shape=(
            jax.ShapeDtypeStruct((8, 8, SHARE), jnp.float32),
            jax.ShapeDtypeStruct((SIDE, 8, SHARE), jnp.float32),
        ),
        in_specs=[SMEM] + [VMEM] * (SIDE + 1),
        out_specs=(VMEM, VMEM),
        scratch_shapes=[
            pltpu.VMEM((EDGE, WIDTH), jnp.bfloat16),
            pltpu.VMEM((SIDE, EXT, WIDTH), jnp.bfloat16),
            pltpu.VMEM((2, SLOTS, SHARE), jnp.int32),
            pltpu.VMEM((EDGE, 128), jnp.int32),
            pltpu.VMEM((SIDE, 8, 128), jnp.int32),
            pltpu.SMEM((SIDE, 8, 128), jnp.int32),
            pltpu.VMEM((TILE, EDGE), jnp.float32),
            pltpu.VMEM((TILE, EDGE), jnp.float32),
            pltpu.VMEM((8, EDGE), jnp.int32),
            pltpu.VMEM((8, EDGE), jnp.float32),
            pltpu.VMEM((8, EDGE), jnp.float32),
            pltpu.VMEM((TILE, 128), jnp.float32),
            pltpu.VMEM((TILE, 128), jnp.float32),
            pltpu.VMEM((TILE, 128), jnp.float32),
            pltpu.SemaphoreType.DMA,
        ],
        compiler_params=pltpu.CompilerParams(vmem_limit_bytes=28 * 1024 * 1024),
        cost_estimate=pl.CostEstimate(
            flops=2 * EDGE * EDGE * WIDTH, bytes_accessed=4 * EDGE * WIDTH, transcendentals=EDGE * EDGE
        ),
        name="pair_sums",
    )(place, *seq_blocks, struct_blocks)


def over_z(block):
    found = {0: block, 1: shifted(block, "z", 1), 7: shifted(block, "z", -1)}
    found[2], found[6] = shifted(found[1], "z", 1), shifted(found[7], "z", -1)
    found[3], found[5] = shifted(found[2], "z", 1), shifted(found[6], "z", -1)
    found[4] = shifted(found[3], "z", 1)
    return [found[place] for place in range(8)]


def per_device(struct_feats, seq_feats, struct_proj, seq_proj, cluster_ids, hard_owner, hard_local, hard_valid):
    place = lambda axes: lax.axis_index(axes).astype(jnp.int32)
    core, yl = place("core"), place("yl")
    keep_s, send_s = project(core.reshape(1), struct_feats, struct_proj, False, "project_struct")
    got_s = shifted(send_s, "core", 1)
    keep_q, send_q = project(core.reshape(1), seq_feats.T, seq_proj, True, "project_seq")
    got_q = shifted(send_q, "core", 1)

    keep2_s, send2_s = merge(yl.reshape(1), keep_s, got_s, "merge_struct")
    got2_s = shifted(send2_s, "yl", 1)
    keep2_q, send2_q = merge(yl.reshape(1), keep_q, got_q, "merge_seq")
    got2_q = shifted(send2_q, "yl", 1)
    cluster_ids, hard_owner, hard_local, hard_valid, send2_q = lax.optimization_barrier(
        (cluster_ids, hard_owner, hard_local, hard_valid, send2_q)
    )
    own = lambda value: lax.dynamic_slice_in_dim(value, place(MP_AXES) * SHARE, SHARE, 0)
    labels = own(cluster_ids)
    owner = own(hard_owner[:, :, 0])
    local = own(hard_local)
    block = (owner >> 3) * 2 + ((local >> 7) & 1)
    chunk = (owner & 7) * 2 + (local >> 8)
    high = jnp.where(hard_valid > 0, block * 16 + chunk, -1).T
    low = (local & 127).T
    wide = lambda value: jnp.broadcast_to(value[None], (EXT, SHARE))
    seq_ext = jnp.concatenate([high, low, wide(labels >> 7), wide(labels & 127)], axis=1).astype(jnp.bfloat16)
    struct_ext = jnp.concatenate([wide(labels >> 7)[0:8], wide(labels & 127)[0:8]], axis=0).astype(jnp.bfloat16)

    struct_peers, seq_block, self_dot = finish(keep2_s, got2_s, keep2_q, got2_q, struct_ext, seq_ext)
    struct_blocks = lax.all_to_all(struct_peers, COL_AXES, split_axis=0, concat_axis=0, tiled=True)
    seq_blocks = [each for held in over_z(seq_block) for each in (held, shifted(held, "core", 1))]

    rows, cols = pair_sums(jnp.stack([place("z"), core]), seq_blocks, struct_blocks)
    rows = jnp.sum(lax.all_to_all(rows, "z", split_axis=0, concat_axis=0, tiled=True), axis=0)
    cols = jnp.sum(lax.all_to_all(cols, COL_AXES, split_axis=0, concat_axis=0, tiled=True), axis=0)
    rows = lax.all_gather(rows, MP_AXES, axis=0, tiled=False).reshape(2, 2, 8, SHARE)
    rows = jnp.sum(rows, axis=1)[:, 0:6].reshape(2, 2, 3, SHARE)

    seq_loss = (jnp.log(rows[:, :, 0]) - jnp.log(rows[:, :, 1])).reshape(4 * SHARE)
    struct_loss = jnp.log(cols[0]) - jnp.log(cols[1])
    self_logits = LOGIT_SCALE * self_dot[0]
    extra = rows[:, :, 2].reshape(4, SHARE)[place(MP_AXES)]
    hard_loss = jnp.log(jnp.exp(self_logits) + extra) - self_logits
    return (seq_loss, struct_loss, hard_loss)


def solution(mesh):
    fine = Mesh(mesh.devices.reshape(8, 2, 4, 2, 2), ("z", "yh", "x", "yl", "core"))
    blk = ("z", "yh", "x")
    both = blk + MP_AXES
    placed = (
        P(blk, MP_AXES),
        P(blk, MP_AXES),
        P(MP_AXES, None),
        P(MP_AXES, None),
        P(blk),
        P(blk, None, None),
        P(blk, None),
        P(both, None),
    )
    return jax.shard_map(
        per_device,
        mesh=fine,
        in_specs=placed,
        out_specs=(P(blk), P(both), P(both)),
        check_vma=False,
    )
```

time: 117 us -> 110 us (0.940)
  waiting for transfers between devices: 26.3 us -> 19.2 us
  starting transfers between devices: 42.5 us -> 46 us
  blocking collectives: 9.51 us -> 6.76 us
  local copies, waits for them, and re-layouts: 6.44 us -> 4.46 us
    all_to_all x1 -> x0, blocking collectives: 9.51 us -> none  [per_device(): lax.all_to_all(cols, COL_AXES, split_axis=0, concat_axis=0, tiled=True)]
    all_gather x0 -> x1, blocking collectives: none -> 6.76 us  [per_device(): lax.all_gather(rows, MP_AXES, axis=0, tiled=False).reshape(2, 2, 8, SHARE)]
    all_to_all x2 -> x3, waiting for transfers between devices: 12.3 us -> 7.68 us  [the longest x1 6.88 us: per_device(): lax.all_to_all(rows, 'z', split_axis=0, concat_axis=0, tiled=True)]
    ppermute x17 -> x19, waiting for transfers between devices: 13.9 us -> 11.6 us  [shifted(): lax.ppermute(value, axes, [((place + steps) % count, place) for place in...]
    all_to_all x2 -> x3, starting transfers between devices: 15.5 us -> 17.8 us  [the longest x1 8.31 us: per_device(): lax.all_to_all(rows, 'z', split_axis=0, concat_axis=0, tiled=True)]
    unnamed x14 -> x12, local copies, waits for them, and re-layouts: 5.82 us -> 3.84 us
    ppermute x17 -> x19, starting transfers between devices: 27 us -> 28.2 us  [shifted(): lax.ppermute(value, axes, [((place + steps) % count, place) for place in...]
    pallas_call x4 -> x6, Pallas kernels: 28.6 us -> 29.1 us  [the longest x1 26.2 us: pair_sums(): pl.pallas_call(pair_kernel, out_shape=(jax.ShapeDtypeStruct((8, 8, SHARE)...]
  transfers between devices with their start and end apart: 19 -> 22, of which waited for: 9 -> 11; matrix products, arithmetic and copies ran while one was open for 2% -> 3% of each run, Pallas kernels for 0% -> 1%
where the time goes in v2:
time: 110 us; the launch traced here: 109 us
  starting transfers between devices  46 us (42%)
  Pallas kernels  29.1 us (26%)
  waiting for transfers between devices  19.2 us (17%)
  blocking collectives  6.76 us (6%)
  local copies, waits for them, and re-layouts  4.46 us (4%)
  other arithmetic  2.68 us (2%)
    ppermute x19, starting transfers between devices, shifted(): lax.ppermute(value, axes, [((place + steps) % count, place) for place in...  28.2 us
    pallas_call x1, Pallas kernels, pair_sums(): pl.pallas_call(pair_kernel, out_shape=(jax.ShapeDtypeStruct((8, 8, SHARE)...  26.2 us
    ppermute x19, waiting for transfers between devices, shifted(): lax.ppermute(value, axes, [((place + steps) % count, place) for place in...  11.6 us
    all_to_all x1, starting transfers between devices, per_device(): lax.all_to_all(rows, 'z', split_axis=0, concat_axis=0, tiled=True)  8.31 us
    all_to_all x1, waiting for transfers between devices, per_device(): lax.all_to_all(rows, 'z', split_axis=0, concat_axis=0, tiled=True)  6.88 us
    all_gather x1, blocking collectives, per_device(): lax.all_gather(rows, MP_AXES, axis=0, tiled=False).reshape(2, 2, 8, SHARE)  6.76 us
    all_to_all x1, starting transfers between devices, per_device(): lax.all_to_all(struct_peers, COL_AXES, split_axis=0, concat_axis=0, tiled...  5.01 us
    all_to_all x1, starting transfers between devices, per_device(): lax.all_to_all(cols, COL_AXES, split_axis=0, concat_axis=0, tiled=True)  4.43 us
  transfers between devices with their start and end apart: 22, of which 11 were waited for; matrix products, arithmetic and copies ran while one was open for 3% of the time, Pallas kernels for 1%

profile of v2, /device:TPU:1, one launch (start us, length us, event | category | flops | bytes accessed | tf_op | source)
XLA Modules:
  0.0 109.1 jit_solution(6240946458382317685)
XLA Ops:
  0.6 0.9 copy-done.2
  1.6 0.9 copy-done.3
  2.9 3.3 %collective-permute-start = (f32[2,128,512]{2,1,0:T(8,128)S(1)}, f32[2,128,512]{2,1,0:T(8,128)S(1)}, u32[]{:S(2)}, u32[]{:S(2)}) collective-permute-start(f32[2,128,512]{2,1,0:T(8,128)S(1)} %get-tuple-element.21), channel_id=1, source_target_pairs={{1,0},{0,1},{3,2},{2,3},{5,4},{4,5},{7,6},{6,7},{9,8},{8,9},{11,10... | collective-permute-start | bytes 1572872 | tf_op jit(solution)/shard_map/ppermute | solution.py:38
  6.2 1.0 copy-done
  7.2 1.0 copy-done.1
  8.2 0.7 project_seq.1
  9.2 1.7 %collective-permute-done.2.got_ref = f32[2,128,512]{2,1,0:T(8,128)S(1)} collective-permute-done((f32[2,128,512]{2,1,0:T(8,128)S(1)}, f32[2,128,512]{2,1,0:T(8,128)S(1)}, u32[]{:S(2)}, u32[]{:S(2)}) %collective-permute-start.2) | collective-permute-done | bytes 524320 | tf_op jit(solution)/shard_map/ppermute | solution.py:38
  11.0 0.8 shift-right-arithmetic_convert_fusion
  11.9 0.7 fusion.5
  12.6 1.1 %collective-permute-done.1.got2_s = bf16[128,512]{1,0:T(8,128)(2,1)S(1)} collective-permute-done((bf16[128,512]{1,0:T(8,128)(2,1)S(1)}, bf16[128,512]{1,0:T(8,128)(2,1)S(1)}, u32[]{:S(2)}, u32[]{:S(2)}) %collective-permute-start.1) | collective-permute-done | bytes 131104 | tf_op jit(solution)/shard_map/ppermute | solution.py:38
  13.8 2.8 %collective-permute-done.3.got2_q = bf16[128,512]{1,0:T(8,128)(2,1)S(1)} collective-permute-done((bf16[128,512]{1,0:T(8,128)(2,1)S(1)}, bf16[128,512]{1,0:T(8,128)(2,1)S(1)}, u32[]{:S(2)}, u32[]{:S(2)}) %collective-permute-start.3) | collective-permute-done | bytes 131104 | tf_op jit(solution)/shard_map/ppermute | solution.py:38
  16.6 1.8 %finish.1 = (bf16[16,528,128]{2,1,0:T(8,128)(2,1)}, bf16[144,512]{1,0:T(8,128)(2,1)S(1)}, f32[8,128]{1,0:T(8,128)S(1)}) custom-call(f32[128,512]{1,0:T(8,128)S(1)} %get-tuple-element.22.keep2_s, bf16[128,512]{1,0:T(8,128)(2,1)S(1)} %collective-permute-done.1.got2_s, f32[128,512]{1,0:T(8,128)S(1)} %get-tuple-element.26.keep2_q, ...), custom_call_target="tpu_custom_call" | custom-call | tf_op jit(solution)/shard_map/finish/pallas_call | solution.py:127
  18.4 5.0 %all-to-all-start = ((bf16[16,528,128]{2,1,0:T(8,128)(2,1)}), bf16[16,528,128]{2,1,0:T(8,128)(2,1)S(1)}, u32[]{:S(2)}, u32[]{:S(2)}) async-start(bf16[16,528,128]{2,1,0:T(8,128)(2,1)} %get-tuple-element.33), calls=%async_computation | async-start | bytes 4325376 | tf_op jit(solution)/shard_map/all_to_all | solution.py:359
  23.4 5.7 %collective-permute-start.5 = (bf16[144,512]{1,0:T(8,128)(2,1)S(1)}, bf16[144,512]{1,0:T(8,128)(2,1)S(1)}, u32[]{:S(2)}, u32[]{:S(2)}) collective-permute-start(bf16[144,512]{1,0:T(8,128)(2,1)S(1)} %get-tuple-element.32.refs_0_), channel_id=1, source_target_pairs={{32,0},{64,32},{96,64},{128,96},{160,128},{192,160},{224,192},{0,2... | collective-permute-start | bytes 442376 | tf_op jit(solution)/shard_map/ppermute | solution.py:38
  29.0 2.1 %collective-permute-done.5.refs_2_ = bf16[144,512]{1,0:T(8,128)(2,1)S(1)} collective-permute-done((bf16[144,512]{1,0:T(8,128)(2,1)S(1)}, bf16[144,512]{1,0:T(8,128)(2,1)S(1)}, u32[]{:S(2)}, u32[]{:S(2)}) %collective-permute-start.5) | collective-permute-done | bytes 147488 | tf_op jit(solution)/shard_map/ppermute | solution.py:38
  31.1 3.1 %collective-permute-start.7 = (bf16[144,512]{1,0:T(8,128)(2,1)S(1)}, bf16[144,512]{1,0:T(8,128)(2,1)S(1)}, u32[]{:S(2)}, u32[]{:S(2)}) collective-permute-start(bf16[144,512]{1,0:T(8,128)(2,1)S(1)} %collective-permute-done.5.refs_2_), channel_id=1, source_target_pairs={{32,0},{64,32},{96,64},{128,96},{160,128},{192,160},{224,192},{0,2... | collective-permute-start | bytes 442376 | tf_op jit(solution)/shard_map/ppermute | solution.py:38
  34.5 1.8 %collective-permute-done.7.refs_4_ = bf16[144,512]{1,0:T(8,128)(2,1)S(1)} collective-permute-done((bf16[144,512]{1,0:T(8,128)(2,1)S(1)}, bf16[144,512]{1,0:T(8,128)(2,1)S(1)}, u32[]{:S(2)}, u32[]{:S(2)}) %collective-permute-start.7) | collective-permute-done | bytes 147488 | tf_op jit(solution)/shard_map/ppermute | solution.py:38
  36.3 3.4 %collective-permute-start.9 = (bf16[144,512]{1,0:T(8,128)(2,1)S(1)}, bf16[144,512]{1,0:T(8,128)(2,1)S(1)}, u32[]{:S(2)}, u32[]{:S(2)}) collective-permute-start(bf16[144,512]{1,0:T(8,128)(2,1)S(1)} %collective-permute-done.7.refs_4_), channel_id=1, source_target_pairs={{32,0},{64,32},{96,64},{128,96},{160,128},{192,160},{224,192},{0,2... | collective-permute-start | bytes 442376 | tf_op jit(solution)/shard_map/ppermute | solution.py:38
  39.7 3.9 %collective-permute-start.4 = (bf16[144,512]{1,0:T(8,128)(2,1)S(1)}, bf16[144,512]{1,0:T(8,128)(2,1)S(1)}, u32[]{:S(2)}, u32[]{:S(2)}) collective-permute-start(bf16[144,512]{1,0:T(8,128)(2,1)S(1)} %get-tuple-element.32.refs_0_), channel_id=1, source_target_pairs={{1,0},{0,1},{3,2},{2,3},{5,4},{4,5},{7,6},{6,7},{9,8},{8,9},{11,10... | collective-permute-start | bytes 442376 | tf_op jit(solution)/shard_map/ppermute | solution.py:38
  44.1 2.7 %collective-permute-start.11 = (bf16[144,512]{1,0:T(8,128)(2,1)S(1)}, bf16[144,512]{1,0:T(8,128)(2,1)}, u32[]{:S(2)}, u32[]{:S(2)}) collective-permute-start(bf16[144,512]{1,0:T(8,128)(2,1)S(1)} %collective-permute-done.9.refs_6_), channel_id=1, source_target_pairs={{32,0},{64,32},{96,64},{128,96},{160,128},{192,160},{224,192},{0,2... | collective-permute-start | bytes 442376 | tf_op jit(solution)/shard_map/ppermute | solution.py:38
  46.8 3.2 %collective-permute-start.17 = (bf16[144,512]{1,0:T(8,128)(2,1)S(1)}, bf16[144,512]{1,0:T(8,128)(2,1)}, u32[]{:S(2)}, u32[]{:S(2)}) collective-permute-start(bf16[144,512]{1,0:T(8,128)(2,1)S(1)} %collective-permute-done.14.refs_12_), channel_id=1, source_target_pairs={{1,0},{0,1},{3,2},{2,3},{5,4},{4,5},{7,6},{6,7},{9,8},{8,9},{11,10... | collective-permute-start | bytes 442376 | tf_op jit(solution)/shard_map/ppermute | solution.py:38
  50.9 0.8 collective-permute-start.16
  51.7 0.9 collective-permute-start.12
  53.1 0.9 collective-permute-done.12.refs_9_
  54.0 0.8 all-to-all-done.refs_16_
  54.8 26.2 %pair_sums.1 = (f32[8,8,128]{2,1,0:T(8,128)}, f32[16,8,128]{2,1,0:T(8,128)}) custom-call(s32[2]{0:T(128)S(1)} %pad_add_fusion.place_ref, bf16[144,512]{1,0:T(8,128)(2,1)S(1)} %get-tuple-element.32.refs_0_, bf16[144,512]{1,0:T(8,128)(2,1)S(1)} %collective-permute-done.4.refs_1_, bf16[144,512]{1,0:T(8,128)(2,1)S(1)} %collective-permute-done.5.refs_2_, ...), custom_call_target="tpu_custom_call" | custom-call | flops 4294967296 | bytes 4194304 | tf_op jit(solution)/shard_map/pair_sums/pallas_call | solution.py:290
  81.0 8.3 %all-to-all-start.1 = ((f32[8,8,128]{2,1,0:T(8,128)}), f32[8,8,128]{2,1,0:T(8,128)S(1)}, u32[]{:S(2)}, u32[]{:S(2)}) async-start(f32[8,8,128]{2,1,0:T(8,128)} %get-tuple-element.34), calls=%async_computation.1 | async-start | bytes 65536 | tf_op jit(solution)/shard_map/all_to_all | solution.py:363
  89.3 6.9 %all-to-all-done.1 = f32[8,8,128]{2,1,0:T(8,128)S(1)} async-done(((f32[8,8,128]{2,1,0:T(8,128)}), f32[8,8,128]{2,1,0:T(8,128)S(1)}, u32[]{:S(2)}, u32[]{:S(2)}) %all-to-all-start.1) | async-done | bytes 32800 | tf_op jit(solution)/shard_map/all_to_all | solution.py:363
  96.2 4.4 %all-to-all-start.2 = ((f32[16,8,128]{2,1,0:T(8,128)}), f32[16,8,128]{2,1,0:T(8,128)S(1)}, u32[]{:S(2)}, u32[]{:S(2)}) async-start(f32[16,8,128]{2,1,0:T(8,128)} %get-tuple-element.35), calls=%async_computation.2 | async-start | bytes 131072 | tf_op jit(solution)/shard_map/all_to_all | solution.py:364
  100.6 6.8 %all-gather = f32[32,128]{1,0:T(8,128)S(1)} all-gather(f32[8,128]{1,0:T(8,128)S(1)} %reduce_sum.27), channel_id=2, replica_groups=mesh['z'=8,'yh'=2,'x'=4,'yl'=2,'core'=2] {'yl','core'}, dimensions={0}, use_global_device_ids=true | all-gather | bytes 20480 | tf_op jit(solution)/shard_map/all_gather | solution.py:365
  107.4 0.5 fusion.10
  107.9 0.6 copy.18
  (50 shorter events, 3.6 us)
Async XLA Ops:
  0.6 1.0 copy-start.2
  1.6 0.9 copy-start.3
  2.5 9.3 %copy-start.4 = (s32[512,16,1]{0,2,1:T(1,128)S(1)}, s32[512,16,1]{0,2,1:T(1,128)}, u32[]{:S(2)}) copy-start(s32[512,16,1]{0,2,1:T(1,128)} %param.13) | copy-start | bytes 98308
  2.5 9.3 %copy-start.5 = (s32[128,16]{0,1:T(8,128)S(1)}, s32[128,16]{0,1:T(8,128)}, u32[]{:S(2)}) copy-start(s32[128,16]{0,1:T(8,128)} %param.15) | copy-start | bytes 24580
  2.9 6.1 %collective-permute-start = (f32[2,128,512]{2,1,0:T(8,128)S(1)}, f32[2,128,512]{2,1,0:T(8,128)S(1)}, u32[]{:S(2)}, u32[]{:S(2)}) collective-permute-start(f32[2,128,512]{2,1,0:T(8,128)S(1)} %get-tuple-element.21), channel_id=1, source_target_pairs={{1,0},{0,1},{3,2},{2,3},{5,4},{4,5},{7,6},{6,7},{9,8},{8,9},{11,10... | collective-permute-start | bytes 1572872 | tf_op jit(solution)/shard_map/ppermute | solution.py:38
  6.2 1.0 copy-start
  7.2 1.0 copy-start.1
  8.9 2.0 %collective-permute-start.2 = (f32[2,128,512]{2,1,0:T(8,128)S(1)}, f32[2,128,512]{2,1,0:T(8,128)S(1)}, u32[]{:S(2)}, u32[]{:S(2)}) collective-permute-start(f32[2,128,512]{2,1,0:T(8,128)S(1)} %get-tuple-element.25), channel_id=1, source_target_pairs={{1,0},{0,1},{3,2},{2,3},{5,4},{4,5},{7,6},{6,7},{9,8},{8,9},{11,10... | collective-permute-start | bytes 1572872 | tf_op jit(solution)/shard_map/ppermute | solution.py:38
  9.1 4.7 %collective-permute-start.1 = (bf16[128,512]{1,0:T(8,128)(2,1)S(1)}, bf16[128,512]{1,0:T(8,128)(2,1)S(1)}, u32[]{:S(2)}, u32[]{:S(2)}) collective-permute-start(bf16[128,512]{1,0:T(8,128)(2,1)S(1)} %get-tuple-element.23), channel_id=1, source_target_pairs={{2,0},{0,2},{3,1},{1,3},{6,4},{4,6},{7,5},{5,7},{10,8},{8,10},{11,... | collective-permute-start | bytes 393224 | tf_op jit(solution)/shard_map/ppermute | solution.py:38
  10.9 5.6 %collective-permute-start.3 = (bf16[128,512]{1,0:T(8,128)(2,1)S(1)}, bf16[128,512]{1,0:T(8,128)(2,1)S(1)}, u32[]{:S(2)}, u32[]{:S(2)}) collective-permute-start(bf16[128,512]{1,0:T(8,128)(2,1)S(1)} %get-tuple-element.27), channel_id=1, source_target_pairs={{2,0},{0,2},{3,1},{1,3},{6,4},{4,6},{7,5},{5,7},{10,8},{8,10},{11,... | collective-permute-start | bytes 393224 | tf_op jit(solution)/shard_map/ppermute | solution.py:38
  18.4 36.4 %all-to-all-start = ((bf16[16,528,128]{2,1,0:T(8,128)(2,1)}), bf16[16,528,128]{2,1,0:T(8,128)(2,1)S(1)}, u32[]{:S(2)}, u32[]{:S(2)}) async-start(bf16[16,528,128]{2,1,0:T(8,128)(2,1)} %get-tuple-element.33), calls=%async_computation | async-start | bytes 4325376 | tf_op jit(solution)/shard_map/all_to_all | solution.py:359
  23.4 7.8 %collective-permute-start.5 = (bf16[144,512]{1,0:T(8,128)(2,1)S(1)}, bf16[144,512]{1,0:T(8,128)(2,1)S(1)}, u32[]{:S(2)}, u32[]{:S(2)}) collective-permute-start(bf16[144,512]{1,0:T(8,128)(2,1)S(1)} %get-tuple-element.32.refs_0_), channel_id=1, source_target_pairs={{32,0},{64,32},{96,64},{128,96},{160,128},{192,160},{224,192},{0,2... | collective-permute-start | bytes 442376 | tf_op jit(solution)/shard_map/ppermute | solution.py:38
  29.0 5.5 %collective-permute-start.13 = (bf16[144,512]{1,0:T(8,128)(2,1)S(1)}, bf16[144,512]{1,0:T(8,128)(2,1)S(1)}, u32[]{:S(2)}, u32[]{:S(2)}) collective-permute-start(bf16[144,512]{1,0:T(8,128)(2,1)S(1)} %get-tuple-element.32.refs_0_), channel_id=1, source_target_pairs={{224,0},{0,32},{32,64},{64,96},{96,128},{128,160},{160,192},{192,2... | collective-permute-start | bytes 442376 | tf_op jit(solution)/shard_map/ppermute | solution.py:38
  31.1 5.2 %collective-permute-start.7 = (bf16[144,512]{1,0:T(8,128)(2,1)S(1)}, bf16[144,512]{1,0:T(8,128)(2,1)S(1)}, u32[]{:S(2)}, u32[]{:S(2)}) collective-permute-start(bf16[144,512]{1,0:T(8,128)(2,1)S(1)} %collective-permute-done.5.refs_2_), channel_id=1, source_target_pairs={{32,0},{64,32},{96,64},{128,96},{160,128},{192,160},{224,192},{0,2... | collective-permute-start | bytes 442376 | tf_op jit(solution)/shard_map/ppermute | solution.py:38
  34.5 9.6 %collective-permute-start.14 = (bf16[144,512]{1,0:T(8,128)(2,1)S(1)}, bf16[144,512]{1,0:T(8,128)(2,1)S(1)}, u32[]{:S(2)}, u32[]{:S(2)}) collective-permute-start(bf16[144,512]{1,0:T(8,128)(2,1)S(1)} %collective-permute-done.13.refs_14_), channel_id=1, source_target_pairs={{224,0},{0,32},{32,64},{64,96},{96,128},{128,160},{160,192},{192,2... | collective-permute-start | bytes 442376 | tf_op jit(solution)/shard_map/ppermute | solution.py:38
  36.3 7.8 %collective-permute-start.9 = (bf16[144,512]{1,0:T(8,128)(2,1)S(1)}, bf16[144,512]{1,0:T(8,128)(2,1)S(1)}, u32[]{:S(2)}, u32[]{:S(2)}) collective-permute-start(bf16[144,512]{1,0:T(8,128)(2,1)S(1)} %collective-permute-done.7.refs_4_), channel_id=1, source_target_pairs={{32,0},{64,32},{96,64},{128,96},{160,128},{192,160},{224,192},{0,2... | collective-permute-start | bytes 442376 | tf_op jit(solution)/shard_map/ppermute | solution.py:38
  39.7 7.1 %collective-permute-start.4 = (bf16[144,512]{1,0:T(8,128)(2,1)S(1)}, bf16[144,512]{1,0:T(8,128)(2,1)S(1)}, u32[]{:S(2)}, u32[]{:S(2)}) collective-permute-start(bf16[144,512]{1,0:T(8,128)(2,1)S(1)} %get-tuple-element.32.refs_0_), channel_id=1, source_target_pairs={{1,0},{0,1},{3,2},{2,3},{5,4},{4,5},{7,6},{6,7},{9,8},{8,9},{11,10... | collective-permute-start | bytes 442376 | tf_op jit(solution)/shard_map/ppermute | solution.py:38
  43.6 6.4 %collective-permute-start.18 = (bf16[144,512]{1,0:T(8,128)(2,1)S(1)}, bf16[144,512]{1,0:T(8,128)(2,1)S(1)}, u32[]{:S(2)}, u32[]{:S(2)}) collective-permute-start(bf16[144,512]{1,0:T(8,128)(2,1)S(1)} %collective-permute-done.13.refs_14_), channel_id=1, source_target_pairs={{1,0},{0,1},{3,2},{2,3},{5,4},{4,5},{7,6},{6,7},{9,8},{8,9},{11,10... | collective-permute-start | bytes 442376 | tf_op jit(solution)/shard_map/ppermute | solution.py:38
  43.6 6.5 %collective-permute-start.6 = (bf16[144,512]{1,0:T(8,128)(2,1)S(1)}, bf16[144,512]{1,0:T(8,128)(2,1)S(1)}, u32[]{:S(2)}, u32[]{:S(2)}) collective-permute-start(bf16[144,512]{1,0:T(8,128)(2,1)S(1)} %collective-permute-done.5.refs_2_), channel_id=1, source_target_pairs={{1,0},{0,1},{3,2},{2,3},{5,4},{4,5},{7,6},{6,7},{9,8},{8,9},{11,10... | collective-permute-start | bytes 442376 | tf_op jit(solution)/shard_map/ppermute | solution.py:38
  44.1 6.8 %collective-permute-start.15 = (bf16[144,512]{1,0:T(8,128)(2,1)S(1)}, bf16[144,512]{1,0:T(8,128)(2,1)}, u32[]{:S(2)}, u32[]{:S(2)}) collective-permute-start(bf16[144,512]{1,0:T(8,128)(2,1)S(1)} %collective-permute-done.14.refs_12_), channel_id=1, source_target_pairs={{224,0},{0,32},{32,64},{64,96},{96,128},{128,160},{160,192},{192,2... | collective-permute-start | bytes 442376 | tf_op jit(solution)/shard_map/ppermute | solution.py:38
  44.1 7.6 %collective-permute-start.11 = (bf16[144,512]{1,0:T(8,128)(2,1)S(1)}, bf16[144,512]{1,0:T(8,128)(2,1)}, u32[]{:S(2)}, u32[]{:S(2)}) collective-permute-start(bf16[144,512]{1,0:T(8,128)(2,1)S(1)} %collective-permute-done.9.refs_6_), channel_id=1, source_target_pairs={{32,0},{64,32},{96,64},{128,96},{160,128},{192,160},{224,192},{0,2... | collective-permute-start | bytes 442376 | tf_op jit(solution)/shard_map/ppermute | solution.py:38
  46.8 5.9 %collective-permute-start.17 = (bf16[144,512]{1,0:T(8,128)(2,1)S(1)}, bf16[144,512]{1,0:T(8,128)(2,1)}, u32[]{:S(2)}, u32[]{:S(2)}) collective-permute-start(bf16[144,512]{1,0:T(8,128)(2,1)S(1)} %collective-permute-done.14.refs_12_), channel_id=1, source_target_pairs={{1,0},{0,1},{3,2},{2,3},{5,4},{4,5},{7,6},{6,7},{9,8},{8,9},{11,10... | collective-permute-start | bytes 442376 | tf_op jit(solution)/shard_map/ppermute | solution.py:38
  50.0 2.8 %collective-permute-start.8 = (bf16[144,512]{1,0:T(8,128)(2,1)S(1)}, bf16[144,512]{1,0:T(8,128)(2,1)}, u32[]{:S(2)}, u32[]{:S(2)}) collective-permute-start(bf16[144,512]{1,0:T(8,128)(2,1)S(1)} %collective-permute-done.7.refs_4_), channel_id=1, source_target_pairs={{1,0},{0,1},{3,2},{2,3},{5,4},{4,5},{7,6},{6,7},{9,8},{8,9},{11,10... | collective-permute-start | bytes 442376 | tf_op jit(solution)/shard_map/ppermute | solution.py:38
  50.1 3.0 %collective-permute-start.10 = (bf16[144,512]{1,0:T(8,128)(2,1)S(1)}, bf16[144,512]{1,0:T(8,128)(2,1)}, u32[]{:S(2)}, u32[]{:S(2)}) collective-permute-start(bf16[144,512]{1,0:T(8,128)(2,1)S(1)} %collective-permute-done.9.refs_6_), channel_id=1, source_target_pairs={{1,0},{0,1},{3,2},{2,3},{5,4},{4,5},{7,6},{6,7},{9,8},{8,9},{11,10... | collective-permute-start | bytes 442376 | tf_op jit(solution)/shard_map/ppermute | solution.py:38
  50.9 2.1 %collective-permute-start.16 = (bf16[144,512]{1,0:T(8,128)(2,1)}, bf16[144,512]{1,0:T(8,128)(2,1)}, u32[]{:S(2)}, u32[]{:S(2)}) collective-permute-start(bf16[144,512]{1,0:T(8,128)(2,1)} %collective-permute-done.15.refs_10_), channel_id=1, source_target_pairs={{1,0},{0,1},{3,2},{2,3},{5,4},{4,5},{7,6},{6,7},{9,8},{8,9},{11,10... | collective-permute-start | bytes 442376 | tf_op jit(solution)/shard_map/ppermute | solution.py:38
  51.7 2.3 %collective-permute-start.12 = (bf16[144,512]{1,0:T(8,128)(2,1)}, bf16[144,512]{1,0:T(8,128)(2,1)}, u32[]{:S(2)}, u32[]{:S(2)}) collective-permute-start(bf16[144,512]{1,0:T(8,128)(2,1)} %collective-permute-done.11.refs_8_), channel_id=1, source_target_pairs={{1,0},{0,1},{3,2},{2,3},{5,4},{4,5},{7,6},{6,7},{9,8},{8,9},{11,10... | collective-permute-start | bytes 442376 | tf_op jit(solution)/shard_map/ppermute | solution.py:38
  81.0 15.2 %all-to-all-start.1 = ((f32[8,8,128]{2,1,0:T(8,128)}), f32[8,8,128]{2,1,0:T(8,128)S(1)}, u32[]{:S(2)}, u32[]{:S(2)}) async-start(f32[8,8,128]{2,1,0:T(8,128)} %get-tuple-element.34), calls=%async_computation.1 | async-start | bytes 65536 | tf_op jit(solution)/shard_map/all_to_all | solution.py:363
  96.2 12.4 %all-to-all-start.2 = ((f32[16,8,128]{2,1,0:T(8,128)}), f32[16,8,128]{2,1,0:T(8,128)S(1)}, u32[]{:S(2)}, u32[]{:S(2)}) async-start(f32[16,8,128]{2,1,0:T(8,128)} %get-tuple-element.35), calls=%async_computation.2 | async-start | bytes 131072 | tf_op jit(solution)/shard_map/all_to_all | solution.py:364

commit v3 on v2

--- a/solution.py
+++ b/solution.py
@@ -11,6 +11,7 @@
 LOGIT_SCALE = 14.285714285714286
 EPSILON = 1e-06
 LOG2E = math.log2(math.e)
+POLYNOMIAL = (4.626287491105563e-06, 0.00010370556301479831, 0.001853591056490648, 0.024912203935707634, 0.22321428590727893, 1.0000000060541538)
 
 SHARE = 128
 SIDE = 16
@@ -19,9 +20,8 @@
 SLOTS = 16
 EXT = 16
 TILE = 512
-STRIP = 256
+STRIP = 512
 SUB = 32
-PICKS = 3
 
 COL_AXES = ("yh", "x", "yl")
 MP_AXES = ("yl", "core")
@@ -142,64 +142,49 @@
     return values.astype(jnp.float32).astype(jnp.int32)
 
 
+def exponential(products):
+    power = products * POLYNOMIAL[0] + POLYNOMIAL[1]
+    for coefficient in POLYNOMIAL[2:]:
+        power = power * products + coefficient
+    for _ in range(6):
+        power = power * power
+    return power
+
+
 def pair_kernel(place_ref, *refs):
     seq_refs, s, rows_ref, cols_ref = refs[0:SIDE], refs[SIDE], refs[SIDE + 1], refs[SIDE + 2]
-    q, ext_all, slots, info, counts, counts_smem, buf0, buf1, lab8, ct, cm, rt, rm, ex, sem = refs[SIDE + 3 :]
+    q, info, buf0, buf1, lab8, ct, cm, rt, rm, ex = refs[SIDE + 3 :]
     tiles = EDGE // TILE
     strips = EDGE // STRIP
     part = TILE // strips
     buffers = (buf0, buf1)
     my_z, my_core = place_ref[0], place_ref[1]
     my_block = my_z * 2 + my_core
-    lane = lax.broadcasted_iota(jnp.int32, (8, 128), 1)
 
     for block in range(SIDE):
-        ext_all[block] = seq_refs[block][SHARE:, :]
-
-    def decode(block, carry):
-        ext = integers(ext_all[block])
+        at = slice(block * SHARE, (block + 1) * SHARE)
+        q[at, :] = seq_refs[block][0:SHARE, :]
+        ext = integers(seq_refs[block][SHARE:, :])
         high, low = ext[:, 0:SHARE], ext[:, SHARE : 2 * SHARE]
         label = ext[:, 2 * SHARE : 3 * SHARE] * 128 + ext[:, 3 * SHARE :]
-        hit = (high >> 4) == my_block
-        slots[0] = jnp.where(hit, 1, 0)
-        slots[1] = jnp.where(hit, (high & 15) * 128 + low + 1, 0)
-        order = lax.broadcasted_iota(jnp.int32, (SLOTS, SHARE), 0)
-        packed = jnp.zeros((SLOTS, SHARE), jnp.int32)
-        found = jnp.zeros((SLOTS, SHARE), jnp.int32)
-        for slot in range(SLOTS):
-            code = jnp.broadcast_to(slots[1, slot : slot + 1, :], (SLOTS, SHARE))
-            packed = packed + jnp.where(order == found, code, 0)
-            found = found + jnp.broadcast_to(slots[0, slot : slot + 1, :], (SLOTS, SHARE))
-        counts[block] = found[0:8]
+        code = jnp.where((high >> 4) == my_block, (high & 15) * 128 + low, -1)
         whole = jnp.concatenate(
-            [packed - 1, label, jnp.zeros((128 - 2 * EXT, SHARE), jnp.int32)], axis=0
+            [code, -1 - label, jnp.full((128 - 2 * EXT, SHARE), -1, jnp.int32)], axis=0
         ).astype(jnp.float32)
-        info[pl.ds(pl.multiple_of(block * SHARE, SHARE), SHARE), :] = whole.T.astype(jnp.int32)
-        return carry
-
-    lax.fori_loop(0, SIDE, decode, 0)
-    most = counts[...].reshape(SIDE * 8, 128)
-    for step in (1, 2, 4, 8, 16, 32):
-        most = jnp.maximum(most, pltpu.roll(most, step, axis=1))
-    counts[...] = most.reshape(SIDE, 8, 128)
-    to_smem = pltpu.make_async_copy(counts, counts_smem, sem)
-    to_smem.start()
-
-    for block in range(SIDE):
-        q[block * SHARE : (block + 1) * SHARE, :] = seq_refs[block][0:SHARE, :]
+        info[at, :] = whole.T.astype(jnp.int32)
     for chunk in range(SIDE):
         labels = integers(s[chunk, WIDTH:, :])
         lab8[:, chunk * 128 : (chunk + 1) * 128] = labels[0:8] * 128 + labels[8:16]
     ct[...] = jnp.zeros_like(ct)
     cm[...] = jnp.zeros_like(cm)
-    to_smem.wait()
     row_of = lax.broadcasted_iota(jnp.int32, (8, SHARE), 0)
 
     for tile in range(tiles + 1):
 
         def body(step, carry, tile=tile):
             if tile < tiles:
-                cols = jnp.concatenate([s[step * 2, 0:WIDTH, :], s[step * 2 + 1, 0:WIDTH, :]], axis=1)
+                wide = STRIP // SHARE
+                cols = jnp.concatenate([s[step * wide + each, 0:WIDTH, :] for each in range(wide)], axis=1)
                 start = pl.multiple_of(step * STRIP, STRIP)
                 buffers[tile % 2][:, pl.ds(start, STRIP)] = lax.dot_general(
                     q[tile * TILE : (tile + 1) * TILE, :],
@@ -208,63 +193,39 @@
                     preferred_element_type=jnp.float32,
                 )
             if tile > 0:
-                logits = buffers[(tile - 1) % 2]
-
-                def rows_at(group):
-                    local = pl.multiple_of(step * part + group * 8, 8)
-                    return local, info[pl.ds(pl.multiple_of((tile - 1) * TILE + local, 8), 8), :]
-
-                def weights(local, chunk):
-                    at = slice(chunk * 128, (chunk + 1) * 128)
-                    return jnp.exp2(logits[pl.ds(local, 8), at] * (LOGIT_SCALE * LOG2E))
-
+                products = buffers[(tile - 1) % 2]
                 zero = jnp.zeros((8, 128), jnp.float32)
+                groups = range(SUB // 8)
                 for sub in range(part // SUB):
-                    groups = range(SUB // 8)
-                    held = [rows_at(sub * (SUB // 8) + group) for group in groups]
-                    label = [jnp.broadcast_to(code[:, SLOTS : SLOTS + 1], (8, 128)) for _, code in held]
-                    wanted = [
-                        [jnp.broadcast_to(code[:, pick : pick + 1], (8, 128)) for pick in range(PICKS)] for _, code in held
-                    ]
-                    row_total = [zero for _ in groups]
-                    row_matched = [zero for _ in groups]
-                    picked = [[zero] * PICKS for _ in groups]
+                    local = [pl.multiple_of(step * part + sub * SUB + group * 8, 8) for group in groups]
+                    code = [info[pl.ds(pl.multiple_of((tile - 1) * TILE + each, 8), 8), :] for each in local]
+                    label = [jnp.broadcast_to(-1 - each[:, SLOTS : SLOTS + 1], (8, 128)) for each in code]
+                    lane = [each & 127 for each in code]
+                    chunk_of = [each >> 7 for each in code]
+                    row_total, row_matched, picked = [zero for _ in groups], [zero for _ in groups], [zero for _ in groups]
                     for chunk in range(SIDE):
                         at = slice(chunk * 128, (chunk + 1) * 128)
-                        col_label, col = lab8[:, at], lane + chunk * 128
+                        col_label = lab8[:, at]
                         col_total, col_matched = ct[:, at], cm[:, at]
                         for group in groups:
-                            expo = weights(held[group][0], chunk)
+                            product = products[pl.ds(local[group], 8), at]
+                            if chunk % 2:
+                                expo = exponential(product)
+                            else:
+                                expo = jnp.exp2(product * (LOGIT_SCALE * LOG2E))
                             kept = jnp.where(label[group] == col_label, expo, 0.0)
                             row_total[group] += expo
                             row_matched[group] += kept
                             col_total += expo
                             col_matched += kept
-                            for pick in range(PICKS):
-                                picked[group][pick] = jnp.where(
-                                    wanted[group][pick] == col, expo, picked[group][pick]
-                                )
+                            found = jnp.take_along_axis(expo, lane[group], axis=1, mode="promise_in_bounds")
+                            picked[group] = jnp.where(chunk_of[group] == chunk, found, picked[group])
                         ct[:, at] = col_total
                         cm[:, at] = col_matched
                     for group in groups:
-                        local = held[group][0]
-                        rt[pl.ds(local, 8), :] = row_total[group]
-                        rm[pl.ds(local, 8), :] = row_matched[group]
-                        ex[pl.ds(local, 8), :] = sum(picked[group][1:], picked[group][0])
-
-                def pick_more(pick, carry):
-                    for group in range(part // 8):
-                        local, code = rows_at(group)
-                        want = jnp.sum(jnp.where(lane == pick, code.astype(jnp.float32), 0.0), axis=1, keepdims=True)
-                        want = jnp.broadcast_to(want.astype(jnp.int32), (8, 128))
-                        found = zero
-                        for chunk in range(SIDE):
-                            found = jnp.where(want == lane + chunk * 128, weights(local, chunk), found)
-                        ex[pl.ds(local, 8), :] += found
-                    return carry
-
-                block = (tile - 1) * (TILE // SHARE) + step // 2
-                lax.fori_loop(PICKS, counts_smem[block, 0, (step % 2) * part + part - 1], pick_more, 0)
+                        rt[pl.ds(local[group], 8), :] = row_total[group]
+                        rm[pl.ds(local[group], 8), :] = row_matched[group]
+                        ex[pl.ds(local[group], 8), :] = picked[group]
             return carry
 
         lax.fori_loop(0, strips, body, 0)
@@ -297,11 +258,7 @@
         out_specs=(VMEM, VMEM),
         scratch_shapes=[
             pltpu.VMEM((EDGE, WIDTH), jnp.bfloat16),
-            pltpu.VMEM((SIDE, EXT, WIDTH), jnp.bfloat16),
-            pltpu.VMEM((2, SLOTS, SHARE), jnp.int32),
             pltpu.VMEM((EDGE, 128), jnp.int32),
-            pltpu.VMEM((SIDE, 8, 128), jnp.int32),
-            pltpu.SMEM((SIDE, 8, 128), jnp.int32),
             pltpu.VMEM((TILE, EDGE), jnp.float32),
             pltpu.VMEM((TILE, EDGE), jnp.float32),
             pltpu.VMEM((8, EDGE), jnp.int32),
@@ -310,7 +267,6 @@
             pltpu.VMEM((TILE, 128), jnp.float32),
             pltpu.VMEM((TILE, 128), jnp.float32),
             pltpu.VMEM((TILE, 128), jnp.float32),
-            pltpu.SemaphoreType.DMA,
         ],
         compiler_params=pltpu.CompilerParams(vmem_limit_bytes=28 * 1024 * 1024),
         cost_estimate=pl.CostEstimate(

time: 110 us -> 104 us (0.945)
  Pallas kernels: 29.1 us -> 23.3 us
  starting transfers between devices: 46 us -> 44.9 us
    pallas_call x1, Pallas kernels: 26.2 us -> 20.4 us  [pair_sums(): pl.pallas_call(pair_kernel, out_shape=(jax.ShapeDtypeStruct((8, 8, SHARE)...]
where the time goes in v3:
time: 104 us; the launch traced here: 103 us
  starting transfers between devices  44.9 us (43%)
  Pallas kernels  23.3 us (22%)
  waiting for transfers between devices  19.2 us (18%)
  blocking collectives  7.82 us (8%)
  local copies, waits for them, and re-layouts  4.46 us (4%)
  other arithmetic  2.68 us (3%)
    ppermute x19, starting transfers between devices, shifted(): lax.ppermute(value, axes, [((place + steps) % count, place) for place in...  28.2 us
    pallas_call x1, Pallas kernels, pair_sums(): pl.pallas_call(pair_kernel, out_shape=(jax.ShapeDtypeStruct((8, 8, SHARE)...  20.4 us
    ppermute x19, waiting for transfers between devices, shifted(): lax.ppermute(value, axes, [((place + steps) % count, place) for place in...  11.6 us
    all_to_all x1, starting transfers between devices, per_device(): lax.all_to_all(rows, 'z', split_axis=0, concat_axis=0, tiled=True)  8.19 us
    all_gather x1, blocking collectives, per_device(): lax.all_gather(rows, MP_AXES, axis=0, tiled=False).reshape(2, 2, 8, SHARE)  7.82 us
    all_to_all x1, waiting for transfers between devices, per_device(): lax.all_to_all(rows, 'z', split_axis=0, concat_axis=0, tiled=True)  6.88 us
    all_to_all x1, starting transfers between devices, per_device(): lax.all_to_all(struct_peers, COL_AXES, split_axis=0, concat_axis=0, tiled...  5.01 us
    unnamed x12, local copies, waits for them, and re-layouts  3.84 us
  transfers between devices with their start and end apart: 22, of which 11 were waited for; matrix products, arithmetic and copies ran while one was open for 3% of the time, Pallas kernels for 1%

profile of v3, /device:TPU:1, one launch (start us, length us, event | category | flops | bytes accessed | tf_op | source)
XLA Modules:
  0.0 103.3 jit_solution(3369116503274348177)
XLA Ops:
  0.6 0.9 copy-done.2
  1.6 0.9 copy-done.3
  2.9 3.3 %collective-permute-start = (f32[2,128,512]{2,1,0:T(8,128)S(1)}, f32[2,128,512]{2,1,0:T(8,128)S(1)}, u32[]{:S(2)}, u32[]{:S(2)}) collective-permute-start(f32[2,128,512]{2,1,0:T(8,128)S(1)} %get-tuple-element.21), channel_id=1, source_target_pairs={{1,0},{0,1},{3,2},{2,3},{5,4},{4,5},{7,6},{6,7},{9,8},{8,9},{11,10... | collective-permute-start | bytes 1572872 | tf_op jit(solution)/shard_map/ppermute | solution.py:38
  6.2 1.0 copy-done
  7.2 1.0 copy-done.1
  8.2 0.7 project_seq.1
  9.2 1.7 %collective-permute-done.2.got_ref = f32[2,128,512]{2,1,0:T(8,128)S(1)} collective-permute-done((f32[2,128,512]{2,1,0:T(8,128)S(1)}, f32[2,128,512]{2,1,0:T(8,128)S(1)}, u32[]{:S(2)}, u32[]{:S(2)}) %collective-permute-start.2) | collective-permute-done | bytes 524320 | tf_op jit(solution)/shard_map/ppermute | solution.py:38
  11.0 0.8 shift-right-arithmetic_convert_fusion
  11.9 0.7 fusion.5
  12.6 1.1 %collective-permute-done.1.got2_s = bf16[128,512]{1,0:T(8,128)(2,1)S(1)} collective-permute-done((bf16[128,512]{1,0:T(8,128)(2,1)S(1)}, bf16[128,512]{1,0:T(8,128)(2,1)S(1)}, u32[]{:S(2)}, u32[]{:S(2)}) %collective-permute-start.1) | collective-permute-done | bytes 131104 | tf_op jit(solution)/shard_map/ppermute | solution.py:38
  13.8 2.8 %collective-permute-done.3.got2_q = bf16[128,512]{1,0:T(8,128)(2,1)S(1)} collective-permute-done((bf16[128,512]{1,0:T(8,128)(2,1)S(1)}, bf16[128,512]{1,0:T(8,128)(2,1)S(1)}, u32[]{:S(2)}, u32[]{:S(2)}) %collective-permute-start.3) | collective-permute-done | bytes 131104 | tf_op jit(solution)/shard_map/ppermute | solution.py:38
  16.6 1.8 %finish.1 = (bf16[16,528,128]{2,1,0:T(8,128)(2,1)}, bf16[144,512]{1,0:T(8,128)(2,1)S(1)}, f32[8,128]{1,0:T(8,128)S(1)}) custom-call(f32[128,512]{1,0:T(8,128)S(1)} %get-tuple-element.22.keep2_s, bf16[128,512]{1,0:T(8,128)(2,1)S(1)} %collective-permute-done.1.got2_s, f32[128,512]{1,0:T(8,128)S(1)} %get-tuple-element.26.keep2_q, ...), custom_call_target="tpu_custom_call" | custom-call | tf_op jit(solution)/shard_map/finish/pallas_call | solution.py:127
  18.4 5.0 %all-to-all-start = ((bf16[16,528,128]{2,1,0:T(8,128)(2,1)}), bf16[16,528,128]{2,1,0:T(8,128)(2,1)S(1)}, u32[]{:S(2)}, u32[]{:S(2)}) async-start(bf16[16,528,128]{2,1,0:T(8,128)(2,1)} %get-tuple-element.33), calls=%async_computation | async-start | bytes 4325376 | tf_op jit(solution)/shard_map/all_to_all | solution.py:315
  23.4 5.7 %collective-permute-start.5 = (bf16[144,512]{1,0:T(8,128)(2,1)S(1)}, bf16[144,512]{1,0:T(8,128)(2,1)S(1)}, u32[]{:S(2)}, u32[]{:S(2)}) collective-permute-start(bf16[144,512]{1,0:T(8,128)(2,1)S(1)} %get-tuple-element.32.refs_0_), channel_id=1, source_target_pairs={{32,0},{64,32},{96,64},{128,96},{160,128},{192,160},{224,192},{0,2... | collective-permute-start | bytes 442376 | tf_op jit(solution)/shard_map/ppermute | solution.py:38
  29.0 2.1 %collective-permute-done.5.refs_2_ = bf16[144,512]{1,0:T(8,128)(2,1)S(1)} collective-permute-done((bf16[144,512]{1,0:T(8,128)(2,1)S(1)}, bf16[144,512]{1,0:T(8,128)(2,1)S(1)}, u32[]{:S(2)}, u32[]{:S(2)}) %collective-permute-start.5) | collective-permute-done | bytes 147488 | tf_op jit(solution)/shard_map/ppermute | solution.py:38
  31.1 3.1 %collective-permute-start.7 = (bf16[144,512]{1,0:T(8,128)(2,1)S(1)}, bf16[144,512]{1,0:T(8,128)(2,1)S(1)}, u32[]{:S(2)}, u32[]{:S(2)}) collective-permute-start(bf16[144,512]{1,0:T(8,128)(2,1)S(1)} %collective-permute-done.5.refs_2_), channel_id=1, source_target_pairs={{32,0},{64,32},{96,64},{128,96},{160,128},{192,160},{224,192},{0,2... | collective-permute-start | bytes 442376 | tf_op jit(solution)/shard_map/ppermute | solution.py:38
  34.5 1.8 %collective-permute-done.7.refs_4_ = bf16[144,512]{1,0:T(8,128)(2,1)S(1)} collective-permute-done((bf16[144,512]{1,0:T(8,128)(2,1)S(1)}, bf16[144,512]{1,0:T(8,128)(2,1)S(1)}, u32[]{:S(2)}, u32[]{:S(2)}) %collective-permute-start.7) | collective-permute-done | bytes 147488 | tf_op jit(solution)/shard_map/ppermute | solution.py:38
  36.3 3.4 %collective-permute-start.9 = (bf16[144,512]{1,0:T(8,128)(2,1)S(1)}, bf16[144,512]{1,0:T(8,128)(2,1)S(1)}, u32[]{:S(2)}, u32[]{:S(2)}) collective-permute-start(bf16[144,512]{1,0:T(8,128)(2,1)S(1)} %collective-permute-done.7.refs_4_), channel_id=1, source_target_pairs={{32,0},{64,32},{96,64},{128,96},{160,128},{192,160},{224,192},{0,2... | collective-permute-start | bytes 442376 | tf_op jit(solution)/shard_map/ppermute | solution.py:38
  39.7 3.9 %collective-permute-start.4 = (bf16[144,512]{1,0:T(8,128)(2,1)S(1)}, bf16[144,512]{1,0:T(8,128)(2,1)S(1)}, u32[]{:S(2)}, u32[]{:S(2)}) collective-permute-start(bf16[144,512]{1,0:T(8,128)(2,1)S(1)} %get-tuple-element.32.refs_0_), channel_id=1, source_target_pairs={{1,0},{0,1},{3,2},{2,3},{5,4},{4,5},{7,6},{6,7},{9,8},{8,9},{11,10... | collective-permute-start | bytes 442376 | tf_op jit(solution)/shard_map/ppermute | solution.py:38
  44.1 2.7 %collective-permute-start.11 = (bf16[144,512]{1,0:T(8,128)(2,1)S(1)}, bf16[144,512]{1,0:T(8,128)(2,1)}, u32[]{:S(2)}, u32[]{:S(2)}) collective-permute-start(bf16[144,512]{1,0:T(8,128)(2,1)S(1)} %collective-permute-done.9.refs_6_), channel_id=1, source_target_pairs={{32,0},{64,32},{96,64},{128,96},{160,128},{192,160},{224,192},{0,2... | collective-permute-start | bytes 442376 | tf_op jit(solution)/shard_map/ppermute | solution.py:38
  46.8 3.2 %collective-permute-start.17 = (bf16[144,512]{1,0:T(8,128)(2,1)S(1)}, bf16[144,512]{1,0:T(8,128)(2,1)}, u32[]{:S(2)}, u32[]{:S(2)}) collective-permute-start(bf16[144,512]{1,0:T(8,128)(2,1)S(1)} %collective-permute-done.14.refs_12_), channel_id=1, source_target_pairs={{1,0},{0,1},{3,2},{2,3},{5,4},{4,5},{7,6},{6,7},{9,8},{8,9},{11,10... | collective-permute-start | bytes 442376 | tf_op jit(solution)/shard_map/ppermute | solution.py:38
  50.9 0.8 collective-permute-start.16
  51.7 0.9 collective-permute-start.12
  53.1 0.9 collective-permute-done.12.refs_9_
  54.0 0.8 all-to-all-done.refs_16_
  54.8 20.4 %pair_sums.1 = (f32[8,8,128]{2,1,0:T(8,128)}, f32[16,8,128]{2,1,0:T(8,128)}) custom-call(s32[2]{0:T(128)S(1)} %pad_add_fusion.place_ref, bf16[144,512]{1,0:T(8,128)(2,1)S(1)} %get-tuple-element.32.refs_0_, bf16[144,512]{1,0:T(8,128)(2,1)S(1)} %collective-permute-done.4.refs_1_, bf16[144,512]{1,0:T(8,128)(2,1)S(1)} %collective-permute-done.5.refs_2_, ...), custom_call_target="tpu_custom_call" | custom-call | flops 4294967296 | bytes 4194304 | tf_op jit(solution)/shard_map/pair_sums/pallas_call | solution.py:251
  75.2 8.2 %all-to-all-start.1 = ((f32[8,8,128]{2,1,0:T(8,128)}), f32[8,8,128]{2,1,0:T(8,128)S(1)}, u32[]{:S(2)}, u32[]{:S(2)}) async-start(f32[8,8,128]{2,1,0:T(8,128)} %get-tuple-element.34), calls=%async_computation.1 | async-start | bytes 65536 | tf_op jit(solution)/shard_map/all_to_all | solution.py:319
  83.4 6.9 %all-to-all-done.1 = f32[8,8,128]{2,1,0:T(8,128)S(1)} async-done(((f32[8,8,128]{2,1,0:T(8,128)}), f32[8,8,128]{2,1,0:T(8,128)S(1)}, u32[]{:S(2)}, u32[]{:S(2)}) %all-to-all-start.1) | async-done | bytes 32800 | tf_op jit(solution)/shard_map/all_to_all | solution.py:319
  90.3 3.5 %all-to-all-start.2 = ((f32[16,8,128]{2,1,0:T(8,128)}), f32[16,8,128]{2,1,0:T(8,128)S(1)}, u32[]{:S(2)}, u32[]{:S(2)}) async-start(f32[16,8,128]{2,1,0:T(8,128)} %get-tuple-element.35), calls=%async_computation.2 | async-start | bytes 131072 | tf_op jit(solution)/shard_map/all_to_all | solution.py:320
  93.8 7.8 %all-gather = f32[32,128]{1,0:T(8,128)S(1)} all-gather(f32[8,128]{1,0:T(8,128)S(1)} %reduce_sum.27), channel_id=2, replica_groups=mesh['z'=8,'yh'=2,'x'=4,'yl'=2,'core'=2] {'yl','core'}, dimensions={0}, use_global_device_ids=true | all-gather | bytes 20480 | tf_op jit(solution)/shard_map/all_gather | solution.py:321
  101.6 0.5 fusion.10
  102.2 0.6 copy.18
  (50 shorter events, 3.6 us)
Async XLA Ops:
  0.6 1.0 copy-start.2
  1.6 0.9 copy-start.3
  2.5 9.3 %copy-start.4 = (s32[512,16,1]{0,2,1:T(1,128)S(1)}, s32[512,16,1]{0,2,1:T(1,128)}, u32[]{:S(2)}) copy-start(s32[512,16,1]{0,2,1:T(1,128)} %param.13) | copy-start | bytes 98308
  2.5 9.3 %copy-start.5 = (s32[128,16]{0,1:T(8,128)S(1)}, s32[128,16]{0,1:T(8,128)}, u32[]{:S(2)}) copy-start(s32[128,16]{0,1:T(8,128)} %param.15) | copy-start | bytes 24580
  2.9 6.1 %collective-permute-start = (f32[2,128,512]{2,1,0:T(8,128)S(1)}, f32[2,128,512]{2,1,0:T(8,128)S(1)}, u32[]{:S(2)}, u32[]{:S(2)}) collective-permute-start(f32[2,128,512]{2,1,0:T(8,128)S(1)} %get-tuple-element.21), channel_id=1, source_target_pairs={{1,0},{0,1},{3,2},{2,3},{5,4},{4,5},{7,6},{6,7},{9,8},{8,9},{11,10... | collective-permute-start | bytes 1572872 | tf_op jit(solution)/shard_map/ppermute | solution.py:38
  6.2 1.0 copy-start
  7.2 1.0 copy-start.1
  8.9 2.0 %collective-permute-start.2 = (f32[2,128,512]{2,1,0:T(8,128)S(1)}, f32[2,128,512]{2,1,0:T(8,128)S(1)}, u32[]{:S(2)}, u32[]{:S(2)}) collective-permute-start(f32[2,128,512]{2,1,0:T(8,128)S(1)} %get-tuple-element.25), channel_id=1, source_target_pairs={{1,0},{0,1},{3,2},{2,3},{5,4},{4,5},{7,6},{6,7},{9,8},{8,9},{11,10... | collective-permute-start | bytes 1572872 | tf_op jit(solution)/shard_map/ppermute | solution.py:38
  9.1 4.7 %collective-permute-start.1 = (bf16[128,512]{1,0:T(8,128)(2,1)S(1)}, bf16[128,512]{1,0:T(8,128)(2,1)S(1)}, u32[]{:S(2)}, u32[]{:S(2)}) collective-permute-start(bf16[128,512]{1,0:T(8,128)(2,1)S(1)} %get-tuple-element.23), channel_id=1, source_target_pairs={{2,0},{0,2},{3,1},{1,3},{6,4},{4,6},{7,5},{5,7},{10,8},{8,10},{11,... | collective-permute-start | bytes 393224 | tf_op jit(solution)/shard_map/ppermute | solution.py:38
  10.9 5.6 %collective-permute-start.3 = (bf16[128,512]{1,0:T(8,128)(2,1)S(1)}, bf16[128,512]{1,0:T(8,128)(2,1)S(1)}, u32[]{:S(2)}, u32[]{:S(2)}) collective-permute-start(bf16[128,512]{1,0:T(8,128)(2,1)S(1)} %get-tuple-element.27), channel_id=1, source_target_pairs={{2,0},{0,2},{3,1},{1,3},{6,4},{4,6},{7,5},{5,7},{10,8},{8,10},{11,... | collective-permute-start | bytes 393224 | tf_op jit(solution)/shard_map/ppermute | solution.py:38
  18.4 36.4 %all-to-all-start = ((bf16[16,528,128]{2,1,0:T(8,128)(2,1)}), bf16[16,528,128]{2,1,0:T(8,128)(2,1)S(1)}, u32[]{:S(2)}, u32[]{:S(2)}) async-start(bf16[16,528,128]{2,1,0:T(8,128)(2,1)} %get-tuple-element.33), calls=%async_computation | async-start | bytes 4325376 | tf_op jit(solution)/shard_map/all_to_all | solution.py:315
  23.4 7.8 %collective-permute-start.5 = (bf16[144,512]{1,0:T(8,128)(2,1)S(1)}, bf16[144,512]{1,0:T(8,128)(2,1)S(1)}, u32[]{:S(2)}, u32[]{:S(2)}) collective-permute-start(bf16[144,512]{1,0:T(8,128)(2,1)S(1)} %get-tuple-element.32.refs_0_), channel_id=1, source_target_pairs={{32,0},{64,32},{96,64},{128,96},{160,128},{192,160},{224,192},{0,2... | collective-permute-start | bytes 442376 | tf_op jit(solution)/shard_map/ppermute | solution.py:38
  29.0 5.5 %collective-permute-start.13 = (bf16[144,512]{1,0:T(8,128)(2,1)S(1)}, bf16[144,512]{1,0:T(8,128)(2,1)S(1)}, u32[]{:S(2)}, u32[]{:S(2)}) collective-permute-start(bf16[144,512]{1,0:T(8,128)(2,1)S(1)} %get-tuple-element.32.refs_0_), channel_id=1, source_target_pairs={{224,0},{0,32},{32,64},{64,96},{96,128},{128,160},{160,192},{192,2... | collective-permute-start | bytes 442376 | tf_op jit(solution)/shard_map/ppermute | solution.py:38
  31.1 5.2 %collective-permute-start.7 = (bf16[144,512]{1,0:T(8,128)(2,1)S(1)}, bf16[144,512]{1,0:T(8,128)(2,1)S(1)}, u32[]{:S(2)}, u32[]{:S(2)}) collective-permute-start(bf16[144,512]{1,0:T(8,128)(2,1)S(1)} %collective-permute-done.5.refs_2_), channel_id=1, source_target_pairs={{32,0},{64,32},{96,64},{128,96},{160,128},{192,160},{224,192},{0,2... | collective-permute-start | bytes 442376 | tf_op jit(solution)/shard_map/ppermute | solution.py:38
  34.5 9.6 %collective-permute-start.14 = (bf16[144,512]{1,0:T(8,128)(2,1)S(1)}, bf16[144,512]{1,0:T(8,128)(2,1)S(1)}, u32[]{:S(2)}, u32[]{:S(2)}) collective-permute-start(bf16[144,512]{1,0:T(8,128)(2,1)S(1)} %collective-permute-done.13.refs_14_), channel_id=1, source_target_pairs={{224,0},{0,32},{32,64},{64,96},{96,128},{128,160},{160,192},{192,2... | collective-permute-start | bytes 442376 | tf_op jit(solution)/shard_map/ppermute | solution.py:38
  36.3 7.8 %collective-permute-start.9 = (bf16[144,512]{1,0:T(8,128)(2,1)S(1)}, bf16[144,512]{1,0:T(8,128)(2,1)S(1)}, u32[]{:S(2)}, u32[]{:S(2)}) collective-permute-start(bf16[144,512]{1,0:T(8,128)(2,1)S(1)} %collective-permute-done.7.refs_4_), channel_id=1, source_target_pairs={{32,0},{64,32},{96,64},{128,96},{160,128},{192,160},{224,192},{0,2... | collective-permute-start | bytes 442376 | tf_op jit(solution)/shard_map/ppermute | solution.py:38
  39.7 7.1 %collective-permute-start.4 = (bf16[144,512]{1,0:T(8,128)(2,1)S(1)}, bf16[144,512]{1,0:T(8,128)(2,1)S(1)}, u32[]{:S(2)}, u32[]{:S(2)}) collective-permute-start(bf16[144,512]{1,0:T(8,128)(2,1)S(1)} %get-tuple-element.32.refs_0_), channel_id=1, source_target_pairs={{1,0},{0,1},{3,2},{2,3},{5,4},{4,5},{7,6},{6,7},{9,8},{8,9},{11,10... | collective-permute-start | bytes 442376 | tf_op jit(solution)/shard_map/ppermute | solution.py:38
  43.6 6.4 %collective-permute-start.18 = (bf16[144,512]{1,0:T(8,128)(2,1)S(1)}, bf16[144,512]{1,0:T(8,128)(2,1)S(1)}, u32[]{:S(2)}, u32[]{:S(2)}) collective-permute-start(bf16[144,512]{1,0:T(8,128)(2,1)S(1)} %collective-permute-done.13.refs_14_), channel_id=1, source_target_pairs={{1,0},{0,1},{3,2},{2,3},{5,4},{4,5},{7,6},{6,7},{9,8},{8,9},{11,10... | collective-permute-start | bytes 442376 | tf_op jit(solution)/shard_map/ppermute | solution.py:38
  43.6 6.5 %collective-permute-start.6 = (bf16[144,512]{1,0:T(8,128)(2,1)S(1)}, bf16[144,512]{1,0:T(8,128)(2,1)S(1)}, u32[]{:S(2)}, u32[]{:S(2)}) collective-permute-start(bf16[144,512]{1,0:T(8,128)(2,1)S(1)} %collective-permute-done.5.refs_2_), channel_id=1, source_target_pairs={{1,0},{0,1},{3,2},{2,3},{5,4},{4,5},{7,6},{6,7},{9,8},{8,9},{11,10... | collective-permute-start | bytes 442376 | tf_op jit(solution)/shard_map/ppermute | solution.py:38
  44.1 6.8 %collective-permute-start.15 = (bf16[144,512]{1,0:T(8,128)(2,1)S(1)}, bf16[144,512]{1,0:T(8,128)(2,1)}, u32[]{:S(2)}, u32[]{:S(2)}) collective-permute-start(bf16[144,512]{1,0:T(8,128)(2,1)S(1)} %collective-permute-done.14.refs_12_), channel_id=1, source_target_pairs={{224,0},{0,32},{32,64},{64,96},{96,128},{128,160},{160,192},{192,2... | collective-permute-start | bytes 442376 | tf_op jit(solution)/shard_map/ppermute | solution.py:38
  44.1 7.6 %collective-permute-start.11 = (bf16[144,512]{1,0:T(8,128)(2,1)S(1)}, bf16[144,512]{1,0:T(8,128)(2,1)}, u32[]{:S(2)}, u32[]{:S(2)}) collective-permute-start(bf16[144,512]{1,0:T(8,128)(2,1)S(1)} %collective-permute-done.9.refs_6_), channel_id=1, source_target_pairs={{32,0},{64,32},{96,64},{128,96},{160,128},{192,160},{224,192},{0,2... | collective-permute-start | bytes 442376 | tf_op jit(solution)/shard_map/ppermute | solution.py:38
  46.8 5.9 %collective-permute-start.17 = (bf16[144,512]{1,0:T(8,128)(2,1)S(1)}, bf16[144,512]{1,0:T(8,128)(2,1)}, u32[]{:S(2)}, u32[]{:S(2)}) collective-permute-start(bf16[144,512]{1,0:T(8,128)(2,1)S(1)} %collective-permute-done.14.refs_12_), channel_id=1, source_target_pairs={{1,0},{0,1},{3,2},{2,3},{5,4},{4,5},{7,6},{6,7},{9,8},{8,9},{11,10... | collective-permute-start | bytes 442376 | tf_op jit(solution)/shard_map/ppermute | solution.py:38
  50.0 2.8 %collective-permute-start.8 = (bf16[144,512]{1,0:T(8,128)(2,1)S(1)}, bf16[144,512]{1,0:T(8,128)(2,1)}, u32[]{:S(2)}, u32[]{:S(2)}) collective-permute-start(bf16[144,512]{1,0:T(8,128)(2,1)S(1)} %collective-permute-done.7.refs_4_), channel_id=1, source_target_pairs={{1,0},{0,1},{3,2},{2,3},{5,4},{4,5},{7,6},{6,7},{9,8},{8,9},{11,10... | collective-permute-start | bytes 442376 | tf_op jit(solution)/shard_map/ppermute | solution.py:38
  50.1 3.0 %collective-permute-start.10 = (bf16[144,512]{1,0:T(8,128)(2,1)S(1)}, bf16[144,512]{1,0:T(8,128)(2,1)}, u32[]{:S(2)}, u32[]{:S(2)}) collective-permute-start(bf16[144,512]{1,0:T(8,128)(2,1)S(1)} %collective-permute-done.9.refs_6_), channel_id=1, source_target_pairs={{1,0},{0,1},{3,2},{2,3},{5,4},{4,5},{7,6},{6,7},{9,8},{8,9},{11,10... | collective-permute-start | bytes 442376 | tf_op jit(solution)/shard_map/ppermute | solution.py:38
  50.9 2.1 %collective-permute-start.16 = (bf16[144,512]{1,0:T(8,128)(2,1)}, bf16[144,512]{1,0:T(8,128)(2,1)}, u32[]{:S(2)}, u32[]{:S(2)}) collective-permute-start(bf16[144,512]{1,0:T(8,128)(2,1)} %collective-permute-done.15.refs_10_), channel_id=1, source_target_pairs={{1,0},{0,1},{3,2},{2,3},{5,4},{4,5},{7,6},{6,7},{9,8},{8,9},{11,10... | collective-permute-start | bytes 442376 | tf_op jit(solution)/shard_map/ppermute | solution.py:38
  51.7 2.3 %collective-permute-start.12 = (bf16[144,512]{1,0:T(8,128)(2,1)}, bf16[144,512]{1,0:T(8,128)(2,1)}, u32[]{:S(2)}, u32[]{:S(2)}) collective-permute-start(bf16[144,512]{1,0:T(8,128)(2,1)} %collective-permute-done.11.refs_8_), channel_id=1, source_target_pairs={{1,0},{0,1},{3,2},{2,3},{5,4},{4,5},{7,6},{6,7},{9,8},{8,9},{11,10... | collective-permute-start | bytes 442376 | tf_op jit(solution)/shard_map/ppermute | solution.py:38
  75.2 15.1 %all-to-all-start.1 = ((f32[8,8,128]{2,1,0:T(8,128)}), f32[8,8,128]{2,1,0:T(8,128)S(1)}, u32[]{:S(2)}, u32[]{:S(2)}) async-start(f32[8,8,128]{2,1,0:T(8,128)} %get-tuple-element.34), calls=%async_computation.1 | async-start | bytes 65536 | tf_op jit(solution)/shard_map/all_to_all | solution.py:319
  90.3 12.5 %all-to-all-start.2 = ((f32[16,8,128]{2,1,0:T(8,128)}), f32[16,8,128]{2,1,0:T(8,128)S(1)}, u32[]{:S(2)}, u32[]{:S(2)}) async-start(f32[16,8,128]{2,1,0:T(8,128)} %get-tuple-element.35), calls=%async_computation.2 | async-start | bytes 131072 | tf_op jit(solution)/shard_map/all_to_all | solution.py:320

commit v4 on v3

--- a/solution.py
+++ b/solution.py
@@ -110,32 +110,49 @@
     return (raw * lax.rsqrt(total + EPSILON)).astype(jnp.bfloat16)
 
 
-def finish_kernel(keep2_s, got2_s, keep2_q, got2_q, struct_ext_ref, seq_ext_ref, peers_ref, seq_ref, self_ref):
-    struct = normalized(keep2_s, got2_s)
+def finish_struct_kernel(keep2_ref, got2_ref, ext_ref, struct_ref, peers_ref):
+    struct = normalized(keep2_ref, got2_ref)
+    struct_ref[...] = struct
     turned = struct.astype(jnp.float32).T.astype(jnp.bfloat16)
-    struct_ext = struct_ext_ref[...]
+    ext = ext_ref[...]
     for peer in range(SIDE):
         peers_ref[peer, 0:WIDTH, :] = turned
-        peers_ref[peer, WIDTH:, :] = struct_ext
-    seq = normalized(keep2_q, got2_q)
+        peers_ref[peer, WIDTH:, :] = ext
+
+
+def finish_struct(keep2, got2, ext):
+    return pl.pallas_call(
+        finish_struct_kernel,
+        out_shape=(
+            jax.ShapeDtypeStruct((SHARE, WIDTH), jnp.bfloat16),
+            jax.ShapeDtypeStruct((SIDE, WIDTH + EXT, SHARE), jnp.bfloat16),
+        ),
+        in_specs=[VMEM] * 3,
+        out_specs=(VMEM,) * 2,
+        compiler_params=pltpu.CompilerParams(vmem_limit_bytes=12 * 1024 * 1024),
+        name="finish_struct",
+    )(keep2, got2, ext)
+
+
+def finish_seq_kernel(keep2_ref, got2_ref, ext_ref, struct_ref, seq_ref, self_ref):
+    seq = normalized(keep2_ref, got2_ref)
     seq_ref[0:SHARE, :] = seq
-    seq_ref[SHARE:, :] = seq_ext_ref[...]
-    self_ref[...] = lanes_summed(seq.astype(jnp.float32) * struct.astype(jnp.float32))
-
-
-def finish(*held):
-    return pl.pallas_call(
-        finish_kernel,
+    seq_ref[SHARE:, :] = ext_ref[...]
+    self_ref[...] = lanes_summed(seq.astype(jnp.float32) * struct_ref[...].astype(jnp.float32))
+
+
+def finish_seq(keep2, got2, ext, struct):
+    return pl.pallas_call(
+        finish_seq_kernel,
         out_shape=(
-            jax.ShapeDtypeStruct((SIDE, WIDTH + EXT, SHARE), jnp.bfloat16),
             jax.ShapeDtypeStruct((SHARE + EXT, WIDTH), jnp.bfloat16),
             jax.ShapeDtypeStruct((8, SHARE), jnp.float32),
         ),
-        in_specs=[VMEM] * 6,
-        out_specs=(VMEM,) * 3,
+        in_specs=[VMEM] * 4,
+        out_specs=(VMEM,) * 2,
         compiler_params=pltpu.CompilerParams(vmem_limit_bytes=12 * 1024 * 1024),
-        name="finish",
-    )(*held)
+        name="finish_seq",
+    )(keep2, got2, ext, struct)
 
 
 def integers(values):
@@ -182,16 +199,20 @@
     for tile in range(tiles + 1):
 
         def body(step, carry, tile=tile):
-            if tile < tiles:
-                wide = STRIP // SHARE
-                cols = jnp.concatenate([s[step * wide + each, 0:WIDTH, :] for each in range(wide)], axis=1)
-                start = pl.multiple_of(step * STRIP, STRIP)
-                buffers[tile % 2][:, pl.ds(start, STRIP)] = lax.dot_general(
-                    q[tile * TILE : (tile + 1) * TILE, :],
-                    cols,
-                    (((1,), (0,)), ((), ())),
-                    preferred_element_type=jnp.float32,
+            def piece(number):
+                if tile == tiles:
+                    return
+                rows = (number % 4) * SHARE
+                first = step * (STRIP // SHARE) + (number // 4) * 2
+                cols = jnp.concatenate([s[first, 0:WIDTH, :], s[first + 1, 0:WIDTH, :]], axis=1)
+                start = pl.multiple_of(first * SHARE, 2 * SHARE)
+                buffers[tile % 2][rows : rows + SHARE, pl.ds(start, 2 * SHARE)] = jnp.dot(
+                    q[tile * TILE + rows : tile * TILE + rows + SHARE, :], cols, preferred_element_type=jnp.float32
                 )
+
+            if tile == 0:
+                for number in range(8):
+                    piece(number)
             if tile > 0:
                 products = buffers[(tile - 1) % 2]
                 zero = jnp.zeros((8, 128), jnp.float32)
@@ -204,6 +225,8 @@
                     chunk_of = [each >> 7 for each in code]
                     row_total, row_matched, picked = [zero for _ in groups], [zero for _ in groups], [zero for _ in groups]
                     for chunk in range(SIDE):
+                        if chunk % 8 == 0:
+                            piece(sub * 2 + chunk // 8)
                         at = slice(chunk * 128, (chunk + 1) * 128)
                         col_label = lab8[:, at]
                         col_total, col_matched = ct[:, at], cm[:, at]
@@ -295,10 +318,10 @@
     keep2_s, send2_s = merge(yl.reshape(1), keep_s, got_s, "merge_struct")
     got2_s = shifted(send2_s, "yl", 1)
     keep2_q, send2_q = merge(yl.reshape(1), keep_q, got_q, "merge_seq")
-    got2_q = shifted(send2_q, "yl", 1)
     cluster_ids, hard_owner, hard_local, hard_valid, send2_q = lax.optimization_barrier(
         (cluster_ids, hard_owner, hard_local, hard_valid, send2_q)
     )
+    got2_q = shifted(send2_q, "yl", 1)
     own = lambda value: lax.dynamic_slice_in_dim(value, place(MP_AXES) * SHARE, SHARE, 0)
     labels = own(cluster_ids)
     owner = own(hard_owner[:, :, 0])
@@ -311,8 +334,9 @@
     seq_ext = jnp.concatenate([high, low, wide(labels >> 7), wide(labels & 127)], axis=1).astype(jnp.bfloat16)
     struct_ext = jnp.concatenate([wide(labels >> 7)[0:8], wide(labels & 127)[0:8]], axis=0).astype(jnp.bfloat16)
 
-    struct_peers, seq_block, self_dot = finish(keep2_s, got2_s, keep2_q, got2_q, struct_ext, seq_ext)
+    own_struct, struct_peers = finish_struct(keep2_s, got2_s, struct_ext)
     struct_blocks = lax.all_to_all(struct_peers, COL_AXES, split_axis=0, concat_axis=0, tiled=True)
+    seq_block, self_dot = finish_seq(keep2_q, got2_q, seq_ext, own_struct)
     seq_blocks = [each for held in over_z(seq_block) for each in (held, shifted(held, "core", 1))]
 
     rows, cols = pair_sums(jnp.stack([place("z"), core]), seq_blocks, struct_blocks)

time: 104 us -> 129 us (1.24)
  starting transfers between devices: 44.9 us -> 59.2 us
  waiting for transfers between devices: 19.2 us -> 29.1 us
  local copies, waits for them, and re-layouts: 4.46 us -> 7.41 us
    all_to_all x1, starting transfers between devices: 3.5 us -> 18.7 us  [per_device(): lax.all_to_all(cols, COL_AXES, split_axis=0, concat_axis=0, tiled=True)]
    ppermute x19, waiting for transfers between devices: 11.6 us -> 22.2 us  [shifted(): lax.ppermute(value, axes, [((place + steps) % count, place) for place in...]
    all_to_all x1, starting transfers between devices: 8.19 us -> 4.78 us  [per_device(): lax.all_to_all(rows, 'z', split_axis=0, concat_axis=0, tiled=True)]
    unnamed x12 -> x18, local copies, waits for them, and re-layouts: 3.84 us -> 6.8 us
    ppermute x19, starting transfers between devices: 28.2 us -> 30.6 us  [shifted(): lax.ppermute(value, axes, [((place + steps) % count, place) for place in...]
  transfers between devices with their start and end apart: 22 -> 22, of which waited for: 11 -> 8; matrix products, arithmetic and copies ran while one was open for 3% -> 2% of each run, Pallas kernels for 1% -> 1%
where the time goes in v4:
time: 129 us
  starting transfers between devices  59.2 us (46%)
  waiting for transfers between devices  29.1 us (23%)
  Pallas kernels  22.6 us (18%)
  local copies, waits for them, and re-layouts  7.41 us (6%)
  blocking collectives  6.98 us (5%)
  other arithmetic  2.67 us (2%)
    ppermute x19, starting transfers between devices, shifted(): lax.ppermute(value, axes, [((place + steps) % count, place) for place in...  30.6 us
    ppermute x19, waiting for transfers between devices, shifted(): lax.ppermute(value, axes, [((place + steps) % count, place) for place in...  22.2 us
    pallas_call x1, Pallas kernels, pair_sums(): pl.pallas_call(pair_kernel, out_shape=(jax.ShapeDtypeStruct((8, 8, SHARE)...  20.7 us
    all_to_all x1, starting transfers between devices, per_device(): lax.all_to_all(cols, COL_AXES, split_axis=0, concat_axis=0, tiled=True)  18.7 us
    all_gather x1, blocking collectives, per_device(): lax.all_gather(rows, MP_AXES, axis=0, tiled=False).reshape(2, 2, 8, SHARE)  6.98 us
    all_to_all x1, waiting for transfers between devices, per_device(): lax.all_to_all(rows, 'z', split_axis=0, concat_axis=0, tiled=True)  6.93 us
    unnamed x18, local copies, waits for them, and re-layouts  6.8 us
    all_to_all x1, starting transfers between devices, per_device(): lax.all_to_all(struct_peers, COL_AXES, split_axis=0, concat_axis=0, tiled...  5.15 us
  transfers between devices with their start and end apart: 22, of which 8 were waited for; matrix products, arithmetic and copies ran while one was open for 2% of the time, Pallas kernels for 1%

profile of v4, /device:TPU:1, one launch (start us, length us, event | category | flops | bytes accessed | tf_op | source)
XLA Modules:
  0.0 128.8 jit_solution(7649819279014536168)
XLA Ops:
  0.6 0.9 copy-done.3
  1.6 0.9 copy-done.4
  2.9 3.3 %collective-permute-start.2 = (f32[2,128,512]{2,1,0:T(8,128)S(1)}, f32[2,128,512]{2,1,0:T(8,128)S(1)}, u32[]{:S(2)}, u32[]{:S(2)}) collective-permute-start(f32[2,128,512]{2,1,0:T(8,128)S(1)} %get-tuple-element.32), channel_id=1, source_target_pairs={{1,0},{0,1},{3,2},{2,3},{5,4},{4,5},{7,6},{6,7},{9,8},{8,9},{11,10... | collective-permute-start | bytes 1572872 | tf_op jit(solution)/shard_map/ppermute | solution.py:38
  6.2 1.0 copy-done.1
  7.2 1.0 copy-done.2
  8.2 0.7 project_seq.1
  9.2 1.7 %collective-permute-done.got_ref = f32[2,128,512]{2,1,0:T(8,128)S(1)} collective-permute-done((f32[2,128,512]{2,1,0:T(8,128)S(1)}, f32[2,128,512]{2,1,0:T(8,128)S(1)}, u32[]{:S(2)}, u32[]{:S(2)}) %collective-permute-start) | collective-permute-done | bytes 524320 | tf_op jit(solution)/shard_map/ppermute | solution.py:38
  10.9 0.8 shift-right-arithmetic_convert_fusion
  11.7 2.0 %collective-permute-done.3.got2_ref = bf16[128,512]{1,0:T(8,128)(2,1)S(1)} collective-permute-done((bf16[128,512]{1,0:T(8,128)(2,1)S(1)}, bf16[128,512]{1,0:T(8,128)(2,1)S(1)}, u32[]{:S(2)}, u32[]{:S(2)}) %collective-permute-start.3) | collective-permute-done | bytes 131104 | tf_op jit(solution)/shard_map/ppermute | solution.py:38
  14.1 1.4 %copy-done = bf16[16,528,128]{2,1,0:T(8,128)(2,1)} copy-done((bf16[16,528,128]{2,1,0:T(8,128)(2,1)}, bf16[16,528,128]{2,1,0:T(8,128)(2,1)S(1)}, u32[]{:S(2)}) %copy-start) | copy-done | bytes 2162712
  15.4 5.2 %all-to-all-start = ((bf16[16,528,128]{2,1,0:T(8,128)(2,1)}), bf16[16,528,128]{2,1,0:T(8,128)(2,1)S(1)}, u32[]{:S(2)}, u32[]{:S(2)}) async-start(bf16[16,528,128]{2,1,0:T(8,128)(2,1)} %copy-done), calls=%async_computation | async-start | bytes 4325376 | tf_op jit(solution)/shard_map/all_to_all | solution.py:338
  20.6 1.4 %collective-permute-start.1 = (bf16[128,512]{1,0:T(8,128)(2,1)S(1)}, bf16[128,512]{1,0:T(8,128)(2,1)S(1)}, u32[]{:S(2)}, u32[]{:S(2)}) collective-permute-start(bf16[128,512]{1,0:T(8,128)(2,1)S(1)} %get-tuple-element.26), channel_id=1, source_target_pairs={{2,0},{0,2},{3,1},{1,3},{6,4},{4,6},{7,5},{5,7},{10,8},{8,10},{11,... | collective-permute-start | bytes 393224 | tf_op jit(solution)/shard_map/ppermute | solution.py:38
  22.1 0.7 fusion.5
  22.8 12.9 %collective-permute-done.1.got2_ref = bf16[128,512]{1,0:T(8,128)(2,1)S(1)} collective-permute-done((bf16[128,512]{1,0:T(8,128)(2,1)S(1)}, bf16[128,512]{1,0:T(8,128)(2,1)S(1)}, u32[]{:S(2)}, u32[]{:S(2)}) %collective-permute-start.1) | collective-permute-done | bytes 131104 | tf_op jit(solution)/shard_map/ppermute | solution.py:38
  36.2 5.6 %collective-permute-start.5 = (bf16[144,512]{1,0:T(8,128)(2,1)S(1)}, bf16[144,512]{1,0:T(8,128)(2,1)S(1)}, u32[]{:S(2)}, u32[]{:S(2)}) collective-permute-start(bf16[144,512]{1,0:T(8,128)(2,1)S(1)} %get-tuple-element.36.refs_0_), channel_id=1, source_target_pairs={{32,0},{64,32},{96,64},{128,96},{160,128},{192,160},{224,192},{0,2... | collective-permute-start | bytes 442376 | tf_op jit(solution)/shard_map/ppermute | solution.py:38
  41.8 2.1 %collective-permute-done.5.refs_2_ = bf16[144,512]{1,0:T(8,128)(2,1)S(1)} collective-permute-done((bf16[144,512]{1,0:T(8,128)(2,1)S(1)}, bf16[144,512]{1,0:T(8,128)(2,1)S(1)}, u32[]{:S(2)}, u32[]{:S(2)}) %collective-permute-start.5) | collective-permute-done | bytes 147488 | tf_op jit(solution)/shard_map/ppermute | solution.py:38
  43.9 3.4 %collective-permute-start.7 = (bf16[144,512]{1,0:T(8,128)(2,1)S(1)}, bf16[144,512]{1,0:T(8,128)(2,1)S(1)}, u32[]{:S(2)}, u32[]{:S(2)}) collective-permute-start(bf16[144,512]{1,0:T(8,128)(2,1)S(1)} %collective-permute-done.5.refs_2_), channel_id=1, source_target_pairs={{32,0},{64,32},{96,64},{128,96},{160,128},{192,160},{224,192},{0,2... | collective-permute-start | bytes 442376 | tf_op jit(solution)/shard_map/ppermute | solution.py:38
  47.3 2.1 %collective-permute-done.7.refs_4_ = bf16[144,512]{1,0:T(8,128)(2,1)S(1)} collective-permute-done((bf16[144,512]{1,0:T(8,128)(2,1)S(1)}, bf16[144,512]{1,0:T(8,128)(2,1)S(1)}, u32[]{:S(2)}, u32[]{:S(2)}) %collective-permute-start.7) | collective-permute-done | bytes 147488 | tf_op jit(solution)/shard_map/ppermute | solution.py:38
  49.4 3.4 %collective-permute-start.9 = (bf16[144,512]{1,0:T(8,128)(2,1)S(1)}, bf16[144,512]{1,0:T(8,128)(2,1)S(1)}, u32[]{:S(2)}, u32[]{:S(2)}) collective-permute-start(bf16[144,512]{1,0:T(8,128)(2,1)S(1)} %collective-permute-done.7.refs_4_), channel_id=1, source_target_pairs={{32,0},{64,32},{96,64},{128,96},{160,128},{192,160},{224,192},{0,2... | collective-permute-start | bytes 442376 | tf_op jit(solution)/shard_map/ppermute | solution.py:38
  52.8 4.8 %collective-permute-start.4 = (bf16[144,512]{1,0:T(8,128)(2,1)S(1)}, bf16[144,512]{1,0:T(8,128)(2,1)S(1)}, u32[]{:S(2)}, u32[]{:S(2)}) collective-permute-start(bf16[144,512]{1,0:T(8,128)(2,1)S(1)} %get-tuple-element.36.refs_0_), channel_id=1, source_target_pairs={{1,0},{0,1},{3,2},{2,3},{5,4},{4,5},{7,6},{6,7},{9,8},{8,9},{11,10... | collective-permute-start | bytes 442376 | tf_op jit(solution)/shard_map/ppermute | solution.py:38
  58.2 2.7 %collective-permute-start.11 = (bf16[144,512]{1,0:T(8,128)(2,1)S(1)}, bf16[144,512]{1,0:T(8,128)(2,1)}, u32[]{:S(2)}, u32[]{:S(2)}) collective-permute-start(bf16[144,512]{1,0:T(8,128)(2,1)S(1)} %collective-permute-done.9.refs_6_), channel_id=1, source_target_pairs={{32,0},{64,32},{96,64},{128,96},{160,128},{192,160},{224,192},{0,2... | collective-permute-start | bytes 442376 | tf_op jit(solution)/shard_map/ppermute | solution.py:38
  60.8 3.2 %collective-permute-start.17 = (bf16[144,512]{1,0:T(8,128)(2,1)S(1)}, bf16[144,512]{1,0:T(8,128)(2,1)}, u32[]{:S(2)}, u32[]{:S(2)}) collective-permute-start(bf16[144,512]{1,0:T(8,128)(2,1)S(1)} %collective-permute-done.14.refs_12_), channel_id=1, source_target_pairs={{1,0},{0,1},{3,2},{2,3},{5,4},{4,5},{7,6},{6,7},{9,8},{8,9},{11,10... | collective-permute-start | bytes 442376 | tf_op jit(solution)/shard_map/ppermute | solution.py:38
  64.1 0.7 copy-done.5
  65.7 0.9 collective-permute-start.12
  67.1 0.9 collective-permute-done.12.refs_9_
  68.0 0.9 copy-done.6
  68.9 20.7 %pair_sums.1 = (f32[8,8,128]{2,1,0:T(8,128)}, f32[16,8,128]{2,1,0:T(8,128)}) custom-call(s32[2]{0:T(128)S(1)} %pad_add_fusion.place_ref, bf16[144,512]{1,0:T(8,128)(2,1)S(1)} %get-tuple-element.36.refs_0_, bf16[144,512]{1,0:T(8,128)(2,1)S(1)} %collective-permute-done.4.refs_1_, bf16[144,512]{1,0:T(8,128)(2,1)S(1)} %collective-permute-done.5.refs_2_, ...), custom_call_target="tpu_custom_call" | custom-call | flops 4294967296 | bytes 4194304 | tf_op jit(solution)/shard_map/pair_sums/pallas_call | solution.py:274
  89.6 4.8 %all-to-all-start.1 = ((f32[8,8,128]{2,1,0:T(8,128)}), f32[8,8,128]{2,1,0:T(8,128)S(1)}, u32[]{:S(2)}, u32[]{:S(2)}) async-start(f32[8,8,128]{2,1,0:T(8,128)} %get-tuple-element.38), calls=%async_computation.1 | async-start | bytes 65536 | tf_op jit(solution)/shard_map/all_to_all | solution.py:343
  94.4 6.9 %all-to-all-done.1 = f32[8,8,128]{2,1,0:T(8,128)S(1)} async-done(((f32[8,8,128]{2,1,0:T(8,128)}), f32[8,8,128]{2,1,0:T(8,128)S(1)}, u32[]{:S(2)}, u32[]{:S(2)}) %all-to-all-start.1) | async-done | bytes 32800 | tf_op jit(solution)/shard_map/all_to_all | solution.py:343
  101.3 18.7 %all-to-all-start.2 = ((f32[16,8,128]{2,1,0:T(8,128)}), f32[16,8,128]{2,1,0:T(8,128)S(1)}, u32[]{:S(2)}, u32[]{:S(2)}) async-start(f32[16,8,128]{2,1,0:T(8,128)} %get-tuple-element.39), calls=%async_computation.2 | async-start | bytes 131072 | tf_op jit(solution)/shard_map/all_to_all | solution.py:344
  120.1 7.0 %all-gather = f32[32,128]{1,0:T(8,128)S(1)} all-gather(f32[8,128]{1,0:T(8,128)S(1)} %reduce_sum.27), channel_id=2, replica_groups=mesh['z'=8,'yh'=2,'x'=4,'yl'=2,'core'=2] {'yl','core'}, dimensions={0}, use_global_device_ids=true | all-gather | bytes 20480 | tf_op jit(solution)/shard_map/all_gather | solution.py:345
  127.6 0.6 copy.18
  (57 shorter events, 4.6 us)
Async XLA Ops:
  0.6 1.0 copy-start.3
  1.6 0.9 copy-start.4
  2.9 6.1 %collective-permute-start.2 = (f32[2,128,512]{2,1,0:T(8,128)S(1)}, f32[2,128,512]{2,1,0:T(8,128)S(1)}, u32[]{:S(2)}, u32[]{:S(2)}) collective-permute-start(f32[2,128,512]{2,1,0:T(8,128)S(1)} %get-tuple-element.32), channel_id=1, source_target_pairs={{1,0},{0,1},{3,2},{2,3},{5,4},{4,5},{7,6},{6,7},{9,8},{8,9},{11,10... | collective-permute-start | bytes 1572872 | tf_op jit(solution)/shard_map/ppermute | solution.py:38
  6.2 1.0 copy-start.1
  7.2 1.0 copy-start.2
  8.9 2.0 %collective-permute-start = (f32[2,128,512]{2,1,0:T(8,128)S(1)}, f32[2,128,512]{2,1,0:T(8,128)S(1)}, u32[]{:S(2)}, u32[]{:S(2)}) collective-permute-start(f32[2,128,512]{2,1,0:T(8,128)S(1)} %get-tuple-element.23), channel_id=1, source_target_pairs={{1,0},{0,1},{3,2},{2,3},{5,4},{4,5},{7,6},{6,7},{9,8},{8,9},{11,10... | collective-permute-start | bytes 1572872 | tf_op jit(solution)/shard_map/ppermute | solution.py:38
  9.1 4.7 %collective-permute-start.3 = (bf16[128,512]{1,0:T(8,128)(2,1)S(1)}, bf16[128,512]{1,0:T(8,128)(2,1)S(1)}, u32[]{:S(2)}, u32[]{:S(2)}) collective-permute-start(bf16[128,512]{1,0:T(8,128)(2,1)S(1)} %get-tuple-element.34), channel_id=1, source_target_pairs={{2,0},{0,2},{3,1},{1,3},{6,4},{4,6},{7,5},{5,7},{10,8},{8,10},{11,... | collective-permute-start | bytes 393224 | tf_op jit(solution)/shard_map/ppermute | solution.py:38
  14.0 1.4 %copy-start = (bf16[16,528,128]{2,1,0:T(8,128)(2,1)}, bf16[16,528,128]{2,1,0:T(8,128)(2,1)S(1)}, u32[]{:S(2)}) copy-start(bf16[16,528,128]{2,1,0:T(8,128)(2,1)S(1)} %get-tuple-element.37) | copy-start | bytes 6488068
  15.4 5.2 %copy-start.7 = (s32[512,16,1]{0,2,1:T(1,128)S(1)}, s32[512,16,1]{0,2,1:T(1,128)}, u32[]{:S(2)}) copy-start(s32[512,16,1]{0,2,1:T(1,128)} %param.13) | copy-start | bytes 98308
  15.4 6.7 %copy-start.8 = (s32[128,16]{0,1:T(8,128)S(1)}, s32[128,16]{0,1:T(8,128)}, u32[]{:S(2)}) copy-start(s32[128,16]{0,1:T(8,128)} %param.15) | copy-start | bytes 24580
  15.4 52.6 %all-to-all-start = ((bf16[16,528,128]{2,1,0:T(8,128)(2,1)}), bf16[16,528,128]{2,1,0:T(8,128)(2,1)S(1)}, u32[]{:S(2)}, u32[]{:S(2)}) async-start(bf16[16,528,128]{2,1,0:T(8,128)(2,1)} %copy-done), calls=%async_computation | async-start | bytes 4325376 | tf_op jit(solution)/shard_map/all_to_all | solution.py:338
  20.6 15.1 %collective-permute-start.1 = (bf16[128,512]{1,0:T(8,128)(2,1)S(1)}, bf16[128,512]{1,0:T(8,128)(2,1)S(1)}, u32[]{:S(2)}, u32[]{:S(2)}) collective-permute-start(bf16[128,512]{1,0:T(8,128)(2,1)S(1)} %get-tuple-element.26), channel_id=1, source_target_pairs={{2,0},{0,2},{3,1},{1,3},{6,4},{4,6},{7,5},{5,7},{10,8},{8,10},{11,... | collective-permute-start | bytes 393224 | tf_op jit(solution)/shard_map/ppermute | solution.py:38
  36.2 7.7 %collective-permute-start.5 = (bf16[144,512]{1,0:T(8,128)(2,1)S(1)}, bf16[144,512]{1,0:T(8,128)(2,1)S(1)}, u32[]{:S(2)}, u32[]{:S(2)}) collective-permute-start(bf16[144,512]{1,0:T(8,128)(2,1)S(1)} %get-tuple-element.36.refs_0_), channel_id=1, source_target_pairs={{32,0},{64,32},{96,64},{128,96},{160,128},{192,160},{224,192},{0,2... | collective-permute-start | bytes 442376 | tf_op jit(solution)/shard_map/ppermute | solution.py:38
  41.8 5.5 %collective-permute-start.13 = (bf16[144,512]{1,0:T(8,128)(2,1)S(1)}, bf16[144,512]{1,0:T(8,128)(2,1)S(1)}, u32[]{:S(2)}, u32[]{:S(2)}) collective-permute-start(bf16[144,512]{1,0:T(8,128)(2,1)S(1)} %get-tuple-element.36.refs_0_), channel_id=1, source_target_pairs={{224,0},{0,32},{32,64},{64,96},{96,128},{128,160},{160,192},{192,2... | collective-permute-start | bytes 442376 | tf_op jit(solution)/shard_map/ppermute | solution.py:38
  43.9 5.5 %collective-permute-start.7 = (bf16[144,512]{1,0:T(8,128)(2,1)S(1)}, bf16[144,512]{1,0:T(8,128)(2,1)S(1)}, u32[]{:S(2)}, u32[]{:S(2)}) collective-permute-start(bf16[144,512]{1,0:T(8,128)(2,1)S(1)} %collective-permute-done.5.refs_2_), channel_id=1, source_target_pairs={{32,0},{64,32},{96,64},{128,96},{160,128},{192,160},{224,192},{0,2... | collective-permute-start | bytes 442376 | tf_op jit(solution)/shard_map/ppermute | solution.py:38
  47.3 10.9 %collective-permute-start.14 = (bf16[144,512]{1,0:T(8,128)(2,1)S(1)}, bf16[144,512]{1,0:T(8,128)(2,1)S(1)}, u32[]{:S(2)}, u32[]{:S(2)}) collective-permute-start(bf16[144,512]{1,0:T(8,128)(2,1)S(1)} %collective-permute-done.13.refs_14_), channel_id=1, source_target_pairs={{224,0},{0,32},{32,64},{64,96},{96,128},{128,160},{160,192},{192,2... | collective-permute-start | bytes 442376 | tf_op jit(solution)/shard_map/ppermute | solution.py:38
  49.4 8.8 %collective-permute-start.9 = (bf16[144,512]{1,0:T(8,128)(2,1)S(1)}, bf16[144,512]{1,0:T(8,128)(2,1)S(1)}, u32[]{:S(2)}, u32[]{:S(2)}) collective-permute-start(bf16[144,512]{1,0:T(8,128)(2,1)S(1)} %collective-permute-done.7.refs_4_), channel_id=1, source_target_pairs={{32,0},{64,32},{96,64},{128,96},{160,128},{192,160},{224,192},{0,2... | collective-permute-start | bytes 442376 | tf_op jit(solution)/shard_map/ppermute | solution.py:38
  52.8 8.0 %collective-permute-start.4 = (bf16[144,512]{1,0:T(8,128)(2,1)S(1)}, bf16[144,512]{1,0:T(8,128)(2,1)S(1)}, u32[]{:S(2)}, u32[]{:S(2)}) collective-permute-start(bf16[144,512]{1,0:T(8,128)(2,1)S(1)} %get-tuple-element.36.refs_0_), channel_id=1, source_target_pairs={{1,0},{0,1},{3,2},{2,3},{5,4},{4,5},{7,6},{6,7},{9,8},{8,9},{11,10... | collective-permute-start | bytes 442376 | tf_op jit(solution)/shard_map/ppermute | solution.py:38
  57.6 6.4 %collective-permute-start.18 = (bf16[144,512]{1,0:T(8,128)(2,1)S(1)}, bf16[144,512]{1,0:T(8,128)(2,1)S(1)}, u32[]{:S(2)}, u32[]{:S(2)}) collective-permute-start(bf16[144,512]{1,0:T(8,128)(2,1)S(1)} %collective-permute-done.13.refs_14_), channel_id=1, source_target_pairs={{1,0},{0,1},{3,2},{2,3},{5,4},{4,5},{7,6},{6,7},{9,8},{8,9},{11,10... | collective-permute-start | bytes 442376 | tf_op jit(solution)/shard_map/ppermute | solution.py:38
  57.6 6.5 %collective-permute-start.6 = (bf16[144,512]{1,0:T(8,128)(2,1)S(1)}, bf16[144,512]{1,0:T(8,128)(2,1)S(1)}, u32[]{:S(2)}, u32[]{:S(2)}) collective-permute-start(bf16[144,512]{1,0:T(8,128)(2,1)S(1)} %collective-permute-done.5.refs_2_), channel_id=1, source_target_pairs={{1,0},{0,1},{3,2},{2,3},{5,4},{4,5},{7,6},{6,7},{9,8},{8,9},{11,10... | collective-permute-start | bytes 442376 | tf_op jit(solution)/shard_map/ppermute | solution.py:38
  58.2 7.0 %collective-permute-start.15 = (bf16[144,512]{1,0:T(8,128)(2,1)S(1)}, bf16[144,512]{1,0:T(8,128)(2,1)}, u32[]{:S(2)}, u32[]{:S(2)}) collective-permute-start(bf16[144,512]{1,0:T(8,128)(2,1)S(1)} %collective-permute-done.14.refs_12_), channel_id=1, source_target_pairs={{224,0},{0,32},{32,64},{64,96},{96,128},{128,160},{160,192},{192,2... | collective-permute-start | bytes 442376 | tf_op jit(solution)/shard_map/ppermute | solution.py:38
  58.2 7.6 %collective-permute-start.11 = (bf16[144,512]{1,0:T(8,128)(2,1)S(1)}, bf16[144,512]{1,0:T(8,128)(2,1)}, u32[]{:S(2)}, u32[]{:S(2)}) collective-permute-start(bf16[144,512]{1,0:T(8,128)(2,1)S(1)} %collective-permute-done.9.refs_6_), channel_id=1, source_target_pairs={{32,0},{64,32},{96,64},{128,96},{160,128},{192,160},{224,192},{0,2... | collective-permute-start | bytes 442376 | tf_op jit(solution)/shard_map/ppermute | solution.py:38
  60.8 5.9 %collective-permute-start.17 = (bf16[144,512]{1,0:T(8,128)(2,1)S(1)}, bf16[144,512]{1,0:T(8,128)(2,1)}, u32[]{:S(2)}, u32[]{:S(2)}) collective-permute-start(bf16[144,512]{1,0:T(8,128)(2,1)S(1)} %collective-permute-done.14.refs_12_), channel_id=1, source_target_pairs={{1,0},{0,1},{3,2},{2,3},{5,4},{4,5},{7,6},{6,7},{9,8},{8,9},{11,10... | collective-permute-start | bytes 442376 | tf_op jit(solution)/shard_map/ppermute | solution.py:38
  64.0 2.8 %collective-permute-start.8 = (bf16[144,512]{1,0:T(8,128)(2,1)S(1)}, bf16[144,512]{1,0:T(8,128)(2,1)}, u32[]{:S(2)}, u32[]{:S(2)}) collective-permute-start(bf16[144,512]{1,0:T(8,128)(2,1)S(1)} %collective-permute-done.7.refs_4_), channel_id=1, source_target_pairs={{1,0},{0,1},{3,2},{2,3},{5,4},{4,5},{7,6},{6,7},{9,8},{8,9},{11,10... | collective-permute-start | bytes 442376 | tf_op jit(solution)/shard_map/ppermute | solution.py:38
  64.1 0.7 copy-start.5
  64.8 2.3 %collective-permute-start.10 = (bf16[144,512]{1,0:T(8,128)(2,1)S(1)}, bf16[144,512]{1,0:T(8,128)(2,1)}, u32[]{:S(2)}, u32[]{:S(2)}) collective-permute-start(bf16[144,512]{1,0:T(8,128)(2,1)S(1)} %collective-permute-done.9.refs_6_), channel_id=1, source_target_pairs={{1,0},{0,1},{3,2},{2,3},{5,4},{4,5},{7,6},{6,7},{9,8},{8,9},{11,10... | collective-permute-start | bytes 442376 | tf_op jit(solution)/shard_map/ppermute | solution.py:38
  65.2 1.9 %collective-permute-start.16 = (bf16[144,512]{1,0:T(8,128)(2,1)}, bf16[144,512]{1,0:T(8,128)(2,1)}, u32[]{:S(2)}, u32[]{:S(2)}) collective-permute-start(bf16[144,512]{1,0:T(8,128)(2,1)} %collective-permute-done.15.refs_10_), channel_id=1, source_target_pairs={{1,0},{0,1},{3,2},{2,3},{5,4},{4,5},{7,6},{6,7},{9,8},{8,9},{11,10... | collective-permute-start | bytes 442376 | tf_op jit(solution)/shard_map/ppermute | solution.py:38
  65.7 2.3 %collective-permute-start.12 = (bf16[144,512]{1,0:T(8,128)(2,1)}, bf16[144,512]{1,0:T(8,128)(2,1)}, u32[]{:S(2)}, u32[]{:S(2)}) collective-permute-start(bf16[144,512]{1,0:T(8,128)(2,1)} %collective-permute-done.11.refs_8_), channel_id=1, source_target_pairs={{1,0},{0,1},{3,2},{2,3},{5,4},{4,5},{7,6},{6,7},{9,8},{8,9},{11,10... | collective-permute-start | bytes 442376 | tf_op jit(solution)/shard_map/ppermute | solution.py:38
  68.0 0.9 copy-start.6
  89.6 11.7 %all-to-all-start.1 = ((f32[8,8,128]{2,1,0:T(8,128)}), f32[8,8,128]{2,1,0:T(8,128)S(1)}, u32[]{:S(2)}, u32[]{:S(2)}) async-start(f32[8,8,128]{2,1,0:T(8,128)} %get-tuple-element.38), calls=%async_computation.1 | async-start | bytes 65536 | tf_op jit(solution)/shard_map/all_to_all | solution.py:343
  101.3 26.9 %all-to-all-start.2 = ((f32[16,8,128]{2,1,0:T(8,128)}), f32[16,8,128]{2,1,0:T(8,128)S(1)}, u32[]{:S(2)}, u32[]{:S(2)}) async-start(f32[16,8,128]{2,1,0:T(8,128)} %get-tuple-element.39), calls=%async_computation.2 | async-start | bytes 131072 | tf_op jit(solution)/shard_map/all_to_all | solution.py:344

commit v5 on v3

--- a/solution.py
+++ b/solution.py
@@ -10,8 +10,6 @@
 
 LOGIT_SCALE = 14.285714285714286
 EPSILON = 1e-06
-LOG2E = math.log2(math.e)
-POLYNOMIAL = (4.626287491105563e-06, 0.00010370556301479831, 0.001853591056490648, 0.024912203935707634, 0.22321428590727893, 1.0000000060541538)
 
 SHARE = 128
 SIDE = 16
@@ -140,15 +138,6 @@
 
 def integers(values):
     return values.astype(jnp.float32).astype(jnp.int32)
-
-
-def exponential(products):
-    power = products * POLYNOMIAL[0] + POLYNOMIAL[1]
-    for coefficient in POLYNOMIAL[2:]:
-        power = power * products + coefficient
-    for _ in range(6):
-        power = power * power
-    return power
 
 
 def pair_kernel(place_ref, *refs):
@@ -209,10 +198,7 @@
                         col_total, col_matched = ct[:, at], cm[:, at]
                         for group in groups:
                             product = products[pl.ds(local[group], 8), at]
-                            if chunk % 2:
-                                expo = exponential(product)
-                            else:
-                                expo = jnp.exp2(product * (LOGIT_SCALE * LOG2E))
+                            expo = jnp.exp(product * LOGIT_SCALE)
                             kept = jnp.where(label[group] == col_label, expo, 0.0)
                             row_total[group] += expo
                             row_matched[group] += kept
@@ -244,7 +230,7 @@
         at = slice(chunk * 128, (chunk + 1) * 128)
         total = jnp.sum(ct[:, at], axis=0, keepdims=True)
         matched = jnp.sum(cm[:, at], axis=0, keepdims=True)
-        cols_ref[chunk] = jnp.where(row_of == 0, total, matched)
+        cols_ref[chunk] = jnp.where(row_of == 6, total, jnp.where(row_of == 7, matched, 0.0))
 
 
 def pair_sums(place, seq_blocks, struct_blocks):
@@ -317,9 +303,10 @@
 
     rows, cols = pair_sums(jnp.stack([place("z"), core]), seq_blocks, struct_blocks)
     rows = jnp.sum(lax.all_to_all(rows, "z", split_axis=0, concat_axis=0, tiled=True), axis=0)
-    cols = jnp.sum(lax.all_to_all(cols, COL_AXES, split_axis=0, concat_axis=0, tiled=True), axis=0)
-    rows = lax.all_gather(rows, MP_AXES, axis=0, tiled=False).reshape(2, 2, 8, SHARE)
-    rows = jnp.sum(rows, axis=1)[:, 0:6].reshape(2, 2, 3, SHARE)
+    rows = rows + shifted(rows, "core", 1)
+    sums = lax.all_to_all(cols + rows[None], COL_AXES, split_axis=0, concat_axis=0, tiled=True)
+    cols = jnp.sum(sums[:, 6:8], axis=0)
+    rows = lax.dynamic_slice_in_dim(sums, (place("yh") * 4 + place("x")) * 2, 2, 0)[:, 0:6].reshape(2, 2, 3, SHARE)
 
     seq_loss = (jnp.log(rows[:, :, 0]) - jnp.log(rows[:, :, 1])).reshape(4 * SHARE)
     struct_loss = jnp.log(cols[0]) - jnp.log(cols[1])

time: 104 us -> 107 us (1.029)
  blocking collectives: 7.82 us -> 14.8 us
  starting transfers between devices: 44.9 us -> 39.3 us
  local copies, waits for them, and re-layouts: 4.46 us -> 6.04 us
    all_to_all x0 -> x1, blocking collectives: none -> 14.8 us  [per_device(): lax.all_to_all(rows, 'z', split_axis=0, concat_axis=0, tiled=True)]
    all_to_all x2 -> x1, starting transfers between devices: 11.7 us -> 3.5 us  [per_device(): lax.all_to_all(cols + rows[None], COL_AXES, split_axis=0, concat_axis=0,...]
    all_gather x1 -> x0, blocking collectives: 7.82 us -> none  [per_device(): lax.all_gather(rows, MP_AXES, axis=0, tiled=False).reshape(2, 2, 8, SHARE)]
    ppermute x19 -> x20, starting transfers between devices: 28.2 us -> 30.8 us  [shifted(): lax.ppermute(value, axes, [((place + steps) % count, place) for place in...]
    unnamed x12 -> x16, local copies, waits for them, and re-layouts: 3.84 us -> 5.42 us
    all_to_all x2 -> x1, waiting for transfers between devices: 6.88 us -> 6.42 us  [per_device(): lax.all_to_all(cols + rows[None], COL_AXES, split_axis=0, concat_axis=0,...]
    ppermute x19 -> x20, waiting for transfers between devices: 11.6 us -> 12 us  [shifted(): lax.ppermute(value, axes, [((place + steps) % count, place) for place in...]
  transfers between devices with their start and end apart: 22 -> 22, of which waited for: 11 -> 11; matrix products, arithmetic and copies ran while one was open for 3% -> 2% of each run, Pallas kernels for 1% -> 1%
where the time goes in v5:
time: 107 us; the launch traced here: 106 us
  starting transfers between devices  39.3 us (37%)
  Pallas kernels  22.9 us (21%)
  waiting for transfers between devices  19.2 us (18%)
  blocking collectives  14.8 us (14%)
  local copies, waits for them, and re-layouts  6.04 us (6%)
  other arithmetic  3.3 us (3%)
    ppermute x20, starting transfers between devices, shifted(): lax.ppermute(value, axes, [((place + steps) % count, place) for place in...  30.8 us
    pallas_call x1, Pallas kernels, pair_sums(): pl.pallas_call(pair_kernel, out_shape=(jax.ShapeDtypeStruct((8, 8, SHARE)...  19.9 us
    all_to_all x1, blocking collectives, per_device(): lax.all_to_all(rows, 'z', split_axis=0, concat_axis=0, tiled=True)  14.8 us
    ppermute x20, waiting for transfers between devices, shifted(): lax.ppermute(value, axes, [((place + steps) % count, place) for place in...  12 us
    all_to_all x1, waiting for transfers between devices, per_device(): lax.all_to_all(cols + rows[None], COL_AXES, split_axis=0, concat_axis=0,...  6.42 us
    unnamed x16, local copies, waits for them, and re-layouts  5.42 us
    all_to_all x1, starting transfers between devices, per_device(): lax.all_to_all(struct_peers, COL_AXES, split_axis=0, concat_axis=0, tiled...  5.01 us
    all_to_all x1, starting transfers between devices, per_device(): lax.all_to_all(cols + rows[None], COL_AXES, split_axis=0, concat_axis=0,...  3.5 us
  transfers between devices with their start and end apart: 22, of which 11 were waited for; matrix products, arithmetic and copies ran while one was open for 2% of the time, Pallas kernels for 1%

profile of v5, /device:TPU:1, one launch (start us, length us, event | category | flops | bytes accessed | tf_op | source)
XLA Modules:
  0.0 106.4 jit_solution(17075484868575357879)
XLA Ops:
  0.6 0.9 copy-done.2
  1.6 0.9 copy-done.3
  2.9 3.3 %collective-permute-start = (f32[2,128,512]{2,1,0:T(8,128)S(1)}, f32[2,128,512]{2,1,0:T(8,128)S(1)}, u32[]{:S(2)}, u32[]{:S(2)}) collective-permute-start(f32[2,128,512]{2,1,0:T(8,128)S(1)} %get-tuple-element.21), channel_id=1, source_target_pairs={{1,0},{0,1},{3,2},{2,3},{5,4},{4,5},{7,6},{6,7},{9,8},{8,9},{11,10... | collective-permute-start | bytes 1572872 | tf_op jit(solution)/shard_map/ppermute | solution.py:36
  6.2 1.0 copy-done
  7.2 1.0 copy-done.1
  8.2 0.7 project_seq.1
  9.2 1.7 %collective-permute-done.2.got_ref = f32[2,128,512]{2,1,0:T(8,128)S(1)} collective-permute-done((f32[2,128,512]{2,1,0:T(8,128)S(1)}, f32[2,128,512]{2,1,0:T(8,128)S(1)}, u32[]{:S(2)}, u32[]{:S(2)}) %collective-permute-start.2) | collective-permute-done | bytes 524320 | tf_op jit(solution)/shard_map/ppermute | solution.py:36
  11.0 0.8 shift-right-arithmetic_convert_fusion
  11.9 0.7 fusion.5
  12.6 1.1 %collective-permute-done.1.got2_s = bf16[128,512]{1,0:T(8,128)(2,1)S(1)} collective-permute-done((bf16[128,512]{1,0:T(8,128)(2,1)S(1)}, bf16[128,512]{1,0:T(8,128)(2,1)S(1)}, u32[]{:S(2)}, u32[]{:S(2)}) %collective-permute-start.1) | collective-permute-done | bytes 131104 | tf_op jit(solution)/shard_map/ppermute | solution.py:36
  13.8 2.8 %collective-permute-done.3.got2_q = bf16[128,512]{1,0:T(8,128)(2,1)S(1)} collective-permute-done((bf16[128,512]{1,0:T(8,128)(2,1)S(1)}, bf16[128,512]{1,0:T(8,128)(2,1)S(1)}, u32[]{:S(2)}, u32[]{:S(2)}) %collective-permute-start.3) | collective-permute-done | bytes 131104 | tf_op jit(solution)/shard_map/ppermute | solution.py:36
  16.6 1.8 %finish.1 = (bf16[16,528,128]{2,1,0:T(8,128)(2,1)}, bf16[144,512]{1,0:T(8,128)(2,1)S(1)}, f32[8,128]{1,0:T(8,128)S(1)}) custom-call(f32[128,512]{1,0:T(8,128)S(1)} %get-tuple-element.22.keep2_s, bf16[128,512]{1,0:T(8,128)(2,1)S(1)} %collective-permute-done.1.got2_s, f32[128,512]{1,0:T(8,128)S(1)} %get-tuple-element.26.keep2_q, ...), custom_call_target="tpu_custom_call" | custom-call | tf_op jit(solution)/shard_map/finish/pallas_call | solution.py:125
  18.4 5.0 %all-to-all-start = ((bf16[16,528,128]{2,1,0:T(8,128)(2,1)}), bf16[16,528,128]{2,1,0:T(8,128)(2,1)S(1)}, u32[]{:S(2)}, u32[]{:S(2)}) async-start(bf16[16,528,128]{2,1,0:T(8,128)(2,1)} %get-tuple-element.33), calls=%async_computation | async-start | bytes 4325376 | tf_op jit(solution)/shard_map/all_to_all | solution.py:301
  23.4 5.7 %collective-permute-start.5 = (bf16[144,512]{1,0:T(8,128)(2,1)S(1)}, bf16[144,512]{1,0:T(8,128)(2,1)S(1)}, u32[]{:S(2)}, u32[]{:S(2)}) collective-permute-start(bf16[144,512]{1,0:T(8,128)(2,1)S(1)} %get-tuple-element.32.refs_0_), channel_id=1, source_target_pairs={{32,0},{64,32},{96,64},{128,96},{160,128},{192,160},{224,192},{0,2... | collective-permute-start | bytes 442376 | tf_op jit(solution)/shard_map/ppermute | solution.py:36
  29.0 2.1 %collective-permute-done.5.refs_2_ = bf16[144,512]{1,0:T(8,128)(2,1)S(1)} collective-permute-done((bf16[144,512]{1,0:T(8,128)(2,1)S(1)}, bf16[144,512]{1,0:T(8,128)(2,1)S(1)}, u32[]{:S(2)}, u32[]{:S(2)}) %collective-permute-start.5) | collective-permute-done | bytes 147488 | tf_op jit(solution)/shard_map/ppermute | solution.py:36
  31.1 3.1 %collective-permute-start.7 = (bf16[144,512]{1,0:T(8,128)(2,1)S(1)}, bf16[144,512]{1,0:T(8,128)(2,1)S(1)}, u32[]{:S(2)}, u32[]{:S(2)}) collective-permute-start(bf16[144,512]{1,0:T(8,128)(2,1)S(1)} %collective-permute-done.5.refs_2_), channel_id=1, source_target_pairs={{32,0},{64,32},{96,64},{128,96},{160,128},{192,160},{224,192},{0,2... | collective-permute-start | bytes 442376 | tf_op jit(solution)/shard_map/ppermute | solution.py:36
  34.5 1.8 %collective-permute-done.7.refs_4_ = bf16[144,512]{1,0:T(8,128)(2,1)S(1)} collective-permute-done((bf16[144,512]{1,0:T(8,128)(2,1)S(1)}, bf16[144,512]{1,0:T(8,128)(2,1)S(1)}, u32[]{:S(2)}, u32[]{:S(2)}) %collective-permute-start.7) | collective-permute-done | bytes 147488 | tf_op jit(solution)/shard_map/ppermute | solution.py:36
  36.4 3.4 %collective-permute-start.9 = (bf16[144,512]{1,0:T(8,128)(2,1)S(1)}, bf16[144,512]{1,0:T(8,128)(2,1)S(1)}, u32[]{:S(2)}, u32[]{:S(2)}) collective-permute-start(bf16[144,512]{1,0:T(8,128)(2,1)S(1)} %collective-permute-done.7.refs_4_), channel_id=1, source_target_pairs={{32,0},{64,32},{96,64},{128,96},{160,128},{192,160},{224,192},{0,2... | collective-permute-start | bytes 442376 | tf_op jit(solution)/shard_map/ppermute | solution.py:36
  39.8 3.9 %collective-permute-start.4 = (bf16[144,512]{1,0:T(8,128)(2,1)S(1)}, bf16[144,512]{1,0:T(8,128)(2,1)S(1)}, u32[]{:S(2)}, u32[]{:S(2)}) collective-permute-start(bf16[144,512]{1,0:T(8,128)(2,1)S(1)} %get-tuple-element.32.refs_0_), channel_id=1, source_target_pairs={{1,0},{0,1},{3,2},{2,3},{5,4},{4,5},{7,6},{6,7},{9,8},{8,9},{11,10... | collective-permute-start | bytes 442376 | tf_op jit(solution)/shard_map/ppermute | solution.py:36
  44.2 2.7 %collective-permute-start.11 = (bf16[144,512]{1,0:T(8,128)(2,1)S(1)}, bf16[144,512]{1,0:T(8,128)(2,1)}, u32[]{:S(2)}, u32[]{:S(2)}) collective-permute-start(bf16[144,512]{1,0:T(8,128)(2,1)S(1)} %collective-permute-done.9.refs_6_), channel_id=1, source_target_pairs={{32,0},{64,32},{96,64},{128,96},{160,128},{192,160},{224,192},{0,2... | collective-permute-start | bytes 442376 | tf_op jit(solution)/shard_map/ppermute | solution.py:36
  46.8 3.2 %collective-permute-start.17 = (bf16[144,512]{1,0:T(8,128)(2,1)S(1)}, bf16[144,512]{1,0:T(8,128)(2,1)}, u32[]{:S(2)}, u32[]{:S(2)}) collective-permute-start(bf16[144,512]{1,0:T(8,128)(2,1)S(1)} %collective-permute-done.14.refs_12_), channel_id=1, source_target_pairs={{1,0},{0,1},{3,2},{2,3},{5,4},{4,5},{7,6},{6,7},{9,8},{8,9},{11,10... | collective-permute-start | bytes 442376 | tf_op jit(solution)/shard_map/ppermute | solution.py:36
  50.1 0.7 copy-done.4
  51.7 0.9 collective-permute-start.12
  53.1 0.9 collective-permute-done.12.refs_9_
  54.0 0.8 all-to-all-done.refs_16_
  54.8 0.9 copy-done.5
  55.7 19.9 %pair_sums.1 = (f32[8,8,128]{2,1,0:T(8,128)S(1)}, f32[16,8,128]{2,1,0:T(8,128)S(1)}) custom-call(s32[2]{0:T(128)S(1)} %pad_add_fusion.place_ref, bf16[144,512]{1,0:T(8,128)(2,1)S(1)} %get-tuple-element.32.refs_0_, bf16[144,512]{1,0:T(8,128)(2,1)S(1)} %collective-permute-done.4.refs_1_, bf16[144,512]{1,0:T(8,128)(2,1)S(1)} %collective-permute-done.5.refs_2_, ...), custom_call_target="tpu_custom_call" | custom-call | flops 4294967296 | bytes 4194304 | tf_op jit(solution)/shard_map/pair_sums/pallas_call | solution.py:237
  75.6 14.8 %all_to_all.15 = f32[8,8,128]{2,1,0:T(8,128)S(1)} all-to-all(f32[8,8,128]{2,1,0:T(8,128)S(1)} %get-tuple-element.35), channel_id=1, replica_groups=mesh['z'=8,'yh'=2,'x'=4,'yl'=2,'core'=2] {'z'}, dimensions={0} | all-to-all | bytes 65536 | tf_op jit(solution)/shard_map/all_to_all | solution.py:305
  90.5 2.9 %collective-permute-start.19 = (f32[8,128]{1,0:T(8,128)S(1)}, f32[8,128]{1,0:T(8,128)S(1)}, u32[]{:S(2)}, u32[]{:S(2)}) collective-permute-start(f32[8,128]{1,0:T(8,128)S(1)} %reduce_sum.18), channel_id=1, source_target_pairs={{1,0},{0,1},{3,2},{2,3},{5,4},{4,5},{7,6},{6,7},{9,8},{8,9},{11,10... | collective-permute-start | bytes 12296 | tf_op jit(solution)/shard_map/ppermute | solution.py:36
  93.3 0.8 collective-permute-done.19
  94.8 3.5 %all-to-all-start.2 = ((f32[16,8,128]{2,1,0:T(8,128)}), f32[16,8,128]{2,1,0:T(8,128)S(1)}, u32[]{:S(2)}, u32[]{:S(2)}) async-start(f32[16,8,128]{2,1,0:T(8,128)} %broadcast_add_fusion), calls=%async_computation.2 | async-start | bytes 131072 | tf_op jit(solution)/shard_map/all_to_all | solution.py:307
  98.3 6.4 %all-to-all-done.2 = f32[16,8,128]{2,1,0:T(8,128)S(1)} async-done(((f32[16,8,128]{2,1,0:T(8,128)}), f32[16,8,128]{2,1,0:T(8,128)S(1)}, u32[]{:S(2)}, u32[]{:S(2)}) %all-to-all-start.2) | async-done | bytes 65568 | tf_op jit(solution)/shard_map/all_to_all | solution.py:307
  (56 shorter events, 5.4 us)
Async XLA Ops:
  0.6 1.0 copy-start.2
  1.6 0.9 copy-start.3
  2.5 9.3 %copy-start.6 = (s32[512,16,1]{0,2,1:T(1,128)S(1)}, s32[512,16,1]{0,2,1:T(1,128)}, u32[]{:S(2)}) copy-start(s32[512,16,1]{0,2,1:T(1,128)} %param.13) | copy-start | bytes 98308
  2.5 9.3 %copy-start.7 = (s32[128,16]{0,1:T(8,128)S(1)}, s32[128,16]{0,1:T(8,128)}, u32[]{:S(2)}) copy-start(s32[128,16]{0,1:T(8,128)} %param.15) | copy-start | bytes 24580
  2.9 6.1 %collective-permute-start = (f32[2,128,512]{2,1,0:T(8,128)S(1)}, f32[2,128,512]{2,1,0:T(8,128)S(1)}, u32[]{:S(2)}, u32[]{:S(2)}) collective-permute-start(f32[2,128,512]{2,1,0:T(8,128)S(1)} %get-tuple-element.21), channel_id=1, source_target_pairs={{1,0},{0,1},{3,2},{2,3},{5,4},{4,5},{7,6},{6,7},{9,8},{8,9},{11,10... | collective-permute-start | bytes 1572872 | tf_op jit(solution)/shard_map/ppermute | solution.py:36
  6.2 1.0 copy-start
  7.2 1.0 copy-start.1
  8.9 2.0 %collective-permute-start.2 = (f32[2,128,512]{2,1,0:T(8,128)S(1)}, f32[2,128,512]{2,1,0:T(8,128)S(1)}, u32[]{:S(2)}, u32[]{:S(2)}) collective-permute-start(f32[2,128,512]{2,1,0:T(8,128)S(1)} %get-tuple-element.25), channel_id=1, source_target_pairs={{1,0},{0,1},{3,2},{2,3},{5,4},{4,5},{7,6},{6,7},{9,8},{8,9},{11,10... | collective-permute-start | bytes 1572872 | tf_op jit(solution)/shard_map/ppermute | solution.py:36
  9.1 4.7 %collective-permute-start.1 = (bf16[128,512]{1,0:T(8,128)(2,1)S(1)}, bf16[128,512]{1,0:T(8,128)(2,1)S(1)}, u32[]{:S(2)}, u32[]{:S(2)}) collective-permute-start(bf16[128,512]{1,0:T(8,128)(2,1)S(1)} %get-tuple-element.23), channel_id=1, source_target_pairs={{2,0},{0,2},{3,1},{1,3},{6,4},{4,6},{7,5},{5,7},{10,8},{8,10},{11,... | collective-permute-start | bytes 393224 | tf_op jit(solution)/shard_map/ppermute | solution.py:36
  10.9 5.6 %collective-permute-start.3 = (bf16[128,512]{1,0:T(8,128)(2,1)S(1)}, bf16[128,512]{1,0:T(8,128)(2,1)S(1)}, u32[]{:S(2)}, u32[]{:S(2)}) collective-permute-start(bf16[128,512]{1,0:T(8,128)(2,1)S(1)} %get-tuple-element.27), channel_id=1, source_target_pairs={{2,0},{0,2},{3,1},{1,3},{6,4},{4,6},{7,5},{5,7},{10,8},{8,10},{11,... | collective-permute-start | bytes 393224 | tf_op jit(solution)/shard_map/ppermute | solution.py:36
  18.4 36.4 %all-to-all-start = ((bf16[16,528,128]{2,1,0:T(8,128)(2,1)}), bf16[16,528,128]{2,1,0:T(8,128)(2,1)S(1)}, u32[]{:S(2)}, u32[]{:S(2)}) async-start(bf16[16,528,128]{2,1,0:T(8,128)(2,1)} %get-tuple-element.33), calls=%async_computation | async-start | bytes 4325376 | tf_op jit(solution)/shard_map/all_to_all | solution.py:301
  23.4 7.8 %collective-permute-start.5 = (bf16[144,512]{1,0:T(8,128)(2,1)S(1)}, bf16[144,512]{1,0:T(8,128)(2,1)S(1)}, u32[]{:S(2)}, u32[]{:S(2)}) collective-permute-start(bf16[144,512]{1,0:T(8,128)(2,1)S(1)} %get-tuple-element.32.refs_0_), channel_id=1, source_target_pairs={{32,0},{64,32},{96,64},{128,96},{160,128},{192,160},{224,192},{0,2... | collective-permute-start | bytes 442376 | tf_op jit(solution)/shard_map/ppermute | solution.py:36
  29.0 5.5 %collective-permute-start.13 = (bf16[144,512]{1,0:T(8,128)(2,1)S(1)}, bf16[144,512]{1,0:T(8,128)(2,1)S(1)}, u32[]{:S(2)}, u32[]{:S(2)}) collective-permute-start(bf16[144,512]{1,0:T(8,128)(2,1)S(1)} %get-tuple-element.32.refs_0_), channel_id=1, source_target_pairs={{224,0},{0,32},{32,64},{64,96},{96,128},{128,160},{160,192},{192,2... | collective-permute-start | bytes 442376 | tf_op jit(solution)/shard_map/ppermute | solution.py:36
  31.1 5.2 %collective-permute-start.7 = (bf16[144,512]{1,0:T(8,128)(2,1)S(1)}, bf16[144,512]{1,0:T(8,128)(2,1)S(1)}, u32[]{:S(2)}, u32[]{:S(2)}) collective-permute-start(bf16[144,512]{1,0:T(8,128)(2,1)S(1)} %collective-permute-done.5.refs_2_), channel_id=1, source_target_pairs={{32,0},{64,32},{96,64},{128,96},{160,128},{192,160},{224,192},{0,2... | collective-permute-start | bytes 442376 | tf_op jit(solution)/shard_map/ppermute | solution.py:36
  34.5 9.6 %collective-permute-start.14 = (bf16[144,512]{1,0:T(8,128)(2,1)S(1)}, bf16[144,512]{1,0:T(8,128)(2,1)S(1)}, u32[]{:S(2)}, u32[]{:S(2)}) collective-permute-start(bf16[144,512]{1,0:T(8,128)(2,1)S(1)} %collective-permute-done.13.refs_14_), channel_id=1, source_target_pairs={{224,0},{0,32},{32,64},{64,96},{96,128},{128,160},{160,192},{192,2... | collective-permute-start | bytes 442376 | tf_op jit(solution)/shard_map/ppermute | solution.py:36
  36.4 7.8 %collective-permute-start.9 = (bf16[144,512]{1,0:T(8,128)(2,1)S(1)}, bf16[144,512]{1,0:T(8,128)(2,1)S(1)}, u32[]{:S(2)}, u32[]{:S(2)}) collective-permute-start(bf16[144,512]{1,0:T(8,128)(2,1)S(1)} %collective-permute-done.7.refs_4_), channel_id=1, source_target_pairs={{32,0},{64,32},{96,64},{128,96},{160,128},{192,160},{224,192},{0,2... | collective-permute-start | bytes 442376 | tf_op jit(solution)/shard_map/ppermute | solution.py:36
  39.8 7.1 %collective-permute-start.4 = (bf16[144,512]{1,0:T(8,128)(2,1)S(1)}, bf16[144,512]{1,0:T(8,128)(2,1)S(1)}, u32[]{:S(2)}, u32[]{:S(2)}) collective-permute-start(bf16[144,512]{1,0:T(8,128)(2,1)S(1)} %get-tuple-element.32.refs_0_), channel_id=1, source_target_pairs={{1,0},{0,1},{3,2},{2,3},{5,4},{4,5},{7,6},{6,7},{9,8},{8,9},{11,10... | collective-permute-start | bytes 442376 | tf_op jit(solution)/shard_map/ppermute | solution.py:36
  43.6 6.4 %collective-permute-start.18 = (bf16[144,512]{1,0:T(8,128)(2,1)S(1)}, bf16[144,512]{1,0:T(8,128)(2,1)S(1)}, u32[]{:S(2)}, u32[]{:S(2)}) collective-permute-start(bf16[144,512]{1,0:T(8,128)(2,1)S(1)} %collective-permute-done.13.refs_14_), channel_id=1, source_target_pairs={{1,0},{0,1},{3,2},{2,3},{5,4},{4,5},{7,6},{6,7},{9,8},{8,9},{11,10... | collective-permute-start | bytes 442376 | tf_op jit(solution)/shard_map/ppermute | solution.py:36
  43.6 6.5 %collective-permute-start.6 = (bf16[144,512]{1,0:T(8,128)(2,1)S(1)}, bf16[144,512]{1,0:T(8,128)(2,1)S(1)}, u32[]{:S(2)}, u32[]{:S(2)}) collective-permute-start(bf16[144,512]{1,0:T(8,128)(2,1)S(1)} %collective-permute-done.5.refs_2_), channel_id=1, source_target_pairs={{1,0},{0,1},{3,2},{2,3},{5,4},{4,5},{7,6},{6,7},{9,8},{8,9},{11,10... | collective-permute-start | bytes 442376 | tf_op jit(solution)/shard_map/ppermute | solution.py:36
  44.2 7.0 %collective-permute-start.15 = (bf16[144,512]{1,0:T(8,128)(2,1)S(1)}, bf16[144,512]{1,0:T(8,128)(2,1)}, u32[]{:S(2)}, u32[]{:S(2)}) collective-permute-start(bf16[144,512]{1,0:T(8,128)(2,1)S(1)} %collective-permute-done.14.refs_12_), channel_id=1, source_target_pairs={{224,0},{0,32},{32,64},{64,96},{96,128},{128,160},{160,192},{192,2... | collective-permute-start | bytes 442376 | tf_op jit(solution)/shard_map/ppermute | solution.py:36
  44.2 7.6 %collective-permute-start.11 = (bf16[144,512]{1,0:T(8,128)(2,1)S(1)}, bf16[144,512]{1,0:T(8,128)(2,1)}, u32[]{:S(2)}, u32[]{:S(2)}) collective-permute-start(bf16[144,512]{1,0:T(8,128)(2,1)S(1)} %collective-permute-done.9.refs_6_), channel_id=1, source_target_pairs={{32,0},{64,32},{96,64},{128,96},{160,128},{192,160},{224,192},{0,2... | collective-permute-start | bytes 442376 | tf_op jit(solution)/shard_map/ppermute | solution.py:36
  46.8 5.9 %collective-permute-start.17 = (bf16[144,512]{1,0:T(8,128)(2,1)S(1)}, bf16[144,512]{1,0:T(8,128)(2,1)}, u32[]{:S(2)}, u32[]{:S(2)}) collective-permute-start(bf16[144,512]{1,0:T(8,128)(2,1)S(1)} %collective-permute-done.14.refs_12_), channel_id=1, source_target_pairs={{1,0},{0,1},{3,2},{2,3},{5,4},{4,5},{7,6},{6,7},{9,8},{8,9},{11,10... | collective-permute-start | bytes 442376 | tf_op jit(solution)/shard_map/ppermute | solution.py:36
  50.0 2.8 %collective-permute-start.8 = (bf16[144,512]{1,0:T(8,128)(2,1)S(1)}, bf16[144,512]{1,0:T(8,128)(2,1)}, u32[]{:S(2)}, u32[]{:S(2)}) collective-permute-start(bf16[144,512]{1,0:T(8,128)(2,1)S(1)} %collective-permute-done.7.refs_4_), channel_id=1, source_target_pairs={{1,0},{0,1},{3,2},{2,3},{5,4},{4,5},{7,6},{6,7},{9,8},{8,9},{11,10... | collective-permute-start | bytes 442376 | tf_op jit(solution)/shard_map/ppermute | solution.py:36
  50.1 0.7 copy-start.4
  50.8 2.3 %collective-permute-start.10 = (bf16[144,512]{1,0:T(8,128)(2,1)S(1)}, bf16[144,512]{1,0:T(8,128)(2,1)}, u32[]{:S(2)}, u32[]{:S(2)}) collective-permute-start(bf16[144,512]{1,0:T(8,128)(2,1)S(1)} %collective-permute-done.9.refs_6_), channel_id=1, source_target_pairs={{1,0},{0,1},{3,2},{2,3},{5,4},{4,5},{7,6},{6,7},{9,8},{8,9},{11,10... | collective-permute-start | bytes 442376 | tf_op jit(solution)/shard_map/ppermute | solution.py:36
  51.2 1.9 %collective-permute-start.16 = (bf16[144,512]{1,0:T(8,128)(2,1)}, bf16[144,512]{1,0:T(8,128)(2,1)}, u32[]{:S(2)}, u32[]{:S(2)}) collective-permute-start(bf16[144,512]{1,0:T(8,128)(2,1)} %collective-permute-done.15.refs_10_), channel_id=1, source_target_pairs={{1,0},{0,1},{3,2},{2,3},{5,4},{4,5},{7,6},{6,7},{9,8},{8,9},{11,10... | collective-permute-start | bytes 442376 | tf_op jit(solution)/shard_map/ppermute | solution.py:36
  51.7 2.3 %collective-permute-start.12 = (bf16[144,512]{1,0:T(8,128)(2,1)}, bf16[144,512]{1,0:T(8,128)(2,1)}, u32[]{:S(2)}, u32[]{:S(2)}) collective-permute-start(bf16[144,512]{1,0:T(8,128)(2,1)} %collective-permute-done.11.refs_8_), channel_id=1, source_target_pairs={{1,0},{0,1},{3,2},{2,3},{5,4},{4,5},{7,6},{6,7},{9,8},{8,9},{11,10... | collective-permute-start | bytes 442376 | tf_op jit(solution)/shard_map/ppermute | solution.py:36
  54.8 0.9 copy-start.5
  90.5 3.7 %collective-permute-start.19 = (f32[8,128]{1,0:T(8,128)S(1)}, f32[8,128]{1,0:T(8,128)S(1)}, u32[]{:S(2)}, u32[]{:S(2)}) collective-permute-start(f32[8,128]{1,0:T(8,128)S(1)} %reduce_sum.18), channel_id=1, source_target_pairs={{1,0},{0,1},{3,2},{2,3},{5,4},{4,5},{7,6},{6,7},{9,8},{8,9},{11,10... | collective-permute-start | bytes 12296 | tf_op jit(solution)/shard_map/ppermute | solution.py:36
  94.8 9.9 %all-to-all-start.2 = ((f32[16,8,128]{2,1,0:T(8,128)}), f32[16,8,128]{2,1,0:T(8,128)S(1)}, u32[]{:S(2)}, u32[]{:S(2)}) async-start(f32[16,8,128]{2,1,0:T(8,128)} %broadcast_add_fusion), calls=%async_computation.2 | async-start | bytes 131072 | tf_op jit(solution)/shard_map/all_to_all | solution.py:307

commit v6 on v5

--- a/solution.py
+++ b/solution.py
@@ -17,8 +17,6 @@
 WIDTH = 512
 SLOTS = 16
 EXT = 16
-TILE = 512
-STRIP = 512
 SUB = 32
 
 COL_AXES = ("yh", "x", "yl")
@@ -143,10 +141,6 @@
 def pair_kernel(place_ref, *refs):
     seq_refs, s, rows_ref, cols_ref = refs[0:SIDE], refs[SIDE], refs[SIDE + 1], refs[SIDE + 2]
     q, info, buf0, buf1, lab8, ct, cm, rt, rm, ex = refs[SIDE + 3 :]
-    tiles = EDGE // TILE
-    strips = EDGE // STRIP
-    part = TILE // strips
-    buffers = (buf0, buf1)
     my_z, my_core = place_ref[0], place_ref[1]
     my_block = my_z * 2 + my_core
 
@@ -168,69 +162,73 @@
     cm[...] = jnp.zeros_like(cm)
     row_of = lax.broadcasted_iota(jnp.int32, (8, SHARE), 0)
 
-    for tile in range(tiles + 1):
-
-        def body(step, carry, tile=tile):
-            if tile < tiles:
-                wide = STRIP // SHARE
-                cols = jnp.concatenate([s[step * wide + each, 0:WIDTH, :] for each in range(wide)], axis=1)
-                start = pl.multiple_of(step * STRIP, STRIP)
-                buffers[tile % 2][:, pl.ds(start, STRIP)] = lax.dot_general(
-                    q[tile * TILE : (tile + 1) * TILE, :],
-                    cols,
-                    (((1,), (0,)), ((), ())),
-                    preferred_element_type=jnp.float32,
-                )
-            if tile > 0:
-                products = buffers[(tile - 1) % 2]
-                zero = jnp.zeros((8, 128), jnp.float32)
-                groups = range(SUB // 8)
-                for sub in range(part // SUB):
-                    local = [pl.multiple_of(step * part + sub * SUB + group * 8, 8) for group in groups]
-                    code = [info[pl.ds(pl.multiple_of((tile - 1) * TILE + each, 8), 8), :] for each in local]
-                    label = [jnp.broadcast_to(-1 - each[:, SLOTS : SLOTS + 1], (8, 128)) for each in code]
-                    lane = [each & 127 for each in code]
-                    chunk_of = [each >> 7 for each in code]
-                    row_total, row_matched, picked = [zero for _ in groups], [zero for _ in groups], [zero for _ in groups]
-                    for chunk in range(SIDE):
-                        at = slice(chunk * 128, (chunk + 1) * 128)
-                        col_label = lab8[:, at]
-                        col_total, col_matched = ct[:, at], cm[:, at]
-                        for group in groups:
-                            product = products[pl.ds(local[group], 8), at]
-                            expo = jnp.exp(product * LOGIT_SCALE)
-                            kept = jnp.where(label[group] == col_label, expo, 0.0)
-                            row_total[group] += expo
-                            row_matched[group] += kept
-                            col_total += expo
-                            col_matched += kept
-                            found = jnp.take_along_axis(expo, lane[group], axis=1, mode="promise_in_bounds")
-                            picked[group] = jnp.where(chunk_of[group] == chunk, found, picked[group])
-                        ct[:, at] = col_total
-                        cm[:, at] = col_matched
-                    for group in groups:
-                        rt[pl.ds(local[group], 8), :] = row_total[group]
-                        rm[pl.ds(local[group], 8), :] = row_matched[group]
-                        ex[pl.ds(local[group], 8), :] = picked[group]
-            return carry
-
-        lax.fori_loop(0, strips, body, 0)
-        if tile > 0:
-            sums = [lanes_summed(each[...]) for each in (rt, rm, ex)]
-            for inner in range(TILE // SHARE):
-                block = (tile - 1) * (TILE // SHARE) + inner
-                at = slice(inner * SHARE, (inner + 1) * SHARE)
-                z, first = (my_z + block // 2) & 7, (my_core ^ (block % 2)) * 3
-                out = jnp.zeros((8, SHARE), jnp.float32) if block % 2 == 0 else rows_ref[z]
-                for which in range(3):
-                    out = jnp.where(row_of == first + which, sums[which][:, at], out)
-                rows_ref[z] = out
+    zero = jnp.zeros((8, 128), jnp.float32)
+    groups = range(SUB // 8)
+
+    def piece(tile, target, pair):
+        cols = jnp.concatenate([s[2 * pair, 0:WIDTH, :], s[2 * pair + 1, 0:WIDTH, :]], axis=1)
+        rows = pl.ds(pl.multiple_of(tile * SHARE, SHARE), SHARE)
+        target[:, 2 * pair * SHARE : 2 * (pair + 1) * SHARE] = jnp.dot(
+            q[rows, :], cols, preferred_element_type=jnp.float32
+        )
+
+    def work(tile, products, next_tile, target):
+        for sub in range(SHARE // SUB):
+            here = [pl.ds(pl.multiple_of(tile * SHARE + sub * SUB + group * 8, 8), 8) for group in groups]
+            code = [info[rows, :] for rows in here]
+            label = [jnp.broadcast_to(-1 - each[:, SLOTS : SLOTS + 1], (8, 128)) for each in code]
+            lane = [each & 127 for each in code]
+            chunk_of = [each >> 7 for each in code]
+            row_total, row_matched, picked = [zero for _ in groups], [zero for _ in groups], [zero for _ in groups]
+            for chunk in range(SIDE):
+                if chunk % 8 == 0:
+                    piece(next_tile, target, sub * 2 + chunk // 8)
+                at = slice(chunk * 128, (chunk + 1) * 128)
+                col_label = lab8[:, at]
+                col_total, col_matched = ct[:, at], cm[:, at]
+                for group in groups:
+                    local = sub * SUB + group * 8
+                    expo = jnp.exp(products[local : local + 8, at] * LOGIT_SCALE)
+                    kept = jnp.where(label[group] == col_label, expo, 0.0)
+                    row_total[group] += expo
+                    row_matched[group] += kept
+                    col_total += expo
+                    col_matched += kept
+                    found = jnp.take_along_axis(expo, lane[group], axis=1, mode="promise_in_bounds")
+                    picked[group] = jnp.where(chunk_of[group] == chunk, found, picked[group])
+                ct[:, at] = col_total
+                cm[:, at] = col_matched
+            for group in groups:
+                rt[here[group], :] = row_total[group]
+                rm[here[group], :] = row_matched[group]
+                ex[here[group], :] = picked[group]
+
+    for pair in range(SIDE // 2):
+        piece(0, buf0, pair)
+
+    def body(step, carry):
+        work(2 * step, buf0, 2 * step + 1, buf1)
+        work(2 * step + 1, buf1, jnp.minimum(2 * step + 2, SIDE - 1), buf0)
+        return carry
+
+    lax.fori_loop(0, SIDE // 2, body, 0)
+    for part in range(4):
+        at = slice(part * 4 * SHARE, (part + 1) * 4 * SHARE)
+        sums = [lanes_summed(each[at, :]) for each in (rt, rm, ex)]
+        for inner in range(4):
+            block = part * 4 + inner
+            at = slice(inner * SHARE, (inner + 1) * SHARE)
+            z, first = (my_z + block // 2) & 7, (my_core ^ (block % 2)) * 3
+            out = jnp.zeros((8, SHARE), jnp.float32) if block % 2 == 0 else rows_ref[z]
+            for which in range(3):
+                out = jnp.where(row_of == first + which, sums[which][:, at], out)
+            rows_ref[z] = out
 
     for chunk in range(SIDE):
         at = slice(chunk * 128, (chunk + 1) * 128)
         total = jnp.sum(ct[:, at], axis=0, keepdims=True)
         matched = jnp.sum(cm[:, at], axis=0, keepdims=True)
-        cols_ref[chunk] = jnp.where(row_of == 6, total, jnp.where(row_of == 7, matched, 0.0))
+        cols_ref[chunk] = jnp.where(row_of == 0, total, matched)
 
 
 def pair_sums(place, seq_blocks, struct_blocks):
@@ -245,14 +243,14 @@
         scratch_shapes=[
             pltpu.VMEM((EDGE, WIDTH), jnp.bfloat16),
             pltpu.VMEM((EDGE, 128), jnp.int32),
-            pltpu.VMEM((TILE, EDGE), jnp.float32),
-            pltpu.VMEM((TILE, EDGE), jnp.float32),
+            pltpu.VMEM((SHARE, EDGE), jnp.float32),
+            pltpu.VMEM((SHARE, EDGE), jnp.float32),
             pltpu.VMEM((8, EDGE), jnp.int32),
             pltpu.VMEM((8, EDGE), jnp.float32),
             pltpu.VMEM((8, EDGE), jnp.float32),
-            pltpu.VMEM((TILE, 128), jnp.float32),
-            pltpu.VMEM((TILE, 128), jnp.float32),
-            pltpu.VMEM((TILE, 128), jnp.float32),
+            pltpu.VMEM((EDGE, 128), jnp.float32),
+            pltpu.VMEM((EDGE, 128), jnp.float32),
+            pltpu.VMEM((EDGE, 128), jnp.float32),
         ],
         compiler_params=pltpu.CompilerParams(vmem_limit_bytes=28 * 1024 * 1024),
         cost_estimate=pl.CostEstimate(
@@ -303,10 +301,9 @@
 
     rows, cols = pair_sums(jnp.stack([place("z"), core]), seq_blocks, struct_blocks)
     rows = jnp.sum(lax.all_to_all(rows, "z", split_axis=0, concat_axis=0, tiled=True), axis=0)
-    rows = rows + shifted(rows, "core", 1)
-    sums = lax.all_to_all(cols + rows[None], COL_AXES, split_axis=0, concat_axis=0, tiled=True)
-    cols = jnp.sum(sums[:, 6:8], axis=0)
-    rows = lax.dynamic_slice_in_dim(sums, (place("yh") * 4 + place("x")) * 2, 2, 0)[:, 0:6].reshape(2, 2, 3, SHARE)
+    cols = jnp.sum(lax.all_to_all(cols, COL_AXES, split_axis=0, concat_axis=0, tiled=True), axis=0)
+    rows = lax.all_gather(rows, MP_AXES, axis=0, tiled=False).reshape(2, 2, 8, SHARE)
+    rows = jnp.sum(rows, axis=1)[:, 0:6].reshape(2, 2, 3, SHARE)
 
     seq_loss = (jnp.log(rows[:, :, 0]) - jnp.log(rows[:, :, 1])).reshape(4 * SHARE)
     struct_loss = jnp.log(cols[0]) - jnp.log(cols[1])

time: 107 us -> 103 us (0.963)
  blocking collectives: 14.8 us -> 7.83 us
  starting transfers between devices: 39.3 us -> 44.9 us
  local copies, waits for them, and re-layouts: 6.04 us -> 4.46 us
    all_to_all x1 -> x0, blocking collectives: 14.8 us -> none  [per_device(): lax.all_to_all(rows, 'z', split_axis=0, concat_axis=0, tiled=True)]
    all_to_all x1 -> x2, starting transfers between devices: 3.5 us -> 11.7 us  [the longest x1 8.18 us: per_device(): lax.all_to_all(rows, 'z', split_axis=0, concat_axis=0, tiled=True)]
    all_gather x0 -> x1, blocking collectives: none -> 7.83 us  [per_device(): lax.all_gather(rows, MP_AXES, axis=0, tiled=False).reshape(2, 2, 8, SHARE)]
    ppermute x20 -> x19, starting transfers between devices: 30.8 us -> 28.2 us  [shifted(): lax.ppermute(value, axes, [((place + steps) % count, place) for place in...]
    unnamed x16 -> x12, local copies, waits for them, and re-layouts: 5.42 us -> 3.84 us
    all_to_all x1 -> x2, waiting for transfers between devices: 6.42 us -> 6.88 us  [the longest x1 6.88 us: per_device(): lax.all_to_all(rows, 'z', split_axis=0, concat_axis=0, tiled=True)]
    ppermute x20 -> x19, waiting for transfers between devices: 12 us -> 11.6 us  [shifted(): lax.ppermute(value, axes, [((place + steps) % count, place) for place in...]
  transfers between devices with their start and end apart: 22 -> 22, of which waited for: 11 -> 11; matrix products, arithmetic and copies ran while one was open for 2% -> 3% of each run, Pallas kernels for 1% -> 1%
where the time goes in v6:
time: 103 us
  starting transfers between devices  44.9 us (44%)
  Pallas kernels  22.6 us (22%)
  waiting for transfers between devices  19.2 us (19%)
  blocking collectives  7.83 us (8%)
  local copies, waits for them, and re-layouts  4.46 us (4%)
  other arithmetic  2.68 us (3%)
    ppermute x19, starting transfers between devices, shifted(): lax.ppermute(value, axes, [((place + steps) % count, place) for place in...  28.2 us
    pallas_call x1, Pallas kernels, pair_sums(): pl.pallas_call(pair_kernel, out_shape=(jax.ShapeDtypeStruct((8, 8, SHARE)...  19.7 us
    ppermute x19, waiting for transfers between devices, shifted(): lax.ppermute(value, axes, [((place + steps) % count, place) for place in...  11.6 us
    all_to_all x1, starting transfers between devices, per_device(): lax.all_to_all(rows, 'z', split_axis=0, concat_axis=0, tiled=True)  8.18 us
    all_gather x1, blocking collectives, per_device(): lax.all_gather(rows, MP_AXES, axis=0, tiled=False).reshape(2, 2, 8, SHARE)  7.83 us
    all_to_all x1, waiting for transfers between devices, per_device(): lax.all_to_all(rows, 'z', split_axis=0, concat_axis=0, tiled=True)  6.88 us
    all_to_all x1, starting transfers between devices, per_device(): lax.all_to_all(struct_peers, COL_AXES, split_axis=0, concat_axis=0, tiled...  5.01 us
    unnamed x12, local copies, waits for them, and re-layouts  3.84 us
  transfers between devices with their start and end apart: 22, of which 11 were waited for; matrix products, arithmetic and copies ran while one was open for 3% of the time, Pallas kernels for 1%

profile of v6, /device:TPU:1, one launch (start us, length us, event | category | flops | bytes accessed | tf_op | source)
XLA Modules:
  0.0 102.6 jit_solution(5864239255605750978)
XLA Ops:
  0.6 0.9 copy-done.2
  1.6 0.9 copy-done.3
  2.9 3.3 %collective-permute-start = (f32[2,128,512]{2,1,0:T(8,128)S(1)}, f32[2,128,512]{2,1,0:T(8,128)S(1)}, u32[]{:S(2)}, u32[]{:S(2)}) collective-permute-start(f32[2,128,512]{2,1,0:T(8,128)S(1)} %get-tuple-element.21), channel_id=1, source_target_pairs={{1,0},{0,1},{3,2},{2,3},{5,4},{4,5},{7,6},{6,7},{9,8},{8,9},{11,10... | collective-permute-start | bytes 1572872 | tf_op jit(solution)/shard_map/ppermute | solution.py:34
  6.2 1.0 copy-done
  7.2 1.0 copy-done.1
  8.2 0.7 project_seq.1
  9.2 1.7 %collective-permute-done.2.got_ref = f32[2,128,512]{2,1,0:T(8,128)S(1)} collective-permute-done((f32[2,128,512]{2,1,0:T(8,128)S(1)}, f32[2,128,512]{2,1,0:T(8,128)S(1)}, u32[]{:S(2)}, u32[]{:S(2)}) %collective-permute-start.2) | collective-permute-done | bytes 524320 | tf_op jit(solution)/shard_map/ppermute | solution.py:34
  11.0 0.8 shift-right-arithmetic_convert_fusion
  11.9 0.7 fusion.5
  12.6 1.1 %collective-permute-done.1.got2_s = bf16[128,512]{1,0:T(8,128)(2,1)S(1)} collective-permute-done((bf16[128,512]{1,0:T(8,128)(2,1)S(1)}, bf16[128,512]{1,0:T(8,128)(2,1)S(1)}, u32[]{:S(2)}, u32[]{:S(2)}) %collective-permute-start.1) | collective-permute-done | bytes 131104 | tf_op jit(solution)/shard_map/ppermute | solution.py:34
  13.8 2.8 %collective-permute-done.3.got2_q = bf16[128,512]{1,0:T(8,128)(2,1)S(1)} collective-permute-done((bf16[128,512]{1,0:T(8,128)(2,1)S(1)}, bf16[128,512]{1,0:T(8,128)(2,1)S(1)}, u32[]{:S(2)}, u32[]{:S(2)}) %collective-permute-start.3) | collective-permute-done | bytes 131104 | tf_op jit(solution)/shard_map/ppermute | solution.py:34
  16.6 1.8 %finish.1 = (bf16[16,528,128]{2,1,0:T(8,128)(2,1)}, bf16[144,512]{1,0:T(8,128)(2,1)S(1)}, f32[8,128]{1,0:T(8,128)S(1)}) custom-call(f32[128,512]{1,0:T(8,128)S(1)} %get-tuple-element.22.keep2_s, bf16[128,512]{1,0:T(8,128)(2,1)S(1)} %collective-permute-done.1.got2_s, f32[128,512]{1,0:T(8,128)S(1)} %get-tuple-element.26.keep2_q, ...), custom_call_target="tpu_custom_call" | custom-call | tf_op jit(solution)/shard_map/finish/pallas_call | solution.py:123
  18.4 5.0 %all-to-all-start = ((bf16[16,528,128]{2,1,0:T(8,128)(2,1)}), bf16[16,528,128]{2,1,0:T(8,128)(2,1)S(1)}, u32[]{:S(2)}, u32[]{:S(2)}) async-start(bf16[16,528,128]{2,1,0:T(8,128)(2,1)} %get-tuple-element.33), calls=%async_computation | async-start | bytes 4325376 | tf_op jit(solution)/shard_map/all_to_all | solution.py:299
  23.4 5.7 %collective-permute-start.5 = (bf16[144,512]{1,0:T(8,128)(2,1)S(1)}, bf16[144,512]{1,0:T(8,128)(2,1)S(1)}, u32[]{:S(2)}, u32[]{:S(2)}) collective-permute-start(bf16[144,512]{1,0:T(8,128)(2,1)S(1)} %get-tuple-element.32.refs_0_), channel_id=1, source_target_pairs={{32,0},{64,32},{96,64},{128,96},{160,128},{192,160},{224,192},{0,2... | collective-permute-start | bytes 442376 | tf_op jit(solution)/shard_map/ppermute | solution.py:34
  29.0 2.1 %collective-permute-done.5.refs_2_ = bf16[144,512]{1,0:T(8,128)(2,1)S(1)} collective-permute-done((bf16[144,512]{1,0:T(8,128)(2,1)S(1)}, bf16[144,512]{1,0:T(8,128)(2,1)S(1)}, u32[]{:S(2)}, u32[]{:S(2)}) %collective-permute-start.5) | collective-permute-done | bytes 147488 | tf_op jit(solution)/shard_map/ppermute | solution.py:34
  31.1 3.1 %collective-permute-start.7 = (bf16[144,512]{1,0:T(8,128)(2,1)S(1)}, bf16[144,512]{1,0:T(8,128)(2,1)S(1)}, u32[]{:S(2)}, u32[]{:S(2)}) collective-permute-start(bf16[144,512]{1,0:T(8,128)(2,1)S(1)} %collective-permute-done.5.refs_2_), channel_id=1, source_target_pairs={{32,0},{64,32},{96,64},{128,96},{160,128},{192,160},{224,192},{0,2... | collective-permute-start | bytes 442376 | tf_op jit(solution)/shard_map/ppermute | solution.py:34
  34.5 1.8 %collective-permute-done.7.refs_4_ = bf16[144,512]{1,0:T(8,128)(2,1)S(1)} collective-permute-done((bf16[144,512]{1,0:T(8,128)(2,1)S(1)}, bf16[144,512]{1,0:T(8,128)(2,1)S(1)}, u32[]{:S(2)}, u32[]{:S(2)}) %collective-permute-start.7) | collective-permute-done | bytes 147488 | tf_op jit(solution)/shard_map/ppermute | solution.py:34
  36.3 3.4 %collective-permute-start.9 = (bf16[144,512]{1,0:T(8,128)(2,1)S(1)}, bf16[144,512]{1,0:T(8,128)(2,1)S(1)}, u32[]{:S(2)}, u32[]{:S(2)}) collective-permute-start(bf16[144,512]{1,0:T(8,128)(2,1)S(1)} %collective-permute-done.7.refs_4_), channel_id=1, source_target_pairs={{32,0},{64,32},{96,64},{128,96},{160,128},{192,160},{224,192},{0,2... | collective-permute-start | bytes 442376 | tf_op jit(solution)/shard_map/ppermute | solution.py:34
  39.7 3.9 %collective-permute-start.4 = (bf16[144,512]{1,0:T(8,128)(2,1)S(1)}, bf16[144,512]{1,0:T(8,128)(2,1)S(1)}, u32[]{:S(2)}, u32[]{:S(2)}) collective-permute-start(bf16[144,512]{1,0:T(8,128)(2,1)S(1)} %get-tuple-element.32.refs_0_), channel_id=1, source_target_pairs={{1,0},{0,1},{3,2},{2,3},{5,4},{4,5},{7,6},{6,7},{9,8},{8,9},{11,10... | collective-permute-start | bytes 442376 | tf_op jit(solution)/shard_map/ppermute | solution.py:34
  44.1 2.7 %collective-permute-start.11 = (bf16[144,512]{1,0:T(8,128)(2,1)S(1)}, bf16[144,512]{1,0:T(8,128)(2,1)}, u32[]{:S(2)}, u32[]{:S(2)}) collective-permute-start(bf16[144,512]{1,0:T(8,128)(2,1)S(1)} %collective-permute-done.9.refs_6_), channel_id=1, source_target_pairs={{32,0},{64,32},{96,64},{128,96},{160,128},{192,160},{224,192},{0,2... | collective-permute-start | bytes 442376 | tf_op jit(solution)/shard_map/ppermute | solution.py:34
  46.8 3.2 %collective-permute-start.17 = (bf16[144,512]{1,0:T(8,128)(2,1)S(1)}, bf16[144,512]{1,0:T(8,128)(2,1)}, u32[]{:S(2)}, u32[]{:S(2)}) collective-permute-start(bf16[144,512]{1,0:T(8,128)(2,1)S(1)} %collective-permute-done.14.refs_12_), channel_id=1, source_target_pairs={{1,0},{0,1},{3,2},{2,3},{5,4},{4,5},{7,6},{6,7},{9,8},{8,9},{11,10... | collective-permute-start | bytes 442376 | tf_op jit(solution)/shard_map/ppermute | solution.py:34
  50.9 0.8 collective-permute-start.16
  51.7 0.9 collective-permute-start.12
  53.1 0.9 collective-permute-done.12.refs_9_
  54.0 0.8 all-to-all-done.refs_16_
  54.8 19.7 %pair_sums.1 = (f32[8,8,128]{2,1,0:T(8,128)}, f32[16,8,128]{2,1,0:T(8,128)}) custom-call(s32[2]{0:T(128)S(1)} %pad_add_fusion.place_ref, bf16[144,512]{1,0:T(8,128)(2,1)S(1)} %get-tuple-element.32.refs_0_, bf16[144,512]{1,0:T(8,128)(2,1)S(1)} %collective-permute-done.4.refs_1_, bf16[144,512]{1,0:T(8,128)(2,1)S(1)} %collective-permute-done.5.refs_2_, ...), custom_call_target="tpu_custom_call" | custom-call | flops 4294967296 | bytes 4194304 | tf_op jit(solution)/shard_map/pair_sums/pallas_call | solution.py:235
  74.5 8.2 %all-to-all-start.1 = ((f32[8,8,128]{2,1,0:T(8,128)}), f32[8,8,128]{2,1,0:T(8,128)S(1)}, u32[]{:S(2)}, u32[]{:S(2)}) async-start(f32[8,8,128]{2,1,0:T(8,128)} %get-tuple-element.34), calls=%async_computation.1 | async-start | bytes 65536 | tf_op jit(solution)/shard_map/all_to_all | solution.py:303
  82.7 6.9 %all-to-all-done.1 = f32[8,8,128]{2,1,0:T(8,128)S(1)} async-done(((f32[8,8,128]{2,1,0:T(8,128)}), f32[8,8,128]{2,1,0:T(8,128)S(1)}, u32[]{:S(2)}, u32[]{:S(2)}) %all-to-all-start.1) | async-done | bytes 32800 | tf_op jit(solution)/shard_map/all_to_all | solution.py:303
  89.5 3.5 %all-to-all-start.2 = ((f32[16,8,128]{2,1,0:T(8,128)}), f32[16,8,128]{2,1,0:T(8,128)S(1)}, u32[]{:S(2)}, u32[]{:S(2)}) async-start(f32[16,8,128]{2,1,0:T(8,128)} %get-tuple-element.35), calls=%async_computation.2 | async-start | bytes 131072 | tf_op jit(solution)/shard_map/all_to_all | solution.py:304
  93.1 7.8 %all-gather = f32[32,128]{1,0:T(8,128)S(1)} all-gather(f32[8,128]{1,0:T(8,128)S(1)} %reduce_sum.27), channel_id=2, replica_groups=mesh['z'=8,'yh'=2,'x'=4,'yl'=2,'core'=2] {'yl','core'}, dimensions={0}, use_global_device_ids=true | all-gather | bytes 20480 | tf_op jit(solution)/shard_map/all_gather | solution.py:305
  100.9 0.5 fusion.10
  101.5 0.6 copy.18
  (50 shorter events, 3.6 us)
Async XLA Ops:
  0.6 1.0 copy-start.2
  1.6 0.9 copy-start.3
  2.5 9.3 %copy-start.4 = (s32[512,16,1]{0,2,1:T(1,128)S(1)}, s32[512,16,1]{0,2,1:T(1,128)}, u32[]{:S(2)}) copy-start(s32[512,16,1]{0,2,1:T(1,128)} %param.13) | copy-start | bytes 98308
  2.5 9.3 %copy-start.5 = (s32[128,16]{0,1:T(8,128)S(1)}, s32[128,16]{0,1:T(8,128)}, u32[]{:S(2)}) copy-start(s32[128,16]{0,1:T(8,128)} %param.15) | copy-start | bytes 24580
  2.9 6.1 %collective-permute-start = (f32[2,128,512]{2,1,0:T(8,128)S(1)}, f32[2,128,512]{2,1,0:T(8,128)S(1)}, u32[]{:S(2)}, u32[]{:S(2)}) collective-permute-start(f32[2,128,512]{2,1,0:T(8,128)S(1)} %get-tuple-element.21), channel_id=1, source_target_pairs={{1,0},{0,1},{3,2},{2,3},{5,4},{4,5},{7,6},{6,7},{9,8},{8,9},{11,10... | collective-permute-start | bytes 1572872 | tf_op jit(solution)/shard_map/ppermute | solution.py:34
  6.2 1.0 copy-start
  7.2 1.0 copy-start.1
  8.9 2.0 %collective-permute-start.2 = (f32[2,128,512]{2,1,0:T(8,128)S(1)}, f32[2,128,512]{2,1,0:T(8,128)S(1)}, u32[]{:S(2)}, u32[]{:S(2)}) collective-permute-start(f32[2,128,512]{2,1,0:T(8,128)S(1)} %get-tuple-element.25), channel_id=1, source_target_pairs={{1,0},{0,1},{3,2},{2,3},{5,4},{4,5},{7,6},{6,7},{9,8},{8,9},{11,10... | collective-permute-start | bytes 1572872 | tf_op jit(solution)/shard_map/ppermute | solution.py:34
  9.1 4.7 %collective-permute-start.1 = (bf16[128,512]{1,0:T(8,128)(2,1)S(1)}, bf16[128,512]{1,0:T(8,128)(2,1)S(1)}, u32[]{:S(2)}, u32[]{:S(2)}) collective-permute-start(bf16[128,512]{1,0:T(8,128)(2,1)S(1)} %get-tuple-element.23), channel_id=1, source_target_pairs={{2,0},{0,2},{3,1},{1,3},{6,4},{4,6},{7,5},{5,7},{10,8},{8,10},{11,... | collective-permute-start | bytes 393224 | tf_op jit(solution)/shard_map/ppermute | solution.py:34
  10.9 5.6 %collective-permute-start.3 = (bf16[128,512]{1,0:T(8,128)(2,1)S(1)}, bf16[128,512]{1,0:T(8,128)(2,1)S(1)}, u32[]{:S(2)}, u32[]{:S(2)}) collective-permute-start(bf16[128,512]{1,0:T(8,128)(2,1)S(1)} %get-tuple-element.27), channel_id=1, source_target_pairs={{2,0},{0,2},{3,1},{1,3},{6,4},{4,6},{7,5},{5,7},{10,8},{8,10},{11,... | collective-permute-start | bytes 393224 | tf_op jit(solution)/shard_map/ppermute | solution.py:34
  18.4 36.4 %all-to-all-start = ((bf16[16,528,128]{2,1,0:T(8,128)(2,1)}), bf16[16,528,128]{2,1,0:T(8,128)(2,1)S(1)}, u32[]{:S(2)}, u32[]{:S(2)}) async-start(bf16[16,528,128]{2,1,0:T(8,128)(2,1)} %get-tuple-element.33), calls=%async_computation | async-start | bytes 4325376 | tf_op jit(solution)/shard_map/all_to_all | solution.py:299
  23.4 7.8 %collective-permute-start.5 = (bf16[144,512]{1,0:T(8,128)(2,1)S(1)}, bf16[144,512]{1,0:T(8,128)(2,1)S(1)}, u32[]{:S(2)}, u32[]{:S(2)}) collective-permute-start(bf16[144,512]{1,0:T(8,128)(2,1)S(1)} %get-tuple-element.32.refs_0_), channel_id=1, source_target_pairs={{32,0},{64,32},{96,64},{128,96},{160,128},{192,160},{224,192},{0,2... | collective-permute-start | bytes 442376 | tf_op jit(solution)/shard_map/ppermute | solution.py:34
  29.0 5.5 %collective-permute-start.13 = (bf16[144,512]{1,0:T(8,128)(2,1)S(1)}, bf16[144,512]{1,0:T(8,128)(2,1)S(1)}, u32[]{:S(2)}, u32[]{:S(2)}) collective-permute-start(bf16[144,512]{1,0:T(8,128)(2,1)S(1)} %get-tuple-element.32.refs_0_), channel_id=1, source_target_pairs={{224,0},{0,32},{32,64},{64,96},{96,128},{128,160},{160,192},{192,2... | collective-permute-start | bytes 442376 | tf_op jit(solution)/shard_map/ppermute | solution.py:34
  31.1 5.2 %collective-permute-start.7 = (bf16[144,512]{1,0:T(8,128)(2,1)S(1)}, bf16[144,512]{1,0:T(8,128)(2,1)S(1)}, u32[]{:S(2)}, u32[]{:S(2)}) collective-permute-start(bf16[144,512]{1,0:T(8,128)(2,1)S(1)} %collective-permute-done.5.refs_2_), channel_id=1, source_target_pairs={{32,0},{64,32},{96,64},{128,96},{160,128},{192,160},{224,192},{0,2... | collective-permute-start | bytes 442376 | tf_op jit(solution)/shard_map/ppermute | solution.py:34
  34.5 9.6 %collective-permute-start.14 = (bf16[144,512]{1,0:T(8,128)(2,1)S(1)}, bf16[144,512]{1,0:T(8,128)(2,1)S(1)}, u32[]{:S(2)}, u32[]{:S(2)}) collective-permute-start(bf16[144,512]{1,0:T(8,128)(2,1)S(1)} %collective-permute-done.13.refs_14_), channel_id=1, source_target_pairs={{224,0},{0,32},{32,64},{64,96},{96,128},{128,160},{160,192},{192,2... | collective-permute-start | bytes 442376 | tf_op jit(solution)/shard_map/ppermute | solution.py:34
  36.3 7.8 %collective-permute-start.9 = (bf16[144,512]{1,0:T(8,128)(2,1)S(1)}, bf16[144,512]{1,0:T(8,128)(2,1)S(1)}, u32[]{:S(2)}, u32[]{:S(2)}) collective-permute-start(bf16[144,512]{1,0:T(8,128)(2,1)S(1)} %collective-permute-done.7.refs_4_), channel_id=1, source_target_pairs={{32,0},{64,32},{96,64},{128,96},{160,128},{192,160},{224,192},{0,2... | collective-permute-start | bytes 442376 | tf_op jit(solution)/shard_map/ppermute | solution.py:34
  39.7 7.1 %collective-permute-start.4 = (bf16[144,512]{1,0:T(8,128)(2,1)S(1)}, bf16[144,512]{1,0:T(8,128)(2,1)S(1)}, u32[]{:S(2)}, u32[]{:S(2)}) collective-permute-start(bf16[144,512]{1,0:T(8,128)(2,1)S(1)} %get-tuple-element.32.refs_0_), channel_id=1, source_target_pairs={{1,0},{0,1},{3,2},{2,3},{5,4},{4,5},{7,6},{6,7},{9,8},{8,9},{11,10... | collective-permute-start | bytes 442376 | tf_op jit(solution)/shard_map/ppermute | solution.py:34
  43.6 6.4 %collective-permute-start.18 = (bf16[144,512]{1,0:T(8,128)(2,1)S(1)}, bf16[144,512]{1,0:T(8,128)(2,1)S(1)}, u32[]{:S(2)}, u32[]{:S(2)}) collective-permute-start(bf16[144,512]{1,0:T(8,128)(2,1)S(1)} %collective-permute-done.13.refs_14_), channel_id=1, source_target_pairs={{1,0},{0,1},{3,2},{2,3},{5,4},{4,5},{7,6},{6,7},{9,8},{8,9},{11,10... | collective-permute-start | bytes 442376 | tf_op jit(solution)/shard_map/ppermute | solution.py:34
  43.6 6.5 %collective-permute-start.6 = (bf16[144,512]{1,0:T(8,128)(2,1)S(1)}, bf16[144,512]{1,0:T(8,128)(2,1)S(1)}, u32[]{:S(2)}, u32[]{:S(2)}) collective-permute-start(bf16[144,512]{1,0:T(8,128)(2,1)S(1)} %collective-permute-done.5.refs_2_), channel_id=1, source_target_pairs={{1,0},{0,1},{3,2},{2,3},{5,4},{4,5},{7,6},{6,7},{9,8},{8,9},{11,10... | collective-permute-start | bytes 442376 | tf_op jit(solution)/shard_map/ppermute | solution.py:34
  44.1 6.8 %collective-permute-start.15 = (bf16[144,512]{1,0:T(8,128)(2,1)S(1)}, bf16[144,512]{1,0:T(8,128)(2,1)}, u32[]{:S(2)}, u32[]{:S(2)}) collective-permute-start(bf16[144,512]{1,0:T(8,128)(2,1)S(1)} %collective-permute-done.14.refs_12_), channel_id=1, source_target_pairs={{224,0},{0,32},{32,64},{64,96},{96,128},{128,160},{160,192},{192,2... | collective-permute-start | bytes 442376 | tf_op jit(solution)/shard_map/ppermute | solution.py:34
  44.1 7.6 %collective-permute-start.11 = (bf16[144,512]{1,0:T(8,128)(2,1)S(1)}, bf16[144,512]{1,0:T(8,128)(2,1)}, u32[]{:S(2)}, u32[]{:S(2)}) collective-permute-start(bf16[144,512]{1,0:T(8,128)(2,1)S(1)} %collective-permute-done.9.refs_6_), channel_id=1, source_target_pairs={{32,0},{64,32},{96,64},{128,96},{160,128},{192,160},{224,192},{0,2... | collective-permute-start | bytes 442376 | tf_op jit(solution)/shard_map/ppermute | solution.py:34
  46.8 5.9 %collective-permute-start.17 = (bf16[144,512]{1,0:T(8,128)(2,1)S(1)}, bf16[144,512]{1,0:T(8,128)(2,1)}, u32[]{:S(2)}, u32[]{:S(2)}) collective-permute-start(bf16[144,512]{1,0:T(8,128)(2,1)S(1)} %collective-permute-done.14.refs_12_), channel_id=1, source_target_pairs={{1,0},{0,1},{3,2},{2,3},{5,4},{4,5},{7,6},{6,7},{9,8},{8,9},{11,10... | collective-permute-start | bytes 442376 | tf_op jit(solution)/shard_map/ppermute | solution.py:34
  50.0 2.8 %collective-permute-start.8 = (bf16[144,512]{1,0:T(8,128)(2,1)S(1)}, bf16[144,512]{1,0:T(8,128)(2,1)}, u32[]{:S(2)}, u32[]{:S(2)}) collective-permute-start(bf16[144,512]{1,0:T(8,128)(2,1)S(1)} %collective-permute-done.7.refs_4_), channel_id=1, source_target_pairs={{1,0},{0,1},{3,2},{2,3},{5,4},{4,5},{7,6},{6,7},{9,8},{8,9},{11,10... | collective-permute-start | bytes 442376 | tf_op jit(solution)/shard_map/ppermute | solution.py:34
  50.1 3.0 %collective-permute-start.10 = (bf16[144,512]{1,0:T(8,128)(2,1)S(1)}, bf16[144,512]{1,0:T(8,128)(2,1)}, u32[]{:S(2)}, u32[]{:S(2)}) collective-permute-start(bf16[144,512]{1,0:T(8,128)(2,1)S(1)} %collective-permute-done.9.refs_6_), channel_id=1, source_target_pairs={{1,0},{0,1},{3,2},{2,3},{5,4},{4,5},{7,6},{6,7},{9,8},{8,9},{11,10... | collective-permute-start | bytes 442376 | tf_op jit(solution)/shard_map/ppermute | solution.py:34
  50.9 2.1 %collective-permute-start.16 = (bf16[144,512]{1,0:T(8,128)(2,1)}, bf16[144,512]{1,0:T(8,128)(2,1)}, u32[]{:S(2)}, u32[]{:S(2)}) collective-permute-start(bf16[144,512]{1,0:T(8,128)(2,1)} %collective-permute-done.15.refs_10_), channel_id=1, source_target_pairs={{1,0},{0,1},{3,2},{2,3},{5,4},{4,5},{7,6},{6,7},{9,8},{8,9},{11,10... | collective-permute-start | bytes 442376 | tf_op jit(solution)/shard_map/ppermute | solution.py:34
  51.7 2.3 %collective-permute-start.12 = (bf16[144,512]{1,0:T(8,128)(2,1)}, bf16[144,512]{1,0:T(8,128)(2,1)}, u32[]{:S(2)}, u32[]{:S(2)}) collective-permute-start(bf16[144,512]{1,0:T(8,128)(2,1)} %collective-permute-done.11.refs_8_), channel_id=1, source_target_pairs={{1,0},{0,1},{3,2},{2,3},{5,4},{4,5},{7,6},{6,7},{9,8},{8,9},{11,10... | collective-permute-start | bytes 442376 | tf_op jit(solution)/shard_map/ppermute | solution.py:34
  74.5 15.1 %all-to-all-start.1 = ((f32[8,8,128]{2,1,0:T(8,128)}), f32[8,8,128]{2,1,0:T(8,128)S(1)}, u32[]{:S(2)}, u32[]{:S(2)}) async-start(f32[8,8,128]{2,1,0:T(8,128)} %get-tuple-element.34), calls=%async_computation.1 | async-start | bytes 65536 | tf_op jit(solution)/shard_map/all_to_all | solution.py:303
  89.5 12.5 %all-to-all-start.2 = ((f32[16,8,128]{2,1,0:T(8,128)}), f32[16,8,128]{2,1,0:T(8,128)S(1)}, u32[]{:S(2)}, u32[]{:S(2)}) async-start(f32[16,8,128]{2,1,0:T(8,128)} %get-tuple-element.35), calls=%async_computation.2 | async-start | bytes 131072 | tf_op jit(solution)/shard_map/all_to_all | solution.py:304

commit v7 on v6

--- a/solution.py
+++ b/solution.py
@@ -17,6 +17,7 @@
 WIDTH = 512
 SLOTS = 16
 EXT = 16
+FIXED = 32000.0
 SUB = 32
 
 COL_AXES = ("yh", "x", "yl")
@@ -151,10 +152,8 @@
         high, low = ext[:, 0:SHARE], ext[:, SHARE : 2 * SHARE]
         label = ext[:, 2 * SHARE : 3 * SHARE] * 128 + ext[:, 3 * SHARE :]
         code = jnp.where((high >> 4) == my_block, (high & 15) * 128 + low, -1)
-        whole = jnp.concatenate(
-            [code, -1 - label, jnp.full((128 - 2 * EXT, SHARE), -1, jnp.int32)], axis=0
-        ).astype(jnp.float32)
-        info[at, :] = whole.T.astype(jnp.int32)
+        info[at, :] = jnp.full((SHARE, 128), -1, jnp.int32)
+        info[at, 0 : 2 * EXT] = jnp.concatenate([code, -1 - label], axis=0).astype(jnp.float32).T.astype(jnp.int32)
     for chunk in range(SIDE):
         labels = integers(s[chunk, WIDTH:, :])
         lab8[:, chunk * 128 : (chunk + 1) * 128] = labels[0:8] * 128 + labels[8:16]
@@ -178,8 +177,10 @@
             code = [info[rows, :] for rows in here]
             label = [jnp.broadcast_to(-1 - each[:, SLOTS : SLOTS + 1], (8, 128)) for each in code]
             lane = [each & 127 for each in code]
-            chunk_of = [each >> 7 for each in code]
-            row_total, row_matched, picked = [zero for _ in groups], [zero for _ in groups], [zero for _ in groups]
+            pair_of = [each >> 8 for each in code]
+            row_total, row_matched = [zero for _ in groups], [zero for _ in groups]
+            picked = [jnp.zeros((8, 128), jnp.int32) for _ in groups]
+            even = [None for _ in groups]
             for chunk in range(SIDE):
                 if chunk % 8 == 0:
                     piece(next_tile, target, sub * 2 + chunk // 8)
@@ -188,20 +189,30 @@
                 col_total, col_matched = ct[:, at], cm[:, at]
                 for group in groups:
                     local = sub * SUB + group * 8
-                    expo = jnp.exp(products[local : local + 8, at] * LOGIT_SCALE)
+                    product = products[local : local + 8, at]
+                    expo = jnp.exp(product * LOGIT_SCALE)
+                    fixed = (product * FIXED).astype(jnp.int32)
                     kept = jnp.where(label[group] == col_label, expo, 0.0)
                     row_total[group] += expo
                     row_matched[group] += kept
                     col_total += expo
                     col_matched += kept
-                    found = jnp.take_along_axis(expo, lane[group], axis=1, mode="promise_in_bounds")
-                    picked[group] = jnp.where(chunk_of[group] == chunk, found, picked[group])
+                    if chunk % 2 == 0:
+                        even[group] = fixed
+                    else:
+                        both = (even[group] << 16) + fixed
+                        found = jnp.take_along_axis(both, lane[group], axis=1, mode="promise_in_bounds")
+                        picked[group] = jnp.where(pair_of[group] == chunk // 2, found, picked[group])
                 ct[:, at] = col_total
                 cm[:, at] = col_matched
             for group in groups:
                 rt[here[group], :] = row_total[group]
                 rm[here[group], :] = row_matched[group]
-                ex[here[group], :] = picked[group]
+                odd = (picked[group] << 16) >> 16
+                fixed = jnp.where((code[group] & 128) > 0, odd, (picked[group] - odd) >> 16).astype(jnp.float32)
+                fixed = fixed + jnp.where(fixed > 0, 0.5, jnp.where(fixed < 0, -0.5, 0.0))
+                hard = jnp.exp(fixed * (LOGIT_SCALE / FIXED))
+                ex[here[group], :] = jnp.where(code[group] >= 0, hard, 0.0)
 
     for pair in range(SIDE // 2):
         piece(0, buf0, pair)

time: 103 us -> 99.8 us (0.969)
  Pallas kernels: 22.6 us -> 19.3 us
    pallas_call x1, Pallas kernels: 19.7 us -> 16.4 us  [pair_sums(): pl.pallas_call(pair_kernel, out_shape=(jax.ShapeDtypeStruct((8, 8, SHARE)...]
where the time goes in v7:
time: 99.8 us; the launch traced here: 99.3 us
  starting transfers between devices  44.9 us (45%)
  Pallas kernels  19.3 us (19%)
  waiting for transfers between devices  19.2 us (19%)
  blocking collectives  7.82 us (8%)
  local copies, waits for them, and re-layouts  4.46 us (4%)
  other arithmetic  2.68 us (3%)
    ppermute x19, starting transfers between devices, shifted(): lax.ppermute(value, axes, [((place + steps) % count, place) for place in...  28.2 us
    pallas_call x1, Pallas kernels, pair_sums(): pl.pallas_call(pair_kernel, out_shape=(jax.ShapeDtypeStruct((8, 8, SHARE)...  16.4 us
    ppermute x19, waiting for transfers between devices, shifted(): lax.ppermute(value, axes, [((place + steps) % count, place) for place in...  11.6 us
    all_to_all x1, starting transfers between devices, per_device(): lax.all_to_all(rows, 'z', split_axis=0, concat_axis=0, tiled=True)  8.19 us
    all_gather x1, blocking collectives, per_device(): lax.all_gather(rows, MP_AXES, axis=0, tiled=False).reshape(2, 2, 8, SHARE)  7.82 us
    all_to_all x1, waiting for transfers between devices, per_device(): lax.all_to_all(rows, 'z', split_axis=0, concat_axis=0, tiled=True)  6.88 us
    all_to_all x1, starting transfers between devices, per_device(): lax.all_to_all(struct_peers, COL_AXES, split_axis=0, concat_axis=0, tiled...  5.01 us
    unnamed x12, local copies, waits for them, and re-layouts  3.84 us
  transfers between devices with their start and end apart: 22, of which 11 were waited for; matrix products, arithmetic and copies ran while one was open for 3% of the time, Pallas kernels for 1%

profile of v7, /device:TPU:1, one launch (start us, length us, event | category | flops | bytes accessed | tf_op | source)
XLA Modules:
  0.0 99.3 jit_solution(16397773418794008295)
XLA Ops:
  0.6 0.9 copy-done.2
  1.6 0.9 copy-done.3
  2.9 3.3 %collective-permute-start = (f32[2,128,512]{2,1,0:T(8,128)S(1)}, f32[2,128,512]{2,1,0:T(8,128)S(1)}, u32[]{:S(2)}, u32[]{:S(2)}) collective-permute-start(f32[2,128,512]{2,1,0:T(8,128)S(1)} %get-tuple-element.21), channel_id=1, source_target_pairs={{1,0},{0,1},{3,2},{2,3},{5,4},{4,5},{7,6},{6,7},{9,8},{8,9},{11,10... | collective-permute-start | bytes 1572872 | tf_op jit(solution)/shard_map/ppermute | solution.py:35
  6.2 1.0 copy-done
  7.2 1.0 copy-done.1
  8.2 0.7 project_seq.1
  9.2 1.7 %collective-permute-done.2.got_ref = f32[2,128,512]{2,1,0:T(8,128)S(1)} collective-permute-done((f32[2,128,512]{2,1,0:T(8,128)S(1)}, f32[2,128,512]{2,1,0:T(8,128)S(1)}, u32[]{:S(2)}, u32[]{:S(2)}) %collective-permute-start.2) | collective-permute-done | bytes 524320 | tf_op jit(solution)/shard_map/ppermute | solution.py:35
  11.0 0.8 shift-right-arithmetic_convert_fusion
  11.9 0.7 fusion.5
  12.6 1.1 %collective-permute-done.1.got2_s = bf16[128,512]{1,0:T(8,128)(2,1)S(1)} collective-permute-done((bf16[128,512]{1,0:T(8,128)(2,1)S(1)}, bf16[128,512]{1,0:T(8,128)(2,1)S(1)}, u32[]{:S(2)}, u32[]{:S(2)}) %collective-permute-start.1) | collective-permute-done | bytes 131104 | tf_op jit(solution)/shard_map/ppermute | solution.py:35
  13.8 2.8 %collective-permute-done.3.got2_q = bf16[128,512]{1,0:T(8,128)(2,1)S(1)} collective-permute-done((bf16[128,512]{1,0:T(8,128)(2,1)S(1)}, bf16[128,512]{1,0:T(8,128)(2,1)S(1)}, u32[]{:S(2)}, u32[]{:S(2)}) %collective-permute-start.3) | collective-permute-done | bytes 131104 | tf_op jit(solution)/shard_map/ppermute | solution.py:35
  16.6 1.8 %finish.1 = (bf16[16,528,128]{2,1,0:T(8,128)(2,1)}, bf16[144,512]{1,0:T(8,128)(2,1)S(1)}, f32[8,128]{1,0:T(8,128)S(1)}) custom-call(f32[128,512]{1,0:T(8,128)S(1)} %get-tuple-element.22.keep2_s, bf16[128,512]{1,0:T(8,128)(2,1)S(1)} %collective-permute-done.1.got2_s, f32[128,512]{1,0:T(8,128)S(1)} %get-tuple-element.26.keep2_q, ...), custom_call_target="tpu_custom_call" | custom-call | tf_op jit(solution)/shard_map/finish/pallas_call | solution.py:124
  18.4 5.0 %all-to-all-start = ((bf16[16,528,128]{2,1,0:T(8,128)(2,1)}), bf16[16,528,128]{2,1,0:T(8,128)(2,1)S(1)}, u32[]{:S(2)}, u32[]{:S(2)}) async-start(bf16[16,528,128]{2,1,0:T(8,128)(2,1)} %get-tuple-element.33), calls=%async_computation | async-start | bytes 4325376 | tf_op jit(solution)/shard_map/all_to_all | solution.py:310
  23.4 5.7 %collective-permute-start.5 = (bf16[144,512]{1,0:T(8,128)(2,1)S(1)}, bf16[144,512]{1,0:T(8,128)(2,1)S(1)}, u32[]{:S(2)}, u32[]{:S(2)}) collective-permute-start(bf16[144,512]{1,0:T(8,128)(2,1)S(1)} %get-tuple-element.32.refs_0_), channel_id=1, source_target_pairs={{32,0},{64,32},{96,64},{128,96},{160,128},{192,160},{224,192},{0,2... | collective-permute-start | bytes 442376 | tf_op jit(solution)/shard_map/ppermute | solution.py:35
  29.0 2.1 %collective-permute-done.5.refs_2_ = bf16[144,512]{1,0:T(8,128)(2,1)S(1)} collective-permute-done((bf16[144,512]{1,0:T(8,128)(2,1)S(1)}, bf16[144,512]{1,0:T(8,128)(2,1)S(1)}, u32[]{:S(2)}, u32[]{:S(2)}) %collective-permute-start.5) | collective-permute-done | bytes 147488 | tf_op jit(solution)/shard_map/ppermute | solution.py:35
  31.1 3.1 %collective-permute-start.7 = (bf16[144,512]{1,0:T(8,128)(2,1)S(1)}, bf16[144,512]{1,0:T(8,128)(2,1)S(1)}, u32[]{:S(2)}, u32[]{:S(2)}) collective-permute-start(bf16[144,512]{1,0:T(8,128)(2,1)S(1)} %collective-permute-done.5.refs_2_), channel_id=1, source_target_pairs={{32,0},{64,32},{96,64},{128,96},{160,128},{192,160},{224,192},{0,2... | collective-permute-start | bytes 442376 | tf_op jit(solution)/shard_map/ppermute | solution.py:35
  34.5 1.8 %collective-permute-done.7.refs_4_ = bf16[144,512]{1,0:T(8,128)(2,1)S(1)} collective-permute-done((bf16[144,512]{1,0:T(8,128)(2,1)S(1)}, bf16[144,512]{1,0:T(8,128)(2,1)S(1)}, u32[]{:S(2)}, u32[]{:S(2)}) %collective-permute-start.7) | collective-permute-done | bytes 147488 | tf_op jit(solution)/shard_map/ppermute | solution.py:35
  36.3 3.4 %collective-permute-start.9 = (bf16[144,512]{1,0:T(8,128)(2,1)S(1)}, bf16[144,512]{1,0:T(8,128)(2,1)S(1)}, u32[]{:S(2)}, u32[]{:S(2)}) collective-permute-start(bf16[144,512]{1,0:T(8,128)(2,1)S(1)} %collective-permute-done.7.refs_4_), channel_id=1, source_target_pairs={{32,0},{64,32},{96,64},{128,96},{160,128},{192,160},{224,192},{0,2... | collective-permute-start | bytes 442376 | tf_op jit(solution)/shard_map/ppermute | solution.py:35
  39.7 3.9 %collective-permute-start.4 = (bf16[144,512]{1,0:T(8,128)(2,1)S(1)}, bf16[144,512]{1,0:T(8,128)(2,1)S(1)}, u32[]{:S(2)}, u32[]{:S(2)}) collective-permute-start(bf16[144,512]{1,0:T(8,128)(2,1)S(1)} %get-tuple-element.32.refs_0_), channel_id=1, source_target_pairs={{1,0},{0,1},{3,2},{2,3},{5,4},{4,5},{7,6},{6,7},{9,8},{8,9},{11,10... | collective-permute-start | bytes 442376 | tf_op jit(solution)/shard_map/ppermute | solution.py:35
  44.1 2.7 %collective-permute-start.11 = (bf16[144,512]{1,0:T(8,128)(2,1)S(1)}, bf16[144,512]{1,0:T(8,128)(2,1)}, u32[]{:S(2)}, u32[]{:S(2)}) collective-permute-start(bf16[144,512]{1,0:T(8,128)(2,1)S(1)} %collective-permute-done.9.refs_6_), channel_id=1, source_target_pairs={{32,0},{64,32},{96,64},{128,96},{160,128},{192,160},{224,192},{0,2... | collective-permute-start | bytes 442376 | tf_op jit(solution)/shard_map/ppermute | solution.py:35
  46.8 3.2 %collective-permute-start.17 = (bf16[144,512]{1,0:T(8,128)(2,1)S(1)}, bf16[144,512]{1,0:T(8,128)(2,1)}, u32[]{:S(2)}, u32[]{:S(2)}) collective-permute-start(bf16[144,512]{1,0:T(8,128)(2,1)S(1)} %collective-permute-done.14.refs_12_), channel_id=1, source_target_pairs={{1,0},{0,1},{3,2},{2,3},{5,4},{4,5},{7,6},{6,7},{9,8},{8,9},{11,10... | collective-permute-start | bytes 442376 | tf_op jit(solution)/shard_map/ppermute | solution.py:35
  50.9 0.8 collective-permute-start.16
  51.7 0.9 collective-permute-start.12
  53.1 0.9 collective-permute-done.12.refs_9_
  54.0 0.8 all-to-all-done.refs_16_
  54.8 16.4 %pair_sums.1 = (f32[8,8,128]{2,1,0:T(8,128)}, f32[16,8,128]{2,1,0:T(8,128)}) custom-call(s32[2]{0:T(128)S(1)} %pad_add_fusion.place_ref, bf16[144,512]{1,0:T(8,128)(2,1)S(1)} %get-tuple-element.32.refs_0_, bf16[144,512]{1,0:T(8,128)(2,1)S(1)} %collective-permute-done.4.refs_1_, bf16[144,512]{1,0:T(8,128)(2,1)S(1)} %collective-permute-done.5.refs_2_, ...), custom_call_target="tpu_custom_call" | custom-call | flops 4294967296 | bytes 4194304 | tf_op jit(solution)/shard_map/pair_sums/pallas_call | solution.py:246
  71.1 8.2 %all-to-all-start.1 = ((f32[8,8,128]{2,1,0:T(8,128)}), f32[8,8,128]{2,1,0:T(8,128)S(1)}, u32[]{:S(2)}, u32[]{:S(2)}) async-start(f32[8,8,128]{2,1,0:T(8,128)} %get-tuple-element.34), calls=%async_computation.1 | async-start | bytes 65536 | tf_op jit(solution)/shard_map/all_to_all | solution.py:314
  79.3 6.9 %all-to-all-done.1 = f32[8,8,128]{2,1,0:T(8,128)S(1)} async-done(((f32[8,8,128]{2,1,0:T(8,128)}), f32[8,8,128]{2,1,0:T(8,128)S(1)}, u32[]{:S(2)}, u32[]{:S(2)}) %all-to-all-start.1) | async-done | bytes 32800 | tf_op jit(solution)/shard_map/all_to_all | solution.py:314
  86.2 3.5 %all-to-all-start.2 = ((f32[16,8,128]{2,1,0:T(8,128)}), f32[16,8,128]{2,1,0:T(8,128)S(1)}, u32[]{:S(2)}, u32[]{:S(2)}) async-start(f32[16,8,128]{2,1,0:T(8,128)} %get-tuple-element.35), calls=%async_computation.2 | async-start | bytes 131072 | tf_op jit(solution)/shard_map/all_to_all | solution.py:315
  89.7 7.8 %all-gather = f32[32,128]{1,0:T(8,128)S(1)} all-gather(f32[8,128]{1,0:T(8,128)S(1)} %reduce_sum.27), channel_id=2, replica_groups=mesh['z'=8,'yh'=2,'x'=4,'yl'=2,'core'=2] {'yl','core'}, dimensions={0}, use_global_device_ids=true | all-gather | bytes 20480 | tf_op jit(solution)/shard_map/all_gather | solution.py:316
  97.6 0.5 fusion.10
  98.1 0.6 copy.18
  (50 shorter events, 3.6 us)
Async XLA Ops:
  0.6 1.0 copy-start.2
  1.6 0.9 copy-start.3
  2.5 9.3 %copy-start.4 = (s32[512,16,1]{0,2,1:T(1,128)S(1)}, s32[512,16,1]{0,2,1:T(1,128)}, u32[]{:S(2)}) copy-start(s32[512,16,1]{0,2,1:T(1,128)} %param.13) | copy-start | bytes 98308
  2.5 9.3 %copy-start.5 = (s32[128,16]{0,1:T(8,128)S(1)}, s32[128,16]{0,1:T(8,128)}, u32[]{:S(2)}) copy-start(s32[128,16]{0,1:T(8,128)} %param.15) | copy-start | bytes 24580
  2.9 6.1 %collective-permute-start = (f32[2,128,512]{2,1,0:T(8,128)S(1)}, f32[2,128,512]{2,1,0:T(8,128)S(1)}, u32[]{:S(2)}, u32[]{:S(2)}) collective-permute-start(f32[2,128,512]{2,1,0:T(8,128)S(1)} %get-tuple-element.21), channel_id=1, source_target_pairs={{1,0},{0,1},{3,2},{2,3},{5,4},{4,5},{7,6},{6,7},{9,8},{8,9},{11,10... | collective-permute-start | bytes 1572872 | tf_op jit(solution)/shard_map/ppermute | solution.py:35
  6.2 1.0 copy-start
  7.2 1.0 copy-start.1
  8.9 2.0 %collective-permute-start.2 = (f32[2,128,512]{2,1,0:T(8,128)S(1)}, f32[2,128,512]{2,1,0:T(8,128)S(1)}, u32[]{:S(2)}, u32[]{:S(2)}) collective-permute-start(f32[2,128,512]{2,1,0:T(8,128)S(1)} %get-tuple-element.25), channel_id=1, source_target_pairs={{1,0},{0,1},{3,2},{2,3},{5,4},{4,5},{7,6},{6,7},{9,8},{8,9},{11,10... | collective-permute-start | bytes 1572872 | tf_op jit(solution)/shard_map/ppermute | solution.py:35
  9.1 4.7 %collective-permute-start.1 = (bf16[128,512]{1,0:T(8,128)(2,1)S(1)}, bf16[128,512]{1,0:T(8,128)(2,1)S(1)}, u32[]{:S(2)}, u32[]{:S(2)}) collective-permute-start(bf16[128,512]{1,0:T(8,128)(2,1)S(1)} %get-tuple-element.23), channel_id=1, source_target_pairs={{2,0},{0,2},{3,1},{1,3},{6,4},{4,6},{7,5},{5,7},{10,8},{8,10},{11,... | collective-permute-start | bytes 393224 | tf_op jit(solution)/shard_map/ppermute | solution.py:35
  10.9 5.6 %collective-permute-start.3 = (bf16[128,512]{1,0:T(8,128)(2,1)S(1)}, bf16[128,512]{1,0:T(8,128)(2,1)S(1)}, u32[]{:S(2)}, u32[]{:S(2)}) collective-permute-start(bf16[128,512]{1,0:T(8,128)(2,1)S(1)} %get-tuple-element.27), channel_id=1, source_target_pairs={{2,0},{0,2},{3,1},{1,3},{6,4},{4,6},{7,5},{5,7},{10,8},{8,10},{11,... | collective-permute-start | bytes 393224 | tf_op jit(solution)/shard_map/ppermute | solution.py:35
  18.4 36.4 %all-to-all-start = ((bf16[16,528,128]{2,1,0:T(8,128)(2,1)}), bf16[16,528,128]{2,1,0:T(8,128)(2,1)S(1)}, u32[]{:S(2)}, u32[]{:S(2)}) async-start(bf16[16,528,128]{2,1,0:T(8,128)(2,1)} %get-tuple-element.33), calls=%async_computation | async-start | bytes 4325376 | tf_op jit(solution)/shard_map/all_to_all | solution.py:310
  23.4 7.8 %collective-permute-start.5 = (bf16[144,512]{1,0:T(8,128)(2,1)S(1)}, bf16[144,512]{1,0:T(8,128)(2,1)S(1)}, u32[]{:S(2)}, u32[]{:S(2)}) collective-permute-start(bf16[144,512]{1,0:T(8,128)(2,1)S(1)} %get-tuple-element.32.refs_0_), channel_id=1, source_target_pairs={{32,0},{64,32},{96,64},{128,96},{160,128},{192,160},{224,192},{0,2... | collective-permute-start | bytes 442376 | tf_op jit(solution)/shard_map/ppermute | solution.py:35
  29.0 5.5 %collective-permute-start.13 = (bf16[144,512]{1,0:T(8,128)(2,1)S(1)}, bf16[144,512]{1,0:T(8,128)(2,1)S(1)}, u32[]{:S(2)}, u32[]{:S(2)}) collective-permute-start(bf16[144,512]{1,0:T(8,128)(2,1)S(1)} %get-tuple-element.32.refs_0_), channel_id=1, source_target_pairs={{224,0},{0,32},{32,64},{64,96},{96,128},{128,160},{160,192},{192,2... | collective-permute-start | bytes 442376 | tf_op jit(solution)/shard_map/ppermute | solution.py:35
  31.1 5.2 %collective-permute-start.7 = (bf16[144,512]{1,0:T(8,128)(2,1)S(1)}, bf16[144,512]{1,0:T(8,128)(2,1)S(1)}, u32[]{:S(2)}, u32[]{:S(2)}) collective-permute-start(bf16[144,512]{1,0:T(8,128)(2,1)S(1)} %collective-permute-done.5.refs_2_), channel_id=1, source_target_pairs={{32,0},{64,32},{96,64},{128,96},{160,128},{192,160},{224,192},{0,2... | collective-permute-start | bytes 442376 | tf_op jit(solution)/shard_map/ppermute | solution.py:35
  34.5 9.6 %collective-permute-start.14 = (bf16[144,512]{1,0:T(8,128)(2,1)S(1)}, bf16[144,512]{1,0:T(8,128)(2,1)S(1)}, u32[]{:S(2)}, u32[]{:S(2)}) collective-permute-start(bf16[144,512]{1,0:T(8,128)(2,1)S(1)} %collective-permute-done.13.refs_14_), channel_id=1, source_target_pairs={{224,0},{0,32},{32,64},{64,96},{96,128},{128,160},{160,192},{192,2... | collective-permute-start | bytes 442376 | tf_op jit(solution)/shard_map/ppermute | solution.py:35
  36.3 7.8 %collective-permute-start.9 = (bf16[144,512]{1,0:T(8,128)(2,1)S(1)}, bf16[144,512]{1,0:T(8,128)(2,1)S(1)}, u32[]{:S(2)}, u32[]{:S(2)}) collective-permute-start(bf16[144,512]{1,0:T(8,128)(2,1)S(1)} %collective-permute-done.7.refs_4_), channel_id=1, source_target_pairs={{32,0},{64,32},{96,64},{128,96},{160,128},{192,160},{224,192},{0,2... | collective-permute-start | bytes 442376 | tf_op jit(solution)/shard_map/ppermute | solution.py:35
  39.7 7.1 %collective-permute-start.4 = (bf16[144,512]{1,0:T(8,128)(2,1)S(1)}, bf16[144,512]{1,0:T(8,128)(2,1)S(1)}, u32[]{:S(2)}, u32[]{:S(2)}) collective-permute-start(bf16[144,512]{1,0:T(8,128)(2,1)S(1)} %get-tuple-element.32.refs_0_), channel_id=1, source_target_pairs={{1,0},{0,1},{3,2},{2,3},{5,4},{4,5},{7,6},{6,7},{9,8},{8,9},{11,10... | collective-permute-start | bytes 442376 | tf_op jit(solution)/shard_map/ppermute | solution.py:35
  43.6 6.4 %collective-permute-start.18 = (bf16[144,512]{1,0:T(8,128)(2,1)S(1)}, bf16[144,512]{1,0:T(8,128)(2,1)S(1)}, u32[]{:S(2)}, u32[]{:S(2)}) collective-permute-start(bf16[144,512]{1,0:T(8,128)(2,1)S(1)} %collective-permute-done.13.refs_14_), channel_id=1, source_target_pairs={{1,0},{0,1},{3,2},{2,3},{5,4},{4,5},{7,6},{6,7},{9,8},{8,9},{11,10... | collective-permute-start | bytes 442376 | tf_op jit(solution)/shard_map/ppermute | solution.py:35
  43.6 6.5 %collective-permute-start.6 = (bf16[144,512]{1,0:T(8,128)(2,1)S(1)}, bf16[144,512]{1,0:T(8,128)(2,1)S(1)}, u32[]{:S(2)}, u32[]{:S(2)}) collective-permute-start(bf16[144,512]{1,0:T(8,128)(2,1)S(1)} %collective-permute-done.5.refs_2_), channel_id=1, source_target_pairs={{1,0},{0,1},{3,2},{2,3},{5,4},{4,5},{7,6},{6,7},{9,8},{8,9},{11,10... | collective-permute-start | bytes 442376 | tf_op jit(solution)/shard_map/ppermute | solution.py:35
  44.1 6.8 %collective-permute-start.15 = (bf16[144,512]{1,0:T(8,128)(2,1)S(1)}, bf16[144,512]{1,0:T(8,128)(2,1)}, u32[]{:S(2)}, u32[]{:S(2)}) collective-permute-start(bf16[144,512]{1,0:T(8,128)(2,1)S(1)} %collective-permute-done.14.refs_12_), channel_id=1, source_target_pairs={{224,0},{0,32},{32,64},{64,96},{96,128},{128,160},{160,192},{192,2... | collective-permute-start | bytes 442376 | tf_op jit(solution)/shard_map/ppermute | solution.py:35
  44.1 7.6 %collective-permute-start.11 = (bf16[144,512]{1,0:T(8,128)(2,1)S(1)}, bf16[144,512]{1,0:T(8,128)(2,1)}, u32[]{:S(2)}, u32[]{:S(2)}) collective-permute-start(bf16[144,512]{1,0:T(8,128)(2,1)S(1)} %collective-permute-done.9.refs_6_), channel_id=1, source_target_pairs={{32,0},{64,32},{96,64},{128,96},{160,128},{192,160},{224,192},{0,2... | collective-permute-start | bytes 442376 | tf_op jit(solution)/shard_map/ppermute | solution.py:35
  46.8 5.9 %collective-permute-start.17 = (bf16[144,512]{1,0:T(8,128)(2,1)S(1)}, bf16[144,512]{1,0:T(8,128)(2,1)}, u32[]{:S(2)}, u32[]{:S(2)}) collective-permute-start(bf16[144,512]{1,0:T(8,128)(2,1)S(1)} %collective-permute-done.14.refs_12_), channel_id=1, source_target_pairs={{1,0},{0,1},{3,2},{2,3},{5,4},{4,5},{7,6},{6,7},{9,8},{8,9},{11,10... | collective-permute-start | bytes 442376 | tf_op jit(solution)/shard_map/ppermute | solution.py:35
  50.0 2.8 %collective-permute-start.8 = (bf16[144,512]{1,0:T(8,128)(2,1)S(1)}, bf16[144,512]{1,0:T(8,128)(2,1)}, u32[]{:S(2)}, u32[]{:S(2)}) collective-permute-start(bf16[144,512]{1,0:T(8,128)(2,1)S(1)} %collective-permute-done.7.refs_4_), channel_id=1, source_target_pairs={{1,0},{0,1},{3,2},{2,3},{5,4},{4,5},{7,6},{6,7},{9,8},{8,9},{11,10... | collective-permute-start | bytes 442376 | tf_op jit(solution)/shard_map/ppermute | solution.py:35
  50.1 3.0 %collective-permute-start.10 = (bf16[144,512]{1,0:T(8,128)(2,1)S(1)}, bf16[144,512]{1,0:T(8,128)(2,1)}, u32[]{:S(2)}, u32[]{:S(2)}) collective-permute-start(bf16[144,512]{1,0:T(8,128)(2,1)S(1)} %collective-permute-done.9.refs_6_), channel_id=1, source_target_pairs={{1,0},{0,1},{3,2},{2,3},{5,4},{4,5},{7,6},{6,7},{9,8},{8,9},{11,10... | collective-permute-start | bytes 442376 | tf_op jit(solution)/shard_map/ppermute | solution.py:35
  50.9 2.1 %collective-permute-start.16 = (bf16[144,512]{1,0:T(8,128)(2,1)}, bf16[144,512]{1,0:T(8,128)(2,1)}, u32[]{:S(2)}, u32[]{:S(2)}) collective-permute-start(bf16[144,512]{1,0:T(8,128)(2,1)} %collective-permute-done.15.refs_10_), channel_id=1, source_target_pairs={{1,0},{0,1},{3,2},{2,3},{5,4},{4,5},{7,6},{6,7},{9,8},{8,9},{11,10... | collective-permute-start | bytes 442376 | tf_op jit(solution)/shard_map/ppermute | solution.py:35
  51.7 2.3 %collective-permute-start.12 = (bf16[144,512]{1,0:T(8,128)(2,1)}, bf16[144,512]{1,0:T(8,128)(2,1)}, u32[]{:S(2)}, u32[]{:S(2)}) collective-permute-start(bf16[144,512]{1,0:T(8,128)(2,1)} %collective-permute-done.11.refs_8_), channel_id=1, source_target_pairs={{1,0},{0,1},{3,2},{2,3},{5,4},{4,5},{7,6},{6,7},{9,8},{8,9},{11,10... | collective-permute-start | bytes 442376 | tf_op jit(solution)/shard_map/ppermute | solution.py:35
  71.1 15.1 %all-to-all-start.1 = ((f32[8,8,128]{2,1,0:T(8,128)}), f32[8,8,128]{2,1,0:T(8,128)S(1)}, u32[]{:S(2)}, u32[]{:S(2)}) async-start(f32[8,8,128]{2,1,0:T(8,128)} %get-tuple-element.34), calls=%async_computation.1 | async-start | bytes 65536 | tf_op jit(solution)/shard_map/all_to_all | solution.py:314
  86.2 12.5 %all-to-all-start.2 = ((f32[16,8,128]{2,1,0:T(8,128)}), f32[16,8,128]{2,1,0:T(8,128)S(1)}, u32[]{:S(2)}, u32[]{:S(2)}) async-start(f32[16,8,128]{2,1,0:T(8,128)} %get-tuple-element.35), calls=%async_computation.2 | async-start | bytes 131072 | tf_op jit(solution)/shard_map/all_to_all | solution.py:315

commit v8 on v7

--- a/solution.py
+++ b/solution.py
@@ -91,23 +91,13 @@
     )(yl, keep, got)
 
 
-def lanes_summed(values):
-    return lax.dot_general(
-        jnp.ones((8, values.shape[1]), jnp.float32),
-        values,
-        (((1,), (1,)), ((), ())),
-        precision=lax.Precision.HIGHEST,
-        preferred_element_type=jnp.float32,
-    )
-
-
 def normalized(keep2_ref, got2_ref):
     raw = keep2_ref[...] + got2_ref[...].astype(jnp.float32)
     total = jnp.sum(raw * raw, axis=1, keepdims=True)
     return (raw * lax.rsqrt(total + EPSILON)).astype(jnp.bfloat16)
 
 
-def finish_kernel(keep2_s, got2_s, keep2_q, got2_q, struct_ext_ref, seq_ext_ref, peers_ref, seq_ref, self_ref):
+def finish_kernel(keep2_s, got2_s, keep2_q, got2_q, struct_ext_ref, seq_ext_ref, peers_ref, seq_ref):
     struct = normalized(keep2_s, got2_s)
     turned = struct.astype(jnp.float32).T.astype(jnp.bfloat16)
     struct_ext = struct_ext_ref[...]
@@ -117,7 +107,6 @@
     seq = normalized(keep2_q, got2_q)
     seq_ref[0:SHARE, :] = seq
     seq_ref[SHARE:, :] = seq_ext_ref[...]
-    self_ref[...] = lanes_summed(seq.astype(jnp.float32) * struct.astype(jnp.float32))
 
 
 def finish(*held):
@@ -126,10 +115,9 @@
         out_shape=(
             jax.ShapeDtypeStruct((SIDE, WIDTH + EXT, SHARE), jnp.bfloat16),
             jax.ShapeDtypeStruct((SHARE + EXT, WIDTH), jnp.bfloat16),
-            jax.ShapeDtypeStruct((8, SHARE), jnp.float32),
         ),
         in_specs=[VMEM] * 6,
-        out_specs=(VMEM,) * 3,
+        out_specs=(VMEM,) * 2,
         compiler_params=pltpu.CompilerParams(vmem_limit_bytes=12 * 1024 * 1024),
         name="finish",
     )(*held)
@@ -140,8 +128,8 @@
 
 
 def pair_kernel(place_ref, *refs):
-    seq_refs, s, rows_ref, cols_ref = refs[0:SIDE], refs[SIDE], refs[SIDE + 1], refs[SIDE + 2]
-    q, info, buf0, buf1, lab8, ct, cm, rt, rm, ex = refs[SIDE + 3 :]
+    seq_refs, s, rows_ref, cols_ref, self_ref = refs[0:SIDE], refs[SIDE], refs[SIDE + 1], refs[SIDE + 2], refs[SIDE + 3]
+    q, info, buf0, buf1, lab8, ct, cm, held0, held1, row_sums, chosen = refs[SIDE + 4 :]
     my_z, my_core = place_ref[0], place_ref[1]
     my_block = my_z * 2 + my_core
 
@@ -160,6 +148,10 @@
     ct[...] = jnp.zeros_like(ct)
     cm[...] = jnp.zeros_like(cm)
     row_of = lax.broadcasted_iota(jnp.int32, (8, SHARE), 0)
+    held1[...] = jnp.zeros_like(held1)
+    lane_of = lax.broadcasted_iota(jnp.int32, (3 * SHARE, 128), 1)
+    for which in range(3):
+        chosen[which * 3 * SHARE : (which + 1) * 3 * SHARE, :] = jnp.where(lane_of == which, 1.0, 0.0).astype(jnp.bfloat16)
 
     zero = jnp.zeros((8, 128), jnp.float32)
     groups = range(SUB // 8)
@@ -171,8 +163,21 @@
             q[rows, :], cols, preferred_element_type=jnp.float32
         )
 
-    def work(tile, products, next_tile, target):
+    def gather_sums(slot, held):
+        parts = []
+        for which in range(3):
+            rest = held[which]
+            for _ in range(3):
+                part = rest.astype(jnp.bfloat16)
+                parts.append(part)
+                rest = rest - part.astype(jnp.float32)
+        summed = jnp.dot(jnp.concatenate(parts, axis=1), chosen[...], preferred_element_type=jnp.float32)
+        row_sums[slot] = summed.T[0:8, :]
+
+    def work(tile, products, next_tile, target, held, last_slot, last_held):
         for sub in range(SHARE // SUB):
+            if sub == 1:
+                gather_sums(last_slot, last_held)
             here = [pl.ds(pl.multiple_of(tile * SHARE + sub * SUB + group * 8, 8), 8) for group in groups]
             code = [info[rows, :] for rows in here]
             label = [jnp.broadcast_to(-1 - each[:, SLOTS : SLOTS + 1], (8, 128)) for each in code]
@@ -206,34 +211,35 @@
                 ct[:, at] = col_total
                 cm[:, at] = col_matched
             for group in groups:
-                rt[here[group], :] = row_total[group]
-                rm[here[group], :] = row_matched[group]
+                local = slice(sub * SUB + group * 8, sub * SUB + group * 8 + 8)
+                held[0, local, :] = row_total[group]
+                held[1, local, :] = row_matched[group]
                 odd = (picked[group] << 16) >> 16
                 fixed = jnp.where((code[group] & 128) > 0, odd, (picked[group] - odd) >> 16).astype(jnp.float32)
                 fixed = fixed + jnp.where(fixed > 0, 0.5, jnp.where(fixed < 0, -0.5, 0.0))
                 hard = jnp.exp(fixed * (LOGIT_SCALE / FIXED))
-                ex[here[group], :] = jnp.where(code[group] >= 0, hard, 0.0)
+                held[2, local, :] = jnp.where(code[group] >= 0, hard, 0.0)
 
     for pair in range(SIDE // 2):
         piece(0, buf0, pair)
 
     def body(step, carry):
-        work(2 * step, buf0, 2 * step + 1, buf1)
-        work(2 * step + 1, buf1, jnp.minimum(2 * step + 2, SIDE - 1), buf0)
+        work(2 * step, buf0, 2 * step + 1, buf1, held0, jnp.where(step == 0, SIDE, 2 * step - 1), held1)
+        work(2 * step + 1, buf1, jnp.minimum(2 * step + 2, SIDE - 1), buf0, held1, 2 * step, held0)
         return carry
 
     lax.fori_loop(0, SIDE // 2, body, 0)
-    for part in range(4):
-        at = slice(part * 4 * SHARE, (part + 1) * 4 * SHARE)
-        sums = [lanes_summed(each[at, :]) for each in (rt, rm, ex)]
-        for inner in range(4):
-            block = part * 4 + inner
-            at = slice(inner * SHARE, (inner + 1) * SHARE)
-            z, first = (my_z + block // 2) & 7, (my_core ^ (block % 2)) * 3
-            out = jnp.zeros((8, SHARE), jnp.float32) if block % 2 == 0 else rows_ref[z]
+    gather_sums(SIDE - 1, held1)
+    for far in range(8):
+        out = jnp.zeros((8, SHARE), jnp.float32)
+        for mate in range(2):
+            first = (my_core ^ mate) * 3
             for which in range(3):
-                out = jnp.where(row_of == first + which, sums[which][:, at], out)
-            rows_ref[z] = out
+                out = jnp.where(row_of == first + which, row_sums[far * 2 + mate][which : which + 1], out)
+        rows_ref[(my_z + far) & 7] = out
+    own = jnp.dot(q[0:SHARE, :], s[place_ref[2], 0:WIDTH, :], preferred_element_type=jnp.float32)
+    diagonal = lax.broadcasted_iota(jnp.int32, own.shape, 0) == lax.broadcasted_iota(jnp.int32, own.shape, 1)
+    self_ref[...] = jnp.broadcast_to(jnp.sum(jnp.where(diagonal, own, 0.0), axis=0, keepdims=True), (8, SHARE))
 
     for chunk in range(SIDE):
         at = slice(chunk * 128, (chunk + 1) * 128)
@@ -248,9 +254,10 @@
         out_shape=(
             jax.ShapeDtypeStruct((8, 8, SHARE), jnp.float32),
             jax.ShapeDtypeStruct((SIDE, 8, SHARE), jnp.float32),
+            jax.ShapeDtypeStruct((8, SHARE), jnp.float32),
         ),
         in_specs=[SMEM] + [VMEM] * (SIDE + 1),
-        out_specs=(VMEM, VMEM),
+        out_specs=(VMEM, VMEM, VMEM),
         scratch_shapes=[
             pltpu.VMEM((EDGE, WIDTH), jnp.bfloat16),
             pltpu.VMEM((EDGE, 128), jnp.int32),
@@ -259,9 +266,10 @@
             pltpu.VMEM((8, EDGE), jnp.int32),
             pltpu.VMEM((8, EDGE), jnp.float32),
             pltpu.VMEM((8, EDGE), jnp.float32),
-            pltpu.VMEM((EDGE, 128), jnp.float32),
-            pltpu.VMEM((EDGE, 128), jnp.float32),
-            pltpu.VMEM((EDGE, 128), jnp.float32),
+            pltpu.VMEM((3, SHARE, 128), jnp.float32),
+            pltpu.VMEM((3, SHARE, 128), jnp.float32),
+            pltpu.VMEM((SIDE + 1, 8, SHARE), jnp.float32),
+            pltpu.VMEM((9 * SHARE, 128), jnp.bfloat16),
         ],
         compiler_params=pltpu.CompilerParams(vmem_limit_bytes=28 * 1024 * 1024),
         cost_estimate=pl.CostEstimate(
@@ -306,11 +314,11 @@
     seq_ext = jnp.concatenate([high, low, wide(labels >> 7), wide(labels & 127)], axis=1).astype(jnp.bfloat16)
     struct_ext = jnp.concatenate([wide(labels >> 7)[0:8], wide(labels & 127)[0:8]], axis=0).astype(jnp.bfloat16)
 
-    struct_peers, seq_block, self_dot = finish(keep2_s, got2_s, keep2_q, got2_q, struct_ext, seq_ext)
+    struct_peers, seq_block = finish(keep2_s, got2_s, keep2_q, got2_q, struct_ext, seq_ext)
     struct_blocks = lax.all_to_all(struct_peers, COL_AXES, split_axis=0, concat_axis=0, tiled=True)
     seq_blocks = [each for held in over_z(seq_block) for each in (held, shifted(held, "core", 1))]
 
-    rows, cols = pair_sums(jnp.stack([place("z"), core]), seq_blocks, struct_blocks)
+    rows, cols, self_dot = pair_sums(jnp.stack([place("z"), core, place(COL_AXES)]), seq_blocks, struct_blocks)
     rows = jnp.sum(lax.all_to_all(rows, "z", split_axis=0, concat_axis=0, tiled=True), axis=0)
     cols = jnp.sum(lax.all_to_all(cols, COL_AXES, split_axis=0, concat_axis=0, tiled=True), axis=0)
     rows = lax.all_gather(rows, MP_AXES, axis=0, tiled=False).reshape(2, 2, 8, SHARE)

time: 99.8 us -> 98.6 us (0.988)
  Pallas kernels: 19.3 us -> 16.8 us
  local copies, waits for them, and re-layouts: 4.46 us -> 5.81 us
    pallas_call x1, Pallas kernels: 1.79 us -> 0.31 us  [finish(): pl.pallas_call(finish_kernel, out_shape=(jax.ShapeDtypeStruct((SIDE, WIDT...]
    unnamed x12 -> x14, local copies, waits for them, and re-layouts: 3.84 us -> 5.2 us
where the time goes in v8:
time: 98.6 us; the launch traced here: 98.1 us
  starting transfers between devices  44.9 us (46%)
  waiting for transfers between devices  19.2 us (19%)
  Pallas kernels  16.8 us (17%)
  blocking collectives  7.82 us (8%)
  local copies, waits for them, and re-layouts  5.81 us (6%)
  other arithmetic  2.68 us (3%)
    ppermute x19, starting transfers between devices, shifted(): lax.ppermute(value, axes, [((place + steps) % count, place) for place in...  28.2 us
    pallas_call x1, Pallas kernels, pair_sums(): pl.pallas_call(pair_kernel, out_shape=(jax.ShapeDtypeStruct((8, 8, SHARE)...  15.4 us
    ppermute x19, waiting for transfers between devices, shifted(): lax.ppermute(value, axes, [((place + steps) % count, place) for place in...  11.6 us
    all_to_all x1, starting transfers between devices, per_device(): lax.all_to_all(rows, 'z', split_axis=0, concat_axis=0, tiled=True)  8.19 us
    all_gather x1, blocking collectives, per_device(): lax.all_gather(rows, MP_AXES, axis=0, tiled=False).reshape(2, 2, 8, SHARE)  7.82 us
    all_to_all x1, waiting for transfers between devices, per_device(): lax.all_to_all(rows, 'z', split_axis=0, concat_axis=0, tiled=True)  6.88 us
    unnamed x14, local copies, waits for them, and re-layouts  5.2 us
    all_to_all x1, starting transfers between devices, per_device(): lax.all_to_all(struct_peers, COL_AXES, split_axis=0, concat_axis=0, tiled...  5.01 us
  transfers between devices with their start and end apart: 22, of which 11 were waited for; matrix products, arithmetic and copies ran while one was open for 3% of the time, Pallas kernels for 1%

profile of v8, /device:TPU:1, one launch (start us, length us, event | category | flops | bytes accessed | tf_op | source)
XLA Modules:
  0.0 98.1 jit_solution(9106744910185599751)
XLA Ops:
  0.6 0.9 copy-done.3
  1.6 0.9 copy-done.4
  2.9 3.3 %collective-permute-start = (f32[2,128,512]{2,1,0:T(8,128)S(1)}, f32[2,128,512]{2,1,0:T(8,128)S(1)}, u32[]{:S(2)}, u32[]{:S(2)}) collective-permute-start(f32[2,128,512]{2,1,0:T(8,128)S(1)} %get-tuple-element.21), channel_id=1, source_target_pairs={{1,0},{0,1},{3,2},{2,3},{5,4},{4,5},{7,6},{6,7},{9,8},{8,9},{11,10... | collective-permute-start | bytes 1572872 | tf_op jit(solution)/shard_map/ppermute | solution.py:35
  6.2 1.0 copy-done.1
  7.2 1.0 copy-done.2
  8.2 0.7 project_seq.1
  9.2 1.7 %collective-permute-done.2.got_ref = f32[2,128,512]{2,1,0:T(8,128)S(1)} collective-permute-done((f32[2,128,512]{2,1,0:T(8,128)S(1)}, f32[2,128,512]{2,1,0:T(8,128)S(1)}, u32[]{:S(2)}, u32[]{:S(2)}) %collective-permute-start.2) | collective-permute-done | bytes 524320 | tf_op jit(solution)/shard_map/ppermute | solution.py:35
  11.0 0.8 shift-right-arithmetic_convert_fusion
  11.9 0.7 fusion.5
  12.6 1.1 %collective-permute-done.1.got2_s = bf16[128,512]{1,0:T(8,128)(2,1)S(1)} collective-permute-done((bf16[128,512]{1,0:T(8,128)(2,1)S(1)}, bf16[128,512]{1,0:T(8,128)(2,1)S(1)}, u32[]{:S(2)}, u32[]{:S(2)}) %collective-permute-start.1) | collective-permute-done | bytes 131104 | tf_op jit(solution)/shard_map/ppermute | solution.py:35
  13.8 2.8 %collective-permute-done.3.got2_q = bf16[128,512]{1,0:T(8,128)(2,1)S(1)} collective-permute-done((bf16[128,512]{1,0:T(8,128)(2,1)S(1)}, bf16[128,512]{1,0:T(8,128)(2,1)S(1)}, u32[]{:S(2)}, u32[]{:S(2)}) %collective-permute-start.3) | collective-permute-done | bytes 131104 | tf_op jit(solution)/shard_map/ppermute | solution.py:35
  16.9 1.4 %copy-done = bf16[16,528,128]{2,1,0:T(8,128)(2,1)} copy-done((bf16[16,528,128]{2,1,0:T(8,128)(2,1)}, bf16[16,528,128]{2,1,0:T(8,128)(2,1)S(1)}, u32[]{:S(2)}) %copy-start) | copy-done | bytes 2162712
  18.2 5.0 %all-to-all-start = ((bf16[16,528,128]{2,1,0:T(8,128)(2,1)}), bf16[16,528,128]{2,1,0:T(8,128)(2,1)S(1)}, u32[]{:S(2)}, u32[]{:S(2)}) async-start(bf16[16,528,128]{2,1,0:T(8,128)(2,1)} %copy-done), calls=%async_computation | async-start | bytes 4325376 | tf_op jit(solution)/shard_map/all_to_all | solution.py:318
  23.3 5.7 %collective-permute-start.5 = (bf16[144,512]{1,0:T(8,128)(2,1)S(1)}, bf16[144,512]{1,0:T(8,128)(2,1)S(1)}, u32[]{:S(2)}, u32[]{:S(2)}) collective-permute-start(bf16[144,512]{1,0:T(8,128)(2,1)S(1)} %get-tuple-element.32.refs_0_), channel_id=1, source_target_pairs={{32,0},{64,32},{96,64},{128,96},{160,128},{192,160},{224,192},{0,2... | collective-permute-start | bytes 442376 | tf_op jit(solution)/shard_map/ppermute | solution.py:35
  28.9 2.1 %collective-permute-done.5.refs_2_ = bf16[144,512]{1,0:T(8,128)(2,1)S(1)} collective-permute-done((bf16[144,512]{1,0:T(8,128)(2,1)S(1)}, bf16[144,512]{1,0:T(8,128)(2,1)S(1)}, u32[]{:S(2)}, u32[]{:S(2)}) %collective-permute-start.5) | collective-permute-done | bytes 147488 | tf_op jit(solution)/shard_map/ppermute | solution.py:35
  31.0 3.1 %collective-permute-start.7 = (bf16[144,512]{1,0:T(8,128)(2,1)S(1)}, bf16[144,512]{1,0:T(8,128)(2,1)S(1)}, u32[]{:S(2)}, u32[]{:S(2)}) collective-permute-start(bf16[144,512]{1,0:T(8,128)(2,1)S(1)} %collective-permute-done.5.refs_2_), channel_id=1, source_target_pairs={{32,0},{64,32},{96,64},{128,96},{160,128},{192,160},{224,192},{0,2... | collective-permute-start | bytes 442376 | tf_op jit(solution)/shard_map/ppermute | solution.py:35
  34.4 1.8 %collective-permute-done.7.refs_4_ = bf16[144,512]{1,0:T(8,128)(2,1)S(1)} collective-permute-done((bf16[144,512]{1,0:T(8,128)(2,1)S(1)}, bf16[144,512]{1,0:T(8,128)(2,1)S(1)}, u32[]{:S(2)}, u32[]{:S(2)}) %collective-permute-start.7) | collective-permute-done | bytes 147488 | tf_op jit(solution)/shard_map/ppermute | solution.py:35
  36.2 3.4 %collective-permute-start.9 = (bf16[144,512]{1,0:T(8,128)(2,1)S(1)}, bf16[144,512]{1,0:T(8,128)(2,1)S(1)}, u32[]{:S(2)}, u32[]{:S(2)}) collective-permute-start(bf16[144,512]{1,0:T(8,128)(2,1)S(1)} %collective-permute-done.7.refs_4_), channel_id=1, source_target_pairs={{32,0},{64,32},{96,64},{128,96},{160,128},{192,160},{224,192},{0,2... | collective-permute-start | bytes 442376 | tf_op jit(solution)/shard_map/ppermute | solution.py:35
  39.6 3.9 %collective-permute-start.4 = (bf16[144,512]{1,0:T(8,128)(2,1)S(1)}, bf16[144,512]{1,0:T(8,128)(2,1)S(1)}, u32[]{:S(2)}, u32[]{:S(2)}) collective-permute-start(bf16[144,512]{1,0:T(8,128)(2,1)S(1)} %get-tuple-element.32.refs_0_), channel_id=1, source_target_pairs={{1,0},{0,1},{3,2},{2,3},{5,4},{4,5},{7,6},{6,7},{9,8},{8,9},{11,10... | collective-permute-start | bytes 442376 | tf_op jit(solution)/shard_map/ppermute | solution.py:35
  44.0 2.7 %collective-permute-start.11 = (bf16[144,512]{1,0:T(8,128)(2,1)S(1)}, bf16[144,512]{1,0:T(8,128)(2,1)}, u32[]{:S(2)}, u32[]{:S(2)}) collective-permute-start(bf16[144,512]{1,0:T(8,128)(2,1)S(1)} %collective-permute-done.9.refs_6_), channel_id=1, source_target_pairs={{32,0},{64,32},{96,64},{128,96},{160,128},{192,160},{224,192},{0,2... | collective-permute-start | bytes 442376 | tf_op jit(solution)/shard_map/ppermute | solution.py:35
  46.7 3.2 %collective-permute-start.17 = (bf16[144,512]{1,0:T(8,128)(2,1)S(1)}, bf16[144,512]{1,0:T(8,128)(2,1)}, u32[]{:S(2)}, u32[]{:S(2)}) collective-permute-start(bf16[144,512]{1,0:T(8,128)(2,1)S(1)} %collective-permute-done.14.refs_12_), channel_id=1, source_target_pairs={{1,0},{0,1},{3,2},{2,3},{5,4},{4,5},{7,6},{6,7},{9,8},{8,9},{11,10... | collective-permute-start | bytes 442376 | tf_op jit(solution)/shard_map/ppermute | solution.py:35
  50.8 0.8 collective-permute-start.16
  51.6 0.9 collective-permute-start.12
  52.9 0.9 collective-permute-done.12.refs_9_
  53.9 0.8 all-to-all-done.refs_16_
  54.7 15.4 %pair_sums.1 = (f32[8,8,128]{2,1,0:T(8,128)}, f32[16,8,128]{2,1,0:T(8,128)}, f32[8,128]{1,0:T(8,128)S(1)}) custom-call(s32[3]{0:T(128)S(1)} %pad_add_fusion.place_ref, bf16[144,512]{1,0:T(8,128)(2,1)S(1)} %get-tuple-element.32.refs_0_, bf16[144,512]{1,0:T(8,128)(2,1)S(1)} %collective-permute-done.4.refs_1_, ...), custom_call_target="tpu_custom_call" | custom-call | flops 4294967296 | bytes 4194304 | tf_op jit(solution)/shard_map/pair_sums/pallas_call | solution.py:252
  70.0 8.2 %all-to-all-start.1 = ((f32[8,8,128]{2,1,0:T(8,128)}), f32[8,8,128]{2,1,0:T(8,128)S(1)}, u32[]{:S(2)}, u32[]{:S(2)}) async-start(f32[8,8,128]{2,1,0:T(8,128)} %get-tuple-element.34), calls=%async_computation.1 | async-start | bytes 65536 | tf_op jit(solution)/shard_map/all_to_all | solution.py:322
  78.2 6.9 %all-to-all-done.1 = f32[8,8,128]{2,1,0:T(8,128)S(1)} async-done(((f32[8,8,128]{2,1,0:T(8,128)}), f32[8,8,128]{2,1,0:T(8,128)S(1)}, u32[]{:S(2)}, u32[]{:S(2)}) %all-to-all-start.1) | async-done | bytes 32800 | tf_op jit(solution)/shard_map/all_to_all | solution.py:322
  85.1 3.5 %all-to-all-start.2 = ((f32[16,8,128]{2,1,0:T(8,128)}), f32[16,8,128]{2,1,0:T(8,128)S(1)}, u32[]{:S(2)}, u32[]{:S(2)}) async-start(f32[16,8,128]{2,1,0:T(8,128)} %get-tuple-element.35), calls=%async_computation.2 | async-start | bytes 131072 | tf_op jit(solution)/shard_map/all_to_all | solution.py:323
  88.6 7.8 %all-gather = f32[32,128]{1,0:T(8,128)S(1)} all-gather(f32[8,128]{1,0:T(8,128)S(1)} %reduce_sum.27), channel_id=2, replica_groups=mesh['z'=8,'yh'=2,'x'=4,'yl'=2,'core'=2] {'yl','core'}, dimensions={0}, use_global_device_ids=true | all-gather | bytes 20480 | tf_op jit(solution)/shard_map/all_gather | solution.py:324
  96.5 0.5 fusion.10
  97.0 0.6 copy.18
  (52 shorter events, 3.9 us)
Async XLA Ops:
  0.6 1.0 copy-start.3
  1.6 0.9 copy-start.4
  2.5 9.3 %copy-start.5 = (s32[512,16,1]{0,2,1:T(1,128)S(1)}, s32[512,16,1]{0,2,1:T(1,128)}, u32[]{:S(2)}) copy-start(s32[512,16,1]{0,2,1:T(1,128)} %param.13) | copy-start | bytes 98308
  2.5 9.3 %copy-start.6 = (s32[128,16]{0,1:T(8,128)S(1)}, s32[128,16]{0,1:T(8,128)}, u32[]{:S(2)}) copy-start(s32[128,16]{0,1:T(8,128)} %param.15) | copy-start | bytes 24580
  2.9 6.1 %collective-permute-start = (f32[2,128,512]{2,1,0:T(8,128)S(1)}, f32[2,128,512]{2,1,0:T(8,128)S(1)}, u32[]{:S(2)}, u32[]{:S(2)}) collective-permute-start(f32[2,128,512]{2,1,0:T(8,128)S(1)} %get-tuple-element.21), channel_id=1, source_target_pairs={{1,0},{0,1},{3,2},{2,3},{5,4},{4,5},{7,6},{6,7},{9,8},{8,9},{11,10... | collective-permute-start | bytes 1572872 | tf_op jit(solution)/shard_map/ppermute | solution.py:35
  6.2 1.0 copy-start.1
  7.2 1.0 copy-start.2
  8.9 2.0 %collective-permute-start.2 = (f32[2,128,512]{2,1,0:T(8,128)S(1)}, f32[2,128,512]{2,1,0:T(8,128)S(1)}, u32[]{:S(2)}, u32[]{:S(2)}) collective-permute-start(f32[2,128,512]{2,1,0:T(8,128)S(1)} %get-tuple-element.25), channel_id=1, source_target_pairs={{1,0},{0,1},{3,2},{2,3},{5,4},{4,5},{7,6},{6,7},{9,8},{8,9},{11,10... | collective-permute-start | bytes 1572872 | tf_op jit(solution)/shard_map/ppermute | solution.py:35
  9.1 4.7 %collective-permute-start.1 = (bf16[128,512]{1,0:T(8,128)(2,1)S(1)}, bf16[128,512]{1,0:T(8,128)(2,1)S(1)}, u32[]{:S(2)}, u32[]{:S(2)}) collective-permute-start(bf16[128,512]{1,0:T(8,128)(2,1)S(1)} %get-tuple-element.23), channel_id=1, source_target_pairs={{2,0},{0,2},{3,1},{1,3},{6,4},{4,6},{7,5},{5,7},{10,8},{8,10},{11,... | collective-permute-start | bytes 393224 | tf_op jit(solution)/shard_map/ppermute | solution.py:35
  10.9 5.6 %collective-permute-start.3 = (bf16[128,512]{1,0:T(8,128)(2,1)S(1)}, bf16[128,512]{1,0:T(8,128)(2,1)S(1)}, u32[]{:S(2)}, u32[]{:S(2)}) collective-permute-start(bf16[128,512]{1,0:T(8,128)(2,1)S(1)} %get-tuple-element.27), channel_id=1, source_target_pairs={{2,0},{0,2},{3,1},{1,3},{6,4},{4,6},{7,5},{5,7},{10,8},{8,10},{11,... | collective-permute-start | bytes 393224 | tf_op jit(solution)/shard_map/ppermute | solution.py:35
  16.9 1.4 %copy-start = (bf16[16,528,128]{2,1,0:T(8,128)(2,1)}, bf16[16,528,128]{2,1,0:T(8,128)(2,1)S(1)}, u32[]{:S(2)}) copy-start(bf16[16,528,128]{2,1,0:T(8,128)(2,1)S(1)} %get-tuple-element.33) | copy-start | bytes 6488068
  18.2 36.4 %all-to-all-start = ((bf16[16,528,128]{2,1,0:T(8,128)(2,1)}), bf16[16,528,128]{2,1,0:T(8,128)(2,1)S(1)}, u32[]{:S(2)}, u32[]{:S(2)}) async-start(bf16[16,528,128]{2,1,0:T(8,128)(2,1)} %copy-done), calls=%async_computation | async-start | bytes 4325376 | tf_op jit(solution)/shard_map/all_to_all | solution.py:318
  23.3 7.8 %collective-permute-start.5 = (bf16[144,512]{1,0:T(8,128)(2,1)S(1)}, bf16[144,512]{1,0:T(8,128)(2,1)S(1)}, u32[]{:S(2)}, u32[]{:S(2)}) collective-permute-start(bf16[144,512]{1,0:T(8,128)(2,1)S(1)} %get-tuple-element.32.refs_0_), channel_id=1, source_target_pairs={{32,0},{64,32},{96,64},{128,96},{160,128},{192,160},{224,192},{0,2... | collective-permute-start | bytes 442376 | tf_op jit(solution)/shard_map/ppermute | solution.py:35
  28.9 5.5 %collective-permute-start.13 = (bf16[144,512]{1,0:T(8,128)(2,1)S(1)}, bf16[144,512]{1,0:T(8,128)(2,1)S(1)}, u32[]{:S(2)}, u32[]{:S(2)}) collective-permute-start(bf16[144,512]{1,0:T(8,128)(2,1)S(1)} %get-tuple-element.32.refs_0_), channel_id=1, source_target_pairs={{224,0},{0,32},{32,64},{64,96},{96,128},{128,160},{160,192},{192,2... | collective-permute-start | bytes 442376 | tf_op jit(solution)/shard_map/ppermute | solution.py:35
  31.0 5.2 %collective-permute-start.7 = (bf16[144,512]{1,0:T(8,128)(2,1)S(1)}, bf16[144,512]{1,0:T(8,128)(2,1)S(1)}, u32[]{:S(2)}, u32[]{:S(2)}) collective-permute-start(bf16[144,512]{1,0:T(8,128)(2,1)S(1)} %collective-permute-done.5.refs_2_), channel_id=1, source_target_pairs={{32,0},{64,32},{96,64},{128,96},{160,128},{192,160},{224,192},{0,2... | collective-permute-start | bytes 442376 | tf_op jit(solution)/shard_map/ppermute | solution.py:35
  34.4 9.6 %collective-permute-start.14 = (bf16[144,512]{1,0:T(8,128)(2,1)S(1)}, bf16[144,512]{1,0:T(8,128)(2,1)S(1)}, u32[]{:S(2)}, u32[]{:S(2)}) collective-permute-start(bf16[144,512]{1,0:T(8,128)(2,1)S(1)} %collective-permute-done.13.refs_14_), channel_id=1, source_target_pairs={{224,0},{0,32},{32,64},{64,96},{96,128},{128,160},{160,192},{192,2... | collective-permute-start | bytes 442376 | tf_op jit(solution)/shard_map/ppermute | solution.py:35
  36.2 7.8 %collective-permute-start.9 = (bf16[144,512]{1,0:T(8,128)(2,1)S(1)}, bf16[144,512]{1,0:T(8,128)(2,1)S(1)}, u32[]{:S(2)}, u32[]{:S(2)}) collective-permute-start(bf16[144,512]{1,0:T(8,128)(2,1)S(1)} %collective-permute-done.7.refs_4_), channel_id=1, source_target_pairs={{32,0},{64,32},{96,64},{128,96},{160,128},{192,160},{224,192},{0,2... | collective-permute-start | bytes 442376 | tf_op jit(solution)/shard_map/ppermute | solution.py:35
  39.6 7.1 %collective-permute-start.4 = (bf16[144,512]{1,0:T(8,128)(2,1)S(1)}, bf16[144,512]{1,0:T(8,128)(2,1)S(1)}, u32[]{:S(2)}, u32[]{:S(2)}) collective-permute-start(bf16[144,512]{1,0:T(8,128)(2,1)S(1)} %get-tuple-element.32.refs_0_), channel_id=1, source_target_pairs={{1,0},{0,1},{3,2},{2,3},{5,4},{4,5},{7,6},{6,7},{9,8},{8,9},{11,10... | collective-permute-start | bytes 442376 | tf_op jit(solution)/shard_map/ppermute | solution.py:35
  43.5 6.4 %collective-permute-start.18 = (bf16[144,512]{1,0:T(8,128)(2,1)S(1)}, bf16[144,512]{1,0:T(8,128)(2,1)S(1)}, u32[]{:S(2)}, u32[]{:S(2)}) collective-permute-start(bf16[144,512]{1,0:T(8,128)(2,1)S(1)} %collective-permute-done.13.refs_14_), channel_id=1, source_target_pairs={{1,0},{0,1},{3,2},{2,3},{5,4},{4,5},{7,6},{6,7},{9,8},{8,9},{11,10... | collective-permute-start | bytes 442376 | tf_op jit(solution)/shard_map/ppermute | solution.py:35
  43.5 6.5 %collective-permute-start.6 = (bf16[144,512]{1,0:T(8,128)(2,1)S(1)}, bf16[144,512]{1,0:T(8,128)(2,1)S(1)}, u32[]{:S(2)}, u32[]{:S(2)}) collective-permute-start(bf16[144,512]{1,0:T(8,128)(2,1)S(1)} %collective-permute-done.5.refs_2_), channel_id=1, source_target_pairs={{1,0},{0,1},{3,2},{2,3},{5,4},{4,5},{7,6},{6,7},{9,8},{8,9},{11,10... | collective-permute-start | bytes 442376 | tf_op jit(solution)/shard_map/ppermute | solution.py:35
  44.0 6.8 %collective-permute-start.15 = (bf16[144,512]{1,0:T(8,128)(2,1)S(1)}, bf16[144,512]{1,0:T(8,128)(2,1)}, u32[]{:S(2)}, u32[]{:S(2)}) collective-permute-start(bf16[144,512]{1,0:T(8,128)(2,1)S(1)} %collective-permute-done.14.refs_12_), channel_id=1, source_target_pairs={{224,0},{0,32},{32,64},{64,96},{96,128},{128,160},{160,192},{192,2... | collective-permute-start | bytes 442376 | tf_op jit(solution)/shard_map/ppermute | solution.py:35
  44.0 7.6 %collective-permute-start.11 = (bf16[144,512]{1,0:T(8,128)(2,1)S(1)}, bf16[144,512]{1,0:T(8,128)(2,1)}, u32[]{:S(2)}, u32[]{:S(2)}) collective-permute-start(bf16[144,512]{1,0:T(8,128)(2,1)S(1)} %collective-permute-done.9.refs_6_), channel_id=1, source_target_pairs={{32,0},{64,32},{96,64},{128,96},{160,128},{192,160},{224,192},{0,2... | collective-permute-start | bytes 442376 | tf_op jit(solution)/shard_map/ppermute | solution.py:35
  46.7 5.9 %collective-permute-start.17 = (bf16[144,512]{1,0:T(8,128)(2,1)S(1)}, bf16[144,512]{1,0:T(8,128)(2,1)}, u32[]{:S(2)}, u32[]{:S(2)}) collective-permute-start(bf16[144,512]{1,0:T(8,128)(2,1)S(1)} %collective-permute-done.14.refs_12_), channel_id=1, source_target_pairs={{1,0},{0,1},{3,2},{2,3},{5,4},{4,5},{7,6},{6,7},{9,8},{8,9},{11,10... | collective-permute-start | bytes 442376 | tf_op jit(solution)/shard_map/ppermute | solution.py:35
  49.9 2.8 %collective-permute-start.8 = (bf16[144,512]{1,0:T(8,128)(2,1)S(1)}, bf16[144,512]{1,0:T(8,128)(2,1)}, u32[]{:S(2)}, u32[]{:S(2)}) collective-permute-start(bf16[144,512]{1,0:T(8,128)(2,1)S(1)} %collective-permute-done.7.refs_4_), channel_id=1, source_target_pairs={{1,0},{0,1},{3,2},{2,3},{5,4},{4,5},{7,6},{6,7},{9,8},{8,9},{11,10... | collective-permute-start | bytes 442376 | tf_op jit(solution)/shard_map/ppermute | solution.py:35
  50.0 3.0 %collective-permute-start.10 = (bf16[144,512]{1,0:T(8,128)(2,1)S(1)}, bf16[144,512]{1,0:T(8,128)(2,1)}, u32[]{:S(2)}, u32[]{:S(2)}) collective-permute-start(bf16[144,512]{1,0:T(8,128)(2,1)S(1)} %collective-permute-done.9.refs_6_), channel_id=1, source_target_pairs={{1,0},{0,1},{3,2},{2,3},{5,4},{4,5},{7,6},{6,7},{9,8},{8,9},{11,10... | collective-permute-start | bytes 442376 | tf_op jit(solution)/shard_map/ppermute | solution.py:35
  50.8 2.1 %collective-permute-start.16 = (bf16[144,512]{1,0:T(8,128)(2,1)}, bf16[144,512]{1,0:T(8,128)(2,1)}, u32[]{:S(2)}, u32[]{:S(2)}) collective-permute-start(bf16[144,512]{1,0:T(8,128)(2,1)} %collective-permute-done.15.refs_10_), channel_id=1, source_target_pairs={{1,0},{0,1},{3,2},{2,3},{5,4},{4,5},{7,6},{6,7},{9,8},{8,9},{11,10... | collective-permute-start | bytes 442376 | tf_op jit(solution)/shard_map/ppermute | solution.py:35
  51.6 2.3 %collective-permute-start.12 = (bf16[144,512]{1,0:T(8,128)(2,1)}, bf16[144,512]{1,0:T(8,128)(2,1)}, u32[]{:S(2)}, u32[]{:S(2)}) collective-permute-start(bf16[144,512]{1,0:T(8,128)(2,1)} %collective-permute-done.11.refs_8_), channel_id=1, source_target_pairs={{1,0},{0,1},{3,2},{2,3},{5,4},{4,5},{7,6},{6,7},{9,8},{8,9},{11,10... | collective-permute-start | bytes 442376 | tf_op jit(solution)/shard_map/ppermute | solution.py:35
  70.0 15.1 %all-to-all-start.1 = ((f32[8,8,128]{2,1,0:T(8,128)}), f32[8,8,128]{2,1,0:T(8,128)S(1)}, u32[]{:S(2)}, u32[]{:S(2)}) async-start(f32[8,8,128]{2,1,0:T(8,128)} %get-tuple-element.34), calls=%async_computation.1 | async-start | bytes 65536 | tf_op jit(solution)/shard_map/all_to_all | solution.py:322
  85.1 12.5 %all-to-all-start.2 = ((f32[16,8,128]{2,1,0:T(8,128)}), f32[16,8,128]{2,1,0:T(8,128)S(1)}, u32[]{:S(2)}, u32[]{:S(2)}) async-start(f32[16,8,128]{2,1,0:T(8,128)} %get-tuple-element.35), calls=%async_computation.2 | async-start | bytes 131072 | tf_op jit(solution)/shard_map/all_to_all | solution.py:323

commit v9 on v8

--- a/solution.py
+++ b/solution.py
@@ -279,6 +279,36 @@
     )(place, *seq_blocks, struct_blocks)
 
 
+def losses_kernel(place_ref, rows_ref, cols_ref, self_ref, seq_ref, struct_ref, hard_ref):
+    rows = jnp.sum(rows_ref[...], axis=0)
+    own, other = rows[0:8], rows[8:16]
+    lower, upper = (place_ref[0] == 0), (place_ref[0] == 1)
+    for place, held in ((0, jnp.where(lower, own, other)), (1, jnp.where(upper, own, other))):
+        for core in range(2):
+            at = slice(place * 2 + core, place * 2 + core + 1)
+            seq_ref[at, :] = jnp.log(held[core * 3 : core * 3 + 1]) - jnp.log(held[core * 3 + 1 : core * 3 + 2])
+    cols = jnp.sum(cols_ref[...], axis=0)
+    struct_ref[...] = jnp.log(cols[0:1]) - jnp.log(cols[1:2])
+    extra = jnp.where(place_ref[1] == 0, own[2:3], own[5:6])
+    self_logits = LOGIT_SCALE * self_ref[0:1]
+    hard_ref[...] = jnp.log(jnp.exp(self_logits) + extra) - self_logits
+
+
+def losses(place, rows, cols, self_dot):
+    return pl.pallas_call(
+        losses_kernel,
+        out_shape=(
+            jax.ShapeDtypeStruct((4, SHARE), jnp.float32),
+            jax.ShapeDtypeStruct((1, SHARE), jnp.float32),
+            jax.ShapeDtypeStruct((1, SHARE), jnp.float32),
+        ),
+        in_specs=[SMEM, VMEM, VMEM, VMEM],
+        out_specs=(VMEM, VMEM, VMEM),
+        compiler_params=pltpu.CompilerParams(vmem_limit_bytes=4 * 1024 * 1024),
+        name="losses",
+    )(place, rows, cols, self_dot)
+
+
 def over_z(block):
     found = {0: block, 1: shifted(block, "z", 1), 7: shifted(block, "z", -1)}
     found[2], found[6] = shifted(found[1], "z", 1), shifted(found[7], "z", -1)
@@ -319,17 +349,13 @@
     seq_blocks = [each for held in over_z(seq_block) for each in (held, shifted(held, "core", 1))]
 
     rows, cols, self_dot = pair_sums(jnp.stack([place("z"), core, place(COL_AXES)]), seq_blocks, struct_blocks)
-    rows = jnp.sum(lax.all_to_all(rows, "z", split_axis=0, concat_axis=0, tiled=True), axis=0)
-    cols = jnp.sum(lax.all_to_all(cols, COL_AXES, split_axis=0, concat_axis=0, tiled=True), axis=0)
-    rows = lax.all_gather(rows, MP_AXES, axis=0, tiled=False).reshape(2, 2, 8, SHARE)
-    rows = jnp.sum(rows, axis=1)[:, 0:6].reshape(2, 2, 3, SHARE)
-
-    seq_loss = (jnp.log(rows[:, :, 0]) - jnp.log(rows[:, :, 1])).reshape(4 * SHARE)
-    struct_loss = jnp.log(cols[0]) - jnp.log(cols[1])
-    self_logits = LOGIT_SCALE * self_dot[0]
-    extra = rows[:, :, 2].reshape(4, SHARE)[place(MP_AXES)]
-    hard_loss = jnp.log(jnp.exp(self_logits) + extra) - self_logits
-    return (seq_loss, struct_loss, hard_loss)
+    cols = lax.all_to_all(cols, COL_AXES, split_axis=0, concat_axis=0, tiled=True)
+    rows = rows + shifted(rows, "core", 1)
+    rows = jnp.concatenate([rows, shifted(rows, "yl", 1)], axis=1)
+    rows, cols = lax.optimization_barrier((rows, cols))
+    rows = lax.all_to_all(rows, "z", split_axis=0, concat_axis=0, tiled=True)
+    seq_loss, struct_loss, hard_loss = losses(jnp.stack([yl, core]), rows, cols, self_dot)
+    return (seq_loss.reshape(4 * SHARE), struct_loss.reshape(SHARE), hard_loss.reshape(SHARE))
 
 
 def solution(mesh):

time: 98.6 us -> 100 us (1.014)
  blocking collectives: 7.82 us -> 0 us
  waiting for transfers between devices: 19.2 us -> 26.2 us
  starting transfers between devices: 44.9 us -> 46.6 us
  Pallas kernels: 16.8 us -> 18 us
    all_gather x1 -> x0, blocking collectives: 7.82 us -> none  [per_device(): lax.all_gather(rows, MP_AXES, axis=0, tiled=False).reshape(2, 2, 8, SHARE)]
    all_to_all x1, waiting for transfers between devices: 0.01 us -> 5.84 us  [per_device(): lax.all_to_all(cols, COL_AXES, split_axis=0, concat_axis=0, tiled=True)]
    all_to_all x1, starting transfers between devices: 8.19 us -> 6.02 us  [per_device(): rows = lax.all_to_all(rows, 'z', split_axis=0, concat_axis=0, tiled=True)]
    all_to_all x1, starting transfers between devices: 3.49 us -> 5.62 us  [per_device(): lax.all_to_all(cols, COL_AXES, split_axis=0, concat_axis=0, tiled=True)]
    ppermute x19 -> x21, starting transfers between devices: 28.2 us -> 29.9 us  [shifted(): lax.ppermute(value, axes, [((place + steps) % count, place) for place in...]
    pallas_call x0 -> x1, Pallas kernels: none -> 1.14 us  [losses(): pl.pallas_call(losses_kernel, out_shape=(jax.ShapeDtypeStruct((4, SHARE),...]
    sub x2 -> x0, other arithmetic: 1.06 us -> none  [the longest x1 0.53 us: per_device(): hard_loss = jnp.log(jnp.exp(self_logits) + extra) - self_logits]
    ppermute x19 -> x21, waiting for transfers between devices: 11.6 us -> 12.4 us  [shifted(): lax.ppermute(value, axes, [((place + steps) % count, place) for place in...]
  transfers between devices with their start and end apart: 22 -> 24, of which waited for: 11 -> 13; matrix products, arithmetic and copies ran while one was open for 3% -> 2% of each run, Pallas kernels for 1% -> 1%
where the time goes in v9:
time: 100 us; the launch traced here: 99.1 us
  starting transfers between devices  46.6 us (47%)
  waiting for transfers between devices  26.2 us (26%)
  Pallas kernels  18 us (18%)
  local copies, waits for them, and re-layouts  5.23 us (5%)
  other arithmetic  2.28 us (2%)
    ppermute x21, starting transfers between devices, shifted(): lax.ppermute(value, axes, [((place + steps) % count, place) for place in...  29.9 us
    pallas_call x1, Pallas kernels, pair_sums(): pl.pallas_call(pair_kernel, out_shape=(jax.ShapeDtypeStruct((8, 8, SHARE)...  15.3 us
    ppermute x21, waiting for transfers between devices, shifted(): lax.ppermute(value, axes, [((place + steps) % count, place) for place in...  12.4 us
    all_to_all x1, waiting for transfers between devices, per_device(): rows = lax.all_to_all(rows, 'z', split_axis=0, concat_axis=0, tiled=True)  7.15 us
    all_to_all x1, starting transfers between devices, per_device(): rows = lax.all_to_all(rows, 'z', split_axis=0, concat_axis=0, tiled=True)  6.02 us
    all_to_all x1, waiting for transfers between devices, per_device(): lax.all_to_all(cols, COL_AXES, split_axis=0, concat_axis=0, tiled=True)  5.84 us
    all_to_all x1, starting transfers between devices, per_device(): lax.all_to_all(cols, COL_AXES, split_axis=0, concat_axis=0, tiled=True)  5.62 us
    unnamed x14, local copies, waits for them, and re-layouts  5.2 us
  transfers between devices with their start and end apart: 24, of which 13 were waited for; matrix products, arithmetic and copies ran while one was open for 2% of the time, Pallas kernels for 1%

profile of v9, /device:TPU:1, one launch (start us, length us, event | category | flops | bytes accessed | tf_op | source)
XLA Modules:
  0.0 99.1 jit_solution(8509584342459491423)
XLA Ops:
  0.6 0.9 copy-done.3
  1.6 0.9 copy-done.4
  2.9 3.3 %collective-permute-start = (f32[2,128,512]{2,1,0:T(8,128)S(1)}, f32[2,128,512]{2,1,0:T(8,128)S(1)}, u32[]{:S(2)}, u32[]{:S(2)}) collective-permute-start(f32[2,128,512]{2,1,0:T(8,128)S(1)} %get-tuple-element.26), channel_id=1, source_target_pairs={{1,0},{0,1},{3,2},{2,3},{5,4},{4,5},{7,6},{6,7},{9,8},{8,9},{11,10... | collective-permute-start | bytes 1572872 | tf_op jit(solution)/shard_map/ppermute | solution.py:35
  6.2 1.0 copy-done.1
  7.2 1.0 copy-done.2
  9.2 1.7 %collective-permute-done.2.got_ref = f32[2,128,512]{2,1,0:T(8,128)S(1)} collective-permute-done((f32[2,128,512]{2,1,0:T(8,128)S(1)}, f32[2,128,512]{2,1,0:T(8,128)S(1)}, u32[]{:S(2)}, u32[]{:S(2)}) %collective-permute-start.2) | collective-permute-done | bytes 524320 | tf_op jit(solution)/shard_map/ppermute | solution.py:35
  11.0 0.8 shift-right-arithmetic_convert_fusion
  11.9 0.7 fusion.5
  12.6 1.1 %collective-permute-done.1.got2_s = bf16[128,512]{1,0:T(8,128)(2,1)S(1)} collective-permute-done((bf16[128,512]{1,0:T(8,128)(2,1)S(1)}, bf16[128,512]{1,0:T(8,128)(2,1)S(1)}, u32[]{:S(2)}, u32[]{:S(2)}) %collective-permute-start.1) | collective-permute-done | bytes 131104 | tf_op jit(solution)/shard_map/ppermute | solution.py:35
  13.8 2.8 %collective-permute-done.3.got2_q = bf16[128,512]{1,0:T(8,128)(2,1)S(1)} collective-permute-done((bf16[128,512]{1,0:T(8,128)(2,1)S(1)}, bf16[128,512]{1,0:T(8,128)(2,1)S(1)}, u32[]{:S(2)}, u32[]{:S(2)}) %collective-permute-start.3) | collective-permute-done | bytes 131104 | tf_op jit(solution)/shard_map/ppermute | solution.py:35
  16.9 1.4 %copy-done = bf16[16,528,128]{2,1,0:T(8,128)(2,1)} copy-done((bf16[16,528,128]{2,1,0:T(8,128)(2,1)}, bf16[16,528,128]{2,1,0:T(8,128)(2,1)S(1)}, u32[]{:S(2)}) %copy-start) | copy-done | bytes 2162712
  18.2 5.0 %all-to-all-start = ((bf16[16,528,128]{2,1,0:T(8,128)(2,1)}), bf16[16,528,128]{2,1,0:T(8,128)(2,1)S(1)}, u32[]{:S(2)}, u32[]{:S(2)}) async-start(bf16[16,528,128]{2,1,0:T(8,128)(2,1)} %copy-done), calls=%async_computation | async-start | bytes 4325376 | tf_op jit(solution)/shard_map/all_to_all | solution.py:348
  23.3 5.7 %collective-permute-start.5 = (bf16[144,512]{1,0:T(8,128)(2,1)S(1)}, bf16[144,512]{1,0:T(8,128)(2,1)S(1)}, u32[]{:S(2)}, u32[]{:S(2)}) collective-permute-start(bf16[144,512]{1,0:T(8,128)(2,1)S(1)} %get-tuple-element.37.refs_0_), channel_id=1, source_target_pairs={{32,0},{64,32},{96,64},{128,96},{160,128},{192,160},{224,192},{0,2... | collective-permute-start | bytes 442376 | tf_op jit(solution)/shard_map/ppermute | solution.py:35
  28.9 2.1 %collective-permute-done.5.refs_2_ = bf16[144,512]{1,0:T(8,128)(2,1)S(1)} collective-permute-done((bf16[144,512]{1,0:T(8,128)(2,1)S(1)}, bf16[144,512]{1,0:T(8,128)(2,1)S(1)}, u32[]{:S(2)}, u32[]{:S(2)}) %collective-permute-start.5) | collective-permute-done | bytes 147488 | tf_op jit(solution)/shard_map/ppermute | solution.py:35
  31.0 3.1 %collective-permute-start.7 = (bf16[144,512]{1,0:T(8,128)(2,1)S(1)}, bf16[144,512]{1,0:T(8,128)(2,1)S(1)}, u32[]{:S(2)}, u32[]{:S(2)}) collective-permute-start(bf16[144,512]{1,0:T(8,128)(2,1)S(1)} %collective-permute-done.5.refs_2_), channel_id=1, source_target_pairs={{32,0},{64,32},{96,64},{128,96},{160,128},{192,160},{224,192},{0,2... | collective-permute-start | bytes 442376 | tf_op jit(solution)/shard_map/ppermute | solution.py:35
  34.4 1.8 %collective-permute-done.7.refs_4_ = bf16[144,512]{1,0:T(8,128)(2,1)S(1)} collective-permute-done((bf16[144,512]{1,0:T(8,128)(2,1)S(1)}, bf16[144,512]{1,0:T(8,128)(2,1)S(1)}, u32[]{:S(2)}, u32[]{:S(2)}) %collective-permute-start.7) | collective-permute-done | bytes 147488 | tf_op jit(solution)/shard_map/ppermute | solution.py:35
  36.2 3.4 %collective-permute-start.9 = (bf16[144,512]{1,0:T(8,128)(2,1)S(1)}, bf16[144,512]{1,0:T(8,128)(2,1)S(1)}, u32[]{:S(2)}, u32[]{:S(2)}) collective-permute-start(bf16[144,512]{1,0:T(8,128)(2,1)S(1)} %collective-permute-done.7.refs_4_), channel_id=1, source_target_pairs={{32,0},{64,32},{96,64},{128,96},{160,128},{192,160},{224,192},{0,2... | collective-permute-start | bytes 442376 | tf_op jit(solution)/shard_map/ppermute | solution.py:35
  39.6 3.9 %collective-permute-start.4 = (bf16[144,512]{1,0:T(8,128)(2,1)S(1)}, bf16[144,512]{1,0:T(8,128)(2,1)S(1)}, u32[]{:S(2)}, u32[]{:S(2)}) collective-permute-start(bf16[144,512]{1,0:T(8,128)(2,1)S(1)} %get-tuple-element.37.refs_0_), channel_id=1, source_target_pairs={{1,0},{0,1},{3,2},{2,3},{5,4},{4,5},{7,6},{6,7},{9,8},{8,9},{11,10... | collective-permute-start | bytes 442376 | tf_op jit(solution)/shard_map/ppermute | solution.py:35
  44.0 2.7 %collective-permute-start.11 = (bf16[144,512]{1,0:T(8,128)(2,1)S(1)}, bf16[144,512]{1,0:T(8,128)(2,1)}, u32[]{:S(2)}, u32[]{:S(2)}) collective-permute-start(bf16[144,512]{1,0:T(8,128)(2,1)S(1)} %collective-permute-done.9.refs_6_), channel_id=1, source_target_pairs={{32,0},{64,32},{96,64},{128,96},{160,128},{192,160},{224,192},{0,2... | collective-permute-start | bytes 442376 | tf_op jit(solution)/shard_map/ppermute | solution.py:35
  46.7 3.2 %collective-permute-start.17 = (bf16[144,512]{1,0:T(8,128)(2,1)S(1)}, bf16[144,512]{1,0:T(8,128)(2,1)}, u32[]{:S(2)}, u32[]{:S(2)}) collective-permute-start(bf16[144,512]{1,0:T(8,128)(2,1)S(1)} %collective-permute-done.14.refs_12_), channel_id=1, source_target_pairs={{1,0},{0,1},{3,2},{2,3},{5,4},{4,5},{7,6},{6,7},{9,8},{8,9},{11,10... | collective-permute-start | bytes 442376 | tf_op jit(solution)/shard_map/ppermute | solution.py:35
  50.8 0.8 collective-permute-start.16
  51.6 0.9 collective-permute-start.12
  53.0 0.9 collective-permute-done.12.refs_9_
  53.9 0.8 all-to-all-done.refs_16_
  54.7 15.3 %pair_sums.1 = (f32[8,8,128]{2,1,0:T(8,128)S(1)}, f32[16,8,128]{2,1,0:T(8,128)}, f32[8,128]{1,0:T(8,128)S(1)}) custom-call(s32[3]{0:T(128)S(1)} %pad_add_fusion.1.place_ref, bf16[144,512]{1,0:T(8,128)(2,1)S(1)} %get-tuple-element.37.refs_0_, bf16[144,512]{1,0:T(8,128)(2,1)S(1)} %collective-permute-done.4.refs_1_, ...), custom_call_target="tpu_custom_call" | custom-call | flops 4294967296 | bytes 4194304 | tf_op jit(solution)/shard_map/pair_sums/pallas_call | solution.py:252
  70.0 1.4 %collective-permute-start.19 = (f32[8,8,128]{2,1,0:T(8,128)S(1)}, f32[8,8,128]{2,1,0:T(8,128)S(1)}, u32[]{:S(2)}, u32[]{:S(2)}) collective-permute-start(f32[8,8,128]{2,1,0:T(8,128)S(1)} %get-tuple-element.39), channel_id=1, source_target_pairs={{1,0},{0,1},{3,2},{2,3},{5,4},{4,5},{7,6},{6,7},{9,8},{8,9},{11,10... | collective-permute-start | bytes 98312 | tf_op jit(solution)/shard_map/ppermute | solution.py:35
  71.4 0.9 collective-permute-done.19
  72.6 5.6 %all-to-all-start.1 = ((f32[16,8,128]{2,1,0:T(8,128)}), f32[16,8,128]{2,1,0:T(8,128)S(1)}, u32[]{:S(2)}, u32[]{:S(2)}) async-start(f32[16,8,128]{2,1,0:T(8,128)} %get-tuple-element.40), calls=%async_computation.1 | async-start | bytes 131072 | tf_op jit(solution)/shard_map/all_to_all | solution.py:352
  78.9 5.8 %all-to-all-done.1.cols_ref = f32[16,8,128]{2,1,0:T(8,128)S(1)} async-done(((f32[16,8,128]{2,1,0:T(8,128)}), f32[16,8,128]{2,1,0:T(8,128)S(1)}, u32[]{:S(2)}, u32[]{:S(2)}) %all-to-all-start.1) | async-done | bytes 65568 | tf_op jit(solution)/shard_map/all_to_all | solution.py:352
  84.7 6.0 %all-to-all-start.2 = ((f32[8,16,128]{2,1,0:T(8,128)}), f32[8,16,128]{2,1,0:T(8,128)S(1)}, u32[]{:S(2)}, u32[]{:S(2)}) async-start(f32[8,16,128]{2,1,0:T(8,128)} %pad_maximum_fusion), calls=%async_computation.2 | async-start | bytes 131072 | tf_op jit(solution)/shard_map/all_to_all | solution.py:356
  90.8 7.2 %all-to-all-done.2.rows_ref = f32[8,16,128]{2,1,0:T(8,128)S(1)} async-done(((f32[8,16,128]{2,1,0:T(8,128)}), f32[8,16,128]{2,1,0:T(8,128)S(1)}, u32[]{:S(2)}, u32[]{:S(2)}) %all-to-all-start.2) | async-done | bytes 65568 | tf_op jit(solution)/shard_map/all_to_all | solution.py:356
  97.9 1.1 %losses.1 = (f32[4,128]{1,0:T(4,128)}, f32[1,128]{1,0:T(1,128)}, f32[1,128]{1,0:T(1,128)}) custom-call(s32[2]{0:T(128)S(1)} %pad_add_fusion.place_ref, f32[8,16,128]{2,1,0:T(8,128)S(1)} %all-to-all-done.2.rows_ref, f32[16,8,128]{2,1,0:T(8,128)S(1)} %all-to-all-done.1.cols_ref, f32[8,128]{1,0:T(8,128)S(1)} %get-tuple-element.43.self_ref), custom_call_target="tpu_custom_call" | custom-call | tf_op jit(solution)/shard_map/losses/pallas_call | solution.py:298
  (50 shorter events, 5.0 us)
Async XLA Ops:
  0.6 1.0 copy-start.3
  1.6 0.9 copy-start.4
  2.5 9.3 %copy-start.5 = (s32[512,16,1]{0,2,1:T(1,128)S(1)}, s32[512,16,1]{0,2,1:T(1,128)}, u32[]{:S(2)}) copy-start(s32[512,16,1]{0,2,1:T(1,128)} %param.13) | copy-start | bytes 98308
  2.5 9.3 %copy-start.6 = (s32[128,16]{0,1:T(8,128)S(1)}, s32[128,16]{0,1:T(8,128)}, u32[]{:S(2)}) copy-start(s32[128,16]{0,1:T(8,128)} %param.15) | copy-start | bytes 24580
  2.9 6.1 %collective-permute-start = (f32[2,128,512]{2,1,0:T(8,128)S(1)}, f32[2,128,512]{2,1,0:T(8,128)S(1)}, u32[]{:S(2)}, u32[]{:S(2)}) collective-permute-start(f32[2,128,512]{2,1,0:T(8,128)S(1)} %get-tuple-element.26), channel_id=1, source_target_pairs={{1,0},{0,1},{3,2},{2,3},{5,4},{4,5},{7,6},{6,7},{9,8},{8,9},{11,10... | collective-permute-start | bytes 1572872 | tf_op jit(solution)/shard_map/ppermute | solution.py:35
  6.2 1.0 copy-start.1
  7.2 1.0 copy-start.2
  8.9 2.0 %collective-permute-start.2 = (f32[2,128,512]{2,1,0:T(8,128)S(1)}, f32[2,128,512]{2,1,0:T(8,128)S(1)}, u32[]{:S(2)}, u32[]{:S(2)}) collective-permute-start(f32[2,128,512]{2,1,0:T(8,128)S(1)} %get-tuple-element.30), channel_id=1, source_target_pairs={{1,0},{0,1},{3,2},{2,3},{5,4},{4,5},{7,6},{6,7},{9,8},{8,9},{11,10... | collective-permute-start | bytes 1572872 | tf_op jit(solution)/shard_map/ppermute | solution.py:35
  9.1 4.7 %collective-permute-start.1 = (bf16[128,512]{1,0:T(8,128)(2,1)S(1)}, bf16[128,512]{1,0:T(8,128)(2,1)S(1)}, u32[]{:S(2)}, u32[]{:S(2)}) collective-permute-start(bf16[128,512]{1,0:T(8,128)(2,1)S(1)} %get-tuple-element.28), channel_id=1, source_target_pairs={{2,0},{0,2},{3,1},{1,3},{6,4},{4,6},{7,5},{5,7},{10,8},{8,10},{11,... | collective-permute-start | bytes 393224 | tf_op jit(solution)/shard_map/ppermute | solution.py:35
  10.9 5.6 %collective-permute-start.3 = (bf16[128,512]{1,0:T(8,128)(2,1)S(1)}, bf16[128,512]{1,0:T(8,128)(2,1)S(1)}, u32[]{:S(2)}, u32[]{:S(2)}) collective-permute-start(bf16[128,512]{1,0:T(8,128)(2,1)S(1)} %get-tuple-element.32), channel_id=1, source_target_pairs={{2,0},{0,2},{3,1},{1,3},{6,4},{4,6},{7,5},{5,7},{10,8},{8,10},{11,... | collective-permute-start | bytes 393224 | tf_op jit(solution)/shard_map/ppermute | solution.py:35
  16.9 1.4 %copy-start = (bf16[16,528,128]{2,1,0:T(8,128)(2,1)}, bf16[16,528,128]{2,1,0:T(8,128)(2,1)S(1)}, u32[]{:S(2)}) copy-start(bf16[16,528,128]{2,1,0:T(8,128)(2,1)S(1)} %get-tuple-element.38) | copy-start | bytes 6488068
  18.2 36.4 %all-to-all-start = ((bf16[16,528,128]{2,1,0:T(8,128)(2,1)}), bf16[16,528,128]{2,1,0:T(8,128)(2,1)S(1)}, u32[]{:S(2)}, u32[]{:S(2)}) async-start(bf16[16,528,128]{2,1,0:T(8,128)(2,1)} %copy-done), calls=%async_computation | async-start | bytes 4325376 | tf_op jit(solution)/shard_map/all_to_all | solution.py:348
  23.3 7.8 %collective-permute-start.5 = (bf16[144,512]{1,0:T(8,128)(2,1)S(1)}, bf16[144,512]{1,0:T(8,128)(2,1)S(1)}, u32[]{:S(2)}, u32[]{:S(2)}) collective-permute-start(bf16[144,512]{1,0:T(8,128)(2,1)S(1)} %get-tuple-element.37.refs_0_), channel_id=1, source_target_pairs={{32,0},{64,32},{96,64},{128,96},{160,128},{192,160},{224,192},{0,2... | collective-permute-start | bytes 442376 | tf_op jit(solution)/shard_map/ppermute | solution.py:35
  28.9 5.5 %collective-permute-start.13 = (bf16[144,512]{1,0:T(8,128)(2,1)S(1)}, bf16[144,512]{1,0:T(8,128)(2,1)S(1)}, u32[]{:S(2)}, u32[]{:S(2)}) collective-permute-start(bf16[144,512]{1,0:T(8,128)(2,1)S(1)} %get-tuple-element.37.refs_0_), channel_id=1, source_target_pairs={{224,0},{0,32},{32,64},{64,96},{96,128},{128,160},{160,192},{192,2... | collective-permute-start | bytes 442376 | tf_op jit(solution)/shard_map/ppermute | solution.py:35
  31.0 5.2 %collective-permute-start.7 = (bf16[144,512]{1,0:T(8,128)(2,1)S(1)}, bf16[144,512]{1,0:T(8,128)(2,1)S(1)}, u32[]{:S(2)}, u32[]{:S(2)}) collective-permute-start(bf16[144,512]{1,0:T(8,128)(2,1)S(1)} %collective-permute-done.5.refs_2_), channel_id=1, source_target_pairs={{32,0},{64,32},{96,64},{128,96},{160,128},{192,160},{224,192},{0,2... | collective-permute-start | bytes 442376 | tf_op jit(solution)/shard_map/ppermute | solution.py:35
  34.4 9.6 %collective-permute-start.14 = (bf16[144,512]{1,0:T(8,128)(2,1)S(1)}, bf16[144,512]{1,0:T(8,128)(2,1)S(1)}, u32[]{:S(2)}, u32[]{:S(2)}) collective-permute-start(bf16[144,512]{1,0:T(8,128)(2,1)S(1)} %collective-permute-done.13.refs_14_), channel_id=1, source_target_pairs={{224,0},{0,32},{32,64},{64,96},{96,128},{128,160},{160,192},{192,2... | collective-permute-start | bytes 442376 | tf_op jit(solution)/shard_map/ppermute | solution.py:35
  36.2 7.8 %collective-permute-start.9 = (bf16[144,512]{1,0:T(8,128)(2,1)S(1)}, bf16[144,512]{1,0:T(8,128)(2,1)S(1)}, u32[]{:S(2)}, u32[]{:S(2)}) collective-permute-start(bf16[144,512]{1,0:T(8,128)(2,1)S(1)} %collective-permute-done.7.refs_4_), channel_id=1, source_target_pairs={{32,0},{64,32},{96,64},{128,96},{160,128},{192,160},{224,192},{0,2... | collective-permute-start | bytes 442376 | tf_op jit(solution)/shard_map/ppermute | solution.py:35
  39.6 7.1 %collective-permute-start.4 = (bf16[144,512]{1,0:T(8,128)(2,1)S(1)}, bf16[144,512]{1,0:T(8,128)(2,1)S(1)}, u32[]{:S(2)}, u32[]{:S(2)}) collective-permute-start(bf16[144,512]{1,0:T(8,128)(2,1)S(1)} %get-tuple-element.37.refs_0_), channel_id=1, source_target_pairs={{1,0},{0,1},{3,2},{2,3},{5,4},{4,5},{7,6},{6,7},{9,8},{8,9},{11,10... | collective-permute-start | bytes 442376 | tf_op jit(solution)/shard_map/ppermute | solution.py:35
  43.5 6.4 %collective-permute-start.18 = (bf16[144,512]{1,0:T(8,128)(2,1)S(1)}, bf16[144,512]{1,0:T(8,128)(2,1)S(1)}, u32[]{:S(2)}, u32[]{:S(2)}) collective-permute-start(bf16[144,512]{1,0:T(8,128)(2,1)S(1)} %collective-permute-done.13.refs_14_), channel_id=1, source_target_pairs={{1,0},{0,1},{3,2},{2,3},{5,4},{4,5},{7,6},{6,7},{9,8},{8,9},{11,10... | collective-permute-start | bytes 442376 | tf_op jit(solution)/shard_map/ppermute | solution.py:35
  43.5 6.5 %collective-permute-start.6 = (bf16[144,512]{1,0:T(8,128)(2,1)S(1)}, bf16[144,512]{1,0:T(8,128)(2,1)S(1)}, u32[]{:S(2)}, u32[]{:S(2)}) collective-permute-start(bf16[144,512]{1,0:T(8,128)(2,1)S(1)} %collective-permute-done.5.refs_2_), channel_id=1, source_target_pairs={{1,0},{0,1},{3,2},{2,3},{5,4},{4,5},{7,6},{6,7},{9,8},{8,9},{11,10... | collective-permute-start | bytes 442376 | tf_op jit(solution)/shard_map/ppermute | solution.py:35
  44.0 6.8 %collective-permute-start.15 = (bf16[144,512]{1,0:T(8,128)(2,1)S(1)}, bf16[144,512]{1,0:T(8,128)(2,1)}, u32[]{:S(2)}, u32[]{:S(2)}) collective-permute-start(bf16[144,512]{1,0:T(8,128)(2,1)S(1)} %collective-permute-done.14.refs_12_), channel_id=1, source_target_pairs={{224,0},{0,32},{32,64},{64,96},{96,128},{128,160},{160,192},{192,2... | collective-permute-start | bytes 442376 | tf_op jit(solution)/shard_map/ppermute | solution.py:35
  44.0 7.6 %collective-permute-start.11 = (bf16[144,512]{1,0:T(8,128)(2,1)S(1)}, bf16[144,512]{1,0:T(8,128)(2,1)}, u32[]{:S(2)}, u32[]{:S(2)}) collective-permute-start(bf16[144,512]{1,0:T(8,128)(2,1)S(1)} %collective-permute-done.9.refs_6_), channel_id=1, source_target_pairs={{32,0},{64,32},{96,64},{128,96},{160,128},{192,160},{224,192},{0,2... | collective-permute-start | bytes 442376 | tf_op jit(solution)/shard_map/ppermute | solution.py:35
  46.7 5.9 %collective-permute-start.17 = (bf16[144,512]{1,0:T(8,128)(2,1)S(1)}, bf16[144,512]{1,0:T(8,128)(2,1)}, u32[]{:S(2)}, u32[]{:S(2)}) collective-permute-start(bf16[144,512]{1,0:T(8,128)(2,1)S(1)} %collective-permute-done.14.refs_12_), channel_id=1, source_target_pairs={{1,0},{0,1},{3,2},{2,3},{5,4},{4,5},{7,6},{6,7},{9,8},{8,9},{11,10... | collective-permute-start | bytes 442376 | tf_op jit(solution)/shard_map/ppermute | solution.py:35
  49.9 2.8 %collective-permute-start.8 = (bf16[144,512]{1,0:T(8,128)(2,1)S(1)}, bf16[144,512]{1,0:T(8,128)(2,1)}, u32[]{:S(2)}, u32[]{:S(2)}) collective-permute-start(bf16[144,512]{1,0:T(8,128)(2,1)S(1)} %collective-permute-done.7.refs_4_), channel_id=1, source_target_pairs={{1,0},{0,1},{3,2},{2,3},{5,4},{4,5},{7,6},{6,7},{9,8},{8,9},{11,10... | collective-permute-start | bytes 442376 | tf_op jit(solution)/shard_map/ppermute | solution.py:35
  50.0 3.0 %collective-permute-start.10 = (bf16[144,512]{1,0:T(8,128)(2,1)S(1)}, bf16[144,512]{1,0:T(8,128)(2,1)}, u32[]{:S(2)}, u32[]{:S(2)}) collective-permute-start(bf16[144,512]{1,0:T(8,128)(2,1)S(1)} %collective-permute-done.9.refs_6_), channel_id=1, source_target_pairs={{1,0},{0,1},{3,2},{2,3},{5,4},{4,5},{7,6},{6,7},{9,8},{8,9},{11,10... | collective-permute-start | bytes 442376 | tf_op jit(solution)/shard_map/ppermute | solution.py:35
  50.8 2.1 %collective-permute-start.16 = (bf16[144,512]{1,0:T(8,128)(2,1)}, bf16[144,512]{1,0:T(8,128)(2,1)}, u32[]{:S(2)}, u32[]{:S(2)}) collective-permute-start(bf16[144,512]{1,0:T(8,128)(2,1)} %collective-permute-done.15.refs_10_), channel_id=1, source_target_pairs={{1,0},{0,1},{3,2},{2,3},{5,4},{4,5},{7,6},{6,7},{9,8},{8,9},{11,10... | collective-permute-start | bytes 442376 | tf_op jit(solution)/shard_map/ppermute | solution.py:35
  51.6 2.3 %collective-permute-start.12 = (bf16[144,512]{1,0:T(8,128)(2,1)}, bf16[144,512]{1,0:T(8,128)(2,1)}, u32[]{:S(2)}, u32[]{:S(2)}) collective-permute-start(bf16[144,512]{1,0:T(8,128)(2,1)} %collective-permute-done.11.refs_8_), channel_id=1, source_target_pairs={{1,0},{0,1},{3,2},{2,3},{5,4},{4,5},{7,6},{6,7},{9,8},{8,9},{11,10... | collective-permute-start | bytes 442376 | tf_op jit(solution)/shard_map/ppermute | solution.py:35
  70.0 2.3 %collective-permute-start.19 = (f32[8,8,128]{2,1,0:T(8,128)S(1)}, f32[8,8,128]{2,1,0:T(8,128)S(1)}, u32[]{:S(2)}, u32[]{:S(2)}) collective-permute-start(f32[8,8,128]{2,1,0:T(8,128)S(1)} %get-tuple-element.39), channel_id=1, source_target_pairs={{1,0},{0,1},{3,2},{2,3},{5,4},{4,5},{7,6},{6,7},{9,8},{8,9},{11,10... | collective-permute-start | bytes 98312 | tf_op jit(solution)/shard_map/ppermute | solution.py:35
  72.3 5.9 %collective-permute-start.20 = (f32[8,8,128]{2,1,0:T(8,128)S(1)}, f32[8,8,128]{2,1,0:T(8,128)S(1)}, u32[]{:S(2)}, u32[]{:S(2)}) collective-permute-start(f32[8,8,128]{2,1,0:T(8,128)S(1)} %add.35), channel_id=1, source_target_pairs={{2,0},{0,2},{3,1},{1,3},{6,4},{4,6},{7,5},{5,7},{10,8},{8,10},{11,... | collective-permute-start | bytes 98312 | tf_op jit(solution)/shard_map/ppermute | solution.py:35
  72.6 12.1 %all-to-all-start.1 = ((f32[16,8,128]{2,1,0:T(8,128)}), f32[16,8,128]{2,1,0:T(8,128)S(1)}, u32[]{:S(2)}, u32[]{:S(2)}) async-start(f32[16,8,128]{2,1,0:T(8,128)} %get-tuple-element.40), calls=%async_computation.1 | async-start | bytes 131072 | tf_op jit(solution)/shard_map/all_to_all | solution.py:352
  84.7 13.2 %all-to-all-start.2 = ((f32[8,16,128]{2,1,0:T(8,128)}), f32[8,16,128]{2,1,0:T(8,128)S(1)}, u32[]{:S(2)}, u32[]{:S(2)}) async-start(f32[8,16,128]{2,1,0:T(8,128)} %pad_maximum_fusion), calls=%async_computation.2 | async-start | bytes 131072 | tf_op jit(solution)/shard_map/all_to_all | solution.py:356

commit v10 on v9

--- a/solution.py
+++ b/solution.py
@@ -10,6 +10,7 @@
 
 LOGIT_SCALE = 14.285714285714286
 EPSILON = 1e-06
+LOG2E = math.log2(math.e)
 
 SHARE = 128
 SIDE = 16
@@ -97,13 +98,10 @@
     return (raw * lax.rsqrt(total + EPSILON)).astype(jnp.bfloat16)
 
 
-def finish_kernel(keep2_s, got2_s, keep2_q, got2_q, struct_ext_ref, seq_ext_ref, peers_ref, seq_ref):
+def finish_kernel(keep2_s, got2_s, keep2_q, got2_q, struct_ext_ref, seq_ext_ref, struct_ref, seq_ref):
     struct = normalized(keep2_s, got2_s)
-    turned = struct.astype(jnp.float32).T.astype(jnp.bfloat16)
-    struct_ext = struct_ext_ref[...]
-    for peer in range(SIDE):
-        peers_ref[peer, 0:WIDTH, :] = turned
-        peers_ref[peer, WIDTH:, :] = struct_ext
+    struct_ref[0:WIDTH, :] = struct.astype(jnp.float32).T.astype(jnp.bfloat16)
+    struct_ref[WIDTH:, :] = struct_ext_ref[...]
     seq = normalized(keep2_q, got2_q)
     seq_ref[0:SHARE, :] = seq
     seq_ref[SHARE:, :] = seq_ext_ref[...]
@@ -113,7 +111,7 @@
     return pl.pallas_call(
         finish_kernel,
         out_shape=(
-            jax.ShapeDtypeStruct((SIDE, WIDTH + EXT, SHARE), jnp.bfloat16),
+            jax.ShapeDtypeStruct((WIDTH + EXT, SHARE), jnp.bfloat16),
             jax.ShapeDtypeStruct((SHARE + EXT, WIDTH), jnp.bfloat16),
         ),
         in_specs=[VMEM] * 6,
@@ -195,7 +193,7 @@
                 for group in groups:
                     local = sub * SUB + group * 8
                     product = products[local : local + 8, at]
-                    expo = jnp.exp(product * LOGIT_SCALE)
+                    expo = jnp.exp2(product * (LOGIT_SCALE * LOG2E))
                     fixed = (product * FIXED).astype(jnp.int32)
                     kept = jnp.where(label[group] == col_label, expo, 0.0)
                     row_total[group] += expo
@@ -279,9 +277,8 @@
     )(place, *seq_blocks, struct_blocks)
 
 
-def losses_kernel(place_ref, rows_ref, cols_ref, self_ref, seq_ref, struct_ref, hard_ref):
-    rows = jnp.sum(rows_ref[...], axis=0)
-    own, other = rows[0:8], rows[8:16]
+def losses_kernel(place_ref, rows_ref, other_ref, cols_ref, self_ref, seq_ref, struct_ref, hard_ref):
+    own, other = rows_ref[...], other_ref[...]
     lower, upper = (place_ref[0] == 0), (place_ref[0] == 1)
     for place, held in ((0, jnp.where(lower, own, other)), (1, jnp.where(upper, own, other))):
         for core in range(2):
@@ -294,7 +291,7 @@
     hard_ref[...] = jnp.log(jnp.exp(self_logits) + extra) - self_logits
 
 
-def losses(place, rows, cols, self_dot):
+def losses(place, rows, other_rows, cols, self_dot):
     return pl.pallas_call(
         losses_kernel,
         out_shape=(
@@ -302,11 +299,11 @@
             jax.ShapeDtypeStruct((1, SHARE), jnp.float32),
             jax.ShapeDtypeStruct((1, SHARE), jnp.float32),
         ),
-        in_specs=[SMEM, VMEM, VMEM, VMEM],
+        in_specs=[SMEM, VMEM, VMEM, VMEM, VMEM],
         out_specs=(VMEM, VMEM, VMEM),
         compiler_params=pltpu.CompilerParams(vmem_limit_bytes=4 * 1024 * 1024),
         name="losses",
-    )(place, rows, cols, self_dot)
+    )(place, rows, other_rows, cols, self_dot)
 
 
 def over_z(block):
@@ -344,17 +341,17 @@
     seq_ext = jnp.concatenate([high, low, wide(labels >> 7), wide(labels & 127)], axis=1).astype(jnp.bfloat16)
     struct_ext = jnp.concatenate([wide(labels >> 7)[0:8], wide(labels & 127)[0:8]], axis=0).astype(jnp.bfloat16)
 
-    struct_peers, seq_block = finish(keep2_s, got2_s, keep2_q, got2_q, struct_ext, seq_ext)
+    struct_block, seq_block = finish(keep2_s, got2_s, keep2_q, got2_q, struct_ext, seq_ext)
+    struct_peers = jnp.broadcast_to(struct_block[None], (SIDE, *struct_block.shape))
     struct_blocks = lax.all_to_all(struct_peers, COL_AXES, split_axis=0, concat_axis=0, tiled=True)
     seq_blocks = [each for held in over_z(seq_block) for each in (held, shifted(held, "core", 1))]
 
     rows, cols, self_dot = pair_sums(jnp.stack([place("z"), core, place(COL_AXES)]), seq_blocks, struct_blocks)
+    rows = jnp.sum(lax.all_to_all(rows, "z", split_axis=0, concat_axis=0, tiled=True), axis=0)
     cols = lax.all_to_all(cols, COL_AXES, split_axis=0, concat_axis=0, tiled=True)
     rows = rows + shifted(rows, "core", 1)
-    rows = jnp.concatenate([rows, shifted(rows, "yl", 1)], axis=1)
-    rows, cols = lax.optimization_barrier((rows, cols))
-    rows = lax.all_to_all(rows, "z", split_axis=0, concat_axis=0, tiled=True)
-    seq_loss, struct_loss, hard_loss = losses(jnp.stack([yl, core]), rows, cols, self_dot)
+    other_rows = shifted(rows, "yl", 1)
+    seq_loss, struct_loss, hard_loss = losses(jnp.stack([yl, core]), rows, other_rows, cols, self_dot)
     return (seq_loss.reshape(4 * SHARE), struct_loss.reshape(SHARE), hard_loss.reshape(SHARE))
 
 

time: 100 us -> 98.9 us (0.989)
  blocking collectives: 0 us -> 14.9 us
  waiting for transfers between devices: 26.2 us -> 17.1 us
  starting transfers between devices: 46.6 us -> 41.2 us
    all_to_all x0 -> x1, blocking collectives: none -> 14.9 us  [per_device(): lax.all_to_all(rows, 'z', split_axis=0, concat_axis=0, tiled=True)]
    all_to_all x1 -> x0, waiting for transfers between devices: 7.15 us -> none  [per_device(): rows = lax.all_to_all(rows, 'z', split_axis=0, concat_axis=0, tiled=True)]
    all_to_all x1 -> x0, starting transfers between devices: 6.02 us -> none  [per_device(): rows = lax.all_to_all(rows, 'z', split_axis=0, concat_axis=0, tiled=True)]
    ppermute x21, starting transfers between devices: 29.9 us -> 32.7 us  [shifted(): lax.ppermute(value, axes, [((place + steps) % count, place) for place in...]
    all_to_all x1, starting transfers between devices: 5.62 us -> 3.48 us  [per_device(): lax.all_to_all(cols, COL_AXES, split_axis=0, concat_axis=0, tiled=True)]
    broadcast_in_dim x0 -> x1, local copies, waits for them, and re-layouts: none -> 1.65 us  [per_device(): jnp.broadcast_to(struct_block[None], (SIDE, *struct_block.shape))]
    ppermute x21, waiting for transfers between devices: 12.4 us -> 11.1 us  [shifted(): lax.ppermute(value, axes, [((place + steps) % count, place) for place in...]
    unnamed x14 -> x12, local copies, waits for them, and re-layouts: 5.2 us -> 3.85 us
  transfers between devices with their start and end apart: 24 -> 23, of which waited for: 13 -> 11; matrix products, arithmetic and copies ran while one was open for 2% -> 2% of each run, Pallas kernels for 1% -> 0%
where the time goes in v10:
time: 98.9 us; the launch traced here: 98.5 us
  starting transfers between devices  41.2 us (42%)
  Pallas kernels  17.3 us (17%)
  waiting for transfers between devices  17.1 us (17%)
  blocking collectives  14.9 us (15%)
  local copies, waits for them, and re-layouts  5.53 us (6%)
  other arithmetic  1.65 us (2%)
    ppermute x21, starting transfers between devices, shifted(): lax.ppermute(value, axes, [((place + steps) % count, place) for place in...  32.7 us
    all_to_all x1, blocking collectives, per_device(): lax.all_to_all(rows, 'z', split_axis=0, concat_axis=0, tiled=True)  14.9 us
    pallas_call x1, Pallas kernels, pair_sums(): pl.pallas_call(pair_kernel, out_shape=(jax.ShapeDtypeStruct((8, 8, SHARE)...  14.7 us
    ppermute x21, waiting for transfers between devices, shifted(): lax.ppermute(value, axes, [((place + steps) % count, place) for place in...  11.1 us
    all_to_all x1, starting transfers between devices, per_device(): lax.all_to_all(struct_peers, COL_AXES, split_axis=0, concat_axis=0, tiled...  5.07 us
    all_to_all x1, waiting for transfers between devices, per_device(): lax.all_to_all(cols, COL_AXES, split_axis=0, concat_axis=0, tiled=True)  5.02 us
    unnamed x12, local copies, waits for them, and re-layouts  3.85 us
    all_to_all x1, starting transfers between devices, per_device(): lax.all_to_all(cols, COL_AXES, split_axis=0, concat_axis=0, tiled=True)  3.48 us
  transfers between devices with their start and end apart: 23, of which 11 were waited for; matrix products, arithmetic and copies ran while one was open for 2% of the time, Pallas kernels for 0%

profile of v10, /device:TPU:1, one launch (start us, length us, event | category | flops | bytes accessed | tf_op | source)
XLA Modules:
  0.0 98.5 jit_solution(17149597468823557128)
XLA Ops:
  0.7 1.0 copy-done
  1.6 1.0 copy-done.1
  2.6 0.7 project_seq.1
  3.3 3.3 %collective-permute-start.2 = (f32[2,128,512]{2,1,0:T(8,128)S(1)}, f32[2,128,512]{2,1,0:T(8,128)S(1)}, u32[]{:S(2)}, u32[]{:S(2)}) collective-permute-start(f32[2,128,512]{2,1,0:T(8,128)S(1)} %get-tuple-element.28), channel_id=1, source_target_pairs={{1,0},{0,1},{3,2},{2,3},{5,4},{4,5},{7,6},{6,7},{9,8},{8,9},{11,10... | collective-permute-start | bytes 1572872 | tf_op jit(solution)/shard_map/ppermute | solution.py:36
  6.6 0.9 copy-done.2
  7.6 0.9 copy-done.3
  9.2 0.8 shift-right-arithmetic_convert_fusion
  10.0 0.9 collective-permute-done.got_ref
  11.6 0.7 fusion.5
  12.4 1.4 %collective-permute-done.3.got2_q = bf16[128,512]{1,0:T(8,128)(2,1)S(1)} collective-permute-done((bf16[128,512]{1,0:T(8,128)(2,1)S(1)}, bf16[128,512]{1,0:T(8,128)(2,1)S(1)}, u32[]{:S(2)}, u32[]{:S(2)}) %collective-permute-start.3) | collective-permute-done | bytes 131104 | tf_op jit(solution)/shard_map/ppermute | solution.py:36
  13.8 2.8 %collective-permute-done.1.got2_s = bf16[128,512]{1,0:T(8,128)(2,1)S(1)} collective-permute-done((bf16[128,512]{1,0:T(8,128)(2,1)S(1)}, bf16[128,512]{1,0:T(8,128)(2,1)S(1)}, u32[]{:S(2)}, u32[]{:S(2)}) %collective-permute-start.1) | collective-permute-done | bytes 131104 | tf_op jit(solution)/shard_map/ppermute | solution.py:36
  16.8 1.7 %broadcast_in_dim.13 = bf16[16,528,128]{2,1,0:T(8,128)(2,1)} broadcast(bf16[528,128]{1,0:T(8,128)(2,1)S(1)} %get-tuple-element.36), dimensions={1,2} | broadcast | bytes 2297856 | tf_op jit(solution)/shard_map/broadcast_in_dim | solution.py:345
  18.5 5.1 %all-to-all-start = ((bf16[16,528,128]{2,1,0:T(8,128)(2,1)}), bf16[16,528,128]{2,1,0:T(8,128)(2,1)S(1)}, u32[]{:S(2)}, u32[]{:S(2)}) async-start(bf16[16,528,128]{2,1,0:T(8,128)(2,1)} %broadcast_in_dim.13), calls=%async_computation | async-start | bytes 4325376 | tf_op jit(solution)/shard_map/all_to_all | solution.py:346
  23.5 5.6 %collective-permute-start.5 = (bf16[144,512]{1,0:T(8,128)(2,1)S(1)}, bf16[144,512]{1,0:T(8,128)(2,1)S(1)}, u32[]{:S(2)}, u32[]{:S(2)}) collective-permute-start(bf16[144,512]{1,0:T(8,128)(2,1)S(1)} %get-tuple-element.35.refs_0_), channel_id=1, source_target_pairs={{32,0},{64,32},{96,64},{128,96},{160,128},{192,160},{224,192},{0,2... | collective-permute-start | bytes 442376 | tf_op jit(solution)/shard_map/ppermute | solution.py:36
  29.2 2.1 %collective-permute-done.5.refs_2_ = bf16[144,512]{1,0:T(8,128)(2,1)S(1)} collective-permute-done((bf16[144,512]{1,0:T(8,128)(2,1)S(1)}, bf16[144,512]{1,0:T(8,128)(2,1)S(1)}, u32[]{:S(2)}, u32[]{:S(2)}) %collective-permute-start.5) | collective-permute-done | bytes 147488 | tf_op jit(solution)/shard_map/ppermute | solution.py:36
  31.3 3.1 %collective-permute-start.7 = (bf16[144,512]{1,0:T(8,128)(2,1)S(1)}, bf16[144,512]{1,0:T(8,128)(2,1)S(1)}, u32[]{:S(2)}, u32[]{:S(2)}) collective-permute-start(bf16[144,512]{1,0:T(8,128)(2,1)S(1)} %collective-permute-done.5.refs_2_), channel_id=1, source_target_pairs={{32,0},{64,32},{96,64},{128,96},{160,128},{192,160},{224,192},{0,2... | collective-permute-start | bytes 442376 | tf_op jit(solution)/shard_map/ppermute | solution.py:36
  34.7 1.8 %collective-permute-done.7.refs_4_ = bf16[144,512]{1,0:T(8,128)(2,1)S(1)} collective-permute-done((bf16[144,512]{1,0:T(8,128)(2,1)S(1)}, bf16[144,512]{1,0:T(8,128)(2,1)S(1)}, u32[]{:S(2)}, u32[]{:S(2)}) %collective-permute-start.7) | collective-permute-done | bytes 147488 | tf_op jit(solution)/shard_map/ppermute | solution.py:36
  36.5 3.4 %collective-permute-start.9 = (bf16[144,512]{1,0:T(8,128)(2,1)S(1)}, bf16[144,512]{1,0:T(8,128)(2,1)S(1)}, u32[]{:S(2)}, u32[]{:S(2)}) collective-permute-start(bf16[144,512]{1,0:T(8,128)(2,1)S(1)} %collective-permute-done.7.refs_4_), channel_id=1, source_target_pairs={{32,0},{64,32},{96,64},{128,96},{160,128},{192,160},{224,192},{0,2... | collective-permute-start | bytes 442376 | tf_op jit(solution)/shard_map/ppermute | solution.py:36
  39.9 3.8 %collective-permute-start.4 = (bf16[144,512]{1,0:T(8,128)(2,1)S(1)}, bf16[144,512]{1,0:T(8,128)(2,1)S(1)}, u32[]{:S(2)}, u32[]{:S(2)}) collective-permute-start(bf16[144,512]{1,0:T(8,128)(2,1)S(1)} %get-tuple-element.35.refs_0_), channel_id=1, source_target_pairs={{1,0},{0,1},{3,2},{2,3},{5,4},{4,5},{7,6},{6,7},{9,8},{8,9},{11,10... | collective-permute-start | bytes 442376 | tf_op jit(solution)/shard_map/ppermute | solution.py:36
  44.3 2.7 %collective-permute-start.11 = (bf16[144,512]{1,0:T(8,128)(2,1)S(1)}, bf16[144,512]{1,0:T(8,128)(2,1)}, u32[]{:S(2)}, u32[]{:S(2)}) collective-permute-start(bf16[144,512]{1,0:T(8,128)(2,1)S(1)} %collective-permute-done.9.refs_6_), channel_id=1, source_target_pairs={{32,0},{64,32},{96,64},{128,96},{160,128},{192,160},{224,192},{0,2... | collective-permute-start | bytes 442376 | tf_op jit(solution)/shard_map/ppermute | solution.py:36
  46.9 3.2 %collective-permute-start.17 = (bf16[144,512]{1,0:T(8,128)(2,1)S(1)}, bf16[144,512]{1,0:T(8,128)(2,1)}, u32[]{:S(2)}, u32[]{:S(2)}) collective-permute-start(bf16[144,512]{1,0:T(8,128)(2,1)S(1)} %collective-permute-done.14.refs_12_), channel_id=1, source_target_pairs={{1,0},{0,1},{3,2},{2,3},{5,4},{4,5},{7,6},{6,7},{9,8},{8,9},{11,10... | collective-permute-start | bytes 442376 | tf_op jit(solution)/shard_map/ppermute | solution.py:36
  51.0 0.8 collective-permute-start.16
  51.8 0.9 collective-permute-start.12
  53.2 0.9 collective-permute-done.12.refs_9_
  54.1 1.0 all-to-all-done.refs_16_
  55.1 14.7 %pair_sums.1 = (f32[8,8,128]{2,1,0:T(8,128)S(1)}, f32[16,8,128]{2,1,0:T(8,128)}, f32[8,128]{1,0:T(8,128)S(1)}) custom-call(s32[3]{0:T(128)S(1)} %pad_add_fusion.1.place_ref, bf16[144,512]{1,0:T(8,128)(2,1)S(1)} %get-tuple-element.35.refs_0_, bf16[144,512]{1,0:T(8,128)(2,1)S(1)} %collective-permute-done.4.refs_1_, ...), custom_call_target="tpu_custom_call" | custom-call | flops 4294967296 | bytes 4194304 | tf_op jit(solution)/shard_map/pair_sums/pallas_call | solution.py:250
  69.8 14.9 %all_to_all.15 = f32[8,8,128]{2,1,0:T(8,128)S(1)} all-to-all(f32[8,8,128]{2,1,0:T(8,128)S(1)} %get-tuple-element.37), channel_id=1, replica_groups=mesh['z'=8,'yh'=2,'x'=4,'yl'=2,'core'=2] {'z'}, dimensions={0} | all-to-all | bytes 65536 | tf_op jit(solution)/shard_map/all_to_all | solution.py:350
  84.8 2.6 %collective-permute-start.19 = (f32[8,128]{1,0:T(8,128)S(1)}, f32[8,128]{1,0:T(8,128)S(1)}, u32[]{:S(2)}, u32[]{:S(2)}) collective-permute-start(f32[8,128]{1,0:T(8,128)S(1)} %reduce_sum.9), channel_id=1, source_target_pairs={{1,0},{0,1},{3,2},{2,3},{5,4},{4,5},{7,6},{6,7},{9,8},{8,9},{11,10... | collective-permute-start | bytes 12296 | tf_op jit(solution)/shard_map/ppermute | solution.py:36
  87.4 3.5 %all-to-all-start.2 = ((f32[16,8,128]{2,1,0:T(8,128)}), f32[16,8,128]{2,1,0:T(8,128)S(1)}, u32[]{:S(2)}, u32[]{:S(2)}) async-start(f32[16,8,128]{2,1,0:T(8,128)} %get-tuple-element.38), calls=%async_computation.2 | async-start | bytes 131072 | tf_op jit(solution)/shard_map/all_to_all | solution.py:351
  90.9 1.3 %collective-permute-start.20 = (f32[8,128]{1,0:T(8,128)S(1)}, f32[8,128]{1,0:T(8,128)S(1)}, u32[]{:S(2)}, u32[]{:S(2)}) collective-permute-start(f32[8,128]{1,0:T(8,128)S(1)} %add.35.rows_ref), channel_id=1, source_target_pairs={{2,0},{0,2},{3,1},{1,3},{6,4},{4,6},{7,5},{5,7},{10,8},{8,10},{11,... | collective-permute-start | bytes 12296 | tf_op jit(solution)/shard_map/ppermute | solution.py:36
  92.3 5.0 %all-to-all-done.2.cols_ref = f32[16,8,128]{2,1,0:T(8,128)S(1)} async-done(((f32[16,8,128]{2,1,0:T(8,128)}), f32[16,8,128]{2,1,0:T(8,128)S(1)}, u32[]{:S(2)}, u32[]{:S(2)}) %all-to-all-start.2) | async-done | bytes 65568 | tf_op jit(solution)/shard_map/all_to_all | solution.py:351
  97.4 1.1 %losses.1 = (f32[4,128]{1,0:T(4,128)}, f32[1,128]{1,0:T(1,128)}, f32[1,128]{1,0:T(1,128)}) custom-call(s32[2]{0:T(128)S(1)} %pad_add_fusion.place_ref, f32[8,128]{1,0:T(8,128)S(1)} %add.35.rows_ref, f32[8,128]{1,0:T(8,128)S(1)} %collective-permute-done.20.other_ref, f32[16,8,128]{2,1,0:T(8,128)S(1)} %all-to-all-done.2.cols_ref, ...), custom_call_target="tpu_custom_call" | custom-call | tf_op jit(solution)/shard_map/losses/pallas_call | solution.py:295
  (48 shorter events, 3.9 us)
Async XLA Ops:
  0.6 11.0 %copy-start.5 = (s32[128,16]{0,1:T(8,128)S(1)}, s32[128,16]{0,1:T(8,128)}, u32[]{:S(2)}) copy-start(s32[128,16]{0,1:T(8,128)} %param.15) | copy-start | bytes 24580
  0.6 1.0 copy-start
  1.6 1.0 copy-start.1
  2.6 6.6 %copy-start.4 = (s32[512,16,1]{0,2,1:T(1,128)S(1)}, s32[512,16,1]{0,2,1:T(1,128)}, u32[]{:S(2)}) copy-start(s32[512,16,1]{0,2,1:T(1,128)} %param.13) | copy-start | bytes 98308
  3.3 5.7 %collective-permute-start.2 = (f32[2,128,512]{2,1,0:T(8,128)S(1)}, f32[2,128,512]{2,1,0:T(8,128)S(1)}, u32[]{:S(2)}, u32[]{:S(2)}) collective-permute-start(f32[2,128,512]{2,1,0:T(8,128)S(1)} %get-tuple-element.28), channel_id=1, source_target_pairs={{1,0},{0,1},{3,2},{2,3},{5,4},{4,5},{7,6},{6,7},{9,8},{8,9},{11,10... | collective-permute-start | bytes 1572872 | tf_op jit(solution)/shard_map/ppermute | solution.py:36
  6.6 0.9 copy-start.2
  7.6 0.9 copy-start.3
  8.9 2.0 %collective-permute-start = (f32[2,128,512]{2,1,0:T(8,128)S(1)}, f32[2,128,512]{2,1,0:T(8,128)S(1)}, u32[]{:S(2)}, u32[]{:S(2)}) collective-permute-start(f32[2,128,512]{2,1,0:T(8,128)S(1)} %get-tuple-element.24), channel_id=1, source_target_pairs={{1,0},{0,1},{3,2},{2,3},{5,4},{4,5},{7,6},{6,7},{9,8},{8,9},{11,10... | collective-permute-start | bytes 1572872 | tf_op jit(solution)/shard_map/ppermute | solution.py:36
  9.1 4.7 %collective-permute-start.3 = (bf16[128,512]{1,0:T(8,128)(2,1)S(1)}, bf16[128,512]{1,0:T(8,128)(2,1)S(1)}, u32[]{:S(2)}, u32[]{:S(2)}) collective-permute-start(bf16[128,512]{1,0:T(8,128)(2,1)S(1)} %get-tuple-element.30), channel_id=1, source_target_pairs={{2,0},{0,2},{3,1},{1,3},{6,4},{4,6},{7,5},{5,7},{10,8},{8,10},{11,... | collective-permute-start | bytes 393224 | tf_op jit(solution)/shard_map/ppermute | solution.py:36
  11.0 5.6 %collective-permute-start.1 = (bf16[128,512]{1,0:T(8,128)(2,1)S(1)}, bf16[128,512]{1,0:T(8,128)(2,1)S(1)}, u32[]{:S(2)}, u32[]{:S(2)}) collective-permute-start(bf16[128,512]{1,0:T(8,128)(2,1)S(1)} %get-tuple-element.26), channel_id=1, source_target_pairs={{2,0},{0,2},{3,1},{1,3},{6,4},{4,6},{7,5},{5,7},{10,8},{8,10},{11,... | collective-permute-start | bytes 393224 | tf_op jit(solution)/shard_map/ppermute | solution.py:36
  18.5 36.6 %all-to-all-start = ((bf16[16,528,128]{2,1,0:T(8,128)(2,1)}), bf16[16,528,128]{2,1,0:T(8,128)(2,1)S(1)}, u32[]{:S(2)}, u32[]{:S(2)}) async-start(bf16[16,528,128]{2,1,0:T(8,128)(2,1)} %broadcast_in_dim.13), calls=%async_computation | async-start | bytes 4325376 | tf_op jit(solution)/shard_map/all_to_all | solution.py:346
  23.5 7.8 %collective-permute-start.5 = (bf16[144,512]{1,0:T(8,128)(2,1)S(1)}, bf16[144,512]{1,0:T(8,128)(2,1)S(1)}, u32[]{:S(2)}, u32[]{:S(2)}) collective-permute-start(bf16[144,512]{1,0:T(8,128)(2,1)S(1)} %get-tuple-element.35.refs_0_), channel_id=1, source_target_pairs={{32,0},{64,32},{96,64},{128,96},{160,128},{192,160},{224,192},{0,2... | collective-permute-start | bytes 442376 | tf_op jit(solution)/shard_map/ppermute | solution.py:36
  29.2 5.5 %collective-permute-start.13 = (bf16[144,512]{1,0:T(8,128)(2,1)S(1)}, bf16[144,512]{1,0:T(8,128)(2,1)S(1)}, u32[]{:S(2)}, u32[]{:S(2)}) collective-permute-start(bf16[144,512]{1,0:T(8,128)(2,1)S(1)} %get-tuple-element.35.refs_0_), channel_id=1, source_target_pairs={{224,0},{0,32},{32,64},{64,96},{96,128},{128,160},{160,192},{192,2... | collective-permute-start | bytes 442376 | tf_op jit(solution)/shard_map/ppermute | solution.py:36
  31.3 5.2 %collective-permute-start.7 = (bf16[144,512]{1,0:T(8,128)(2,1)S(1)}, bf16[144,512]{1,0:T(8,128)(2,1)S(1)}, u32[]{:S(2)}, u32[]{:S(2)}) collective-permute-start(bf16[144,512]{1,0:T(8,128)(2,1)S(1)} %collective-permute-done.5.refs_2_), channel_id=1, source_target_pairs={{32,0},{64,32},{96,64},{128,96},{160,128},{192,160},{224,192},{0,2... | collective-permute-start | bytes 442376 | tf_op jit(solution)/shard_map/ppermute | solution.py:36
  34.7 9.5 %collective-permute-start.14 = (bf16[144,512]{1,0:T(8,128)(2,1)S(1)}, bf16[144,512]{1,0:T(8,128)(2,1)S(1)}, u32[]{:S(2)}, u32[]{:S(2)}) collective-permute-start(bf16[144,512]{1,0:T(8,128)(2,1)S(1)} %collective-permute-done.13.refs_14_), channel_id=1, source_target_pairs={{224,0},{0,32},{32,64},{64,96},{96,128},{128,160},{160,192},{192,2... | collective-permute-start | bytes 442376 | tf_op jit(solution)/shard_map/ppermute | solution.py:36
  36.5 7.7 %collective-permute-start.9 = (bf16[144,512]{1,0:T(8,128)(2,1)S(1)}, bf16[144,512]{1,0:T(8,128)(2,1)S(1)}, u32[]{:S(2)}, u32[]{:S(2)}) collective-permute-start(bf16[144,512]{1,0:T(8,128)(2,1)S(1)} %collective-permute-done.7.refs_4_), channel_id=1, source_target_pairs={{32,0},{64,32},{96,64},{128,96},{160,128},{192,160},{224,192},{0,2... | collective-permute-start | bytes 442376 | tf_op jit(solution)/shard_map/ppermute | solution.py:36
  39.9 7.0 %collective-permute-start.4 = (bf16[144,512]{1,0:T(8,128)(2,1)S(1)}, bf16[144,512]{1,0:T(8,128)(2,1)S(1)}, u32[]{:S(2)}, u32[]{:S(2)}) collective-permute-start(bf16[144,512]{1,0:T(8,128)(2,1)S(1)} %get-tuple-element.35.refs_0_), channel_id=1, source_target_pairs={{1,0},{0,1},{3,2},{2,3},{5,4},{4,5},{7,6},{6,7},{9,8},{8,9},{11,10... | collective-permute-start | bytes 442376 | tf_op jit(solution)/shard_map/ppermute | solution.py:36
  43.7 6.4 %collective-permute-start.18 = (bf16[144,512]{1,0:T(8,128)(2,1)S(1)}, bf16[144,512]{1,0:T(8,128)(2,1)S(1)}, u32[]{:S(2)}, u32[]{:S(2)}) collective-permute-start(bf16[144,512]{1,0:T(8,128)(2,1)S(1)} %collective-permute-done.13.refs_14_), channel_id=1, source_target_pairs={{1,0},{0,1},{3,2},{2,3},{5,4},{4,5},{7,6},{6,7},{9,8},{8,9},{11,10... | collective-permute-start | bytes 442376 | tf_op jit(solution)/shard_map/ppermute | solution.py:36
  43.7 6.5 %collective-permute-start.6 = (bf16[144,512]{1,0:T(8,128)(2,1)S(1)}, bf16[144,512]{1,0:T(8,128)(2,1)S(1)}, u32[]{:S(2)}, u32[]{:S(2)}) collective-permute-start(bf16[144,512]{1,0:T(8,128)(2,1)S(1)} %collective-permute-done.5.refs_2_), channel_id=1, source_target_pairs={{1,0},{0,1},{3,2},{2,3},{5,4},{4,5},{7,6},{6,7},{9,8},{8,9},{11,10... | collective-permute-start | bytes 442376 | tf_op jit(solution)/shard_map/ppermute | solution.py:36
  44.2 6.8 %collective-permute-start.15 = (bf16[144,512]{1,0:T(8,128)(2,1)S(1)}, bf16[144,512]{1,0:T(8,128)(2,1)}, u32[]{:S(2)}, u32[]{:S(2)}) collective-permute-start(bf16[144,512]{1,0:T(8,128)(2,1)S(1)} %collective-permute-done.14.refs_12_), channel_id=1, source_target_pairs={{224,0},{0,32},{32,64},{64,96},{96,128},{128,160},{160,192},{192,2... | collective-permute-start | bytes 442376 | tf_op jit(solution)/shard_map/ppermute | solution.py:36
  44.3 7.6 %collective-permute-start.11 = (bf16[144,512]{1,0:T(8,128)(2,1)S(1)}, bf16[144,512]{1,0:T(8,128)(2,1)}, u32[]{:S(2)}, u32[]{:S(2)}) collective-permute-start(bf16[144,512]{1,0:T(8,128)(2,1)S(1)} %collective-permute-done.9.refs_6_), channel_id=1, source_target_pairs={{32,0},{64,32},{96,64},{128,96},{160,128},{192,160},{224,192},{0,2... | collective-permute-start | bytes 442376 | tf_op jit(solution)/shard_map/ppermute | solution.py:36
  46.9 5.9 %collective-permute-start.17 = (bf16[144,512]{1,0:T(8,128)(2,1)S(1)}, bf16[144,512]{1,0:T(8,128)(2,1)}, u32[]{:S(2)}, u32[]{:S(2)}) collective-permute-start(bf16[144,512]{1,0:T(8,128)(2,1)S(1)} %collective-permute-done.14.refs_12_), channel_id=1, source_target_pairs={{1,0},{0,1},{3,2},{2,3},{5,4},{4,5},{7,6},{6,7},{9,8},{8,9},{11,10... | collective-permute-start | bytes 442376 | tf_op jit(solution)/shard_map/ppermute | solution.py:36
  50.1 2.8 %collective-permute-start.8 = (bf16[144,512]{1,0:T(8,128)(2,1)S(1)}, bf16[144,512]{1,0:T(8,128)(2,1)}, u32[]{:S(2)}, u32[]{:S(2)}) collective-permute-start(bf16[144,512]{1,0:T(8,128)(2,1)S(1)} %collective-permute-done.7.refs_4_), channel_id=1, source_target_pairs={{1,0},{0,1},{3,2},{2,3},{5,4},{4,5},{7,6},{6,7},{9,8},{8,9},{11,10... | collective-permute-start | bytes 442376 | tf_op jit(solution)/shard_map/ppermute | solution.py:36
  50.2 2.7 %collective-permute-start.10 = (bf16[144,512]{1,0:T(8,128)(2,1)S(1)}, bf16[144,512]{1,0:T(8,128)(2,1)}, u32[]{:S(2)}, u32[]{:S(2)}) collective-permute-start(bf16[144,512]{1,0:T(8,128)(2,1)S(1)} %collective-permute-done.9.refs_6_), channel_id=1, source_target_pairs={{1,0},{0,1},{3,2},{2,3},{5,4},{4,5},{7,6},{6,7},{9,8},{8,9},{11,10... | collective-permute-start | bytes 442376 | tf_op jit(solution)/shard_map/ppermute | solution.py:36
  51.0 2.1 %collective-permute-start.16 = (bf16[144,512]{1,0:T(8,128)(2,1)}, bf16[144,512]{1,0:T(8,128)(2,1)}, u32[]{:S(2)}, u32[]{:S(2)}) collective-permute-start(bf16[144,512]{1,0:T(8,128)(2,1)} %collective-permute-done.15.refs_10_), channel_id=1, source_target_pairs={{1,0},{0,1},{3,2},{2,3},{5,4},{4,5},{7,6},{6,7},{9,8},{8,9},{11,10... | collective-permute-start | bytes 442376 | tf_op jit(solution)/shard_map/ppermute | solution.py:36
  51.8 2.3 %collective-permute-start.12 = (bf16[144,512]{1,0:T(8,128)(2,1)}, bf16[144,512]{1,0:T(8,128)(2,1)}, u32[]{:S(2)}, u32[]{:S(2)}) collective-permute-start(bf16[144,512]{1,0:T(8,128)(2,1)} %collective-permute-done.11.refs_8_), channel_id=1, source_target_pairs={{1,0},{0,1},{3,2},{2,3},{5,4},{4,5},{7,6},{6,7},{9,8},{8,9},{11,10... | collective-permute-start | bytes 442376 | tf_op jit(solution)/shard_map/ppermute | solution.py:36
  84.8 6.1 %collective-permute-start.19 = (f32[8,128]{1,0:T(8,128)S(1)}, f32[8,128]{1,0:T(8,128)S(1)}, u32[]{:S(2)}, u32[]{:S(2)}) collective-permute-start(f32[8,128]{1,0:T(8,128)S(1)} %reduce_sum.9), channel_id=1, source_target_pairs={{1,0},{0,1},{3,2},{2,3},{5,4},{4,5},{7,6},{6,7},{9,8},{8,9},{11,10... | collective-permute-start | bytes 12296 | tf_op jit(solution)/shard_map/ppermute | solution.py:36
  87.4 9.9 %all-to-all-start.2 = ((f32[16,8,128]{2,1,0:T(8,128)}), f32[16,8,128]{2,1,0:T(8,128)S(1)}, u32[]{:S(2)}, u32[]{:S(2)}) async-start(f32[16,8,128]{2,1,0:T(8,128)} %get-tuple-element.38), calls=%async_computation.2 | async-start | bytes 131072 | tf_op jit(solution)/shard_map/all_to_all | solution.py:351
  90.9 6.4 %collective-permute-start.20 = (f32[8,128]{1,0:T(8,128)S(1)}, f32[8,128]{1,0:T(8,128)S(1)}, u32[]{:S(2)}, u32[]{:S(2)}) collective-permute-start(f32[8,128]{1,0:T(8,128)S(1)} %add.35.rows_ref), channel_id=1, source_target_pairs={{2,0},{0,2},{3,1},{1,3},{6,4},{4,6},{7,5},{5,7},{10,8},{8,10},{11,... | collective-permute-start | bytes 12296 | tf_op jit(solution)/shard_map/ppermute | solution.py:36

commit v11 on v10

--- a/solution.py
+++ b/solution.py
@@ -36,40 +36,43 @@
     return lax.ppermute(value, axes, [((place + steps) % count, place) for place in range(count)])
 
 
-def project_kernel(core_ref, feats_hbm, proj_hbm, keep_ref, send_ref, feats_ref, proj_ref, sems, *, turned):
+def project_kernel(core_ref, struct_hbm, ws_hbm, seq_hbm, wq_hbm, *refs):
     core = core_ref[0]
-    copies = [
-        pltpu.make_async_copy(feats_hbm, feats_ref, sems.at[0]),
-        pltpu.make_async_copy(proj_hbm, proj_ref, sems.at[1]),
-    ]
+    keep_s, send_s, keep_q, send_q, struct_ref, ws_ref, seq_ref, wq_ref, sems = refs
+    held = ((struct_hbm, struct_ref), (ws_hbm, ws_ref), (seq_hbm, seq_ref), (wq_hbm, wq_ref))
+    copies = [pltpu.make_async_copy(source, target, sems.at[place]) for place, (source, target) in enumerate(held)]
     for copy in copies:
         copy.start()
-    for copy in copies:
-        copy.wait()
-    for out, which in ((send_ref, 1 - core), (keep_ref, core)):
+    rows_of = lambda half, which: pl.ds(pl.multiple_of((half * 2 + which) * SHARE, SHARE), SHARE)
+    copies[0].wait()
+    copies[1].wait()
+    for out, which in ((send_s, 1 - core), (keep_s, core)):
         for half in range(2):
-            rows = pl.ds(pl.multiple_of((half * 2 + which) * SHARE, SHARE), SHARE)
-            feats, over = (feats_ref[:, rows], 0) if turned else (feats_ref[rows, :], 1)
+            out[half] = jnp.dot(struct_ref[rows_of(half, which), :], ws_ref[...], preferred_element_type=jnp.float32)
+    copies[2].wait()
+    copies[3].wait()
+    for out, which in ((send_q, 1 - core), (keep_q, core)):
+        for half in range(2):
             out[half] = lax.dot_general(
-                feats, proj_ref[...], (((over,), (0,)), ((), ())), preferred_element_type=jnp.float32
+                seq_ref[:, rows_of(half, which)],
+                wq_ref[...],
+                (((0,), (0,)), ((), ())),
+                preferred_element_type=jnp.float32,
             )
 
 
-def project(core, feats, proj, turned, name):
+def project(core, struct_feats, struct_proj, seq_feats_turned, seq_proj):
     shape = jax.ShapeDtypeStruct((2, SHARE, WIDTH), jnp.float32)
-    return pl.pallas_call(
-        functools.partial(project_kernel, turned=turned),
-        out_shape=(shape, shape),
-        in_specs=[SMEM, HBM, HBM],
-        out_specs=(VMEM, VMEM),
-        scratch_shapes=[
-            pltpu.VMEM(feats.shape, feats.dtype),
-            pltpu.VMEM(proj.shape, proj.dtype),
-            pltpu.SemaphoreType.DMA((2,)),
-        ],
-        compiler_params=pltpu.CompilerParams(vmem_limit_bytes=12 * 1024 * 1024),
-        name=name,
-    )(core, feats, proj)
+    held = (struct_feats, struct_proj, seq_feats_turned, seq_proj)
+    return pl.pallas_call(
+        project_kernel,
+        out_shape=(shape,) * 4,
+        in_specs=[SMEM] + [HBM] * 4,
+        out_specs=(VMEM,) * 4,
+        scratch_shapes=[pltpu.VMEM(each.shape, each.dtype) for each in held] + [pltpu.SemaphoreType.DMA((4,))],
+        compiler_params=pltpu.CompilerParams(vmem_limit_bytes=56 * 1024 * 1024),
+        name="project",
+    )(core, *held)
 
 
 def merge_kernel(yl_ref, keep_ref, got_ref, keep2_ref, send2_ref):
@@ -317,9 +320,8 @@
 def per_device(struct_feats, seq_feats, struct_proj, seq_proj, cluster_ids, hard_owner, hard_local, hard_valid):
     place = lambda axes: lax.axis_index(axes).astype(jnp.int32)
     core, yl = place("core"), place("yl")
-    keep_s, send_s = project(core.reshape(1), struct_feats, struct_proj, False, "project_struct")
+    keep_s, send_s, keep_q, send_q = project(core.reshape(1), struct_feats, struct_proj, seq_feats.T, seq_proj)
     got_s = shifted(send_s, "core", 1)
-    keep_q, send_q = project(core.reshape(1), seq_feats.T, seq_proj, True, "project_seq")
     got_q = shifted(send_q, "core", 1)
 
     keep2_s, send2_s = merge(yl.reshape(1), keep_s, got_s, "merge_struct")

time: 98.9 us -> 99.3 us (level)
  local copies, waits for them, and re-layouts: 5.53 us -> 3.78 us
  starting transfers between devices: 41.2 us -> 42.9 us
  Pallas kernels: 17.3 us -> 18.9 us
  waiting for transfers between devices: 17.1 us -> 15.9 us
    ppermute x21, starting transfers between devices: 32.7 us -> 34.6 us  [shifted(): lax.ppermute(value, axes, [((place + steps) % count, place) for place in...]
    unnamed x12 -> x8, local copies, waits for them, and re-layouts: 3.85 us -> 2.08 us
    pallas_call x2 -> x1, Pallas kernels: 1.06 us -> 2.71 us  [project(): pl.pallas_call(project_kernel, out_shape=(shape,) * 4, in_specs=[SMEM] +...]
  transfers between devices with their start and end apart: 23 -> 23, of which waited for: 11 -> 10; matrix products, arithmetic and copies ran while one was open for 2% -> 2% of each run, Pallas kernels for 0% -> 0%
where the time goes in v11:
time: 99.3 us; the launch traced here: 98.8 us
  starting transfers between devices  42.9 us (43%)
  Pallas kernels  18.9 us (19%)
  waiting for transfers between devices  15.9 us (16%)
  blocking collectives  14.8 us (15%)
  local copies, waits for them, and re-layouts  3.78 us (4%)
  other arithmetic  1.65 us (2%)
    ppermute x21, starting transfers between devices, shifted(): lax.ppermute(value, axes, [((place + steps) % count, place) for place in...  34.6 us
    all_to_all x1, blocking collectives, per_device(): lax.all_to_all(rows, 'z', split_axis=0, concat_axis=0, tiled=True)  14.8 us
    pallas_call x1, Pallas kernels, pair_sums(): pl.pallas_call(pair_kernel, out_shape=(jax.ShapeDtypeStruct((8, 8, SHARE)...  14.7 us
    ppermute x21, waiting for transfers between devices, shifted(): lax.ppermute(value, axes, [((place + steps) % count, place) for place in...  10.9 us
    all_to_all x1, waiting for transfers between devices, per_device(): lax.all_to_all(cols, COL_AXES, split_axis=0, concat_axis=0, tiled=True)  5.02 us
    all_to_all x1, starting transfers between devices, per_device(): lax.all_to_all(struct_peers, COL_AXES, split_axis=0, concat_axis=0, tiled...  4.86 us
    all_to_all x1, starting transfers between devices, per_device(): lax.all_to_all(cols, COL_AXES, split_axis=0, concat_axis=0, tiled=True)  3.49 us
    pallas_call x1, Pallas kernels, project(): pl.pallas_call(project_kernel, out_shape=(shape,) * 4, in_specs=[SMEM] +...  2.71 us
  transfers between devices with their start and end apart: 23, of which 10 were waited for; matrix products, arithmetic and copies ran while one was open for 2% of the time, Pallas kernels for 0%

profile of v11, /device:TPU:1, one launch (start us, length us, event | category | flops | bytes accessed | tf_op | source)
XLA Modules:
  0.0 98.8 jit_solution(4488285346694718181)
XLA Ops:
  0.7 2.7 %project.1 = (f32[2,128,512]{2,1,0:T(8,128)}, f32[2,128,512]{2,1,0:T(8,128)}, f32[2,128,512]{2,1,0:T(8,128)}, f32[2,128,512]{2,1,0:T(8,128)}) custom-call(s32[1]{0:T(128)} %bitcast.1.core_ref, bf16[512,256]{1,0:T(8,128)(2,1)} %struct_hbm.1, bf16[256,512]{1,0:T(8,128)(2,1)} %ws_hbm.1, bf16[320,512]{1,0:T(8,128)(2,1)} %bitcast.30, bf16[320,512]{1,0:T(8,128)(2,1)} %wq_hbm.1), custom_call_target="tpu_custom_call" | custom-call | tf_op jit(solution)/shard_map/project/pallas_call | solution.py:67
  3.4 3.3 %collective-permute-start.2 = (f32[2,128,512]{2,1,0:T(8,128)}, f32[2,128,512]{2,1,0:T(8,128)S(1)}, u32[]{:S(2)}, u32[]{:S(2)}) collective-permute-start(f32[2,128,512]{2,1,0:T(8,128)} %get-tuple-element.28), channel_id=1, source_target_pairs={{1,0},{0,1},{3,2},{2,3},{5,4},{4,5},{7,6},{6,7},{9,8},{8,9},{11,10... | collective-permute-start | bytes 1572872 | tf_op jit(solution)/shard_map/ppermute | solution.py:36
  6.8 1.6 %collective-permute-done.2.got_ref = f32[2,128,512]{2,1,0:T(8,128)S(1)} collective-permute-done((f32[2,128,512]{2,1,0:T(8,128)}, f32[2,128,512]{2,1,0:T(8,128)S(1)}, u32[]{:S(2)}, u32[]{:S(2)}) %collective-permute-start.2) | collective-permute-done | bytes 524320 | tf_op jit(solution)/shard_map/ppermute | solution.py:36
  8.4 1.0 %copy-done.1 = f32[2,128,512]{2,1,0:T(8,128)S(1)} copy-done((f32[2,128,512]{2,1,0:T(8,128)S(1)}, f32[2,128,512]{2,1,0:T(8,128)}, u32[]{:S(2)}) %copy-start.1) | copy-done | bytes 524312
  9.7 0.8 shift-right-arithmetic_convert_fusion
  10.5 1.0 %copy-done = f32[2,128,512]{2,1,0:T(8,128)S(1)} copy-done((f32[2,128,512]{2,1,0:T(8,128)S(1)}, f32[2,128,512]{2,1,0:T(8,128)}, u32[]{:S(2)}) %copy-start) | copy-done | bytes 524312
  11.6 1.5 %collective-permute-start.1 = (bf16[128,512]{1,0:T(8,128)(2,1)S(1)}, bf16[128,512]{1,0:T(8,128)(2,1)S(1)}, u32[]{:S(2)}, u32[]{:S(2)}) collective-permute-start(bf16[128,512]{1,0:T(8,128)(2,1)S(1)} %get-tuple-element.26), channel_id=1, source_target_pairs={{2,0},{0,2},{3,1},{1,3},{6,4},{4,6},{7,5},{5,7},{10,8},{8,10},{11,... | collective-permute-start | bytes 393224 | tf_op jit(solution)/shard_map/ppermute | solution.py:36
  13.1 0.7 fusion.5
  13.8 0.5 collective-permute-done.3.got2_q
  14.3 2.8 %collective-permute-done.1.got2_s = bf16[128,512]{1,0:T(8,128)(2,1)S(1)} collective-permute-done((bf16[128,512]{1,0:T(8,128)(2,1)S(1)}, bf16[128,512]{1,0:T(8,128)(2,1)S(1)}, u32[]{:S(2)}, u32[]{:S(2)}) %collective-permute-start.1) | collective-permute-done | bytes 131104 | tf_op jit(solution)/shard_map/ppermute | solution.py:36
  17.4 1.7 %broadcast_in_dim.13 = bf16[16,528,128]{2,1,0:T(8,128)(2,1)} broadcast(bf16[528,128]{1,0:T(8,128)(2,1)S(1)} %get-tuple-element.36), dimensions={1,2} | broadcast | bytes 2297856 | tf_op jit(solution)/shard_map/broadcast_in_dim | solution.py:347
  19.1 4.9 %all-to-all-start = ((bf16[16,528,128]{2,1,0:T(8,128)(2,1)}), bf16[16,528,128]{2,1,0:T(8,128)(2,1)S(1)}, u32[]{:S(2)}, u32[]{:S(2)}) async-start(bf16[16,528,128]{2,1,0:T(8,128)(2,1)} %broadcast_in_dim.13), calls=%async_computation | async-start | bytes 4325376 | tf_op jit(solution)/shard_map/all_to_all | solution.py:348
  23.9 5.7 %collective-permute-start.5 = (bf16[144,512]{1,0:T(8,128)(2,1)S(1)}, bf16[144,512]{1,0:T(8,128)(2,1)S(1)}, u32[]{:S(2)}, u32[]{:S(2)}) collective-permute-start(bf16[144,512]{1,0:T(8,128)(2,1)S(1)} %get-tuple-element.35.refs_0_), channel_id=1, source_target_pairs={{32,0},{64,32},{96,64},{128,96},{160,128},{192,160},{224,192},{0,2... | collective-permute-start | bytes 442376 | tf_op jit(solution)/shard_map/ppermute | solution.py:36
  29.6 2.1 %collective-permute-done.5.refs_2_ = bf16[144,512]{1,0:T(8,128)(2,1)S(1)} collective-permute-done((bf16[144,512]{1,0:T(8,128)(2,1)S(1)}, bf16[144,512]{1,0:T(8,128)(2,1)S(1)}, u32[]{:S(2)}, u32[]{:S(2)}) %collective-permute-start.5) | collective-permute-done | bytes 147488 | tf_op jit(solution)/shard_map/ppermute | solution.py:36
  31.7 3.1 %collective-permute-start.7 = (bf16[144,512]{1,0:T(8,128)(2,1)S(1)}, bf16[144,512]{1,0:T(8,128)(2,1)S(1)}, u32[]{:S(2)}, u32[]{:S(2)}) collective-permute-start(bf16[144,512]{1,0:T(8,128)(2,1)S(1)} %collective-permute-done.5.refs_2_), channel_id=1, source_target_pairs={{32,0},{64,32},{96,64},{128,96},{160,128},{192,160},{224,192},{0,2... | collective-permute-start | bytes 442376 | tf_op jit(solution)/shard_map/ppermute | solution.py:36
  35.1 1.8 %collective-permute-done.7.refs_4_ = bf16[144,512]{1,0:T(8,128)(2,1)S(1)} collective-permute-done((bf16[144,512]{1,0:T(8,128)(2,1)S(1)}, bf16[144,512]{1,0:T(8,128)(2,1)S(1)}, u32[]{:S(2)}, u32[]{:S(2)}) %collective-permute-start.7) | collective-permute-done | bytes 147488 | tf_op jit(solution)/shard_map/ppermute | solution.py:36
  36.9 3.4 %collective-permute-start.9 = (bf16[144,512]{1,0:T(8,128)(2,1)S(1)}, bf16[144,512]{1,0:T(8,128)(2,1)S(1)}, u32[]{:S(2)}, u32[]{:S(2)}) collective-permute-start(bf16[144,512]{1,0:T(8,128)(2,1)S(1)} %collective-permute-done.7.refs_4_), channel_id=1, source_target_pairs={{32,0},{64,32},{96,64},{128,96},{160,128},{192,160},{224,192},{0,2... | collective-permute-start | bytes 442376 | tf_op jit(solution)/shard_map/ppermute | solution.py:36
  40.3 4.1 %collective-permute-start.4 = (bf16[144,512]{1,0:T(8,128)(2,1)S(1)}, bf16[144,512]{1,0:T(8,128)(2,1)S(1)}, u32[]{:S(2)}, u32[]{:S(2)}) collective-permute-start(bf16[144,512]{1,0:T(8,128)(2,1)S(1)} %get-tuple-element.35.refs_0_), channel_id=1, source_target_pairs={{1,0},{0,1},{3,2},{2,3},{5,4},{4,5},{7,6},{6,7},{9,8},{8,9},{11,10... | collective-permute-start | bytes 442376 | tf_op jit(solution)/shard_map/ppermute | solution.py:36
  44.4 0.5 collective-permute-start.6
  44.9 2.7 %collective-permute-start.11 = (bf16[144,512]{1,0:T(8,128)(2,1)S(1)}, bf16[144,512]{1,0:T(8,128)(2,1)}, u32[]{:S(2)}, u32[]{:S(2)}) collective-permute-start(bf16[144,512]{1,0:T(8,128)(2,1)S(1)} %collective-permute-done.9.refs_6_), channel_id=1, source_target_pairs={{32,0},{64,32},{96,64},{128,96},{160,128},{192,160},{224,192},{0,2... | collective-permute-start | bytes 442376 | tf_op jit(solution)/shard_map/ppermute | solution.py:36
  47.6 3.2 %collective-permute-start.17 = (bf16[144,512]{1,0:T(8,128)(2,1)S(1)}, bf16[144,512]{1,0:T(8,128)(2,1)}, u32[]{:S(2)}, u32[]{:S(2)}) collective-permute-start(bf16[144,512]{1,0:T(8,128)(2,1)S(1)} %collective-permute-done.14.refs_12_), channel_id=1, source_target_pairs={{1,0},{0,1},{3,2},{2,3},{5,4},{4,5},{7,6},{6,7},{9,8},{8,9},{11,10... | collective-permute-start | bytes 442376 | tf_op jit(solution)/shard_map/ppermute | solution.py:36
  51.3 0.4 collective-permute-done.15.refs_10_
  51.7 0.8 collective-permute-start.16
  52.5 0.9 collective-permute-start.12
  53.8 0.9 collective-permute-done.12.refs_9_
  54.8 14.7 %pair_sums.1 = (f32[8,8,128]{2,1,0:T(8,128)S(1)}, f32[16,8,128]{2,1,0:T(8,128)}, f32[8,128]{1,0:T(8,128)S(1)}) custom-call(s32[3]{0:T(128)S(1)} %pad_add_fusion.1.place_ref, bf16[144,512]{1,0:T(8,128)(2,1)S(1)} %get-tuple-element.35.refs_0_, bf16[144,512]{1,0:T(8,128)(2,1)S(1)} %collective-permute-done.4.refs_1_, ...), custom_call_target="tpu_custom_call" | custom-call | flops 4294967296 | bytes 4194304 | tf_op jit(solution)/shard_map/pair_sums/pallas_call | solution.py:253
  69.5 14.8 %all_to_all.15 = f32[8,8,128]{2,1,0:T(8,128)S(1)} all-to-all(f32[8,8,128]{2,1,0:T(8,128)S(1)} %get-tuple-element.37), channel_id=1, replica_groups=mesh['z'=8,'yh'=2,'x'=4,'yl'=2,'core'=2] {'z'}, dimensions={0} | all-to-all | bytes 65536 | tf_op jit(solution)/shard_map/all_to_all | solution.py:352
  84.3 3.4 %collective-permute-start.19 = (f32[8,128]{1,0:T(8,128)S(1)}, f32[8,128]{1,0:T(8,128)S(1)}, u32[]{:S(2)}, u32[]{:S(2)}) collective-permute-start(f32[8,128]{1,0:T(8,128)S(1)} %reduce_sum.9), channel_id=1, source_target_pairs={{1,0},{0,1},{3,2},{2,3},{5,4},{4,5},{7,6},{6,7},{9,8},{8,9},{11,10... | collective-permute-start | bytes 12296 | tf_op jit(solution)/shard_map/ppermute | solution.py:36
  87.7 3.5 %all-to-all-start.2 = ((f32[16,8,128]{2,1,0:T(8,128)}), f32[16,8,128]{2,1,0:T(8,128)S(1)}, u32[]{:S(2)}, u32[]{:S(2)}) async-start(f32[16,8,128]{2,1,0:T(8,128)} %get-tuple-element.38), calls=%async_computation.2 | async-start | bytes 131072 | tf_op jit(solution)/shard_map/all_to_all | solution.py:353
  91.3 1.3 %collective-permute-start.20 = (f32[8,128]{1,0:T(8,128)S(1)}, f32[8,128]{1,0:T(8,128)S(1)}, u32[]{:S(2)}, u32[]{:S(2)}) collective-permute-start(f32[8,128]{1,0:T(8,128)S(1)} %add.35.rows_ref), channel_id=1, source_target_pairs={{2,0},{0,2},{3,1},{1,3},{6,4},{4,6},{7,5},{5,7},{10,8},{8,10},{11,... | collective-permute-start | bytes 12296 | tf_op jit(solution)/shard_map/ppermute | solution.py:36
  92.7 5.0 %all-to-all-done.2.cols_ref = f32[16,8,128]{2,1,0:T(8,128)S(1)} async-done(((f32[16,8,128]{2,1,0:T(8,128)}), f32[16,8,128]{2,1,0:T(8,128)S(1)}, u32[]{:S(2)}, u32[]{:S(2)}) %all-to-all-start.2) | async-done | bytes 65568 | tf_op jit(solution)/shard_map/all_to_all | solution.py:353
  97.7 1.1 %losses.1 = (f32[4,128]{1,0:T(4,128)}, f32[1,128]{1,0:T(1,128)}, f32[1,128]{1,0:T(1,128)}) custom-call(s32[2]{0:T(128)S(1)} %pad_add_fusion.place_ref, f32[8,128]{1,0:T(8,128)S(1)} %add.35.rows_ref, f32[8,128]{1,0:T(8,128)S(1)} %collective-permute-done.20.other_ref, f32[16,8,128]{2,1,0:T(8,128)S(1)} %all-to-all-done.2.cols_ref, ...), custom_call_target="tpu_custom_call" | custom-call | tf_op jit(solution)/shard_map/losses/pallas_call | solution.py:298
  (43 shorter events, 1.9 us)
Async XLA Ops:
  0.6 9.0 %copy-start.2 = (s32[512,16,1]{0,2,1:T(1,128)S(1)}, s32[512,16,1]{0,2,1:T(1,128)}, u32[]{:S(2)}) copy-start(s32[512,16,1]{0,2,1:T(1,128)} %param.13) | copy-start | bytes 98308
  0.6 12.4 %copy-start.3 = (s32[128,16]{0,1:T(8,128)S(1)}, s32[128,16]{0,1:T(8,128)}, u32[]{:S(2)}) copy-start(s32[128,16]{0,1:T(8,128)} %param.15) | copy-start | bytes 24580
  3.4 5.1 %collective-permute-start.2 = (f32[2,128,512]{2,1,0:T(8,128)}, f32[2,128,512]{2,1,0:T(8,128)S(1)}, u32[]{:S(2)}, u32[]{:S(2)}) collective-permute-start(f32[2,128,512]{2,1,0:T(8,128)} %get-tuple-element.28), channel_id=1, source_target_pairs={{1,0},{0,1},{3,2},{2,3},{5,4},{4,5},{7,6},{6,7},{9,8},{8,9},{11,10... | collective-permute-start | bytes 1572872 | tf_op jit(solution)/shard_map/ppermute | solution.py:36
  6.7 3.8 %collective-permute-start = (f32[2,128,512]{2,1,0:T(8,128)}, f32[2,128,512]{2,1,0:T(8,128)S(1)}, u32[]{:S(2)}, u32[]{:S(2)}) collective-permute-start(f32[2,128,512]{2,1,0:T(8,128)} %get-tuple-element.24), channel_id=1, source_target_pairs={{1,0},{0,1},{3,2},{2,3},{5,4},{4,5},{7,6},{6,7},{9,8},{8,9},{11,10... | collective-permute-start | bytes 1572872 | tf_op jit(solution)/shard_map/ppermute | solution.py:36
  8.4 1.0 %copy-start.1 = (f32[2,128,512]{2,1,0:T(8,128)S(1)}, f32[2,128,512]{2,1,0:T(8,128)}, u32[]{:S(2)}) copy-start(f32[2,128,512]{2,1,0:T(8,128)} %get-tuple-element.27.keep_ref) | copy-start | bytes 1572868
  9.5 4.8 %collective-permute-start.3 = (bf16[128,512]{1,0:T(8,128)(2,1)S(1)}, bf16[128,512]{1,0:T(8,128)(2,1)S(1)}, u32[]{:S(2)}, u32[]{:S(2)}) collective-permute-start(bf16[128,512]{1,0:T(8,128)(2,1)S(1)} %get-tuple-element.30), channel_id=1, source_target_pairs={{2,0},{0,2},{3,1},{1,3},{6,4},{4,6},{7,5},{5,7},{10,8},{8,10},{11,... | collective-permute-start | bytes 393224 | tf_op jit(solution)/shard_map/ppermute | solution.py:36
  10.5 1.0 %copy-start = (f32[2,128,512]{2,1,0:T(8,128)S(1)}, f32[2,128,512]{2,1,0:T(8,128)}, u32[]{:S(2)}) copy-start(f32[2,128,512]{2,1,0:T(8,128)} %get-tuple-element.23.keep_ref) | copy-start | bytes 1572868
  11.6 5.6 %collective-permute-start.1 = (bf16[128,512]{1,0:T(8,128)(2,1)S(1)}, bf16[128,512]{1,0:T(8,128)(2,1)S(1)}, u32[]{:S(2)}, u32[]{:S(2)}) collective-permute-start(bf16[128,512]{1,0:T(8,128)(2,1)S(1)} %get-tuple-element.26), channel_id=1, source_target_pairs={{2,0},{0,2},{3,1},{1,3},{6,4},{4,6},{7,5},{5,7},{10,8},{8,10},{11,... | collective-permute-start | bytes 393224 | tf_op jit(solution)/shard_map/ppermute | solution.py:36
  19.1 35.7 %all-to-all-start = ((bf16[16,528,128]{2,1,0:T(8,128)(2,1)}), bf16[16,528,128]{2,1,0:T(8,128)(2,1)S(1)}, u32[]{:S(2)}, u32[]{:S(2)}) async-start(bf16[16,528,128]{2,1,0:T(8,128)(2,1)} %broadcast_in_dim.13), calls=%async_computation | async-start | bytes 4325376 | tf_op jit(solution)/shard_map/all_to_all | solution.py:348
  23.9 7.8 %collective-permute-start.5 = (bf16[144,512]{1,0:T(8,128)(2,1)S(1)}, bf16[144,512]{1,0:T(8,128)(2,1)S(1)}, u32[]{:S(2)}, u32[]{:S(2)}) collective-permute-start(bf16[144,512]{1,0:T(8,128)(2,1)S(1)} %get-tuple-element.35.refs_0_), channel_id=1, source_target_pairs={{32,0},{64,32},{96,64},{128,96},{160,128},{192,160},{224,192},{0,2... | collective-permute-start | bytes 442376 | tf_op jit(solution)/shard_map/ppermute | solution.py:36
  29.6 5.5 %collective-permute-start.13 = (bf16[144,512]{1,0:T(8,128)(2,1)S(1)}, bf16[144,512]{1,0:T(8,128)(2,1)S(1)}, u32[]{:S(2)}, u32[]{:S(2)}) collective-permute-start(bf16[144,512]{1,0:T(8,128)(2,1)S(1)} %get-tuple-element.35.refs_0_), channel_id=1, source_target_pairs={{224,0},{0,32},{32,64},{64,96},{96,128},{128,160},{160,192},{192,2... | collective-permute-start | bytes 442376 | tf_op jit(solution)/shard_map/ppermute | solution.py:36
  31.7 5.2 %collective-permute-start.7 = (bf16[144,512]{1,0:T(8,128)(2,1)S(1)}, bf16[144,512]{1,0:T(8,128)(2,1)S(1)}, u32[]{:S(2)}, u32[]{:S(2)}) collective-permute-start(bf16[144,512]{1,0:T(8,128)(2,1)S(1)} %collective-permute-done.5.refs_2_), channel_id=1, source_target_pairs={{32,0},{64,32},{96,64},{128,96},{160,128},{192,160},{224,192},{0,2... | collective-permute-start | bytes 442376 | tf_op jit(solution)/shard_map/ppermute | solution.py:36
  35.1 9.8 %collective-permute-start.14 = (bf16[144,512]{1,0:T(8,128)(2,1)S(1)}, bf16[144,512]{1,0:T(8,128)(2,1)S(1)}, u32[]{:S(2)}, u32[]{:S(2)}) collective-permute-start(bf16[144,512]{1,0:T(8,128)(2,1)S(1)} %collective-permute-done.13.refs_14_), channel_id=1, source_target_pairs={{224,0},{0,32},{32,64},{64,96},{96,128},{128,160},{160,192},{192,2... | collective-permute-start | bytes 442376 | tf_op jit(solution)/shard_map/ppermute | solution.py:36
  36.9 8.0 %collective-permute-start.9 = (bf16[144,512]{1,0:T(8,128)(2,1)S(1)}, bf16[144,512]{1,0:T(8,128)(2,1)S(1)}, u32[]{:S(2)}, u32[]{:S(2)}) collective-permute-start(bf16[144,512]{1,0:T(8,128)(2,1)S(1)} %collective-permute-done.7.refs_4_), channel_id=1, source_target_pairs={{32,0},{64,32},{96,64},{128,96},{160,128},{192,160},{224,192},{0,2... | collective-permute-start | bytes 442376 | tf_op jit(solution)/shard_map/ppermute | solution.py:36
  40.3 7.3 %collective-permute-start.4 = (bf16[144,512]{1,0:T(8,128)(2,1)S(1)}, bf16[144,512]{1,0:T(8,128)(2,1)S(1)}, u32[]{:S(2)}, u32[]{:S(2)}) collective-permute-start(bf16[144,512]{1,0:T(8,128)(2,1)S(1)} %get-tuple-element.35.refs_0_), channel_id=1, source_target_pairs={{1,0},{0,1},{3,2},{2,3},{5,4},{4,5},{7,6},{6,7},{9,8},{8,9},{11,10... | collective-permute-start | bytes 442376 | tf_op jit(solution)/shard_map/ppermute | solution.py:36
  44.4 6.4 %collective-permute-start.18 = (bf16[144,512]{1,0:T(8,128)(2,1)S(1)}, bf16[144,512]{1,0:T(8,128)(2,1)S(1)}, u32[]{:S(2)}, u32[]{:S(2)}) collective-permute-start(bf16[144,512]{1,0:T(8,128)(2,1)S(1)} %collective-permute-done.13.refs_14_), channel_id=1, source_target_pairs={{1,0},{0,1},{3,2},{2,3},{5,4},{4,5},{7,6},{6,7},{9,8},{8,9},{11,10... | collective-permute-start | bytes 442376 | tf_op jit(solution)/shard_map/ppermute | solution.py:36
  44.4 6.5 %collective-permute-start.6 = (bf16[144,512]{1,0:T(8,128)(2,1)S(1)}, bf16[144,512]{1,0:T(8,128)(2,1)S(1)}, u32[]{:S(2)}, u32[]{:S(2)}) collective-permute-start(bf16[144,512]{1,0:T(8,128)(2,1)S(1)} %collective-permute-done.5.refs_2_), channel_id=1, source_target_pairs={{1,0},{0,1},{3,2},{2,3},{5,4},{4,5},{7,6},{6,7},{9,8},{8,9},{11,10... | collective-permute-start | bytes 442376 | tf_op jit(solution)/shard_map/ppermute | solution.py:36
  44.9 6.8 %collective-permute-start.15 = (bf16[144,512]{1,0:T(8,128)(2,1)S(1)}, bf16[144,512]{1,0:T(8,128)(2,1)}, u32[]{:S(2)}, u32[]{:S(2)}) collective-permute-start(bf16[144,512]{1,0:T(8,128)(2,1)S(1)} %collective-permute-done.14.refs_12_), channel_id=1, source_target_pairs={{224,0},{0,32},{32,64},{64,96},{96,128},{128,160},{160,192},{192,2... | collective-permute-start | bytes 442376 | tf_op jit(solution)/shard_map/ppermute | solution.py:36
  44.9 7.6 %collective-permute-start.11 = (bf16[144,512]{1,0:T(8,128)(2,1)S(1)}, bf16[144,512]{1,0:T(8,128)(2,1)}, u32[]{:S(2)}, u32[]{:S(2)}) collective-permute-start(bf16[144,512]{1,0:T(8,128)(2,1)S(1)} %collective-permute-done.9.refs_6_), channel_id=1, source_target_pairs={{32,0},{64,32},{96,64},{128,96},{160,128},{192,160},{224,192},{0,2... | collective-permute-start | bytes 442376 | tf_op jit(solution)/shard_map/ppermute | solution.py:36
  47.6 5.9 %collective-permute-start.17 = (bf16[144,512]{1,0:T(8,128)(2,1)S(1)}, bf16[144,512]{1,0:T(8,128)(2,1)}, u32[]{:S(2)}, u32[]{:S(2)}) collective-permute-start(bf16[144,512]{1,0:T(8,128)(2,1)S(1)} %collective-permute-done.14.refs_12_), channel_id=1, source_target_pairs={{1,0},{0,1},{3,2},{2,3},{5,4},{4,5},{7,6},{6,7},{9,8},{8,9},{11,10... | collective-permute-start | bytes 442376 | tf_op jit(solution)/shard_map/ppermute | solution.py:36
  50.7 2.8 %collective-permute-start.8 = (bf16[144,512]{1,0:T(8,128)(2,1)S(1)}, bf16[144,512]{1,0:T(8,128)(2,1)}, u32[]{:S(2)}, u32[]{:S(2)}) collective-permute-start(bf16[144,512]{1,0:T(8,128)(2,1)S(1)} %collective-permute-done.7.refs_4_), channel_id=1, source_target_pairs={{1,0},{0,1},{3,2},{2,3},{5,4},{4,5},{7,6},{6,7},{9,8},{8,9},{11,10... | collective-permute-start | bytes 442376 | tf_op jit(solution)/shard_map/ppermute | solution.py:36
  50.8 2.7 %collective-permute-start.10 = (bf16[144,512]{1,0:T(8,128)(2,1)S(1)}, bf16[144,512]{1,0:T(8,128)(2,1)}, u32[]{:S(2)}, u32[]{:S(2)}) collective-permute-start(bf16[144,512]{1,0:T(8,128)(2,1)S(1)} %collective-permute-done.9.refs_6_), channel_id=1, source_target_pairs={{1,0},{0,1},{3,2},{2,3},{5,4},{4,5},{7,6},{6,7},{9,8},{8,9},{11,10... | collective-permute-start | bytes 442376 | tf_op jit(solution)/shard_map/ppermute | solution.py:36
  51.7 2.1 %collective-permute-start.16 = (bf16[144,512]{1,0:T(8,128)(2,1)}, bf16[144,512]{1,0:T(8,128)(2,1)}, u32[]{:S(2)}, u32[]{:S(2)}) collective-permute-start(bf16[144,512]{1,0:T(8,128)(2,1)} %collective-permute-done.15.refs_10_), channel_id=1, source_target_pairs={{1,0},{0,1},{3,2},{2,3},{5,4},{4,5},{7,6},{6,7},{9,8},{8,9},{11,10... | collective-permute-start | bytes 442376 | tf_op jit(solution)/shard_map/ppermute | solution.py:36
  52.5 2.3 %collective-permute-start.12 = (bf16[144,512]{1,0:T(8,128)(2,1)}, bf16[144,512]{1,0:T(8,128)(2,1)}, u32[]{:S(2)}, u32[]{:S(2)}) collective-permute-start(bf16[144,512]{1,0:T(8,128)(2,1)} %collective-permute-done.11.refs_8_), channel_id=1, source_target_pairs={{1,0},{0,1},{3,2},{2,3},{5,4},{4,5},{7,6},{6,7},{9,8},{8,9},{11,10... | collective-permute-start | bytes 442376 | tf_op jit(solution)/shard_map/ppermute | solution.py:36
  84.3 6.9 %collective-permute-start.19 = (f32[8,128]{1,0:T(8,128)S(1)}, f32[8,128]{1,0:T(8,128)S(1)}, u32[]{:S(2)}, u32[]{:S(2)}) collective-permute-start(f32[8,128]{1,0:T(8,128)S(1)} %reduce_sum.9), channel_id=1, source_target_pairs={{1,0},{0,1},{3,2},{2,3},{5,4},{4,5},{7,6},{6,7},{9,8},{8,9},{11,10... | collective-permute-start | bytes 12296 | tf_op jit(solution)/shard_map/ppermute | solution.py:36
  87.7 9.9 %all-to-all-start.2 = ((f32[16,8,128]{2,1,0:T(8,128)}), f32[16,8,128]{2,1,0:T(8,128)S(1)}, u32[]{:S(2)}, u32[]{:S(2)}) async-start(f32[16,8,128]{2,1,0:T(8,128)} %get-tuple-element.38), calls=%async_computation.2 | async-start | bytes 131072 | tf_op jit(solution)/shard_map/all_to_all | solution.py:353
  91.3 6.4 %collective-permute-start.20 = (f32[8,128]{1,0:T(8,128)S(1)}, f32[8,128]{1,0:T(8,128)S(1)}, u32[]{:S(2)}, u32[]{:S(2)}) collective-permute-start(f32[8,128]{1,0:T(8,128)S(1)} %add.35.rows_ref), channel_id=1, source_target_pairs={{2,0},{0,2},{3,1},{1,3},{6,4},{4,6},{7,5},{5,7},{10,8},{8,10},{11,... | collective-permute-start | bytes 12296 | tf_op jit(solution)/shard_map/ppermute | solution.py:36

commit v12 on v10

--- a/solution.py
+++ b/solution.py
@@ -326,8 +326,8 @@
     got2_s = shifted(send2_s, "yl", 1)
     keep2_q, send2_q = merge(yl.reshape(1), keep_q, got_q, "merge_seq")
     got2_q = shifted(send2_q, "yl", 1)
-    cluster_ids, hard_owner, hard_local, hard_valid, send2_q = lax.optimization_barrier(
-        (cluster_ids, hard_owner, hard_local, hard_valid, send2_q)
+    cluster_ids, hard_owner, hard_local, hard_valid, send2_s, send2_q = lax.optimization_barrier(
+        (cluster_ids, hard_owner, hard_local, hard_valid, send2_s, send2_q)
     )
     own = lambda value: lax.dynamic_slice_in_dim(value, place(MP_AXES) * SHARE, SHARE, 0)
     labels = own(cluster_ids)

time: 98.9 us -> 98.9 us (level)
  no operation moved by 1% of the time
where the time goes in v12:
time: 98.9 us; the launch traced here: 98.4 us
  starting transfers between devices  40.9 us (41%)
  waiting for transfers between devices  17.4 us (18%)
  Pallas kernels  17.3 us (17%)
  blocking collectives  14.8 us (15%)
  local copies, waits for them, and re-layouts  5.53 us (6%)
  other arithmetic  1.66 us (2%)
    ppermute x21, starting transfers between devices, shifted(): lax.ppermute(value, axes, [((place + steps) % count, place) for place in...  32.4 us
    all_to_all x1, blocking collectives, per_device(): lax.all_to_all(rows, 'z', split_axis=0, concat_axis=0, tiled=True)  14.8 us
    pallas_call x1, Pallas kernels, pair_sums(): pl.pallas_call(pair_kernel, out_shape=(jax.ShapeDtypeStruct((8, 8, SHARE)...  14.7 us
    ppermute x21, waiting for transfers between devices, shifted(): lax.ppermute(value, axes, [((place + steps) % count, place) for place in...  11.6 us
    all_to_all x1, waiting for transfers between devices, per_device(): lax.all_to_all(cols, COL_AXES, split_axis=0, concat_axis=0, tiled=True)  5.02 us
    all_to_all x1, starting transfers between devices, per_device(): lax.all_to_all(struct_peers, COL_AXES, split_axis=0, concat_axis=0, tiled...  5.01 us
    unnamed x12, local copies, waits for them, and re-layouts  3.85 us
    all_to_all x1, starting transfers between devices, per_device(): lax.all_to_all(cols, COL_AXES, split_axis=0, concat_axis=0, tiled=True)  3.48 us
  transfers between devices with their start and end apart: 23, of which 11 were waited for; matrix products, arithmetic and copies ran while one was open for 2% of the time, Pallas kernels for 0%

profile of v12, /device:TPU:1, one launch (start us, length us, event | category | flops | bytes accessed | tf_op | source)
XLA Modules:
  0.0 98.4 jit_solution(9833121926115292612)
XLA Ops:
  0.7 1.0 copy-done
  1.6 1.0 copy-done.1
  2.6 0.7 project_seq.1
  3.3 3.3 %collective-permute-start.2 = (f32[2,128,512]{2,1,0:T(8,128)S(1)}, f32[2,128,512]{2,1,0:T(8,128)S(1)}, u32[]{:S(2)}, u32[]{:S(2)}) collective-permute-start(f32[2,128,512]{2,1,0:T(8,128)S(1)} %get-tuple-element.28), channel_id=1, source_target_pairs={{1,0},{0,1},{3,2},{2,3},{5,4},{4,5},{7,6},{6,7},{9,8},{8,9},{11,10... | collective-permute-start | bytes 1572872 | tf_op jit(solution)/shard_map/ppermute | solution.py:36
  6.6 0.9 copy-done.2
  7.6 0.9 copy-done.3
  9.2 1.7 %collective-permute-done.got_ref = f32[2,128,512]{2,1,0:T(8,128)S(1)} collective-permute-done((f32[2,128,512]{2,1,0:T(8,128)S(1)}, f32[2,128,512]{2,1,0:T(8,128)S(1)}, u32[]{:S(2)}, u32[]{:S(2)}) %collective-permute-start) | collective-permute-done | bytes 524320 | tf_op jit(solution)/shard_map/ppermute | solution.py:36
  11.1 0.8 shift-right-arithmetic_convert_fusion
  11.9 0.7 fusion.5
  12.7 1.1 %collective-permute-done.3.got2_q = bf16[128,512]{1,0:T(8,128)(2,1)S(1)} collective-permute-done((bf16[128,512]{1,0:T(8,128)(2,1)S(1)}, bf16[128,512]{1,0:T(8,128)(2,1)S(1)}, u32[]{:S(2)}, u32[]{:S(2)}) %collective-permute-start.3) | collective-permute-done | bytes 131104 | tf_op jit(solution)/shard_map/ppermute | solution.py:36
  13.8 2.8 %collective-permute-done.1.got2_s = bf16[128,512]{1,0:T(8,128)(2,1)S(1)} collective-permute-done((bf16[128,512]{1,0:T(8,128)(2,1)S(1)}, bf16[128,512]{1,0:T(8,128)(2,1)S(1)}, u32[]{:S(2)}, u32[]{:S(2)}) %collective-permute-start.1) | collective-permute-done | bytes 131104 | tf_op jit(solution)/shard_map/ppermute | solution.py:36
  16.8 1.7 %broadcast_in_dim.13 = bf16[16,528,128]{2,1,0:T(8,128)(2,1)} broadcast(bf16[528,128]{1,0:T(8,128)(2,1)S(1)} %get-tuple-element.36), dimensions={1,2} | broadcast | bytes 2297856 | tf_op jit(solution)/shard_map/broadcast_in_dim | solution.py:345
  18.5 5.0 %all-to-all-start = ((bf16[16,528,128]{2,1,0:T(8,128)(2,1)}), bf16[16,528,128]{2,1,0:T(8,128)(2,1)S(1)}, u32[]{:S(2)}, u32[]{:S(2)}) async-start(bf16[16,528,128]{2,1,0:T(8,128)(2,1)} %broadcast_in_dim.13), calls=%async_computation | async-start | bytes 4325376 | tf_op jit(solution)/shard_map/all_to_all | solution.py:346
  23.5 5.6 %collective-permute-start.5 = (bf16[144,512]{1,0:T(8,128)(2,1)S(1)}, bf16[144,512]{1,0:T(8,128)(2,1)S(1)}, u32[]{:S(2)}, u32[]{:S(2)}) collective-permute-start(bf16[144,512]{1,0:T(8,128)(2,1)S(1)} %get-tuple-element.35.refs_0_), channel_id=1, source_target_pairs={{32,0},{64,32},{96,64},{128,96},{160,128},{192,160},{224,192},{0,2... | collective-permute-start | bytes 442376 | tf_op jit(solution)/shard_map/ppermute | solution.py:36
  29.1 2.1 %collective-permute-done.5.refs_2_ = bf16[144,512]{1,0:T(8,128)(2,1)S(1)} collective-permute-done((bf16[144,512]{1,0:T(8,128)(2,1)S(1)}, bf16[144,512]{1,0:T(8,128)(2,1)S(1)}, u32[]{:S(2)}, u32[]{:S(2)}) %collective-permute-start.5) | collective-permute-done | bytes 147488 | tf_op jit(solution)/shard_map/ppermute | solution.py:36
  31.2 3.1 %collective-permute-start.7 = (bf16[144,512]{1,0:T(8,128)(2,1)S(1)}, bf16[144,512]{1,0:T(8,128)(2,1)S(1)}, u32[]{:S(2)}, u32[]{:S(2)}) collective-permute-start(bf16[144,512]{1,0:T(8,128)(2,1)S(1)} %collective-permute-done.5.refs_2_), channel_id=1, source_target_pairs={{32,0},{64,32},{96,64},{128,96},{160,128},{192,160},{224,192},{0,2... | collective-permute-start | bytes 442376 | tf_op jit(solution)/shard_map/ppermute | solution.py:36
  34.6 1.8 %collective-permute-done.7.refs_4_ = bf16[144,512]{1,0:T(8,128)(2,1)S(1)} collective-permute-done((bf16[144,512]{1,0:T(8,128)(2,1)S(1)}, bf16[144,512]{1,0:T(8,128)(2,1)S(1)}, u32[]{:S(2)}, u32[]{:S(2)}) %collective-permute-start.7) | collective-permute-done | bytes 147488 | tf_op jit(solution)/shard_map/ppermute | solution.py:36
  36.4 3.4 %collective-permute-start.9 = (bf16[144,512]{1,0:T(8,128)(2,1)S(1)}, bf16[144,512]{1,0:T(8,128)(2,1)S(1)}, u32[]{:S(2)}, u32[]{:S(2)}) collective-permute-start(bf16[144,512]{1,0:T(8,128)(2,1)S(1)} %collective-permute-done.7.refs_4_), channel_id=1, source_target_pairs={{32,0},{64,32},{96,64},{128,96},{160,128},{192,160},{224,192},{0,2... | collective-permute-start | bytes 442376 | tf_op jit(solution)/shard_map/ppermute | solution.py:36
  39.8 3.9 %collective-permute-start.4 = (bf16[144,512]{1,0:T(8,128)(2,1)S(1)}, bf16[144,512]{1,0:T(8,128)(2,1)S(1)}, u32[]{:S(2)}, u32[]{:S(2)}) collective-permute-start(bf16[144,512]{1,0:T(8,128)(2,1)S(1)} %get-tuple-element.35.refs_0_), channel_id=1, source_target_pairs={{1,0},{0,1},{3,2},{2,3},{5,4},{4,5},{7,6},{6,7},{9,8},{8,9},{11,10... | collective-permute-start | bytes 442376 | tf_op jit(solution)/shard_map/ppermute | solution.py:36
  44.3 2.7 %collective-permute-start.11 = (bf16[144,512]{1,0:T(8,128)(2,1)S(1)}, bf16[144,512]{1,0:T(8,128)(2,1)}, u32[]{:S(2)}, u32[]{:S(2)}) collective-permute-start(bf16[144,512]{1,0:T(8,128)(2,1)S(1)} %collective-permute-done.9.refs_6_), channel_id=1, source_target_pairs={{32,0},{64,32},{96,64},{128,96},{160,128},{192,160},{224,192},{0,2... | collective-permute-start | bytes 442376 | tf_op jit(solution)/shard_map/ppermute | solution.py:36
  46.9 3.2 %collective-permute-start.17 = (bf16[144,512]{1,0:T(8,128)(2,1)S(1)}, bf16[144,512]{1,0:T(8,128)(2,1)}, u32[]{:S(2)}, u32[]{:S(2)}) collective-permute-start(bf16[144,512]{1,0:T(8,128)(2,1)S(1)} %collective-permute-done.14.refs_12_), channel_id=1, source_target_pairs={{1,0},{0,1},{3,2},{2,3},{5,4},{4,5},{7,6},{6,7},{9,8},{8,9},{11,10... | collective-permute-start | bytes 442376 | tf_op jit(solution)/shard_map/ppermute | solution.py:36
  51.0 0.8 collective-permute-start.16
  51.8 0.9 collective-permute-start.12
  53.2 0.9 collective-permute-done.12.refs_9_
  54.1 0.8 all-to-all-done.refs_16_
  54.9 14.7 %pair_sums.1 = (f32[8,8,128]{2,1,0:T(8,128)S(1)}, f32[16,8,128]{2,1,0:T(8,128)}, f32[8,128]{1,0:T(8,128)S(1)}) custom-call(s32[3]{0:T(128)S(1)} %pad_add_fusion.1.place_ref, bf16[144,512]{1,0:T(8,128)(2,1)S(1)} %get-tuple-element.35.refs_0_, bf16[144,512]{1,0:T(8,128)(2,1)S(1)} %collective-permute-done.4.refs_1_, ...), custom_call_target="tpu_custom_call" | custom-call | flops 4294967296 | bytes 4194304 | tf_op jit(solution)/shard_map/pair_sums/pallas_call | solution.py:250
  69.6 14.8 %all_to_all.15 = f32[8,8,128]{2,1,0:T(8,128)S(1)} all-to-all(f32[8,8,128]{2,1,0:T(8,128)S(1)} %get-tuple-element.37), channel_id=1, replica_groups=mesh['z'=8,'yh'=2,'x'=4,'yl'=2,'core'=2] {'z'}, dimensions={0} | all-to-all | bytes 65536 | tf_op jit(solution)/shard_map/all_to_all | solution.py:350
  84.5 2.9 %collective-permute-start.19 = (f32[8,128]{1,0:T(8,128)S(1)}, f32[8,128]{1,0:T(8,128)S(1)}, u32[]{:S(2)}, u32[]{:S(2)}) collective-permute-start(f32[8,128]{1,0:T(8,128)S(1)} %reduce_sum.9), channel_id=1, source_target_pairs={{1,0},{0,1},{3,2},{2,3},{5,4},{4,5},{7,6},{6,7},{9,8},{8,9},{11,10... | collective-permute-start | bytes 12296 | tf_op jit(solution)/shard_map/ppermute | solution.py:36
  87.4 3.5 %all-to-all-start.2 = ((f32[16,8,128]{2,1,0:T(8,128)}), f32[16,8,128]{2,1,0:T(8,128)S(1)}, u32[]{:S(2)}, u32[]{:S(2)}) async-start(f32[16,8,128]{2,1,0:T(8,128)} %get-tuple-element.38), calls=%async_computation.2 | async-start | bytes 131072 | tf_op jit(solution)/shard_map/all_to_all | solution.py:351
  90.9 1.3 %collective-permute-start.20 = (f32[8,128]{1,0:T(8,128)S(1)}, f32[8,128]{1,0:T(8,128)S(1)}, u32[]{:S(2)}, u32[]{:S(2)}) collective-permute-start(f32[8,128]{1,0:T(8,128)S(1)} %add.35.rows_ref), channel_id=1, source_target_pairs={{2,0},{0,2},{3,1},{1,3},{6,4},{4,6},{7,5},{5,7},{10,8},{8,10},{11,... | collective-permute-start | bytes 12296 | tf_op jit(solution)/shard_map/ppermute | solution.py:36
  92.3 5.0 %all-to-all-done.2.cols_ref = f32[16,8,128]{2,1,0:T(8,128)S(1)} async-done(((f32[16,8,128]{2,1,0:T(8,128)}), f32[16,8,128]{2,1,0:T(8,128)S(1)}, u32[]{:S(2)}, u32[]{:S(2)}) %all-to-all-start.2) | async-done | bytes 65568 | tf_op jit(solution)/shard_map/all_to_all | solution.py:351
  97.3 1.1 %losses.1 = (f32[4,128]{1,0:T(4,128)}, f32[1,128]{1,0:T(1,128)}, f32[1,128]{1,0:T(1,128)}) custom-call(s32[2]{0:T(128)S(1)} %pad_add_fusion.place_ref, f32[8,128]{1,0:T(8,128)S(1)} %add.35.rows_ref, f32[8,128]{1,0:T(8,128)S(1)} %collective-permute-done.20.other_ref, f32[16,8,128]{2,1,0:T(8,128)S(1)} %all-to-all-done.2.cols_ref, ...), custom_call_target="tpu_custom_call" | custom-call | tf_op jit(solution)/shard_map/losses/pallas_call | solution.py:295
  (48 shorter events, 3.3 us)
Async XLA Ops:
  0.6 11.2 %copy-start.5 = (s32[128,16]{0,1:T(8,128)S(1)}, s32[128,16]{0,1:T(8,128)}, u32[]{:S(2)}) copy-start(s32[128,16]{0,1:T(8,128)} %param.15) | copy-start | bytes 24580
  0.6 1.0 copy-start
  1.6 1.0 copy-start.1
  2.6 8.5 %copy-start.4 = (s32[512,16,1]{0,2,1:T(1,128)S(1)}, s32[512,16,1]{0,2,1:T(1,128)}, u32[]{:S(2)}) copy-start(s32[512,16,1]{0,2,1:T(1,128)} %param.13) | copy-start | bytes 98308
  3.3 5.7 %collective-permute-start.2 = (f32[2,128,512]{2,1,0:T(8,128)S(1)}, f32[2,128,512]{2,1,0:T(8,128)S(1)}, u32[]{:S(2)}, u32[]{:S(2)}) collective-permute-start(f32[2,128,512]{2,1,0:T(8,128)S(1)} %get-tuple-element.28), channel_id=1, source_target_pairs={{1,0},{0,1},{3,2},{2,3},{5,4},{4,5},{7,6},{6,7},{9,8},{8,9},{11,10... | collective-permute-start | bytes 1572872 | tf_op jit(solution)/shard_map/ppermute | solution.py:36
  6.6 0.9 copy-start.2
  7.6 0.9 copy-start.3
  8.9 2.0 %collective-permute-start = (f32[2,128,512]{2,1,0:T(8,128)S(1)}, f32[2,128,512]{2,1,0:T(8,128)S(1)}, u32[]{:S(2)}, u32[]{:S(2)}) collective-permute-start(f32[2,128,512]{2,1,0:T(8,128)S(1)} %get-tuple-element.24), channel_id=1, source_target_pairs={{1,0},{0,1},{3,2},{2,3},{5,4},{4,5},{7,6},{6,7},{9,8},{8,9},{11,10... | collective-permute-start | bytes 1572872 | tf_op jit(solution)/shard_map/ppermute | solution.py:36
  9.1 4.7 %collective-permute-start.3 = (bf16[128,512]{1,0:T(8,128)(2,1)S(1)}, bf16[128,512]{1,0:T(8,128)(2,1)S(1)}, u32[]{:S(2)}, u32[]{:S(2)}) collective-permute-start(bf16[128,512]{1,0:T(8,128)(2,1)S(1)} %get-tuple-element.30), channel_id=1, source_target_pairs={{2,0},{0,2},{3,1},{1,3},{6,4},{4,6},{7,5},{5,7},{10,8},{8,10},{11,... | collective-permute-start | bytes 393224 | tf_op jit(solution)/shard_map/ppermute | solution.py:36
  11.0 5.6 %collective-permute-start.1 = (bf16[128,512]{1,0:T(8,128)(2,1)S(1)}, bf16[128,512]{1,0:T(8,128)(2,1)S(1)}, u32[]{:S(2)}, u32[]{:S(2)}) collective-permute-start(bf16[128,512]{1,0:T(8,128)(2,1)S(1)} %get-tuple-element.26), channel_id=1, source_target_pairs={{2,0},{0,2},{3,1},{1,3},{6,4},{4,6},{7,5},{5,7},{10,8},{8,10},{11,... | collective-permute-start | bytes 393224 | tf_op jit(solution)/shard_map/ppermute | solution.py:36
  18.5 36.4 %all-to-all-start = ((bf16[16,528,128]{2,1,0:T(8,128)(2,1)}), bf16[16,528,128]{2,1,0:T(8,128)(2,1)S(1)}, u32[]{:S(2)}, u32[]{:S(2)}) async-start(bf16[16,528,128]{2,1,0:T(8,128)(2,1)} %broadcast_in_dim.13), calls=%async_computation | async-start | bytes 4325376 | tf_op jit(solution)/shard_map/all_to_all | solution.py:346
  23.5 7.8 %collective-permute-start.5 = (bf16[144,512]{1,0:T(8,128)(2,1)S(1)}, bf16[144,512]{1,0:T(8,128)(2,1)S(1)}, u32[]{:S(2)}, u32[]{:S(2)}) collective-permute-start(bf16[144,512]{1,0:T(8,128)(2,1)S(1)} %get-tuple-element.35.refs_0_), channel_id=1, source_target_pairs={{32,0},{64,32},{96,64},{128,96},{160,128},{192,160},{224,192},{0,2... | collective-permute-start | bytes 442376 | tf_op jit(solution)/shard_map/ppermute | solution.py:36
  29.1 5.5 %collective-permute-start.13 = (bf16[144,512]{1,0:T(8,128)(2,1)S(1)}, bf16[144,512]{1,0:T(8,128)(2,1)S(1)}, u32[]{:S(2)}, u32[]{:S(2)}) collective-permute-start(bf16[144,512]{1,0:T(8,128)(2,1)S(1)} %get-tuple-element.35.refs_0_), channel_id=1, source_target_pairs={{224,0},{0,32},{32,64},{64,96},{96,128},{128,160},{160,192},{192,2... | collective-permute-start | bytes 442376 | tf_op jit(solution)/shard_map/ppermute | solution.py:36
  31.2 5.2 %collective-permute-start.7 = (bf16[144,512]{1,0:T(8,128)(2,1)S(1)}, bf16[144,512]{1,0:T(8,128)(2,1)S(1)}, u32[]{:S(2)}, u32[]{:S(2)}) collective-permute-start(bf16[144,512]{1,0:T(8,128)(2,1)S(1)} %collective-permute-done.5.refs_2_), channel_id=1, source_target_pairs={{32,0},{64,32},{96,64},{128,96},{160,128},{192,160},{224,192},{0,2... | collective-permute-start | bytes 442376 | tf_op jit(solution)/shard_map/ppermute | solution.py:36
  34.6 9.6 %collective-permute-start.14 = (bf16[144,512]{1,0:T(8,128)(2,1)S(1)}, bf16[144,512]{1,0:T(8,128)(2,1)S(1)}, u32[]{:S(2)}, u32[]{:S(2)}) collective-permute-start(bf16[144,512]{1,0:T(8,128)(2,1)S(1)} %collective-permute-done.13.refs_14_), channel_id=1, source_target_pairs={{224,0},{0,32},{32,64},{64,96},{96,128},{128,160},{160,192},{192,2... | collective-permute-start | bytes 442376 | tf_op jit(solution)/shard_map/ppermute | solution.py:36
  36.4 7.8 %collective-permute-start.9 = (bf16[144,512]{1,0:T(8,128)(2,1)S(1)}, bf16[144,512]{1,0:T(8,128)(2,1)S(1)}, u32[]{:S(2)}, u32[]{:S(2)}) collective-permute-start(bf16[144,512]{1,0:T(8,128)(2,1)S(1)} %collective-permute-done.7.refs_4_), channel_id=1, source_target_pairs={{32,0},{64,32},{96,64},{128,96},{160,128},{192,160},{224,192},{0,2... | collective-permute-start | bytes 442376 | tf_op jit(solution)/shard_map/ppermute | solution.py:36
  39.8 7.1 %collective-permute-start.4 = (bf16[144,512]{1,0:T(8,128)(2,1)S(1)}, bf16[144,512]{1,0:T(8,128)(2,1)S(1)}, u32[]{:S(2)}, u32[]{:S(2)}) collective-permute-start(bf16[144,512]{1,0:T(8,128)(2,1)S(1)} %get-tuple-element.35.refs_0_), channel_id=1, source_target_pairs={{1,0},{0,1},{3,2},{2,3},{5,4},{4,5},{7,6},{6,7},{9,8},{8,9},{11,10... | collective-permute-start | bytes 442376 | tf_op jit(solution)/shard_map/ppermute | solution.py:36
  43.7 6.4 %collective-permute-start.18 = (bf16[144,512]{1,0:T(8,128)(2,1)S(1)}, bf16[144,512]{1,0:T(8,128)(2,1)S(1)}, u32[]{:S(2)}, u32[]{:S(2)}) collective-permute-start(bf16[144,512]{1,0:T(8,128)(2,1)S(1)} %collective-permute-done.13.refs_14_), channel_id=1, source_target_pairs={{1,0},{0,1},{3,2},{2,3},{5,4},{4,5},{7,6},{6,7},{9,8},{8,9},{11,10... | collective-permute-start | bytes 442376 | tf_op jit(solution)/shard_map/ppermute | solution.py:36
  43.7 6.5 %collective-permute-start.6 = (bf16[144,512]{1,0:T(8,128)(2,1)S(1)}, bf16[144,512]{1,0:T(8,128)(2,1)S(1)}, u32[]{:S(2)}, u32[]{:S(2)}) collective-permute-start(bf16[144,512]{1,0:T(8,128)(2,1)S(1)} %collective-permute-done.5.refs_2_), channel_id=1, source_target_pairs={{1,0},{0,1},{3,2},{2,3},{5,4},{4,5},{7,6},{6,7},{9,8},{8,9},{11,10... | collective-permute-start | bytes 442376 | tf_op jit(solution)/shard_map/ppermute | solution.py:36
  44.2 6.8 %collective-permute-start.15 = (bf16[144,512]{1,0:T(8,128)(2,1)S(1)}, bf16[144,512]{1,0:T(8,128)(2,1)}, u32[]{:S(2)}, u32[]{:S(2)}) collective-permute-start(bf16[144,512]{1,0:T(8,128)(2,1)S(1)} %collective-permute-done.14.refs_12_), channel_id=1, source_target_pairs={{224,0},{0,32},{32,64},{64,96},{96,128},{128,160},{160,192},{192,2... | collective-permute-start | bytes 442376 | tf_op jit(solution)/shard_map/ppermute | solution.py:36
  44.3 7.6 %collective-permute-start.11 = (bf16[144,512]{1,0:T(8,128)(2,1)S(1)}, bf16[144,512]{1,0:T(8,128)(2,1)}, u32[]{:S(2)}, u32[]{:S(2)}) collective-permute-start(bf16[144,512]{1,0:T(8,128)(2,1)S(1)} %collective-permute-done.9.refs_6_), channel_id=1, source_target_pairs={{32,0},{64,32},{96,64},{128,96},{160,128},{192,160},{224,192},{0,2... | collective-permute-start | bytes 442376 | tf_op jit(solution)/shard_map/ppermute | solution.py:36
  46.9 5.9 %collective-permute-start.17 = (bf16[144,512]{1,0:T(8,128)(2,1)S(1)}, bf16[144,512]{1,0:T(8,128)(2,1)}, u32[]{:S(2)}, u32[]{:S(2)}) collective-permute-start(bf16[144,512]{1,0:T(8,128)(2,1)S(1)} %collective-permute-done.14.refs_12_), channel_id=1, source_target_pairs={{1,0},{0,1},{3,2},{2,3},{5,4},{4,5},{7,6},{6,7},{9,8},{8,9},{11,10... | collective-permute-start | bytes 442376 | tf_op jit(solution)/shard_map/ppermute | solution.py:36
  50.1 2.8 %collective-permute-start.8 = (bf16[144,512]{1,0:T(8,128)(2,1)S(1)}, bf16[144,512]{1,0:T(8,128)(2,1)}, u32[]{:S(2)}, u32[]{:S(2)}) collective-permute-start(bf16[144,512]{1,0:T(8,128)(2,1)S(1)} %collective-permute-done.7.refs_4_), channel_id=1, source_target_pairs={{1,0},{0,1},{3,2},{2,3},{5,4},{4,5},{7,6},{6,7},{9,8},{8,9},{11,10... | collective-permute-start | bytes 442376 | tf_op jit(solution)/shard_map/ppermute | solution.py:36
  50.2 2.7 %collective-permute-start.10 = (bf16[144,512]{1,0:T(8,128)(2,1)S(1)}, bf16[144,512]{1,0:T(8,128)(2,1)}, u32[]{:S(2)}, u32[]{:S(2)}) collective-permute-start(bf16[144,512]{1,0:T(8,128)(2,1)S(1)} %collective-permute-done.9.refs_6_), channel_id=1, source_target_pairs={{1,0},{0,1},{3,2},{2,3},{5,4},{4,5},{7,6},{6,7},{9,8},{8,9},{11,10... | collective-permute-start | bytes 442376 | tf_op jit(solution)/shard_map/ppermute | solution.py:36
  51.0 2.1 %collective-permute-start.16 = (bf16[144,512]{1,0:T(8,128)(2,1)}, bf16[144,512]{1,0:T(8,128)(2,1)}, u32[]{:S(2)}, u32[]{:S(2)}) collective-permute-start(bf16[144,512]{1,0:T(8,128)(2,1)} %collective-permute-done.15.refs_10_), channel_id=1, source_target_pairs={{1,0},{0,1},{3,2},{2,3},{5,4},{4,5},{7,6},{6,7},{9,8},{8,9},{11,10... | collective-permute-start | bytes 442376 | tf_op jit(solution)/shard_map/ppermute | solution.py:36
  51.8 2.3 %collective-permute-start.12 = (bf16[144,512]{1,0:T(8,128)(2,1)}, bf16[144,512]{1,0:T(8,128)(2,1)}, u32[]{:S(2)}, u32[]{:S(2)}) collective-permute-start(bf16[144,512]{1,0:T(8,128)(2,1)} %collective-permute-done.11.refs_8_), channel_id=1, source_target_pairs={{1,0},{0,1},{3,2},{2,3},{5,4},{4,5},{7,6},{6,7},{9,8},{8,9},{11,10... | collective-permute-start | bytes 442376 | tf_op jit(solution)/shard_map/ppermute | solution.py:36
  84.5 6.3 %collective-permute-start.19 = (f32[8,128]{1,0:T(8,128)S(1)}, f32[8,128]{1,0:T(8,128)S(1)}, u32[]{:S(2)}, u32[]{:S(2)}) collective-permute-start(f32[8,128]{1,0:T(8,128)S(1)} %reduce_sum.9), channel_id=1, source_target_pairs={{1,0},{0,1},{3,2},{2,3},{5,4},{4,5},{7,6},{6,7},{9,8},{8,9},{11,10... | collective-permute-start | bytes 12296 | tf_op jit(solution)/shard_map/ppermute | solution.py:36
  87.4 9.9 %all-to-all-start.2 = ((f32[16,8,128]{2,1,0:T(8,128)}), f32[16,8,128]{2,1,0:T(8,128)S(1)}, u32[]{:S(2)}, u32[]{:S(2)}) async-start(f32[16,8,128]{2,1,0:T(8,128)} %get-tuple-element.38), calls=%async_computation.2 | async-start | bytes 131072 | tf_op jit(solution)/shard_map/all_to_all | solution.py:351
  90.9 6.4 %collective-permute-start.20 = (f32[8,128]{1,0:T(8,128)S(1)}, f32[8,128]{1,0:T(8,128)S(1)}, u32[]{:S(2)}, u32[]{:S(2)}) collective-permute-start(f32[8,128]{1,0:T(8,128)S(1)} %add.35.rows_ref), channel_id=1, source_target_pairs={{2,0},{0,2},{3,1},{1,3},{6,4},{4,6},{7,5},{5,7},{10,8},{8,10},{11,... | collective-permute-start | bytes 12296 | tf_op jit(solution)/shard_map/ppermute | solution.py:36

commit v13 on v12

--- a/solution.py
+++ b/solution.py
@@ -100,8 +100,10 @@
 
 def finish_kernel(keep2_s, got2_s, keep2_q, got2_q, struct_ext_ref, seq_ext_ref, struct_ref, seq_ref):
     struct = normalized(keep2_s, got2_s)
-    struct_ref[0:WIDTH, :] = struct.astype(jnp.float32).T.astype(jnp.bfloat16)
-    struct_ref[WIDTH:, :] = struct_ext_ref[...]
+    turned = struct.astype(jnp.float32).T.astype(jnp.bfloat16)
+    for peer in range(SIDE):
+        struct_ref[peer, 0:WIDTH, :] = turned
+        struct_ref[peer, WIDTH:, :] = struct_ext_ref[...]
     seq = normalized(keep2_q, got2_q)
     seq_ref[0:SHARE, :] = seq
     seq_ref[SHARE:, :] = seq_ext_ref[...]
@@ -111,7 +113,7 @@
     return pl.pallas_call(
         finish_kernel,
         out_shape=(
-            jax.ShapeDtypeStruct((WIDTH + EXT, SHARE), jnp.bfloat16),
+            jax.ShapeDtypeStruct((SIDE, WIDTH + EXT, SHARE), jnp.bfloat16),
             jax.ShapeDtypeStruct((SHARE + EXT, WIDTH), jnp.bfloat16),
         ),
         in_specs=[VMEM] * 6,
@@ -342,8 +344,7 @@
     struct_ext = jnp.concatenate([wide(labels >> 7)[0:8], wide(labels & 127)[0:8]], axis=0).astype(jnp.bfloat16)
 
     struct_block, seq_block = finish(keep2_s, got2_s, keep2_q, got2_q, struct_ext, seq_ext)
-    struct_peers = jnp.broadcast_to(struct_block[None], (SIDE, *struct_block.shape))
-    struct_blocks = lax.all_to_all(struct_peers, COL_AXES, split_axis=0, concat_axis=0, tiled=True)
+    struct_blocks = lax.all_to_all(struct_block, COL_AXES, split_axis=0, concat_axis=0, tiled=True)
     seq_blocks = [each for held in over_z(seq_block) for each in (held, shifted(held, "core", 1))]
 
     rows, cols, self_dot = pair_sums(jnp.stack([place("z"), core, place(COL_AXES)]), seq_blocks, struct_blocks)

time: 98.9 us -> 98.7 us (level)
    broadcast_in_dim x1 -> x0, local copies, waits for them, and re-layouts: 1.65 us -> none  [per_device(): jnp.broadcast_to(struct_block[None], (SIDE, *struct_block.shape))]
    unnamed x12 -> x14, local copies, waits for them, and re-layouts: 3.85 us -> 5.22 us
  transfers between devices with their start and end apart: 23 -> 23, of which waited for: 11 -> 11; matrix products, arithmetic and copies ran while one was open for 2% -> 2% of each run, Pallas kernels for 0% -> 1%
where the time goes in v13:
time: 98.7 us; the launch traced here: 98.2 us
  starting transfers between devices  40.9 us (41%)
  Pallas kernels  17.4 us (18%)
  waiting for transfers between devices  17.4 us (18%)
  blocking collectives  14.8 us (15%)
  local copies, waits for them, and re-layouts  5.25 us (5%)
  other arithmetic  1.66 us (2%)
    ppermute x21, starting transfers between devices, shifted(): lax.ppermute(value, axes, [((place + steps) % count, place) for place in...  32.4 us
    all_to_all x1, blocking collectives, per_device(): lax.all_to_all(rows, 'z', split_axis=0, concat_axis=0, tiled=True)  14.8 us
    pallas_call x1, Pallas kernels, pair_sums(): pl.pallas_call(pair_kernel, out_shape=(jax.ShapeDtypeStruct((8, 8, SHARE)...  14.7 us
    ppermute x21, waiting for transfers between devices, shifted(): lax.ppermute(value, axes, [((place + steps) % count, place) for place in...  11.6 us
    unnamed x14, local copies, waits for them, and re-layouts  5.22 us
    all_to_all x1, waiting for transfers between devices, per_device(): lax.all_to_all(cols, COL_AXES, split_axis=0, concat_axis=0, tiled=True)  5.02 us
    all_to_all x1, starting transfers between devices, per_device(): lax.all_to_all(struct_block, COL_AXES, split_axis=0, concat_axis=0, tiled...  5.01 us
    all_to_all x1, starting transfers between devices, per_device(): lax.all_to_all(cols, COL_AXES, split_axis=0, concat_axis=0, tiled=True)  3.49 us
  transfers between devices with their start and end apart: 23, of which 11 were waited for; matrix products, arithmetic and copies ran while one was open for 2% of the time, Pallas kernels for 1%

profile of v13, /device:TPU:1, one launch (start us, length us, event | category | flops | bytes accessed | tf_op | source)
XLA Modules:
  0.0 98.2 jit_solution(16138546405485354164)
XLA Ops:
  0.6 0.9 copy-done.3
  1.6 0.9 copy-done.4
  2.9 3.3 %collective-permute-start = (f32[2,128,512]{2,1,0:T(8,128)S(1)}, f32[2,128,512]{2,1,0:T(8,128)S(1)}, u32[]{:S(2)}, u32[]{:S(2)}) collective-permute-start(f32[2,128,512]{2,1,0:T(8,128)S(1)} %get-tuple-element.24), channel_id=1, source_target_pairs={{1,0},{0,1},{3,2},{2,3},{5,4},{4,5},{7,6},{6,7},{9,8},{8,9},{11,10... | collective-permute-start | bytes 1572872 | tf_op jit(solution)/shard_map/ppermute | solution.py:36
  6.2 1.0 copy-done.1
  7.2 1.0 copy-done.2
  8.2 0.7 project_seq.1
  9.2 1.7 %collective-permute-done.2.got_ref = f32[2,128,512]{2,1,0:T(8,128)S(1)} collective-permute-done((f32[2,128,512]{2,1,0:T(8,128)S(1)}, f32[2,128,512]{2,1,0:T(8,128)S(1)}, u32[]{:S(2)}, u32[]{:S(2)}) %collective-permute-start.2) | collective-permute-done | bytes 524320 | tf_op jit(solution)/shard_map/ppermute | solution.py:36
  11.0 0.8 shift-right-arithmetic_convert_fusion
  11.9 0.7 fusion.5
  12.6 1.1 %collective-permute-done.1.got2_s = bf16[128,512]{1,0:T(8,128)(2,1)S(1)} collective-permute-done((bf16[128,512]{1,0:T(8,128)(2,1)S(1)}, bf16[128,512]{1,0:T(8,128)(2,1)S(1)}, u32[]{:S(2)}, u32[]{:S(2)}) %collective-permute-start.1) | collective-permute-done | bytes 131104 | tf_op jit(solution)/shard_map/ppermute | solution.py:36
  13.8 2.8 %collective-permute-done.3.got2_q = bf16[128,512]{1,0:T(8,128)(2,1)S(1)} collective-permute-done((bf16[128,512]{1,0:T(8,128)(2,1)S(1)}, bf16[128,512]{1,0:T(8,128)(2,1)S(1)}, u32[]{:S(2)}, u32[]{:S(2)}) %collective-permute-start.3) | collective-permute-done | bytes 131104 | tf_op jit(solution)/shard_map/ppermute | solution.py:36
  16.9 1.4 %copy-done = bf16[16,528,128]{2,1,0:T(8,128)(2,1)} copy-done((bf16[16,528,128]{2,1,0:T(8,128)(2,1)}, bf16[16,528,128]{2,1,0:T(8,128)(2,1)S(1)}, u32[]{:S(2)}) %copy-start) | copy-done | bytes 2162712
  18.3 5.0 %all-to-all-start = ((bf16[16,528,128]{2,1,0:T(8,128)(2,1)}), bf16[16,528,128]{2,1,0:T(8,128)(2,1)S(1)}, u32[]{:S(2)}, u32[]{:S(2)}) async-start(bf16[16,528,128]{2,1,0:T(8,128)(2,1)} %copy-done), calls=%async_computation | async-start | bytes 4325376 | tf_op jit(solution)/shard_map/all_to_all | solution.py:347
  23.3 5.7 %collective-permute-start.5 = (bf16[144,512]{1,0:T(8,128)(2,1)S(1)}, bf16[144,512]{1,0:T(8,128)(2,1)S(1)}, u32[]{:S(2)}, u32[]{:S(2)}) collective-permute-start(bf16[144,512]{1,0:T(8,128)(2,1)S(1)} %get-tuple-element.35.refs_0_), channel_id=1, source_target_pairs={{32,0},{64,32},{96,64},{128,96},{160,128},{192,160},{224,192},{0,2... | collective-permute-start | bytes 442376 | tf_op jit(solution)/shard_map/ppermute | solution.py:36
  28.9 2.1 %collective-permute-done.5.refs_2_ = bf16[144,512]{1,0:T(8,128)(2,1)S(1)} collective-permute-done((bf16[144,512]{1,0:T(8,128)(2,1)S(1)}, bf16[144,512]{1,0:T(8,128)(2,1)S(1)}, u32[]{:S(2)}, u32[]{:S(2)}) %collective-permute-start.5) | collective-permute-done | bytes 147488 | tf_op jit(solution)/shard_map/ppermute | solution.py:36
  31.0 3.1 %collective-permute-start.7 = (bf16[144,512]{1,0:T(8,128)(2,1)S(1)}, bf16[144,512]{1,0:T(8,128)(2,1)S(1)}, u32[]{:S(2)}, u32[]{:S(2)}) collective-permute-start(bf16[144,512]{1,0:T(8,128)(2,1)S(1)} %collective-permute-done.5.refs_2_), channel_id=1, source_target_pairs={{32,0},{64,32},{96,64},{128,96},{160,128},{192,160},{224,192},{0,2... | collective-permute-start | bytes 442376 | tf_op jit(solution)/shard_map/ppermute | solution.py:36
  34.4 1.8 %collective-permute-done.7.refs_4_ = bf16[144,512]{1,0:T(8,128)(2,1)S(1)} collective-permute-done((bf16[144,512]{1,0:T(8,128)(2,1)S(1)}, bf16[144,512]{1,0:T(8,128)(2,1)S(1)}, u32[]{:S(2)}, u32[]{:S(2)}) %collective-permute-start.7) | collective-permute-done | bytes 147488 | tf_op jit(solution)/shard_map/ppermute | solution.py:36
  36.2 3.4 %collective-permute-start.9 = (bf16[144,512]{1,0:T(8,128)(2,1)S(1)}, bf16[144,512]{1,0:T(8,128)(2,1)S(1)}, u32[]{:S(2)}, u32[]{:S(2)}) collective-permute-start(bf16[144,512]{1,0:T(8,128)(2,1)S(1)} %collective-permute-done.7.refs_4_), channel_id=1, source_target_pairs={{32,0},{64,32},{96,64},{128,96},{160,128},{192,160},{224,192},{0,2... | collective-permute-start | bytes 442376 | tf_op jit(solution)/shard_map/ppermute | solution.py:36
  39.6 3.9 %collective-permute-start.4 = (bf16[144,512]{1,0:T(8,128)(2,1)S(1)}, bf16[144,512]{1,0:T(8,128)(2,1)S(1)}, u32[]{:S(2)}, u32[]{:S(2)}) collective-permute-start(bf16[144,512]{1,0:T(8,128)(2,1)S(1)} %get-tuple-element.35.refs_0_), channel_id=1, source_target_pairs={{1,0},{0,1},{3,2},{2,3},{5,4},{4,5},{7,6},{6,7},{9,8},{8,9},{11,10... | collective-permute-start | bytes 442376 | tf_op jit(solution)/shard_map/ppermute | solution.py:36
  44.0 2.7 %collective-permute-start.11 = (bf16[144,512]{1,0:T(8,128)(2,1)S(1)}, bf16[144,512]{1,0:T(8,128)(2,1)}, u32[]{:S(2)}, u32[]{:S(2)}) collective-permute-start(bf16[144,512]{1,0:T(8,128)(2,1)S(1)} %collective-permute-done.9.refs_6_), channel_id=1, source_target_pairs={{32,0},{64,32},{96,64},{128,96},{160,128},{192,160},{224,192},{0,2... | collective-permute-start | bytes 442376 | tf_op jit(solution)/shard_map/ppermute | solution.py:36
  46.7 3.2 %collective-permute-start.17 = (bf16[144,512]{1,0:T(8,128)(2,1)S(1)}, bf16[144,512]{1,0:T(8,128)(2,1)}, u32[]{:S(2)}, u32[]{:S(2)}) collective-permute-start(bf16[144,512]{1,0:T(8,128)(2,1)S(1)} %collective-permute-done.14.refs_12_), channel_id=1, source_target_pairs={{1,0},{0,1},{3,2},{2,3},{5,4},{4,5},{7,6},{6,7},{9,8},{8,9},{11,10... | collective-permute-start | bytes 442376 | tf_op jit(solution)/shard_map/ppermute | solution.py:36
  50.8 0.8 collective-permute-start.16
  51.6 0.9 collective-permute-start.12
  53.0 0.9 collective-permute-done.12.refs_9_
  53.9 0.8 all-to-all-done.refs_16_
  54.7 14.7 %pair_sums.1 = (f32[8,8,128]{2,1,0:T(8,128)S(1)}, f32[16,8,128]{2,1,0:T(8,128)}, f32[8,128]{1,0:T(8,128)S(1)}) custom-call(s32[3]{0:T(128)S(1)} %pad_add_fusion.1.place_ref, bf16[144,512]{1,0:T(8,128)(2,1)S(1)} %get-tuple-element.35.refs_0_, bf16[144,512]{1,0:T(8,128)(2,1)S(1)} %collective-permute-done.4.refs_1_, ...), custom_call_target="tpu_custom_call" | custom-call | flops 4294967296 | bytes 4194304 | tf_op jit(solution)/shard_map/pair_sums/pallas_call | solution.py:252
  69.4 14.8 %all_to_all.15 = f32[8,8,128]{2,1,0:T(8,128)S(1)} all-to-all(f32[8,8,128]{2,1,0:T(8,128)S(1)} %get-tuple-element.37), channel_id=1, replica_groups=mesh['z'=8,'yh'=2,'x'=4,'yl'=2,'core'=2] {'z'}, dimensions={0} | all-to-all | bytes 65536 | tf_op jit(solution)/shard_map/all_to_all | solution.py:351
  84.3 2.9 %collective-permute-start.19 = (f32[8,128]{1,0:T(8,128)S(1)}, f32[8,128]{1,0:T(8,128)S(1)}, u32[]{:S(2)}, u32[]{:S(2)}) collective-permute-start(f32[8,128]{1,0:T(8,128)S(1)} %reduce_sum.9), channel_id=1, source_target_pairs={{1,0},{0,1},{3,2},{2,3},{5,4},{4,5},{7,6},{6,7},{9,8},{8,9},{11,10... | collective-permute-start | bytes 12296 | tf_op jit(solution)/shard_map/ppermute | solution.py:36
  87.2 3.5 %all-to-all-start.2 = ((f32[16,8,128]{2,1,0:T(8,128)}), f32[16,8,128]{2,1,0:T(8,128)S(1)}, u32[]{:S(2)}, u32[]{:S(2)}) async-start(f32[16,8,128]{2,1,0:T(8,128)} %get-tuple-element.38), calls=%async_computation.2 | async-start | bytes 131072 | tf_op jit(solution)/shard_map/all_to_all | solution.py:352
  90.7 1.3 %collective-permute-start.20 = (f32[8,128]{1,0:T(8,128)S(1)}, f32[8,128]{1,0:T(8,128)S(1)}, u32[]{:S(2)}, u32[]{:S(2)}) collective-permute-start(f32[8,128]{1,0:T(8,128)S(1)} %add.35.rows_ref), channel_id=1, source_target_pairs={{2,0},{0,2},{3,1},{1,3},{6,4},{4,6},{7,5},{5,7},{10,8},{8,10},{11,... | collective-permute-start | bytes 12296 | tf_op jit(solution)/shard_map/ppermute | solution.py:36
  92.1 5.0 %all-to-all-done.2.cols_ref = f32[16,8,128]{2,1,0:T(8,128)S(1)} async-done(((f32[16,8,128]{2,1,0:T(8,128)}), f32[16,8,128]{2,1,0:T(8,128)S(1)}, u32[]{:S(2)}, u32[]{:S(2)}) %all-to-all-start.2) | async-done | bytes 65568 | tf_op jit(solution)/shard_map/all_to_all | solution.py:352
  97.1 1.1 %losses.1 = (f32[4,128]{1,0:T(4,128)}, f32[1,128]{1,0:T(1,128)}, f32[1,128]{1,0:T(1,128)}) custom-call(s32[2]{0:T(128)S(1)} %pad_add_fusion.place_ref, f32[8,128]{1,0:T(8,128)S(1)} %add.35.rows_ref, f32[8,128]{1,0:T(8,128)S(1)} %collective-permute-done.20.other_ref, f32[16,8,128]{2,1,0:T(8,128)S(1)} %all-to-all-done.2.cols_ref, ...), custom_call_target="tpu_custom_call" | custom-call | tf_op jit(solution)/shard_map/losses/pallas_call | solution.py:297
  (49 shorter events, 3.4 us)
Async XLA Ops:
  0.6 1.0 copy-start.3
  1.6 0.9 copy-start.4
  2.5 9.3 %copy-start.5 = (s32[512,16,1]{0,2,1:T(1,128)S(1)}, s32[512,16,1]{0,2,1:T(1,128)}, u32[]{:S(2)}) copy-start(s32[512,16,1]{0,2,1:T(1,128)} %param.13) | copy-start | bytes 98308
  2.5 9.3 %copy-start.6 = (s32[128,16]{0,1:T(8,128)S(1)}, s32[128,16]{0,1:T(8,128)}, u32[]{:S(2)}) copy-start(s32[128,16]{0,1:T(8,128)} %param.15) | copy-start | bytes 24580
  2.9 6.1 %collective-permute-start = (f32[2,128,512]{2,1,0:T(8,128)S(1)}, f32[2,128,512]{2,1,0:T(8,128)S(1)}, u32[]{:S(2)}, u32[]{:S(2)}) collective-permute-start(f32[2,128,512]{2,1,0:T(8,128)S(1)} %get-tuple-element.24), channel_id=1, source_target_pairs={{1,0},{0,1},{3,2},{2,3},{5,4},{4,5},{7,6},{6,7},{9,8},{8,9},{11,10... | collective-permute-start | bytes 1572872 | tf_op jit(solution)/shard_map/ppermute | solution.py:36
  6.2 1.0 copy-start.1
  7.2 1.0 copy-start.2
  8.9 2.0 %collective-permute-start.2 = (f32[2,128,512]{2,1,0:T(8,128)S(1)}, f32[2,128,512]{2,1,0:T(8,128)S(1)}, u32[]{:S(2)}, u32[]{:S(2)}) collective-permute-start(f32[2,128,512]{2,1,0:T(8,128)S(1)} %get-tuple-element.28), channel_id=1, source_target_pairs={{1,0},{0,1},{3,2},{2,3},{5,4},{4,5},{7,6},{6,7},{9,8},{8,9},{11,10... | collective-permute-start | bytes 1572872 | tf_op jit(solution)/shard_map/ppermute | solution.py:36
  9.1 4.7 %collective-permute-start.1 = (bf16[128,512]{1,0:T(8,128)(2,1)S(1)}, bf16[128,512]{1,0:T(8,128)(2,1)S(1)}, u32[]{:S(2)}, u32[]{:S(2)}) collective-permute-start(bf16[128,512]{1,0:T(8,128)(2,1)S(1)} %get-tuple-element.26), channel_id=1, source_target_pairs={{2,0},{0,2},{3,1},{1,3},{6,4},{4,6},{7,5},{5,7},{10,8},{8,10},{11,... | collective-permute-start | bytes 393224 | tf_op jit(solution)/shard_map/ppermute | solution.py:36
  10.9 5.6 %collective-permute-start.3 = (bf16[128,512]{1,0:T(8,128)(2,1)S(1)}, bf16[128,512]{1,0:T(8,128)(2,1)S(1)}, u32[]{:S(2)}, u32[]{:S(2)}) collective-permute-start(bf16[128,512]{1,0:T(8,128)(2,1)S(1)} %get-tuple-element.30), channel_id=1, source_target_pairs={{2,0},{0,2},{3,1},{1,3},{6,4},{4,6},{7,5},{5,7},{10,8},{8,10},{11,... | collective-permute-start | bytes 393224 | tf_op jit(solution)/shard_map/ppermute | solution.py:36
  16.9 1.4 %copy-start = (bf16[16,528,128]{2,1,0:T(8,128)(2,1)}, bf16[16,528,128]{2,1,0:T(8,128)(2,1)S(1)}, u32[]{:S(2)}) copy-start(bf16[16,528,128]{2,1,0:T(8,128)(2,1)S(1)} %get-tuple-element.36) | copy-start | bytes 6488068
  18.3 36.4 %all-to-all-start = ((bf16[16,528,128]{2,1,0:T(8,128)(2,1)}), bf16[16,528,128]{2,1,0:T(8,128)(2,1)S(1)}, u32[]{:S(2)}, u32[]{:S(2)}) async-start(bf16[16,528,128]{2,1,0:T(8,128)(2,1)} %copy-done), calls=%async_computation | async-start | bytes 4325376 | tf_op jit(solution)/shard_map/all_to_all | solution.py:347
  23.3 7.8 %collective-permute-start.5 = (bf16[144,512]{1,0:T(8,128)(2,1)S(1)}, bf16[144,512]{1,0:T(8,128)(2,1)S(1)}, u32[]{:S(2)}, u32[]{:S(2)}) collective-permute-start(bf16[144,512]{1,0:T(8,128)(2,1)S(1)} %get-tuple-element.35.refs_0_), channel_id=1, source_target_pairs={{32,0},{64,32},{96,64},{128,96},{160,128},{192,160},{224,192},{0,2... | collective-permute-start | bytes 442376 | tf_op jit(solution)/shard_map/ppermute | solution.py:36
  28.9 5.5 %collective-permute-start.13 = (bf16[144,512]{1,0:T(8,128)(2,1)S(1)}, bf16[144,512]{1,0:T(8,128)(2,1)S(1)}, u32[]{:S(2)}, u32[]{:S(2)}) collective-permute-start(bf16[144,512]{1,0:T(8,128)(2,1)S(1)} %get-tuple-element.35.refs_0_), channel_id=1, source_target_pairs={{224,0},{0,32},{32,64},{64,96},{96,128},{128,160},{160,192},{192,2... | collective-permute-start | bytes 442376 | tf_op jit(solution)/shard_map/ppermute | solution.py:36
  31.0 5.2 %collective-permute-start.7 = (bf16[144,512]{1,0:T(8,128)(2,1)S(1)}, bf16[144,512]{1,0:T(8,128)(2,1)S(1)}, u32[]{:S(2)}, u32[]{:S(2)}) collective-permute-start(bf16[144,512]{1,0:T(8,128)(2,1)S(1)} %collective-permute-done.5.refs_2_), channel_id=1, source_target_pairs={{32,0},{64,32},{96,64},{128,96},{160,128},{192,160},{224,192},{0,2... | collective-permute-start | bytes 442376 | tf_op jit(solution)/shard_map/ppermute | solution.py:36
  34.4 9.6 %collective-permute-start.14 = (bf16[144,512]{1,0:T(8,128)(2,1)S(1)}, bf16[144,512]{1,0:T(8,128)(2,1)S(1)}, u32[]{:S(2)}, u32[]{:S(2)}) collective-permute-start(bf16[144,512]{1,0:T(8,128)(2,1)S(1)} %collective-permute-done.13.refs_14_), channel_id=1, source_target_pairs={{224,0},{0,32},{32,64},{64,96},{96,128},{128,160},{160,192},{192,2... | collective-permute-start | bytes 442376 | tf_op jit(solution)/shard_map/ppermute | solution.py:36
  36.2 7.8 %collective-permute-start.9 = (bf16[144,512]{1,0:T(8,128)(2,1)S(1)}, bf16[144,512]{1,0:T(8,128)(2,1)S(1)}, u32[]{:S(2)}, u32[]{:S(2)}) collective-permute-start(bf16[144,512]{1,0:T(8,128)(2,1)S(1)} %collective-permute-done.7.refs_4_), channel_id=1, source_target_pairs={{32,0},{64,32},{96,64},{128,96},{160,128},{192,160},{224,192},{0,2... | collective-permute-start | bytes 442376 | tf_op jit(solution)/shard_map/ppermute | solution.py:36
  39.6 7.1 %collective-permute-start.4 = (bf16[144,512]{1,0:T(8,128)(2,1)S(1)}, bf16[144,512]{1,0:T(8,128)(2,1)S(1)}, u32[]{:S(2)}, u32[]{:S(2)}) collective-permute-start(bf16[144,512]{1,0:T(8,128)(2,1)S(1)} %get-tuple-element.35.refs_0_), channel_id=1, source_target_pairs={{1,0},{0,1},{3,2},{2,3},{5,4},{4,5},{7,6},{6,7},{9,8},{8,9},{11,10... | collective-permute-start | bytes 442376 | tf_op jit(solution)/shard_map/ppermute | solution.py:36
  43.5 6.4 %collective-permute-start.18 = (bf16[144,512]{1,0:T(8,128)(2,1)S(1)}, bf16[144,512]{1,0:T(8,128)(2,1)S(1)}, u32[]{:S(2)}, u32[]{:S(2)}) collective-permute-start(bf16[144,512]{1,0:T(8,128)(2,1)S(1)} %collective-permute-done.13.refs_14_), channel_id=1, source_target_pairs={{1,0},{0,1},{3,2},{2,3},{5,4},{4,5},{7,6},{6,7},{9,8},{8,9},{11,10... | collective-permute-start | bytes 442376 | tf_op jit(solution)/shard_map/ppermute | solution.py:36
  43.5 6.5 %collective-permute-start.6 = (bf16[144,512]{1,0:T(8,128)(2,1)S(1)}, bf16[144,512]{1,0:T(8,128)(2,1)S(1)}, u32[]{:S(2)}, u32[]{:S(2)}) collective-permute-start(bf16[144,512]{1,0:T(8,128)(2,1)S(1)} %collective-permute-done.5.refs_2_), channel_id=1, source_target_pairs={{1,0},{0,1},{3,2},{2,3},{5,4},{4,5},{7,6},{6,7},{9,8},{8,9},{11,10... | collective-permute-start | bytes 442376 | tf_op jit(solution)/shard_map/ppermute | solution.py:36
  44.0 6.8 %collective-permute-start.15 = (bf16[144,512]{1,0:T(8,128)(2,1)S(1)}, bf16[144,512]{1,0:T(8,128)(2,1)}, u32[]{:S(2)}, u32[]{:S(2)}) collective-permute-start(bf16[144,512]{1,0:T(8,128)(2,1)S(1)} %collective-permute-done.14.refs_12_), channel_id=1, source_target_pairs={{224,0},{0,32},{32,64},{64,96},{96,128},{128,160},{160,192},{192,2... | collective-permute-start | bytes 442376 | tf_op jit(solution)/shard_map/ppermute | solution.py:36
  44.0 7.6 %collective-permute-start.11 = (bf16[144,512]{1,0:T(8,128)(2,1)S(1)}, bf16[144,512]{1,0:T(8,128)(2,1)}, u32[]{:S(2)}, u32[]{:S(2)}) collective-permute-start(bf16[144,512]{1,0:T(8,128)(2,1)S(1)} %collective-permute-done.9.refs_6_), channel_id=1, source_target_pairs={{32,0},{64,32},{96,64},{128,96},{160,128},{192,160},{224,192},{0,2... | collective-permute-start | bytes 442376 | tf_op jit(solution)/shard_map/ppermute | solution.py:36
  46.7 5.9 %collective-permute-start.17 = (bf16[144,512]{1,0:T(8,128)(2,1)S(1)}, bf16[144,512]{1,0:T(8,128)(2,1)}, u32[]{:S(2)}, u32[]{:S(2)}) collective-permute-start(bf16[144,512]{1,0:T(8,128)(2,1)S(1)} %collective-permute-done.14.refs_12_), channel_id=1, source_target_pairs={{1,0},{0,1},{3,2},{2,3},{5,4},{4,5},{7,6},{6,7},{9,8},{8,9},{11,10... | collective-permute-start | bytes 442376 | tf_op jit(solution)/shard_map/ppermute | solution.py:36
  49.9 2.8 %collective-permute-start.8 = (bf16[144,512]{1,0:T(8,128)(2,1)S(1)}, bf16[144,512]{1,0:T(8,128)(2,1)}, u32[]{:S(2)}, u32[]{:S(2)}) collective-permute-start(bf16[144,512]{1,0:T(8,128)(2,1)S(1)} %collective-permute-done.7.refs_4_), channel_id=1, source_target_pairs={{1,0},{0,1},{3,2},{2,3},{5,4},{4,5},{7,6},{6,7},{9,8},{8,9},{11,10... | collective-permute-start | bytes 442376 | tf_op jit(solution)/shard_map/ppermute | solution.py:36
  50.0 3.0 %collective-permute-start.10 = (bf16[144,512]{1,0:T(8,128)(2,1)S(1)}, bf16[144,512]{1,0:T(8,128)(2,1)}, u32[]{:S(2)}, u32[]{:S(2)}) collective-permute-start(bf16[144,512]{1,0:T(8,128)(2,1)S(1)} %collective-permute-done.9.refs_6_), channel_id=1, source_target_pairs={{1,0},{0,1},{3,2},{2,3},{5,4},{4,5},{7,6},{6,7},{9,8},{8,9},{11,10... | collective-permute-start | bytes 442376 | tf_op jit(solution)/shard_map/ppermute | solution.py:36
  50.8 2.1 %collective-permute-start.16 = (bf16[144,512]{1,0:T(8,128)(2,1)}, bf16[144,512]{1,0:T(8,128)(2,1)}, u32[]{:S(2)}, u32[]{:S(2)}) collective-permute-start(bf16[144,512]{1,0:T(8,128)(2,1)} %collective-permute-done.15.refs_10_), channel_id=1, source_target_pairs={{1,0},{0,1},{3,2},{2,3},{5,4},{4,5},{7,6},{6,7},{9,8},{8,9},{11,10... | collective-permute-start | bytes 442376 | tf_op jit(solution)/shard_map/ppermute | solution.py:36
  51.6 2.3 %collective-permute-start.12 = (bf16[144,512]{1,0:T(8,128)(2,1)}, bf16[144,512]{1,0:T(8,128)(2,1)}, u32[]{:S(2)}, u32[]{:S(2)}) collective-permute-start(bf16[144,512]{1,0:T(8,128)(2,1)} %collective-permute-done.11.refs_8_), channel_id=1, source_target_pairs={{1,0},{0,1},{3,2},{2,3},{5,4},{4,5},{7,6},{6,7},{9,8},{8,9},{11,10... | collective-permute-start | bytes 442376 | tf_op jit(solution)/shard_map/ppermute | solution.py:36
  84.3 6.4 %collective-permute-start.19 = (f32[8,128]{1,0:T(8,128)S(1)}, f32[8,128]{1,0:T(8,128)S(1)}, u32[]{:S(2)}, u32[]{:S(2)}) collective-permute-start(f32[8,128]{1,0:T(8,128)S(1)} %reduce_sum.9), channel_id=1, source_target_pairs={{1,0},{0,1},{3,2},{2,3},{5,4},{4,5},{7,6},{6,7},{9,8},{8,9},{11,10... | collective-permute-start | bytes 12296 | tf_op jit(solution)/shard_map/ppermute | solution.py:36
  87.2 9.9 %all-to-all-start.2 = ((f32[16,8,128]{2,1,0:T(8,128)}), f32[16,8,128]{2,1,0:T(8,128)S(1)}, u32[]{:S(2)}, u32[]{:S(2)}) async-start(f32[16,8,128]{2,1,0:T(8,128)} %get-tuple-element.38), calls=%async_computation.2 | async-start | bytes 131072 | tf_op jit(solution)/shard_map/all_to_all | solution.py:352
  90.7 6.4 %collective-permute-start.20 = (f32[8,128]{1,0:T(8,128)S(1)}, f32[8,128]{1,0:T(8,128)S(1)}, u32[]{:S(2)}, u32[]{:S(2)}) collective-permute-start(f32[8,128]{1,0:T(8,128)S(1)} %add.35.rows_ref), channel_id=1, source_target_pairs={{2,0},{0,2},{3,1},{1,3},{6,4},{4,6},{7,5},{5,7},{10,8},{8,10},{11,... | collective-permute-start | bytes 12296 | tf_op jit(solution)/shard_map/ppermute | solution.py:36
